TPU v7x, 256 devices: a whole 4x4x8 slice. The times are simulated.
256 devices in a mesh: blk: 16 (over x_lo, z), dp: 16 (over x_hi, y, core).
Axes of the slice: x: 4 (x_hi: 2, x_lo: 2; x = x_hi * 2 + x_lo), y: 4, z: 8, core: 2. Of those that a mesh axis runs over, the one named last changes fastest.
Arguments:
- user_emb: bfloat16 [65536, 256], P(('blk', 'dp')), may hold values from -6 to 6
- pos_feat: bfloat16 [65536, 256], P(('blk', 'dp')), may hold values from -6 to 6
- pos_id: int32 [65536], P(('blk', 'dp')), may hold values from 0 to 4095
- neg_feat: bfloat16 [131072, 256], P(('blk', 'dp')), may hold values from -6 to 6
- neg_id: int32 [131072], P(('blk', 'dp')), may hold values from 0 to 4095
- neg_bucket: int32 [131072], P(('blk', 'dp')), may hold values from 0 to 1023
- logq_table: float32 [1024], replicated, may hold values from -4 to 0
- w_in: bfloat16 [256, 2048], replicated, may hold values from -0.375 to 0.375
- w_out: bfloat16 [2048, 256], replicated, may hold values from -0.125 to 0.125
Outputs:
- user_grad: float32 [65536, 256], P(('blk', 'dp'))
- w_in_grad: float32 [256, 2048], replicated
- w_out_grad: float32 [2048, 256], replicated
All inputs are finite; a program needn't handle non-finite values.
Results may differ from a plain program's by a relative error of at most 0.008.
Values may be sent and summed in bfloat16 or wider, within the bound.
No kernel may reach another device: no remote copies, remote signals or barrier semaphores. Data moves between devices by JAX's collectives and lax.ppermute only.
A program may use at most 128 MiB of HBM per device.

v0:
```python
import math

import jax
import jax.numpy as jnp
from jax import lax
from jax.sharding import PartitionSpec as P

score_gain = 2.0


def tower(feat, w_in, w_out):
    hidden = jnp.maximum(jnp.dot(feat, w_in, preferred_element_type=jnp.float32), 0.0).astype(
        jnp.bfloat16
    )
    emb = jnp.dot(hidden, w_out, preferred_element_type=jnp.float32).astype(jnp.bfloat16)
    return (hidden, emb)


def tower_grads(feat, hidden, emb_grad, w_out):
    back = jnp.dot(emb_grad, w_out.T, preferred_element_type=jnp.float32)
    back = jnp.where(hidden > 0, back, 0.0).astype(jnp.bfloat16)
    return (
        jnp.dot(feat.T, back, preferred_element_type=jnp.float32),
        jnp.dot(hidden.T, emb_grad, preferred_element_type=jnp.float32),
    )


def on_device(user_emb, pos_feat, pos_id, neg_feat, neg_id, neg_bucket, logq_table, w_in, w_out):
    scale = score_gain / math.sqrt(user_emb.shape[1])
    neg_hidden, neg_emb = tower(neg_feat, w_in, w_out)
    pos_hidden, pos_emb = tower(pos_feat, w_in, w_out)
    pos_score = scale * jnp.einsum(
        "ue,ue->u", user_emb, pos_emb, preferred_element_type=jnp.float32
    )
    pos_exp = jnp.exp(pos_score)
    all_emb, all_ids, all_buckets = (
        lax.all_gather(neg_emb, "blk", axis=0, tiled=True),
        lax.all_gather(neg_id, "blk", axis=0, tiled=True),
        lax.all_gather(neg_bucket, "blk", axis=0, tiled=True),
    )
    all_bias = jnp.take(logq_table, all_buckets)
    scores = (
        scale * jnp.dot(user_emb, all_emb.T, preferred_element_type=jnp.float32) - all_bias[None, :]
    )
    kept = jnp.where(all_ids[None, :] != pos_id[:, None], jnp.exp(scores), jnp.float32(0.0))
    total = pos_exp + jnp.sum(kept, axis=1)
    prob = (kept / total[:, None]).astype(jnp.bfloat16)
    pos_prob = pos_exp / total
    user_grad = scale * jnp.dot(prob, all_emb, preferred_element_type=jnp.float32) + scale * (
        pos_prob - 1.0
    )[:, None] * pos_emb.astype(jnp.float32)
    neg_grad = lax.psum_scatter(
        scale * jnp.dot(prob.T, user_emb, preferred_element_type=jnp.float32),
        "blk",
        scatter_dimension=0,
        tiled=True,
    ).astype(jnp.bfloat16)
    pos_grad = (scale * (pos_prob - 1.0)[:, None] * user_emb.astype(jnp.float32)).astype(
        jnp.bfloat16
    )
    neg_in, neg_out = tower_grads(neg_feat, neg_hidden, neg_grad, w_out)
    pos_in, pos_out = tower_grads(pos_feat, pos_hidden, pos_grad, w_out)
    w_in_grad, w_out_grad = lax.psum((neg_in + pos_in, neg_out + pos_out), ("blk", "dp"))
    return (user_grad, w_in_grad, w_out_grad)


def solution(mesh):
    return jax.shard_map(
        on_device,
        mesh=mesh,
        in_specs=(
            P(("blk", "dp"), None),
            P(("blk", "dp"), None),
            P(("blk", "dp")),
            P(("blk", "dp"), None),
            P(("blk", "dp")),
            P(("blk", "dp")),
            P(),
            P(),
            P(),
        ),
        out_specs=(P(("blk", "dp"), None), P(), P()),
        check_vma=False,
    )
```

profile of v0, /device:TPU:1, one launch (start us, length us, event | category | flops | bytes accessed | tf_op | source)
XLA Modules:
  0.0 515.1 jit_solution(11676487283757321345)
XLA Ops:
  7.2 0.0 copy-start
  7.2 0.0 all-gather.4.cloned.1.call-start
  7.2 1.1 copy-done
  8.4 1.7 maximum_convert_fusion
  10.1 0.0 copy-start.3
  10.1 1.3 copy-done.3
  11.4 2.6 convolution_convert_fusion
  14.0 0.0 all-gather.4.cloned.1.call-update
  14.1 0.0 reduce-scatter.2.cloned.1.call-start
  14.1 31.1 %all-gather.1 = s32[16,1,512]{2,1,0:T(1,128)S(1)} all-gather(s32[1,1,512]{2,1,0:T(1,128)S(1)} %bitcast.33), channel_id=1, replica_groups=mesh['blk'=16,'dp'=16] {'blk'}, dimensions={0}, use_global_device_ids=true | all-gather | bytes 34816 | tf_op jit(solution)/shard_map/all_gather | solution.py:39
  45.3 32.9 %gather_fusion = f32[8192]{0:T(1024)S(1)} fusion(f32[1024]{0:T(1024)S(1)} %copy-done.1, s32[8192]{0:T(1024)S(1)} %fusion.22), kind=kCustom, calls=%fused_computation | custom fusion | bytes 98304 | tf_op jit(solution)/shard_map/jit(_take)/gather | solution.py:41
  78.2 23.9 %all-gather = s32[16,1,512]{2,1,0:T(1,128)S(1)} all-gather(s32[1,1,512]{2,1,0:T(1,128)S(1)} %bitcast.34), channel_id=1, replica_groups=mesh['blk'=16,'dp'=16] {'blk'}, dimensions={0}, use_global_device_ids=true | all-gather | bytes 34816 | tf_op jit(solution)/shard_map/all_gather | solution.py:38
  102.1 0.4 fusion.5
  102.5 1.0 copy-done.4
  103.5 1.2 fusion.13
  104.7 6.7 %fusion.28 = (f32[256]{0:T(256)S(1)}, f32[256,8192]{0,1:T(8,128)S(1)}) fusion(f32[8192]{0:T(1024)S(1)} %and_select_fusion, bf16[8192,256]{1,0:T(8,128)(2,1)} %all-gather.4.cloned.1.call-done, bf16[256,256]{1,0:T(8,128)(2,1)S(1)} %copy-done.6, s32[256]{0:T(256)S(1)} %copy-done.13, s32[8192]{0:T(1024)S(1)} %bitcast.32), kind=kOutput, calls=%fused_computation.43 | convolution fusion | flops 1084227328 | bytes 12781568 | tf_op jit(solution)/shard_map/dot_general | solution.py:43
  111.4 0.8 divide_convert_fusion
  112.2 1.9 copy-done.2
  114.1 4.5 convolution_multiply_fusion
  118.6 0.0 reduce-scatter.2.cloned.1.call-update
  118.6 0.0 all-reduce.3.cloned.1.call-start
  118.7 1.8 fusion.18
  120.5 3.7 fusion.7
  124.2 105.3 %reduce-scatter.2.cloned.1.call-done = f32[512,256]{1,0:T(8,128)} async-done(((f32[8192,256]{1,0:T(8,128)}), f32[512,256]{1,0:T(8,128)}) %reduce-scatter.2.cloned.1.call-update) | async-done | bytes 524304 | tf_op jit(solution)/shard_map/reduce_scatter | solution.py:52
  229.5 3.7 convolution_add_fusion
  233.3 5.3 %fusion.4 = f32[256,2048]{0,1:T(8,128)} fusion(f32[2048,256]{1,0:T(8,128)} %fusion.7, bf16[512,256]{1,0:T(8,128)(2,1)S(1)} %copy-done.10, bf16[512,2048]{1,0:T(8,128)(2,1)} %copy-done.3, bf16[2048,256]{1,0:T(8,128)(2,1)} %param.17, f32[512,256]{1,0:T(8,128)} %reduce-scatter.2.cloned.1.call-done), kind=kOutput, calls=%fused_computation.13 | convolution fusion | flops 1077542912 | bytes 8126464 | tf_op jit(solution)/shard_map/dot_general | solution.py:23
  238.6 0.0 all-reduce.3.cloned.1.call-update
  238.6 0.9 copy-done.9
  239.5 5.4 %fusion.8 = f32[256,256]{1,0:T(8,128)} fusion(bf16[256,8192]{0,1:T(8,128)(2,1)} %copy-done.2, bf16[8192,256]{1,0:T(8,128)(2,1)} %all-gather.4.cloned.1.call-done, f32[256,256]{1,0:T(8,128)S(1)} %copy-done.9, f32[256]{0:T(256)S(1)} %get-tuple-element.14), kind=kOutput, calls=%fused_computation.20 | convolution fusion | flops 1073938432 | bytes 8913920 | tf_op jit(solution)/shard_map/dot_general | solution.py:49
  245.0 259.2 %all-reduce.3.cloned.1.call-done = (f32[256,2048]{0,1:T(8,128)}, f32[2048,256]{1,0:T(8,128)}) async-done(((f32[256,2048]{0,1:T(8,128)}, f32[2048,256]{1,0:T(8,128)}), (f32[256,2048]{0,1:T(8,128)}, f32[2048,256]{1,0:T(8,128)})) %all-reduce.3.cloned.1.call-update) | async-done | bytes 4194320 | tf_op jit(solution)/shard_map/psum | solution.py:63
  504.2 3.0 copy.14
  507.2 1.3 copy.22
  (25 shorter events, 0.1 us)
Async XLA Ops:
  7.2 1.2 copy-start
  7.2 6.9 %copy-start.11 = (s32[512]{0:T(512)S(1)}, s32[512]{0:T(512)}, u32[]{:S(2)}) copy-start(s32[512]{0:T(512)} %param.14) | copy-start | bytes 6148
  7.2 38.0 %copy-start.1 = (f32[1024]{0:T(1024)S(1)}, f32[1024]{0:T(1024)}, u32[]{:S(2)}) copy-start(f32[1024]{0:T(1024)} %param.15) | copy-start | bytes 12292
  7.2 97.5 %all-gather.4.cloned.1.call-start = ((), (), s32[]{:S(2)}) async-start(), calls=%async_computation.1 | async-start | bytes 4456448 | tf_op jit(solution)/shard_map/all_gather | solution.py:37
  10.1 1.3 copy-start.3
  14.1 215.5 %reduce-scatter.2.cloned.1.call-start = ((), (), s32[]{:S(2)}) async-start(), calls=%async_computation.2 | async-start | bytes 8912896 | tf_op jit(solution)/shard_map/reduce_scatter | solution.py:52
  45.2 32.9 %copy-start.12 = (s32[512]{0:T(512)S(1)}, s32[512]{0:T(512)}, u32[]{:S(2)}) copy-start(s32[512]{0:T(512)} %param.13) | copy-start | bytes 6148
  45.2 56.9 %copy-start.8 = (bf16[256,256]{1,0:T(8,128)(2,1)S(1)}, bf16[256,256]{1,0:T(8,128)(2,1)}, u32[]{:S(2)}) copy-start(bf16[256,256]{1,0:T(8,128)(2,1)} %param.10) | copy-start | bytes 393220
  45.2 58.3 %copy-start.5 = (bf16[2048,256]{1,0:T(8,128)(2,1)S(1)}, bf16[2048,256]{1,0:T(8,128)(2,1)}, u32[]{:S(2)}) copy-start(bf16[2048,256]{1,0:T(8,128)(2,1)} %param.17) | copy-start | bytes 3145732
  45.2 58.3 %copy-start.6 = (bf16[256,256]{1,0:T(8,128)(2,1)S(1)}, bf16[256,256]{1,0:T(8,128)(2,1)}, u32[]{:S(2)}) copy-start(bf16[256,256]{1,0:T(8,128)(2,1)} %param.9) | copy-start | bytes 393220
  78.1 26.5 %copy-start.13 = (s32[256]{0:T(256)S(1)}, s32[256]{0:T(256)}, u32[]{:S(2)}) copy-start(s32[256]{0:T(256)} %param.11) | copy-start | bytes 3076
  102.5 1.0 copy-start.4
  112.2 1.9 copy-start.2
  118.6 385.6 %all-reduce.3.cloned.1.call-start = ((), (), s32[]{:S(2)}) async-start(), calls=%async_computation.3 | async-start | bytes 8388608 | tf_op jit(solution)/shard_map/psum | solution.py:63
  124.2 109.1 %copy-start.10 = (bf16[512,256]{1,0:T(8,128)(2,1)S(1)}, bf16[512,256]{1,0:T(8,128)(2,1)}, u32[]{:S(2)}) copy-start(bf16[512,256]{1,0:T(8,128)(2,1)} %param.12) | copy-start | bytes 786436
  238.6 0.9 copy-start.9
  504.2 3.0 copy-start.7
Sparse Core Ops, SparseCore 0:
  14.2 71.5 all-gather.3
  118.8 110.7 reduce-scatter.1
  238.7 265.4 all-reduce.2
where the time goes:
time: 516 us; the launch traced here: 515 us
  waiting for transfers between devices  365 us (71%)
  blocking collectives  55 us (11%)
  local copies, waits for them, and re-layouts  43.6 us (8%)
  matrix products  37.1 us (7%)
  between operations  13.9 us (3%)
    psum x1, waiting for transfers between devices, on_device(): lax.psum((neg_in + pos_in, neg_out + pos_out), ('blk', 'dp'))  259 us
    reduce_scatter x1, waiting for transfers between devices, on_device(): lax.psum_scatter(scale * jnp.dot(prob.T, user_emb, preferred_element_type...  105 us
    gather x1, local copies, waits for them, and re-layouts, on_device(): all_bias = jnp.take(logq_table, all_buckets)  32.9 us
    all_gather x1, blocking collectives, on_device(): lax.all_gather(neg_bucket, 'blk', axis=0, tiled=True)  31.1 us
    all_gather x1, blocking collectives, on_device(): lax.all_gather(neg_id, 'blk', axis=0, tiled=True)  23.9 us
    unnamed x30, local copies, waits for them, and re-layouts  10.7 us
  transfers between devices with their start and end apart: 3, of which 2 were waited for; matrix products, arithmetic and copies ran while one was open for 9% of the time, Pallas kernels for 0%

commit v1 on v0

v1 whole, which is shorter than its diff:
```python
import jax
import jax.numpy as jnp
from jax import lax
from jax.experimental import pallas as pl
from jax.experimental.pallas import tpu as pltpu
from jax.sharding import Mesh, PartitionSpec as P

AXES = ("x_lo", "z", "x_hi", "y", "core")
SIZES = (2, 8, 2, 4, 2)
BF, F32, I32 = jnp.bfloat16, jnp.float32, jnp.int32
SCALE = 0.125
SMALL = 2.0**-64
E, H, U, N = 256, 2048, 256, 512
NN = 2 * N
ROWS = NN + U
TILE = 256
CHUNKS = H // TILE
NZ = 8
VMEM_LIMIT = 40 * 1024 * 1024

NT = (((1,), (1,)), ((), ()))


def params():
    return pltpu.CompilerParams(vmem_limit_bytes=VMEM_LIMIT)


def cost(flops, nbytes, trans=0):
    return pl.CostEstimate(flops=int(flops), bytes_accessed=int(nbytes), transcendentals=int(trans))


def whole(shape):
    return pl.BlockSpec(shape, lambda *_: (0,) * len(shape))


def mm(a, b):
    return jnp.dot(a, b, preferred_element_type=F32)


def tower_kernel(own_ref, far_ref, pos_ref, w_in_ref, w_out_ref, hid_ref, emb_ref, embt_ref, pemb_ref, featt_ref, feat, acc):
    j = pl.program_id(0)

    @pl.when(j == 0)
    def _():
        feat[0:N] = own_ref[...]
        feat[N:NN] = far_ref[0:N]
        feat[NN:ROWS] = pos_ref[...]
        acc[...] = jnp.zeros_like(acc)
        featt_ref[...] = feat[...].T

    for m in range(ROWS // TILE):
        rows = slice(m * TILE, (m + 1) * TILE)
        hid = jnp.maximum(mm(feat[rows], w_in_ref[...]), 0.0).astype(BF)
        hid_ref[0, rows] = hid
        acc[rows] += mm(hid, w_out_ref[...])

    @pl.when(j == CHUNKS - 1)
    def _():
        emb = acc[0:NN].astype(BF)
        emb_ref[...] = emb
        embt_ref[...] = emb.T
        pemb_ref[...] = acc[NN:ROWS].astype(BF)


def tower(own, far, pos, w_in, w_out):
    return pl.pallas_call(
        tower_kernel,
        grid=(CHUNKS,),
        in_specs=[
            whole((N, E)),
            whole(far.shape),
            whole((U, E)),
            pl.BlockSpec((E, TILE), lambda j: (0, j)),
            pl.BlockSpec((TILE, E), lambda j: (j, 0)),
        ],
        out_specs=[
            pl.BlockSpec((1, ROWS, TILE), lambda j: (j, 0, 0)),
            whole((NN, E)),
            whole((E, NN)),
            whole((U, E)),
            whole((E, ROWS)),
        ],
        out_shape=[
            jax.ShapeDtypeStruct((CHUNKS, ROWS, TILE), BF),
            jax.ShapeDtypeStruct((NN, E), BF),
            jax.ShapeDtypeStruct((E, NN), BF),
            jax.ShapeDtypeStruct((U, E), BF),
            jax.ShapeDtypeStruct((E, ROWS), BF),
        ],
        scratch_shapes=[pltpu.VMEM((ROWS, E), BF), pltpu.VMEM((ROWS, E), F32)],
        compiler_params=params(),
        cost_estimate=cost(4 * ROWS * E * H, 10e6),
        name="tower",
    )(own, far, pos, w_in, w_out)


def score_kernel(s_ref, emb_ref, nid_ref, bias_ref, pexp_ref, *rest):
    users = rest[:NZ]
    tloc_ref, tin_ref, kept_ref, idb, bb, kf, kb, sems = rest[NZ:]
    z = s_ref[0]
    idb[...] = jnp.broadcast_to(nid_ref[...], (NN, U))
    bb[...] = jnp.broadcast_to(bias_ref[...], (NN, U))
    copies = []
    for k in range(NZ):
        u = users[k][0:U]
        tail = users[k][U : U + 16].astype(F32)
        pid = tail[0:1] * 64.0 + tail[1:2]
        total = jnp.zeros((8, U), F32)
        for m in range(NN // TILE):
            rows = slice(m * TILE, (m + 1) * TILE)
            e = (emb_ref[rows].astype(F32) * SCALE).astype(BF)
            sc = lax.dot_general(e, u, NT, preferred_element_type=F32) - bb[rows]
            kept = jnp.where(idb[rows] != pid, jnp.exp(sc), 0.0)
            kf[rows] = kept
            total = total + jnp.sum(kept.reshape(TILE // 8, 8, U), axis=0)
        t = jnp.sum(total, axis=0, keepdims=True)
        shrink = jnp.where(t > 1.0, SMALL, 1.0)
        inv = jnp.where(t > 0.0, 1.0 / (t * shrink), 0.0)
        for m in range(NN // TILE):
            rows = slice(m * TILE, (m + 1) * TILE)
            kb[k, rows] = ((kf[rows] * shrink) * inv).astype(BF)
        row = pl.ds(jnp.bitwise_xor(z, k), 1)
        tloc_ref[row, :] = t
        tin_ref[row, :] = t + pexp_ref[...] if k == 0 else t
        copy = pltpu.make_async_copy(kb.at[k], kept_ref.at[k], sems.at[k])
        copy.start()
        copies.append(copy)
    for copy in copies:
        copy.wait()


def score(scalars, emb, nid, bias, pexp, users):
    vm = pl.BlockSpec(memory_space=pltpu.VMEM)
    return pl.pallas_call(
        score_kernel,
        in_specs=[pl.BlockSpec(memory_space=pltpu.SMEM)] + [vm] * (4 + NZ),
        out_specs=[vm, vm, pl.BlockSpec(memory_space=pl.ANY)],
        out_shape=[
            jax.ShapeDtypeStruct((NZ, U), F32),
            jax.ShapeDtypeStruct((NZ, U), F32),
            jax.ShapeDtypeStruct((NZ, NN, U), BF),
        ],
        scratch_shapes=[
            pltpu.VMEM((NN, U), F32),
            pltpu.VMEM((NN, U), F32),
            pltpu.VMEM((NN, U), F32),
            pltpu.VMEM((NZ, NN, U), BF),
            pltpu.SemaphoreType.DMA((NZ,)),
        ],
        compiler_params=params(),
        cost_estimate=cost(2 * NZ * U * NN * E, 6e6, NZ * U * NN),
        name="score",
    )(scalars, emb, nid, bias, pexp, *users)


def grad_kernel(s_ref, tot_ref, tloc_ref, pexp_ref, embt_ref, pemb_ref, kept_ref, *rest):
    users = rest[:NZ]
    ug_ref, g_ref, pterm_ref, kb, wu, ratio, rel, sems = rest[NZ:]
    z = s_ref[0]
    copies = []
    for k in range(NZ):
        copy = pltpu.make_async_copy(kept_ref.at[k], kb.at[:, pl.ds(k * U, U)], sems.at[k])
        copy.start()
        copies.append(copy)
    tot = tot_ref[...]
    shrink = jnp.where(tot > 1.0, SMALL, 1.0)
    ratio[...] = (tloc_ref[...] * shrink) * (1.0 / (tot * shrink))
    own = tot_ref[pl.ds(z, 1), :]
    shrink = jnp.where(own > 1.0, SMALL, 1.0)
    pprob = (pexp_ref[...] * shrink) * (1.0 / (own * shrink))
    rel[...] = jnp.zeros_like(rel)
    for k in range(NZ):
        rel[k : k + 1] = SCALE * ratio[pl.ds(jnp.bitwise_xor(z, k), 1), :]
    rel[NZ : NZ + 1] = SCALE * (pprob - 1.0)
    cols = rel[...].T
    for k in range(NZ):
        wu[k * U : (k + 1) * U] = (users[k][0:U].astype(F32) * cols[:, k : k + 1]).astype(BF)
    coef = cols[:, NZ : NZ + 1]
    g_ref[NN:ROWS] = (users[0][0:U].astype(F32) * coef).astype(BF)
    pterm_ref[...] = pemb_ref[...].astype(F32) * coef
    for k in range(NZ):
        copies[k].wait()
        ut = mm(embt_ref[...], kb[:, k * U : (k + 1) * U])
        ug_ref[jnp.bitwise_xor(z, k)] = (ut * rel[k : k + 1]).astype(BF)
    for m in range(NN // TILE):
        rows = slice(m * TILE, (m + 1) * TILE)
        g_ref[rows] = mm(kb[rows], wu[...]).astype(BF)


def grads(scalars, tot, tloc, pexp, embt, pemb, kept, users):
    vm = pl.BlockSpec(memory_space=pltpu.VMEM)
    return pl.pallas_call(
        grad_kernel,
        in_specs=[pl.BlockSpec(memory_space=pltpu.SMEM)] + [vm] * 5 + [pl.BlockSpec(memory_space=pl.ANY)] + [vm] * NZ,
        out_specs=[vm, vm, vm],
        out_shape=[
            jax.ShapeDtypeStruct((NZ, E, U), BF),
            jax.ShapeDtypeStruct((ROWS, E), BF),
            jax.ShapeDtypeStruct((U, E), F32),
        ],
        scratch_shapes=[
            pltpu.VMEM((NN, NZ * U), BF),
            pltpu.VMEM((NZ * U, E), BF),
            pltpu.VMEM((NZ, U), F32),
            pltpu.VMEM((128, U), F32),
            pltpu.SemaphoreType.DMA((NZ,)),
        ],
        compiler_params=params(),
        cost_estimate=cost(4 * NZ * U * NN * E, 8e6),
        name="grads",
    )(scalars, tot, tloc, pexp, embt, pemb, kept, *users)


def back_kernel(s_ref, g_ref, featt_ref, w_out_ref, hid_ref, mine_ref, theirs_ref, gt):
    @pl.when(pl.program_id(0) == 0)
    def _():
        gt[...] = g_ref[...].T

    first, second, core = s_ref[1], s_ref[2], s_ref[3]
    hid = hid_ref[0]
    back = lax.dot_general(g_ref[...], w_out_ref[...], NT, preferred_element_type=F32)
    back = jnp.where(hid > 0, back, 0.0).astype(BF)
    w_in = mm(featt_ref[...], back)
    w_out = mm(gt[...], hid).T
    mine = jnp.where(core == 0, w_in, w_out).astype(BF)
    theirs = jnp.where(core == 0, w_out, w_in).astype(BF)
    for half in range(2):
        rows = slice(half * 128, (half + 1) * 128)
        mine_ref[0, jnp.bitwise_xor(second & 1, half)] = mine[rows]
        theirs_ref[0, jnp.bitwise_xor(first & 1, half)] = theirs[rows]


def place(outer, inner):
    def index(j, s):
        return (jnp.bitwise_xor(j // 2, s[outer]), jnp.bitwise_xor(j % 2, s[inner] // 2), 0, 0)

    return pl.BlockSpec((1, 2, 128, TILE), index)


def backward(scalars, g, featt, w_out, hid):
    return pl.pallas_call(
        back_kernel,
        grid_spec=pltpu.PrefetchScalarGridSpec(
            num_scalar_prefetch=1,
            grid=(CHUNKS,),
            in_specs=[
                whole((ROWS, E)),
                whole((E, ROWS)),
                pl.BlockSpec((TILE, E), lambda j, s: (j, 0)),
                pl.BlockSpec((1, ROWS, TILE), lambda j, s: (j, 0, 0)),
            ],
            out_specs=[place(1, 2), place(2, 1)],
            scratch_shapes=[pltpu.VMEM((E, ROWS), BF)],
        ),
        out_shape=[jax.ShapeDtypeStruct((4, 4, 128, TILE), BF)] * 2,
        compiler_params=params(),
        cost_estimate=cost(6 * ROWS * E * H, 10e6),
        name="backward",
    )(scalars, g, featt, w_out, hid)


def finish_kernel(s_ref, mine_ref, other_ref, w_in_ref, w_out_ref):
    first, second, core = s_ref[1], s_ref[2], s_ref[3]
    for half in range(2):
        rows = slice(half * 128, (half + 1) * 128)
        mine = mine_ref[0, jnp.bitwise_xor(second & 1, half)].astype(F32)
        other = other_ref[0, jnp.bitwise_xor(first & 1, half)].astype(F32)
        w_in_ref[rows] = jnp.where(core == 0, mine, other)
        w_out_ref[rows] = jnp.where(core == 0, other, mine)


def finish(scalars, mine, other):
    return pl.pallas_call(
        finish_kernel,
        grid_spec=pltpu.PrefetchScalarGridSpec(
            num_scalar_prefetch=1,
            grid=(CHUNKS,),
            in_specs=[place(1, 2), place(2, 1)],
            out_specs=[
                pl.BlockSpec((E, TILE), lambda j, s: (0, j)),
                pl.BlockSpec((TILE, E), lambda j, s: (j, 0)),
            ],
        ),
        out_shape=[jax.ShapeDtypeStruct((E, H), F32), jax.ShapeDtypeStruct((H, E), F32)],
        compiler_params=params(),
        cost_estimate=cost(0, 6e6),
        name="finish",
    )(scalars, mine, other)


def swap(x, axis, k):
    return lax.ppermute(x, axis, [(i, i ^ k) for i in range(SIZES[AXES.index(axis)])])


def device(x_lo, z, x_hi, y, core):
    return (((x_lo * 8 + z) * 2 + x_hi) * 4 + y) * 2 + core


def plane_swap(x, k, x_core):
    pairs = []
    for z in range(8):
        for xx in range(4):
            for y in range(4):
                for core in range(2):
                    to_x, to_y = (xx ^ k, y) if core == x_core else (xx, y ^ k)
                    pairs.append(
                        (device(xx & 1, z, xx >> 1, y, core), device(to_x & 1, z, to_x >> 1, to_y, core))
                    )
    return lax.ppermute(x, AXES, pairs)


def add(*terms):
    return sum(t.astype(F32) for t in terms)


def all_reduce(mine, theirs):
    half = add(mine, swap(theirs, "core", 1)).astype(BF)
    quarter = add(half[0], *[plane_swap(half[k], k, 0) for k in (1, 2, 3)]).astype(BF)
    part = add(quarter[0], *[plane_swap(quarter[k], k, 1) for k in (1, 2, 3)])
    for k in (1, 2, 4):
        part = part + swap(part.astype(BF), "z", k).astype(F32)
    part = part.astype(BF)
    quarter = jnp.stack([part] + [plane_swap(part, k, 1) for k in (1, 2, 3)])
    half = jnp.stack([quarter] + [plane_swap(quarter, k, 0) for k in (1, 2, 3)])
    return half, swap(half, "core", 1)


def digits(ids, base):
    ids = ids.reshape(-1, 256)
    return [(ids // base).astype(BF), (ids % base).astype(BF)]


def on_device(user_emb, pos_feat, pos_id, neg_feat, neg_id, neg_bucket, logq_table, w_in, w_out):
    x_lo, z, x_hi, y, core = [lax.axis_index(a) for a in AXES]
    xx = x_hi * 2 + x_lo
    scalars = jnp.stack([z, jnp.where(core == 0, xx, y), jnp.where(core == 0, y, xx), core]).astype(I32)

    near = jnp.concatenate(
        [neg_feat] + digits(neg_id, 64) + digits(neg_bucket, 32) + [jnp.zeros((8, E), BF)], axis=0
    )
    far = swap(near, "x_lo", 1)
    mine = jnp.concatenate([user_emb] + digits(pos_id, 64) + [jnp.zeros((14, E), BF)], axis=0)
    users = [mine] + [swap(mine, "z", k) for k in range(1, NZ)]

    tail = far[N : N + 8].astype(F32)
    far_id = tail[0:2] * 64.0 + tail[2:4]
    far_bucket = (tail[4:6] * 32.0 + tail[6:8]).astype(I32)
    nid = jnp.concatenate([neg_id.astype(F32), far_id.reshape(-1)]).reshape(NN, 1)
    bucket = jnp.concatenate([neg_bucket, far_bucket.reshape(-1)])
    bias = jnp.take(logq_table, bucket).reshape(NN, 1)

    hid, emb, embt, pemb, featt = tower(neg_feat, far, pos_feat, w_in, w_out)
    pos_score = SCALE * jnp.sum(user_emb.astype(F32) * pemb.astype(F32), axis=1)
    pexp = jnp.exp(pos_score).reshape(1, U)

    tloc, tot, kept = score(scalars, emb, nid, bias, pexp, users)
    for k in (1, 2, 4):
        tot = tot + swap(tot, "z", k)
    ug, g, pterm = grads(scalars, tot, tloc, pexp, embt, pemb, kept, users)
    user_sum = lax.psum_scatter(ug, "z", scatter_dimension=0, tiled=False)
    mine_g, theirs_g = backward(scalars, g, featt, w_out, hid)
    half, other = all_reduce(mine_g, theirs_g)
    w_in_grad, w_out_grad = finish(scalars, half, other)
    user_grad = user_sum.astype(F32).T + pterm
    return user_grad, w_in_grad, w_out_grad


def solution(mesh):
    rows = P(AXES, None)
    ids = P(AXES)
    return jax.shard_map(
        on_device,
        mesh=Mesh(mesh.devices.reshape(SIZES), AXES),
        in_specs=(rows, rows, ids, rows, ids, ids, P(), P(), P()),
        out_specs=(rows, P(), P()),
        check_vma=False,
    )
```

time: 516 us -> 176 us (0.34)
  waiting for transfers between devices: 365 us -> 46 us
  starting transfers between devices: 0.12 us -> 57.3 us
  blocking collectives: 55 us -> 0 us
  matrix products: 37.1 us -> 0 us
  Pallas kernels: 0 us -> 31.6 us
  local copies, waits for them, and re-layouts: 43.6 us -> 18.9 us
  other arithmetic: 0.83 us -> 7.45 us
    psum x1 -> x0, waiting for transfers between devices: 259 us -> none  [on_device(): lax.psum((neg_in + pos_in, neg_out + pos_out), ('blk', 'dp'))]
    reduce_scatter x1, waiting for transfers between devices: 105 us -> 0.01 us  [on_device(): user_sum = lax.psum_scatter(ug, 'z', scatter_dimension=0, tiled=False)]
    ppermute x0 -> x28, starting transfers between devices: none -> 57.3 us  [the longest x16 43.1 us: swap(): lax.ppermute(x, axis, [(i, i ^ k) for i in range(SIZES[AXES.index(axis)])])]
    all_gather x2 -> x0, blocking collectives: 55 us -> none  [the longest x1 31.1 us: on_device(): lax.all_gather(neg_bucket, 'blk', axis=0, tiled=True)]
    ppermute x0 -> x28, waiting for transfers between devices: none -> 45.9 us  [the longest x16 24.4 us: swap(): lax.ppermute(x, axis, [(i, i ^ k) for i in range(SIZES[AXES.index(axis)])])]
    dot_general x11 -> x0, matrix products: 37.1 us -> none  [the longest x2 9.04 us: tower_grads(): jnp.dot(feat.T, back, preferred_element_type=jnp.float32)]
    pallas_call x0 -> x5, Pallas kernels: none -> 31.6 us  [the longest x1 10.3 us: backward(): pl.pallas_call(back_kernel, grid_spec=pltpu.PrefetchScalarGridSpec(num_sc...]
    gather x1 -> x2, local copies, waits for them, and re-layouts: 32.9 us -> 5.55 us  [on_device(): bias = jnp.take(logq_table, bucket).reshape(NN, 1)]
  transfers between devices with their start and end apart: 3 -> 29, of which waited for: 2 -> 19; matrix products, arithmetic and copies ran while one was open for 9% -> 8% of each run, Pallas kernels for 0% -> 3%
where the time goes in v1:
time: 176 us
  starting transfers between devices  57.3 us (33%)
  waiting for transfers between devices  46 us (26%)
  Pallas kernels  31.6 us (18%)
  local copies, waits for them, and re-layouts  18.9 us (11%)
  between operations  14.4 us (8%)
  other arithmetic  7.45 us (4%)
    ppermute x16, starting transfers between devices, swap(): lax.ppermute(x, axis, [(i, i ^ k) for i in range(SIZES[AXES.index(axis)])])  43.1 us
    ppermute x16, waiting for transfers between devices, swap(): lax.ppermute(x, axis, [(i, i ^ k) for i in range(SIZES[AXES.index(axis)])])  24.4 us
    ppermute x12, waiting for transfers between devices, plane_swap(): return lax.ppermute(x, AXES, pairs)  21.6 us
    ppermute x12, starting transfers between devices, plane_swap(): return lax.ppermute(x, AXES, pairs)  14.3 us
    pallas_call x1, Pallas kernels, backward(): pl.pallas_call(back_kernel, grid_spec=pltpu.PrefetchScalarGridSpec(num_sc...  10.3 us
    unnamed x40, local copies, waits for them, and re-layouts  8.54 us
    pallas_call x1, Pallas kernels, grads(): pl.pallas_call(grad_kernel, in_specs=[pl.BlockSpec(memory_space=pltpu.SME...  6.2 us
    pallas_call x1, Pallas kernels, tower(): pl.pallas_call(tower_kernel, grid=(CHUNKS,), in_specs=[whole((N, E)), who...  5.73 us
  transfers between devices with their start and end apart: 29, of which 19 were waited for; matrix products, arithmetic and copies ran while one was open for 8% of the time, Pallas kernels for 3%

profile of v1, /device:TPU:1, one launch (start us, length us, event | category | flops | bytes accessed | tf_op | source)
XLA Modules:
  0.0 175.7 jit_solution(12760161078619702543)
XLA Ops:
  9.7 2.1 %collective-permute-start = (bf16[528,256]{1,0:T(8,128)(2,1)S(1)}, bf16[528,256]{1,0:T(8,128)(2,1)S(1)}, u32[]{:S(2)}, u32[]{:S(2)}) collective-permute-start(bf16[528,256]{1,0:T(8,128)(2,1)S(1)} %concatenate.47), channel_id=1, source_target_pairs={{0,128},{128,0},{1,129},{129,1},{2,130},{130,2},{3,131},{131,3},{4... | collective-permute-start | bytes 811016 | tf_op jit(solution)/shard_map/ppermute | solution.py:292
  13.6 5.7 %collective-permute-start.7 = (bf16[272,256]{1,0:T(8,128)(2,1)S(1)}, bf16[272,256]{1,0:T(8,128)(2,1)S(1)}, u32[]{:S(2)}, u32[]{:S(2)}) collective-permute-start(bf16[272,256]{1,0:T(8,128)(2,1)S(1)} %maximum_maximum_fusion.rest_0_), channel_id=1, source_target_pairs={{0,112},{16,96},{32,80},{48,64},{64,48},{80,32},{96,16},{112,0},{1... | collective-permute-start | bytes 417800 | tf_op jit(solution)/shard_map/ppermute | solution.py:292
  19.8 3.5 %collective-permute-start.5 = (bf16[272,256]{1,0:T(8,128)(2,1)S(1)}, bf16[272,256]{1,0:T(8,128)(2,1)S(1)}, u32[]{:S(2)}, u32[]{:S(2)}) collective-permute-start(bf16[272,256]{1,0:T(8,128)(2,1)S(1)} %maximum_maximum_fusion.rest_0_), channel_id=1, source_target_pairs={{0,80},{16,64},{32,112},{48,96},{64,16},{80,0},{96,48},{112,32},{1... | collective-permute-start | bytes 417800 | tf_op jit(solution)/shard_map/ppermute | solution.py:292
  23.3 1.8 %collective-permute-start.4 = (bf16[272,256]{1,0:T(8,128)(2,1)S(1)}, bf16[272,256]{1,0:T(8,128)(2,1)S(1)}, u32[]{:S(2)}, u32[]{:S(2)}) collective-permute-start(bf16[272,256]{1,0:T(8,128)(2,1)S(1)} %maximum_maximum_fusion.rest_0_), channel_id=1, source_target_pairs={{0,64},{16,80},{32,96},{48,112},{64,0},{80,16},{96,32},{112,48},{1... | collective-permute-start | bytes 417800 | tf_op jit(solution)/shard_map/ppermute | solution.py:292
  29.8 4.5 %gather_fusion = f32[1024]{0:T(1024)S(1)} fusion(f32[1024]{0:T(1024)S(1)} %copy-done, s32[1024]{0:T(1024)S(1)} %broadcast_clamp_fusion), kind=kCustom, calls=%fused_computation | custom fusion | bytes 12288 | tf_op jit(solution)/shard_map/jit(_take)/gather | solution.py:350
  38.2 5.7 %tower.1 = (bf16[8,1280,256]{2,1,0:T(8,128)(2,1)S(1)}, bf16[1024,256]{1,0:T(8,128)(2,1)S(1)}, bf16[256,1024]{1,0:T(8,128)(2,1)S(1)}, bf16[256,256]{1,0:T(8,128)(2,1)S(1)}, bf16[256,1280]{1,0:T(8,128)(2,1)S(1)}) custom-call(bf16[512,256]{1,0:T(8,128)(2,1)S(1)} %copy-done.1, bf16[528,256]{1,0:T(8,128)(2,1)S(1)} %collective-permute-done.far_ref, ...), custom_call_target="tpu_custom_call" | custom-call | flops 2684354560 | bytes 10000000 | tf_op jit(solution)/shard_map/tower/pallas_call | solution.py:66
  45.5 2.3 %copy-done.12 = bf16[8,1280,256]{2,1,0:T(8,128)(2,1)} copy-done((bf16[8,1280,256]{2,1,0:T(8,128)(2,1)}, bf16[8,1280,256]{2,1,0:T(8,128)(2,1)S(1)}, u32[]{:S(2)}) %copy-start.12) | copy-done | bytes 5242904
  49.2 1.9 %collective-permute-start.1 = (bf16[272,256]{1,0:T(8,128)(2,1)S(1)}, bf16[272,256]{1,0:T(8,128)(2,1)S(1)}, u32[]{:S(2)}, u32[]{:S(2)}) collective-permute-start(bf16[272,256]{1,0:T(8,128)(2,1)S(1)} %maximum_maximum_fusion.rest_0_), channel_id=1, source_target_pairs={{0,16},{16,0},{32,48},{48,32},{64,80},{80,64},{96,112},{112,96},{1... | collective-permute-start | bytes 417800 | tf_op jit(solution)/shard_map/ppermute | solution.py:292
  51.1 4.7 %collective-permute-done.2.rest_2_ = bf16[272,256]{1,0:T(8,128)(2,1)S(1)} collective-permute-done((bf16[272,256]{1,0:T(8,128)(2,1)S(1)}, bf16[272,256]{1,0:T(8,128)(2,1)S(1)}, u32[]{:S(2)}, u32[]{:S(2)}) %collective-permute-start.2) | collective-permute-done | bytes 139296 | tf_op jit(solution)/shard_map/ppermute | solution.py:292
  56.8 5.3 %score.1 = (f32[8,256]{1,0:T(8,128)S(1)}, f32[8,256]{1,0:T(8,128)S(1)}, bf16[8,1024,256]{2,1,0:T(8,128)(2,1)S(1)}) custom-call(s32[4]{0:T(128)S(1)} %pad_add_fusion.1.s_ref, bf16[1024,256]{1,0:T(8,128)(2,1)S(1)} %copy-done.9, f32[1024,1]{1,0:T(8,128)S(1)} %copy.31.nid_ref, f32[1024,1]{1,0:T(8,128)S(1)} %and_select_fusion.bias_ref, f32[1,256]{1,0:T(1,128)S(1)} %bitcast.55, ...), custom_call_target="tpu_custom_call" | custom-call | flops 1073741824 | bytes 6000000 | tf_op jit(solution)/shard_map/score/pallas_call | solution.py:134
  62.9 2.0 %collective-permute-done.8 = f32[8,256]{1,0:T(8,128)S(1)} collective-permute-done((f32[8,256]{1,0:T(8,128)S(1)}, f32[8,256]{1,0:T(8,128)S(1)}, u32[]{:S(2)}, u32[]{:S(2)}) %collective-permute-start.8) | collective-permute-done | bytes 8224 | tf_op jit(solution)/shard_map/ppermute | solution.py:292
  65.9 2.5 %collective-permute-done.9 = f32[8,256]{1,0:T(8,128)S(1)} collective-permute-done((f32[8,256]{1,0:T(8,128)S(1)}, f32[8,256]{1,0:T(8,128)S(1)}, u32[]{:S(2)}, u32[]{:S(2)}) %collective-permute-start.9) | collective-permute-done | bytes 8224 | tf_op jit(solution)/shard_map/ppermute | solution.py:292
  68.4 3.6 %collective-permute-start.10 = (f32[8,256]{1,0:T(8,128)S(1)}, f32[8,256]{1,0:T(8,128)S(1)}, u32[]{:S(2)}, u32[]{:S(2)}) collective-permute-start(f32[8,256]{1,0:T(8,128)S(1)} %add.104), channel_id=1, source_target_pairs={{0,64},{16,80},{32,96},{48,112},{64,0},{80,16},{96,32},{112,48},{1... | collective-permute-start | bytes 24584 | tf_op jit(solution)/shard_map/ppermute | solution.py:292
  72.0 2.8 %collective-permute-done.10 = f32[8,256]{1,0:T(8,128)S(1)} collective-permute-done((f32[8,256]{1,0:T(8,128)S(1)}, f32[8,256]{1,0:T(8,128)S(1)}, u32[]{:S(2)}, u32[]{:S(2)}) %collective-permute-start.10) | collective-permute-done | bytes 8224 | tf_op jit(solution)/shard_map/ppermute | solution.py:292
  75.7 6.2 %grads.1 = (bf16[8,256,256]{2,1,0:T(8,128)(2,1)S(1)}, bf16[1280,256]{1,0:T(8,128)(2,1)S(1)}, f32[256,256]{1,0:T(8,128)S(1)}) custom-call(s32[4]{0:T(128)S(1)} %pad_add_fusion.1.s_ref, f32[8,256]{1,0:T(8,128)S(1)} %add.105.tot_ref, f32[8,256]{1,0:T(8,128)S(1)} %get-tuple-element.21.tloc_ref, f32[1,256]{1,0:T(1,128)S(1)} %bitcast.56, ...), custom_call_target="tpu_custom_call" | custom-call | flops 2147483648 | bytes 8000000 | tf_op jit(solution)/shard_map/grads/pallas_call | solution.py:192
  81.9 10.3 %backward.1 = (bf16[4,4,128,256]{3,2,1,0:T(8,128)(2,1)S(1)}, bf16[4,4,128,256]{3,2,1,0:T(8,128)(2,1)S(1)}) custom-call(s32[4]{0:T(128)S(1)} %pad_add_fusion.1.s_ref, bf16[1280,256]{1,0:T(8,128)(2,1)S(1)} %get-tuple-element.26.g_ref, bf16[256,1280]{1,0:T(8,128)(2,1)S(1)} %copy-done.15, bf16[2048,256]{1,0:T(8,128)(2,1)S(1)} %copy-done.4, ...), custom_call_target="tpu_custom_call" | custom-call | flops 4026531840 | bytes 10000000 | tf_op jit(solution)/shard_map/backward/pallas_call | solution.py:241
  92.2 6.4 %collective-permute-start.11 = (bf16[4,4,128,256]{3,2,1,0:T(8,128)(2,1)S(1)}, bf16[4,4,128,256]{3,2,1,0:T(8,128)(2,1)S(1)}, u32[]{:S(2)}, u32[]{:S(2)}) collective-permute-start(bf16[4,4,128,256]{3,2,1,0:T(8,128)(2,1)S(1)} %get-tuple-element.30), channel_id=1, source_target_pairs={{0,1},{1,0},{2,3},{3,2},{4,5},{5,4},{6,7},{7,6},{8,9},{9,8},{10,11... | collective-permute-start | bytes 3145736 | tf_op jit(solution)/shard_map/ppermute | solution.py:292
  98.6 2.3 %collective-permute-done.11 = bf16[4,4,128,256]{3,2,1,0:T(8,128)(2,1)S(1)} collective-permute-done((bf16[4,4,128,256]{3,2,1,0:T(8,128)(2,1)S(1)}, bf16[4,4,128,256]{3,2,1,0:T(8,128)(2,1)S(1)}, u32[]{:S(2)}, u32[]{:S(2)}) %collective-permute-start.11) | collective-permute-done | bytes 1048608 | tf_op jit(solution)/shard_map/ppermute | solution.py:292
  102.7 1.9 %collective-permute-start.14 = (bf16[4,128,256]{2,1,0:T(8,128)(2,1)S(1)}, bf16[4,128,256]{2,1,0:T(8,128)(2,1)S(1)}, u32[]{:S(2)}, u32[]{:S(2)}) collective-permute-start(bf16[4,128,256]{2,1,0:T(8,128)(2,1)S(1)} %get-tuple-element.38), channel_id=1, source_target_pairs={{0,136},{1,7},{2,138},{3,5},{4,140},{5,3},{6,142},{7,1},{128,8},{1... | collective-permute-start | bytes 786440 | tf_op jit(solution)/shard_map/ppermute | solution.py:309
  106.9 3.8 %collective-permute-done.14 = bf16[4,128,256]{2,1,0:T(8,128)(2,1)S(1)} collective-permute-done((bf16[4,128,256]{2,1,0:T(8,128)(2,1)S(1)}, bf16[4,128,256]{2,1,0:T(8,128)(2,1)S(1)}, u32[]{:S(2)}, u32[]{:S(2)}) %collective-permute-start.14) | collective-permute-done | bytes 262176 | tf_op jit(solution)/shard_map/ppermute | solution.py:309
  112.4 2.5 %collective-permute-start.17 = (bf16[128,256]{1,0:T(8,128)(2,1)S(1)}, bf16[128,256]{1,0:T(8,128)(2,1)S(1)}, u32[]{:S(2)}, u32[]{:S(2)}) collective-permute-start(bf16[128,256]{1,0:T(8,128)(2,1)S(1)} %get-tuple-element.43), channel_id=1, source_target_pairs={{0,6},{1,137},{2,4},{3,139},{4,2},{5,141},{6,0},{7,143},{128,134},... | collective-permute-start | bytes 196616 | tf_op jit(solution)/shard_map/ppermute | solution.py:309
  116.8 2.7 %collective-permute-done.16 = bf16[128,256]{1,0:T(8,128)(2,1)S(1)} collective-permute-done((bf16[128,256]{1,0:T(8,128)(2,1)S(1)}, bf16[128,256]{1,0:T(8,128)(2,1)S(1)}, u32[]{:S(2)}, u32[]{:S(2)}) %collective-permute-start.16) | collective-permute-done | bytes 65568 | tf_op jit(solution)/shard_map/ppermute | solution.py:309
  121.0 1.8 %collective-permute-done.18 = bf16[128,256]{1,0:T(8,128)(2,1)S(1)} collective-permute-done((bf16[128,256]{1,0:T(8,128)(2,1)S(1)}, bf16[128,256]{1,0:T(8,128)(2,1)S(1)}, u32[]{:S(2)}, u32[]{:S(2)}) %collective-permute-start.18) | collective-permute-done | bytes 65568 | tf_op jit(solution)/shard_map/ppermute | solution.py:292
  123.3 4.1 %collective-permute-done.19 = bf16[128,256]{1,0:T(8,128)(2,1)S(1)} collective-permute-done((bf16[128,256]{1,0:T(8,128)(2,1)S(1)}, bf16[128,256]{1,0:T(8,128)(2,1)S(1)}, u32[]{:S(2)}, u32[]{:S(2)}) %collective-permute-start.19) | collective-permute-done | bytes 65568 | tf_op jit(solution)/shard_map/ppermute | solution.py:292
  127.5 4.2 %collective-permute-start.20 = (bf16[128,256]{1,0:T(8,128)(2,1)S(1)}, bf16[128,256]{1,0:T(8,128)(2,1)S(1)}, u32[]{:S(2)}, u32[]{:S(2)}) collective-permute-start(bf16[128,256]{1,0:T(8,128)(2,1)S(1)} %fusion.7), channel_id=1, source_target_pairs={{0,64},{16,80},{32,96},{48,112},{64,0},{80,16},{96,32},{112,48},{1... | collective-permute-start | bytes 196616 | tf_op jit(solution)/shard_map/ppermute | solution.py:292
  131.7 3.5 %collective-permute-done.20 = bf16[128,256]{1,0:T(8,128)(2,1)S(1)} collective-permute-done((bf16[128,256]{1,0:T(8,128)(2,1)S(1)}, bf16[128,256]{1,0:T(8,128)(2,1)S(1)}, u32[]{:S(2)}, u32[]{:S(2)}) %collective-permute-start.20) | collective-permute-done | bytes 65568 | tf_op jit(solution)/shard_map/ppermute | solution.py:292
  135.5 1.9 %collective-permute-start.22 = (bf16[128,256]{1,0:T(8,128)(2,1)S(1)}, bf16[128,256]{1,0:T(8,128)(2,1)S(1)}, u32[]{:S(2)}, u32[]{:S(2)}) collective-permute-start(bf16[128,256]{1,0:T(8,128)(2,1)S(1)} %add_convert_fusion.1), channel_id=1, source_target_pairs={{0,4},{1,9},{2,6},{3,11},{4,0},{5,13},{6,2},{7,15},{128,132},{129,... | collective-permute-start | bytes 196616 | tf_op jit(solution)/shard_map/ppermute | solution.py:309
  138.8 2.2 %collective-permute-done.23 = bf16[128,256]{1,0:T(8,128)(2,1)S(1)} collective-permute-done((bf16[128,256]{1,0:T(8,128)(2,1)S(1)}, bf16[128,256]{1,0:T(8,128)(2,1)S(1)}, u32[]{:S(2)}, u32[]{:S(2)}) %collective-permute-start.23) | collective-permute-done | bytes 65568 | tf_op jit(solution)/shard_map/ppermute | solution.py:309
  144.9 4.6 %collective-permute-done.25 = bf16[4,128,256]{2,1,0:T(8,128)(2,1)S(1)} collective-permute-done((bf16[4,128,256]{2,1,0:T(8,128)(2,1)S(1)}, bf16[4,128,256]{2,1,0:T(8,128)(2,1)S(1)}, u32[]{:S(2)}, u32[]{:S(2)}) %collective-permute-start.25) | collective-permute-done | bytes 262176 | tf_op jit(solution)/shard_map/ppermute | solution.py:309
  149.5 2.4 %collective-permute-done.24 = bf16[4,128,256]{2,1,0:T(8,128)(2,1)S(1)} collective-permute-done((bf16[4,128,256]{2,1,0:T(8,128)(2,1)S(1)}, bf16[4,128,256]{2,1,0:T(8,128)(2,1)S(1)}, u32[]{:S(2)}, u32[]{:S(2)}) %collective-permute-start.24) | collective-permute-done | bytes 262176 | tf_op jit(solution)/shard_map/ppermute | solution.py:309
  153.1 9.3 %collective-permute-start.27 = (bf16[4,4,128,256]{3,2,1,0:T(8,128)(2,1)S(1)}, bf16[4,4,128,256]{3,2,1,0:T(8,128)(2,1)S(1)}, u32[]{:S(2)}, u32[]{:S(2)}) collective-permute-start(bf16[4,4,128,256]{3,2,1,0:T(8,128)(2,1)S(1)} %pad_maximum_fusion.mine_ref), channel_id=1, source_target_pairs={{0,1},{1,0},{2,3},{3,2},{4,5},{5,4},{6,7},{7,6},{8,9},{9,8},{10,11... | collective-permute-start | bytes 3145736 | tf_op jit(solution)/shard_map/ppermute | solution.py:292
  164.8 4.1 %finish.1 = (f32[256,2048]{1,0:T(8,128)}, f32[2048,256]{1,0:T(8,128)}) custom-call(s32[4]{0:T(128)S(1)} %pad_add_fusion.1.s_ref, bf16[4,4,128,256]{3,2,1,0:T(8,128)(2,1)S(1)} %pad_maximum_fusion.mine_ref, bf16[4,4,128,256]{3,2,1,0:T(8,128)(2,1)S(1)} %collective-permute-done.27.other_ref), custom_call_target="tpu_custom_call" | custom-call | bytes 6000000 | tf_op jit(solution)/shard_map/finish/pallas_call | solution.py:273
  (116 shorter events, 38.8 us)
Async XLA Ops:
  7.2 22.7 %copy-start = (f32[1024]{0:T(1024)S(1)}, f32[1024]{0:T(1024)}, u32[]{:S(2)}) copy-start(f32[1024]{0:T(1024)} %param.15) | copy-start | bytes 12292
  7.2 155.3 %reduce-scatter.2.cloned.1.call-start = ((), (), s32[]{:S(2)}) async-start(), calls=%async_computation.1 | async-start | bytes 1179648 | tf_op jit(solution)/shard_map/reduce_scatter | solution.py:360
  9.7 16.2 %collective-permute-start = (bf16[528,256]{1,0:T(8,128)(2,1)S(1)}, bf16[528,256]{1,0:T(8,128)(2,1)S(1)}, u32[]{:S(2)}, u32[]{:S(2)}) collective-permute-start(bf16[528,256]{1,0:T(8,128)(2,1)S(1)} %concatenate.47), channel_id=1, source_target_pairs={{0,128},{128,0},{1,129},{129,1},{2,130},{130,2},{3,131},{131,3},{4... | collective-permute-start | bytes 811016 | tf_op jit(solution)/shard_map/ppermute | solution.py:292
  13.6 35.4 %collective-permute-start.7 = (bf16[272,256]{1,0:T(8,128)(2,1)S(1)}, bf16[272,256]{1,0:T(8,128)(2,1)S(1)}, u32[]{:S(2)}, u32[]{:S(2)}) collective-permute-start(bf16[272,256]{1,0:T(8,128)(2,1)S(1)} %maximum_maximum_fusion.rest_0_), channel_id=1, source_target_pairs={{0,112},{16,96},{32,80},{48,64},{64,48},{80,32},{96,16},{112,0},{1... | collective-permute-start | bytes 417800 | tf_op jit(solution)/shard_map/ppermute | solution.py:292
  19.3 29.9 %collective-permute-start.6 = (bf16[272,256]{1,0:T(8,128)(2,1)S(1)}, bf16[272,256]{1,0:T(8,128)(2,1)S(1)}, u32[]{:S(2)}, u32[]{:S(2)}) collective-permute-start(bf16[272,256]{1,0:T(8,128)(2,1)S(1)} %maximum_maximum_fusion.rest_0_), channel_id=1, source_target_pairs={{0,96},{16,112},{32,64},{48,80},{64,32},{80,48},{96,0},{112,16},{1... | collective-permute-start | bytes 417800 | tf_op jit(solution)/shard_map/ppermute | solution.py:292
  19.8 31.3 %collective-permute-start.5 = (bf16[272,256]{1,0:T(8,128)(2,1)S(1)}, bf16[272,256]{1,0:T(8,128)(2,1)S(1)}, u32[]{:S(2)}, u32[]{:S(2)}) collective-permute-start(bf16[272,256]{1,0:T(8,128)(2,1)S(1)} %maximum_maximum_fusion.rest_0_), channel_id=1, source_target_pairs={{0,80},{16,64},{32,112},{48,96},{64,16},{80,0},{96,48},{112,32},{1... | collective-permute-start | bytes 417800 | tf_op jit(solution)/shard_map/ppermute | solution.py:292
  23.3 27.8 %collective-permute-start.4 = (bf16[272,256]{1,0:T(8,128)(2,1)S(1)}, bf16[272,256]{1,0:T(8,128)(2,1)S(1)}, u32[]{:S(2)}, u32[]{:S(2)}) collective-permute-start(bf16[272,256]{1,0:T(8,128)(2,1)S(1)} %maximum_maximum_fusion.rest_0_), channel_id=1, source_target_pairs={{0,64},{16,80},{32,96},{48,112},{64,0},{80,16},{96,32},{112,48},{1... | collective-permute-start | bytes 417800 | tf_op jit(solution)/shard_map/ppermute | solution.py:292
  25.9 25.2 %collective-permute-start.3 = (bf16[272,256]{1,0:T(8,128)(2,1)S(1)}, bf16[272,256]{1,0:T(8,128)(2,1)S(1)}, u32[]{:S(2)}, u32[]{:S(2)}) collective-permute-start(bf16[272,256]{1,0:T(8,128)(2,1)S(1)} %maximum_maximum_fusion.rest_0_), channel_id=1, source_target_pairs={{0,48},{16,32},{32,16},{48,0},{64,112},{80,96},{96,80},{112,64},{1... | collective-permute-start | bytes 417800 | tf_op jit(solution)/shard_map/ppermute | solution.py:292
  48.7 26.1 %copy-start.11 = (bf16[256,1024]{1,0:T(8,128)(2,1)S(1)}, bf16[256,1024]{1,0:T(8,128)(2,1)}, u32[]{:S(2)}) copy-start(bf16[256,1024]{1,0:T(8,128)(2,1)} %copy-done.10) | copy-start | bytes 1572868
  49.1 6.7 %collective-permute-start.2 = (bf16[272,256]{1,0:T(8,128)(2,1)S(1)}, bf16[272,256]{1,0:T(8,128)(2,1)S(1)}, u32[]{:S(2)}, u32[]{:S(2)}) collective-permute-start(bf16[272,256]{1,0:T(8,128)(2,1)S(1)} %maximum_maximum_fusion.rest_0_), channel_id=1, source_target_pairs={{0,32},{16,48},{32,0},{48,16},{64,96},{80,112},{96,64},{112,80},{1... | collective-permute-start | bytes 417800 | tf_op jit(solution)/shard_map/ppermute | solution.py:292
  49.2 6.6 %collective-permute-start.1 = (bf16[272,256]{1,0:T(8,128)(2,1)S(1)}, bf16[272,256]{1,0:T(8,128)(2,1)S(1)}, u32[]{:S(2)}, u32[]{:S(2)}) collective-permute-start(bf16[272,256]{1,0:T(8,128)(2,1)S(1)} %maximum_maximum_fusion.rest_0_), channel_id=1, source_target_pairs={{0,16},{16,0},{32,48},{48,32},{64,80},{80,64},{96,112},{112,96},{1... | collective-permute-start | bytes 417800 | tf_op jit(solution)/shard_map/ppermute | solution.py:292
  51.1 23.7 %copy-start.5 = (bf16[272,256]{1,0:T(8,128)(2,1)}, bf16[272,256]{1,0:T(8,128)(2,1)S(1)}, u32[]{:S(2)}) copy-start(bf16[272,256]{1,0:T(8,128)(2,1)S(1)} %collective-permute-done.3.rest_3_) | copy-start | bytes 417796
  62.2 2.8 %collective-permute-start.8 = (f32[8,256]{1,0:T(8,128)S(1)}, f32[8,256]{1,0:T(8,128)S(1)}, u32[]{:S(2)}, u32[]{:S(2)}) collective-permute-start(f32[8,256]{1,0:T(8,128)S(1)} %get-tuple-element.20), channel_id=1, source_target_pairs={{0,16},{16,0},{32,48},{48,32},{64,80},{80,64},{96,112},{112,96},{1... | collective-permute-start | bytes 24584 | tf_op jit(solution)/shard_map/ppermute | solution.py:292
  64.9 3.4 %collective-permute-start.9 = (f32[8,256]{1,0:T(8,128)S(1)}, f32[8,256]{1,0:T(8,128)S(1)}, u32[]{:S(2)}, u32[]{:S(2)}) collective-permute-start(f32[8,256]{1,0:T(8,128)S(1)} %add.103), channel_id=1, source_target_pairs={{0,32},{16,48},{32,0},{48,16},{64,96},{80,112},{96,64},{112,80},{1... | collective-permute-start | bytes 24584 | tf_op jit(solution)/shard_map/ppermute | solution.py:292
  68.4 6.4 %collective-permute-start.10 = (f32[8,256]{1,0:T(8,128)S(1)}, f32[8,256]{1,0:T(8,128)S(1)}, u32[]{:S(2)}, u32[]{:S(2)}) collective-permute-start(f32[8,256]{1,0:T(8,128)S(1)} %add.104), channel_id=1, source_target_pairs={{0,64},{16,80},{32,96},{48,112},{64,0},{80,16},{96,32},{112,48},{1... | collective-permute-start | bytes 24584 | tf_op jit(solution)/shard_map/ppermute | solution.py:292
  92.2 8.7 %collective-permute-start.11 = (bf16[4,4,128,256]{3,2,1,0:T(8,128)(2,1)S(1)}, bf16[4,4,128,256]{3,2,1,0:T(8,128)(2,1)S(1)}, u32[]{:S(2)}, u32[]{:S(2)}) collective-permute-start(bf16[4,4,128,256]{3,2,1,0:T(8,128)(2,1)S(1)} %get-tuple-element.30), channel_id=1, source_target_pairs={{0,1},{1,0},{2,3},{3,2},{4,5},{5,4},{6,7},{7,6},{8,9},{9,8},{10,11... | collective-permute-start | bytes 3145736 | tf_op jit(solution)/shard_map/ppermute | solution.py:292
  101.3 5.6 %collective-permute-start.12 = (bf16[4,128,256]{2,1,0:T(8,128)(2,1)S(1)}, bf16[4,128,256]{2,1,0:T(8,128)(2,1)S(1)}, u32[]{:S(2)}, u32[]{:S(2)}) collective-permute-start(bf16[4,128,256]{2,1,0:T(8,128)(2,1)S(1)} %get-tuple-element.37), channel_id=1, source_target_pairs={{0,128},{1,3},{2,130},{3,1},{4,132},{5,7},{6,134},{7,5},{128,0},{1... | collective-permute-start | bytes 786440 | tf_op jit(solution)/shard_map/ppermute | solution.py:309
  102.7 8.0 %collective-permute-start.14 = (bf16[4,128,256]{2,1,0:T(8,128)(2,1)S(1)}, bf16[4,128,256]{2,1,0:T(8,128)(2,1)S(1)}, u32[]{:S(2)}, u32[]{:S(2)}) collective-permute-start(bf16[4,128,256]{2,1,0:T(8,128)(2,1)S(1)} %get-tuple-element.38), channel_id=1, source_target_pairs={{0,136},{1,7},{2,138},{3,5},{4,140},{5,3},{6,142},{7,1},{128,8},{1... | collective-permute-start | bytes 786440 | tf_op jit(solution)/shard_map/ppermute | solution.py:309
  104.6 7.6 %collective-permute-start.13 = (bf16[4,128,256]{2,1,0:T(8,128)(2,1)S(1)}, bf16[4,128,256]{2,1,0:T(8,128)(2,1)S(1)}, u32[]{:S(2)}, u32[]{:S(2)}) collective-permute-start(bf16[4,128,256]{2,1,0:T(8,128)(2,1)S(1)} %get-tuple-element.39), channel_id=1, source_target_pairs={{0,8},{1,5},{2,10},{3,7},{4,12},{5,1},{6,14},{7,3},{128,136},{129,... | collective-permute-start | bytes 786440 | tf_op jit(solution)/shard_map/ppermute | solution.py:309
  112.3 3.3 %collective-permute-start.15 = (bf16[128,256]{1,0:T(8,128)(2,1)S(1)}, bf16[128,256]{1,0:T(8,128)(2,1)S(1)}, u32[]{:S(2)}, u32[]{:S(2)}) collective-permute-start(bf16[128,256]{1,0:T(8,128)(2,1)S(1)} %get-tuple-element.42), channel_id=1, source_target_pairs={{0,2},{1,129},{2,0},{3,131},{4,6},{5,133},{6,4},{7,135},{128,130},... | collective-permute-start | bytes 196616 | tf_op jit(solution)/shard_map/ppermute | solution.py:309
  112.4 4.4 %collective-permute-start.17 = (bf16[128,256]{1,0:T(8,128)(2,1)S(1)}, bf16[128,256]{1,0:T(8,128)(2,1)S(1)}, u32[]{:S(2)}, u32[]{:S(2)}) collective-permute-start(bf16[128,256]{1,0:T(8,128)(2,1)S(1)} %get-tuple-element.43), channel_id=1, source_target_pairs={{0,6},{1,137},{2,4},{3,139},{4,2},{5,141},{6,0},{7,143},{128,134},... | collective-permute-start | bytes 196616 | tf_op jit(solution)/shard_map/ppermute | solution.py:309
  114.9 4.6 %collective-permute-start.16 = (bf16[128,256]{1,0:T(8,128)(2,1)S(1)}, bf16[128,256]{1,0:T(8,128)(2,1)S(1)}, u32[]{:S(2)}, u32[]{:S(2)}) collective-permute-start(bf16[128,256]{1,0:T(8,128)(2,1)S(1)} %get-tuple-element.44), channel_id=1, source_target_pairs={{0,4},{1,9},{2,6},{3,11},{4,0},{5,13},{6,2},{7,15},{128,132},{129,... | collective-permute-start | bytes 196616 | tf_op jit(solution)/shard_map/ppermute | solution.py:309
  119.6 3.2 %collective-permute-start.18 = (bf16[128,256]{1,0:T(8,128)(2,1)S(1)}, bf16[128,256]{1,0:T(8,128)(2,1)S(1)}, u32[]{:S(2)}, u32[]{:S(2)}) collective-permute-start(bf16[128,256]{1,0:T(8,128)(2,1)S(1)} %get-tuple-element.33), channel_id=1, source_target_pairs={{0,16},{16,0},{32,48},{48,32},{64,80},{80,64},{96,112},{112,96},{1... | collective-permute-start | bytes 196616 | tf_op jit(solution)/shard_map/ppermute | solution.py:292
  122.8 4.7 %collective-permute-start.19 = (bf16[128,256]{1,0:T(8,128)(2,1)S(1)}, bf16[128,256]{1,0:T(8,128)(2,1)S(1)}, u32[]{:S(2)}, u32[]{:S(2)}) collective-permute-start(bf16[128,256]{1,0:T(8,128)(2,1)S(1)} %fusion.6), channel_id=1, source_target_pairs={{0,32},{16,48},{32,0},{48,16},{64,96},{80,112},{96,64},{112,80},{1... | collective-permute-start | bytes 196616 | tf_op jit(solution)/shard_map/ppermute | solution.py:292
  127.5 7.7 %collective-permute-start.20 = (bf16[128,256]{1,0:T(8,128)(2,1)S(1)}, bf16[128,256]{1,0:T(8,128)(2,1)S(1)}, u32[]{:S(2)}, u32[]{:S(2)}) collective-permute-start(bf16[128,256]{1,0:T(8,128)(2,1)S(1)} %fusion.7), channel_id=1, source_target_pairs={{0,64},{16,80},{32,96},{48,112},{64,0},{80,16},{96,32},{112,48},{1... | collective-permute-start | bytes 196616 | tf_op jit(solution)/shard_map/ppermute | solution.py:292
  135.2 5.7 %collective-permute-start.23 = (bf16[128,256]{1,0:T(8,128)(2,1)S(1)}, bf16[128,256]{1,0:T(8,128)(2,1)S(1)}, u32[]{:S(2)}, u32[]{:S(2)}) collective-permute-start(bf16[128,256]{1,0:T(8,128)(2,1)S(1)} %add_convert_fusion.1), channel_id=1, source_target_pairs={{0,6},{1,137},{2,4},{3,139},{4,2},{5,141},{6,0},{7,143},{128,134},... | collective-permute-start | bytes 196616 | tf_op jit(solution)/shard_map/ppermute | solution.py:309
  135.5 5.4 %collective-permute-start.22 = (bf16[128,256]{1,0:T(8,128)(2,1)S(1)}, bf16[128,256]{1,0:T(8,128)(2,1)S(1)}, u32[]{:S(2)}, u32[]{:S(2)}) collective-permute-start(bf16[128,256]{1,0:T(8,128)(2,1)S(1)} %add_convert_fusion.1), channel_id=1, source_target_pairs={{0,4},{1,9},{2,6},{3,11},{4,0},{5,13},{6,2},{7,15},{128,132},{129,... | collective-permute-start | bytes 196616 | tf_op jit(solution)/shard_map/ppermute | solution.py:309
  137.4 4.1 %collective-permute-start.21 = (bf16[128,256]{1,0:T(8,128)(2,1)S(1)}, bf16[128,256]{1,0:T(8,128)(2,1)S(1)}, u32[]{:S(2)}, u32[]{:S(2)}) collective-permute-start(bf16[128,256]{1,0:T(8,128)(2,1)S(1)} %add_convert_fusion.1), channel_id=1, source_target_pairs={{0,2},{1,129},{2,0},{3,131},{4,6},{5,133},{6,4},{7,135},{128,130},... | collective-permute-start | bytes 196616 | tf_op jit(solution)/shard_map/ppermute | solution.py:309
  141.6 7.9 %collective-permute-start.25 = (bf16[4,128,256]{2,1,0:T(8,128)(2,1)S(1)}, bf16[4,128,256]{2,1,0:T(8,128)(2,1)S(1)}, u32[]{:S(2)}, u32[]{:S(2)}) collective-permute-start(bf16[4,128,256]{2,1,0:T(8,128)(2,1)S(1)} %get-tuple-element.41), channel_id=1, source_target_pairs={{0,8},{1,5},{2,10},{3,7},{4,12},{5,1},{6,14},{7,3},{128,136},{129,... | collective-permute-start | bytes 786440 | tf_op jit(solution)/shard_map/ppermute | solution.py:309
  142.7 9.2 %collective-permute-start.24 = (bf16[4,128,256]{2,1,0:T(8,128)(2,1)S(1)}, bf16[4,128,256]{2,1,0:T(8,128)(2,1)S(1)}, u32[]{:S(2)}, u32[]{:S(2)}) collective-permute-start(bf16[4,128,256]{2,1,0:T(8,128)(2,1)S(1)} %get-tuple-element.41), channel_id=1, source_target_pairs={{0,128},{1,3},{2,130},{3,1},{4,132},{5,7},{6,134},{7,5},{128,0},{1... | collective-permute-start | bytes 786440 | tf_op jit(solution)/shard_map/ppermute | solution.py:309
  143.4 9.6 %collective-permute-start.26 = (bf16[4,128,256]{2,1,0:T(8,128)(2,1)S(1)}, bf16[4,128,256]{2,1,0:T(8,128)(2,1)S(1)}, u32[]{:S(2)}, u32[]{:S(2)}) collective-permute-start(bf16[4,128,256]{2,1,0:T(8,128)(2,1)S(1)} %get-tuple-element.41), channel_id=1, source_target_pairs={{0,136},{1,7},{2,138},{3,5},{4,140},{5,3},{6,142},{7,1},{128,8},{1... | collective-permute-start | bytes 786440 | tf_op jit(solution)/shard_map/ppermute | solution.py:309
  153.1 11.6 %collective-permute-start.27 = (bf16[4,4,128,256]{3,2,1,0:T(8,128)(2,1)S(1)}, bf16[4,4,128,256]{3,2,1,0:T(8,128)(2,1)S(1)}, u32[]{:S(2)}, u32[]{:S(2)}) collective-permute-start(bf16[4,4,128,256]{3,2,1,0:T(8,128)(2,1)S(1)} %pad_maximum_fusion.mine_ref), channel_id=1, source_target_pairs={{0,1},{1,0},{2,3},{3,2},{4,5},{5,4},{6,7},{7,6},{8,9},{9,8},{10,11... | collective-permute-start | bytes 3145736 | tf_op jit(solution)/shard_map/ppermute | solution.py:292
  (16 other events, 51.7 us)
Sparse Core Ops, SparseCore 0:
  121.1 35.2 reduce-scatter.1

commit v2 on v1

v2 whole, which is shorter than its diff:
```python
import jax
import jax.numpy as jnp
from jax import lax
from jax.experimental import pallas as pl
from jax.experimental.pallas import tpu as pltpu
from jax.sharding import Mesh, PartitionSpec as P

AXES = ("x_lo", "z", "x_hi", "y", "core")
SIZES = (2, 8, 2, 4, 2)
BF, F32, I32 = jnp.bfloat16, jnp.float32, jnp.int32
SCALE = 0.125
SMALL = 2.0**-64
E, H, U, N = 256, 2048, 256, 512
NN = 2 * N
ROWS = NN + U
TILE = 256
CHUNKS = H // TILE
NZ = 8
EARLY = 3
VMEM_LIMIT = 24 * 1024 * 1024

WIDE = 512
NT = (((1,), (1,)), ((), ()))
TN = (((0,), (0,)), ((), ()))


def params(limit=VMEM_LIMIT):
    return pltpu.CompilerParams(vmem_limit_bytes=limit)


def cost(flops, nbytes, trans=0):
    return pl.CostEstimate(flops=int(flops), bytes_accessed=int(nbytes), transcendentals=int(trans))


def whole(shape):
    return pl.BlockSpec(shape, lambda *_: (0,) * len(shape))


def mm(a, b):
    return jnp.dot(a, b, preferred_element_type=F32)


def pack_kernel(user_ref, pid_ref, feat_ref, nid_ref, bucket_ref, mine_ref, near_ref):
    row = lax.broadcasted_iota(I32, (16, E), 0)

    def tail(digits):
        out = jnp.zeros((16, E), F32)
        for i, digit in enumerate(digits):
            out = jnp.where(row == i, digit.astype(F32), out)
        return out.astype(BF)

    def digits(ids, bits):
        ids = [ids[:, i : i + 256] for i in range(0, ids.shape[1], 256)]
        return [i >> bits for i in ids] + [i & (2**bits - 1) for i in ids]

    mine_ref[0:U] = user_ref[...]
    mine_ref[U : U + 16] = tail(digits(pid_ref[...], 6))
    near_ref[0:N] = feat_ref[...]
    near_ref[N : N + 16] = tail(digits(nid_ref[...], 6) + digits(bucket_ref[...], 5))


def pack(user_emb, pos_id, neg_feat, neg_id, neg_bucket):
    vm = pl.BlockSpec(memory_space=pltpu.VMEM)
    return pl.pallas_call(
        pack_kernel,
        in_specs=[vm] * 5,
        out_specs=[vm] * 2,
        out_shape=[jax.ShapeDtypeStruct((U + 16, E), BF), jax.ShapeDtypeStruct((N + 16, E), BF)],
        compiler_params=params(60 * 1024 * 1024),
        cost_estimate=cost(0, 1e6),
        name="pack",
    )(user_emb, pos_id.reshape(1, U), neg_feat, neg_id.reshape(1, N), neg_bucket.reshape(1, N))


def tower_kernel(near_ref, far_ref, pos_ref, mine_ref, w_in_ref, w_out_ref, table_ref, early_ref, *outs):
    del early_ref
    hid_ref, emb_ref, pemb_ref, feat_ref, nid_ref, bias_ref, pexp_ref = outs
    sources = [(near_ref, 0), (near_ref, 256), (far_ref, 0), (far_ref, 256), (pos_ref, 0)]
    lane = lax.broadcasted_iota(I32, (TILE, 128), 1).astype(F32)
    for m, (ref, start) in enumerate(sources):
        rows = slice(m * TILE, (m + 1) * TILE)
        feat = ref[start : start + TILE]
        feat_ref[rows] = feat
        hid = jnp.maximum(mm(feat, w_in_ref[...]), 0.0).astype(BF)
        hid_ref[rows] = hid
        emb = mm(hid, w_out_ref[...]).astype(BF)
        if m < 4:
            emb_ref[rows] = emb
        else:
            pemb_ref[...] = emb
            prod = mine_ref[0:U].astype(F32) * emb.astype(F32)
            prod = (prod[:, 0:128] + prod[:, 128:256]).T
            pexp_ref[...] = jnp.exp(SCALE * jnp.sum(prod, axis=0, keepdims=True))
    for side, ref in enumerate((near_ref, far_ref)):
        tail = jnp.concatenate([ref[N : N + 16].astype(F32), jnp.zeros((112, E), F32)], axis=0).T
        for block in range(2):
            rows = slice((2 * side + block) * TILE, (2 * side + block + 1) * TILE)
            nid = tail[:, block : block + 1] * 64.0 + tail[:, block + 2 : block + 3]
            nid_ref[rows] = jnp.broadcast_to(nid, (TILE, 128))
            bucket = tail[:, block + 4 : block + 5] * 32.0 + tail[:, block + 6 : block + 7]
            found = jnp.zeros((TILE, 128), F32)
            for b in range(8):
                found = found + jnp.where(bucket == lane + 128.0 * b, table_ref[b : b + 1], 0.0)
            bias_ref[rows] = jnp.broadcast_to(jnp.sum(found, axis=1, keepdims=True), (TILE, 128))


def tower(near, far, pos, mine, w_in, w_out, table, early):
    vm = pl.BlockSpec(memory_space=pltpu.VMEM)
    return pl.pallas_call(
        tower_kernel,
        in_specs=[vm] * 7 + [pl.BlockSpec(memory_space=pl.ANY)],
        out_specs=[vm] * 7,
        out_shape=[
            jax.ShapeDtypeStruct((ROWS, H), BF),
            jax.ShapeDtypeStruct((NN, E), BF),
            jax.ShapeDtypeStruct((U, E), BF),
            jax.ShapeDtypeStruct((ROWS, E), BF),
            jax.ShapeDtypeStruct((NN, 128), F32),
            jax.ShapeDtypeStruct((NN, 128), F32),
            jax.ShapeDtypeStruct((1, U), F32),
        ],
        compiler_params=params(),
        cost_estimate=cost(4 * ROWS * E * H, 10e6),
        name="tower",
    )(near, far, pos, mine, w_in, w_out, table, early)


def twice(x):
    return jnp.concatenate([x, x], axis=1)


def score_kernel(s_ref, emb_ref, nid_ref, bias_ref, pexp_ref, *rest):
    users = rest[:NZ]
    tloc_ref, tin_ref, kept_ref, kf = rest[NZ:]
    z = s_ref[0]
    for k in range(NZ):
        u = (users[k][0:U].astype(F32) * SCALE).astype(BF)
        tail = users[k][U : U + 16].astype(F32)
        pid = tail[0:1] * 64.0 + tail[1:2]
        total = jnp.zeros((8, U), F32)
        for m in range(NN // TILE):
            rows = slice(m * TILE, (m + 1) * TILE)
            sc = lax.dot_general(emb_ref[rows], u, NT, preferred_element_type=F32) - twice(bias_ref[rows])
            kept = jnp.where(twice(nid_ref[rows]) != pid, jnp.exp(sc), 0.0)
            kf[rows] = kept
            total = total + jnp.sum(kept.reshape(TILE // 8, 8, U), axis=0)
        t = jnp.sum(total, axis=0, keepdims=True)
        shrink = jnp.where(t > 1.0, SMALL, 1.0)
        inv = jnp.where(t > 0.0, 1.0 / (t * shrink), 0.0)
        for m in range(NN // TILE):
            rows = slice(m * TILE, (m + 1) * TILE)
            kept_ref[rows, k * U : (k + 1) * U] = ((kf[rows] * shrink) * inv).astype(BF)
        row = pl.ds(jnp.bitwise_xor(z, k), 1)
        tloc_ref[row, :] = t
        tin_ref[row, :] = t + pexp_ref[...] if k == 0 else t


def score(scalars, emb, nid, bias, pexp, users):
    vm = pl.BlockSpec(memory_space=pltpu.VMEM)
    return pl.pallas_call(
        score_kernel,
        in_specs=[pl.BlockSpec(memory_space=pltpu.SMEM)] + [vm] * (4 + NZ),
        out_specs=[vm] * 3,
        out_shape=[
            jax.ShapeDtypeStruct((NZ, U), F32),
            jax.ShapeDtypeStruct((NZ, U), F32),
            jax.ShapeDtypeStruct((NN, NZ * U), BF),
        ],
        scratch_shapes=[pltpu.VMEM((NN, U), F32)],
        compiler_params=params(),
        cost_estimate=cost(2 * NZ * U * NN * E, 6e6, NZ * U * NN),
        name="score",
    )(scalars, emb, nid, bias, pexp, *users)


def grad_kernel(s_ref, tot_ref, tloc_ref, pexp_ref, emb_ref, pemb_ref, kept_ref, *rest):
    users = rest[:NZ]
    ug_ref, g_ref, pterm_ref, wu, ratio, rel = rest[NZ:]
    z = s_ref[0]
    tot = tot_ref[...]
    shrink = jnp.where(tot > 1.0, SMALL, 1.0)
    ratio[...] = (tloc_ref[...] * shrink) * (1.0 / (tot * shrink))
    own = tot_ref[pl.ds(z, 1), :]
    shrink = jnp.where(own > 1.0, SMALL, 1.0)
    pprob = (pexp_ref[...] * shrink) * (1.0 / (own * shrink))
    rel[...] = jnp.zeros_like(rel)
    for k in range(NZ):
        rel[k : k + 1] = SCALE * ratio[pl.ds(jnp.bitwise_xor(z, k), 1), :]
    rel[NZ : NZ + 1] = SCALE * (pprob - 1.0)
    cols = rel[...].T
    for k in range(NZ):
        wu[k * U : (k + 1) * U] = (users[k][0:U].astype(F32) * cols[:, k : k + 1]).astype(BF)
    coef = cols[:, NZ : NZ + 1]
    g_ref[NN:ROWS] = (users[0][0:U].astype(F32) * coef).astype(BF)
    pterm_ref[...] = pemb_ref[...].astype(F32) * coef
    for k in range(NZ):
        ug = lax.dot_general(kept_ref[:, k * U : (k + 1) * U], emb_ref[...], TN, preferred_element_type=F32)
        ug_ref[jnp.bitwise_xor(z, k)] = (ug * cols[:, k : k + 1]).astype(BF)
    for m in range(NN // TILE):
        rows = slice(m * TILE, (m + 1) * TILE)
        g_ref[rows] = mm(kept_ref[rows], wu[...]).astype(BF)


def grads(scalars, tot, tloc, pexp, emb, pemb, kept, users):
    vm = pl.BlockSpec(memory_space=pltpu.VMEM)
    return pl.pallas_call(
        grad_kernel,
        in_specs=[pl.BlockSpec(memory_space=pltpu.SMEM)] + [vm] * (6 + NZ),
        out_specs=[vm, vm, vm],
        out_shape=[
            jax.ShapeDtypeStruct((NZ, U, E), BF),
            jax.ShapeDtypeStruct((ROWS, E), BF),
            jax.ShapeDtypeStruct((U, E), F32),
        ],
        scratch_shapes=[
            pltpu.VMEM((NZ * U, E), BF),
            pltpu.VMEM((NZ, U), F32),
            pltpu.VMEM((128, U), F32),
        ],
        compiler_params=params(),
        cost_estimate=cost(4 * NZ * U * NN * E, 8e6),
        name="grads",
    )(scalars, tot, tloc, pexp, emb, pemb, kept, *users)


def back_kernel(s_ref, g_ref, feat_ref, w_out_ref, hid_ref, mine_ref, theirs_ref):
    first, second, core = s_ref[1], s_ref[2], s_ref[3]
    for c in range(H // WIDE):
        cols = slice(c * WIDE, (c + 1) * WIDE)
        hid = hid_ref[:, cols]
        back = lax.dot_general(g_ref[...], w_out_ref[cols], NT, preferred_element_type=F32)
        back = jnp.where(hid > 0, back, 0.0).astype(BF)
        w_in = lax.dot_general(feat_ref[...], back, TN, preferred_element_type=F32)
        w_out = lax.dot_general(hid, g_ref[...], TN, preferred_element_type=F32)
        to_mine, to_theirs = jnp.bitwise_xor(first, c), jnp.bitwise_xor(second, c)
        for t in range(WIDE // TILE):
            a, b = w_in[:, t * TILE : (t + 1) * TILE], w_out[t * TILE : (t + 1) * TILE]
            mine = jnp.where(core == 0, a, b).astype(BF)
            theirs = jnp.where(core == 0, b, a).astype(BF)
            for half in range(2):
                rows = slice(half * 128, (half + 1) * 128)
                mine_ref[to_mine, jnp.bitwise_xor(second, 2 * t + half)] = mine[rows]
                theirs_ref[to_theirs, jnp.bitwise_xor(first, 2 * t + half)] = theirs[rows]


def backward(scalars, g, feat, w_out, hid):
    vm = pl.BlockSpec(memory_space=pltpu.VMEM)
    return pl.pallas_call(
        back_kernel,
        in_specs=[pl.BlockSpec(memory_space=pltpu.SMEM)] + [vm] * 4,
        out_specs=[vm, vm],
        out_shape=[jax.ShapeDtypeStruct((4, 4, 128, TILE), BF)] * 2,
        compiler_params=params(),
        cost_estimate=cost(6 * ROWS * E * H, 10e6),
        name="backward",
    )(scalars, g, feat, w_out, hid)


def finish_kernel(s_ref, mine_ref, other_ref, w_in_ref, w_out_ref):
    first, second, core = s_ref[1], s_ref[2], s_ref[3]
    for t in range(2):
        for half in range(2):
            rows = slice(half * 128, (half + 1) * 128)
            mine = mine_ref[0, jnp.bitwise_xor(second, 2 * t + half)].astype(F32)
            other = other_ref[0, jnp.bitwise_xor(first, 2 * t + half)].astype(F32)
            w_in_ref[rows, t * TILE : (t + 1) * TILE] = jnp.where(core == 0, mine, other)
            start = t * TILE + half * 128
            w_out_ref[start : start + 128] = jnp.where(core == 0, other, mine)


def finish(scalars, mine, other):
    def place(outer):
        return pl.BlockSpec((1, 4, 128, TILE), lambda j, s: (jnp.bitwise_xor(j, s[outer]), 0, 0, 0))

    return pl.pallas_call(
        finish_kernel,
        grid_spec=pltpu.PrefetchScalarGridSpec(
            num_scalar_prefetch=1,
            grid=(4,),
            in_specs=[place(1), place(2)],
            out_specs=[
                pl.BlockSpec((E, 512), lambda j, s: (0, j)),
                pl.BlockSpec((512, E), lambda j, s: (j, 0)),
            ],
        ),
        out_shape=[jax.ShapeDtypeStruct((E, H), F32), jax.ShapeDtypeStruct((H, E), F32)],
        compiler_params=params(),
        cost_estimate=cost(0, 6e6),
        name="finish",
    )(scalars, mine, other)


def swap(x, axis, k):
    return lax.ppermute(x, axis, [(i, i ^ k) for i in range(SIZES[AXES.index(axis)])])


def device(x_lo, z, x_hi, y, core):
    return (((x_lo * 8 + z) * 2 + x_hi) * 4 + y) * 2 + core


def plane_swap(x, k, x_core):
    pairs = []
    for z in range(8):
        for xx in range(4):
            for y in range(4):
                for core in range(2):
                    to_x, to_y = (xx ^ k, y) if core == x_core else (xx, y ^ k)
                    pairs.append(
                        (device(xx & 1, z, xx >> 1, y, core), device(to_x & 1, z, to_x >> 1, to_y, core))
                    )
    return lax.ppermute(x, AXES, pairs)


def add(*terms):
    return sum(t.astype(F32) for t in terms)


def sum_over_z(x, rounds, dtype):
    for ks in rounds:
        sent = x.astype(dtype)
        terms = [t.astype(F32) for t in [sent] + [swap(sent, "z", k) for k in ks]]
        while len(terms) > 1:
            terms = [a + b for a, b in zip(terms[::2], terms[1::2])]
        x = terms[0]
    return x


def all_reduce(mine, theirs):
    half = add(mine, swap(theirs, "core", 1)).astype(BF)
    quarter = add(half[0], *[plane_swap(half[k], k, 0) for k in (1, 2, 3)]).astype(BF)
    part = add(quarter[0], *[plane_swap(quarter[k], k, 1) for k in (1, 2, 3)])
    part = sum_over_z(part, ((1,), (2, 4, 6)), BF).astype(BF)
    quarter = jnp.stack([part] + [plane_swap(part, k, 1) for k in (1, 2, 3)])
    half = jnp.stack([quarter] + [plane_swap(quarter, k, 0) for k in (1, 2, 3)])
    return half, swap(half, "core", 1)


def on_device(user_emb, pos_feat, pos_id, neg_feat, neg_id, neg_bucket, logq_table, w_in, w_out):
    x_lo, z, x_hi, y, core = [lax.axis_index(a) for a in AXES]
    xx = x_hi * 2 + x_lo
    scalars = jnp.stack([z, jnp.where(core == 0, xx, y), jnp.where(core == 0, y, xx), core]).astype(I32)

    mine, near = pack(user_emb, pos_id, neg_feat, neg_id, neg_bucket)
    far = swap(near, "x_lo", 1)
    users = [mine] + [swap(mine, "z", k) for k in range(1, NZ)]

    hid, emb, pemb, feat, nid, bias, pexp = tower(
        near, far, pos_feat, mine, w_in, w_out, logq_table.reshape(8, 128), users[EARLY]
    )
    tloc, tot, kept = score(scalars, emb, nid, bias, pexp, users)
    tot = sum_over_z(tot, ((1, 6, 7), (2,)), F32)
    ug, g, pterm = grads(scalars, tot, tloc, pexp, emb, pemb, kept, users)
    user_sum = lax.psum_scatter(ug, "z", scatter_dimension=0, tiled=False)
    mine_g, theirs_g = backward(scalars, g, feat, w_out, hid)
    half, other = all_reduce(mine_g, theirs_g)
    w_in_grad, w_out_grad = finish(scalars, half, other)
    user_grad = user_sum.astype(F32) + pterm
    return user_grad, w_in_grad, w_out_grad


def solution(mesh):
    rows = P(AXES, None)
    ids = P(AXES)
    return jax.shard_map(
        on_device,
        mesh=Mesh(mesh.devices.reshape(SIZES), AXES),
        in_specs=(rows, rows, ids, rows, ids, ids, P(), P(), P()),
        out_specs=(rows, P(), P()),
        check_vma=False,
    )
```

time: 176 us -> 149 us (0.85)
  local copies, waits for them, and re-layouts: 18.9 us -> 5.97 us
  Pallas kernels: 31.6 us -> 21.7 us
  starting transfers between devices: 57.3 us -> 65.5 us
  waiting for transfers between devices: 46 us -> 38.4 us
  other arithmetic: 7.45 us -> 2.46 us
    ppermute x16 -> x18, waiting for transfers between devices: 24.4 us -> 15.8 us  [swap(): lax.ppermute(x, axis, [(i, i ^ k) for i in range(SIZES[AXES.index(axis)])])]
    ppermute x16 -> x18, starting transfers between devices: 43.1 us -> 51.1 us  [swap(): lax.ppermute(x, axis, [(i, i ^ k) for i in range(SIZES[AXES.index(axis)])])]
    pallas_call x2 -> x3, Pallas kernels: 16 us -> 10.4 us  [the longest x1 5.15 us: backward(): pl.pallas_call(back_kernel, in_specs=[pl.BlockSpec(memory_space=pltpu.SME...]
    gather x2 -> x0, local copies, waits for them, and re-layouts: 5.55 us -> none  [on_device(): bias = jnp.take(logq_table, bucket).reshape(NN, 1)]
    unnamed x40 -> x14, local copies, waits for them, and re-layouts: 8.54 us -> 5.9 us
    pallas_call x1, Pallas kernels: 6.2 us -> 4.15 us  [grads(): pl.pallas_call(grad_kernel, in_specs=[pl.BlockSpec(memory_space=pltpu.SME...]
  transfers between devices with their start and end apart: 29 -> 31, of which waited for: 19 -> 19; matrix products, arithmetic and copies ran while one was open for 8% -> 1% of each run, Pallas kernels for 3% -> 2%
where the time goes in v2:
time: 149 us; the launch traced here: 148 us
  starting transfers between devices  65.5 us (44%)
  waiting for transfers between devices  38.4 us (26%)
  Pallas kernels  21.7 us (15%)
  between operations  14.2 us (10%)
  local copies, waits for them, and re-layouts  5.97 us (4%)
  other arithmetic  2.46 us (2%)
    ppermute x18, starting transfers between devices, swap(): lax.ppermute(x, axis, [(i, i ^ k) for i in range(SIZES[AXES.index(axis)])])  51.1 us
    ppermute x12, waiting for transfers between devices, plane_swap(): return lax.ppermute(x, AXES, pairs)  22.6 us
    ppermute x18, waiting for transfers between devices, swap(): lax.ppermute(x, axis, [(i, i ^ k) for i in range(SIZES[AXES.index(axis)])])  15.8 us
    ppermute x12, starting transfers between devices, plane_swap(): return lax.ppermute(x, AXES, pairs)  14.3 us
    unnamed x14, local copies, waits for them, and re-layouts  5.9 us
    pallas_call x1, Pallas kernels, backward(): pl.pallas_call(back_kernel, in_specs=[pl.BlockSpec(memory_space=pltpu.SME...  5.15 us
    pallas_call x1, Pallas kernels, score(): pl.pallas_call(score_kernel, in_specs=[pl.BlockSpec(memory_space=pltpu.SM...  4.17 us
    pallas_call x1, Pallas kernels, grads(): pl.pallas_call(grad_kernel, in_specs=[pl.BlockSpec(memory_space=pltpu.SME...  4.15 us
  transfers between devices with their start and end apart: 31, of which 19 were waited for; matrix products, arithmetic and copies ran while one was open for 1% of the time, Pallas kernels for 2%

profile of v2, /device:TPU:1, one launch (start us, length us, event | category | flops | bytes accessed | tf_op | source)
XLA Modules:
  0.0 148.2 jit_solution(2068297043679536391)
XLA Ops:
  7.2 1.8 %pack.1 = (bf16[272,256]{1,0:T(8,128)(2,1)}, bf16[528,256]{1,0:T(8,128)(2,1)}) custom-call(bf16[256,256]{1,0:T(8,128)(2,1)} %user_ref.1, s32[1,256]{1,0:T(1,128)} %bitcast.52, bf16[512,256]{1,0:T(8,128)(2,1)} %feat_ref.1, s32[1,512]{1,0:T(1,128)} %bitcast.50, s32[1,512]{1,0:T(1,128)} %bitcast.51), custom_call_target="tpu_custom_call" | custom-call | bytes 1000000 | tf_op jit(solution)/shard_map/pack/pallas_call | solution.py:64
  9.0 2.0 %collective-permute-start = (bf16[528,256]{1,0:T(8,128)(2,1)}, bf16[528,256]{1,0:T(8,128)(2,1)S(1)}, u32[]{:S(2)}, u32[]{:S(2)}) collective-permute-start(bf16[528,256]{1,0:T(8,128)(2,1)} %get-tuple-element.22.near_ref), channel_id=1, source_target_pairs={{0,128},{128,0},{1,129},{129,1},{2,130},{130,2},{3,131},{131,3},{4... | collective-permute-start | bytes 811016 | tf_op jit(solution)/shard_map/ppermute | solution.py:294
  11.1 5.6 %collective-permute-start.7 = (bf16[272,256]{1,0:T(8,128)(2,1)}, bf16[272,256]{1,0:T(8,128)(2,1)S(1)}, u32[]{:S(2)}, u32[]{:S(2)}) collective-permute-start(bf16[272,256]{1,0:T(8,128)(2,1)} %get-tuple-element.23.mine_ref.rest_0_), channel_id=1, source_target_pairs={{0,112},{16,96},{32,80},{48,64},{64,48},{80,32},{96,16},{112,0},{1... | collective-permute-start | bytes 417800 | tf_op jit(solution)/shard_map/ppermute | solution.py:294
  16.6 1.6 %collective-permute-start.1 = (bf16[272,256]{1,0:T(8,128)(2,1)}, bf16[272,256]{1,0:T(8,128)(2,1)S(1)}, u32[]{:S(2)}, u32[]{:S(2)}) collective-permute-start(bf16[272,256]{1,0:T(8,128)(2,1)} %get-tuple-element.23.mine_ref.rest_0_), channel_id=1, source_target_pairs={{0,48},{16,32},{32,16},{48,0},{64,112},{80,96},{96,80},{112,64},{1... | collective-permute-start | bytes 417800 | tf_op jit(solution)/shard_map/ppermute | solution.py:294
  18.3 4.0 %collective-permute-start.5 = (bf16[272,256]{1,0:T(8,128)(2,1)}, bf16[272,256]{1,0:T(8,128)(2,1)S(1)}, u32[]{:S(2)}, u32[]{:S(2)}) collective-permute-start(bf16[272,256]{1,0:T(8,128)(2,1)} %get-tuple-element.23.mine_ref.rest_0_), channel_id=1, source_target_pairs={{0,80},{16,64},{32,112},{48,96},{64,16},{80,0},{96,48},{112,32},{1... | collective-permute-start | bytes 417800 | tf_op jit(solution)/shard_map/ppermute | solution.py:294
  23.1 2.8 %collective-permute-start.4 = (bf16[272,256]{1,0:T(8,128)(2,1)}, bf16[272,256]{1,0:T(8,128)(2,1)S(1)}, u32[]{:S(2)}, u32[]{:S(2)}) collective-permute-start(bf16[272,256]{1,0:T(8,128)(2,1)} %get-tuple-element.23.mine_ref.rest_0_), channel_id=1, source_target_pairs={{0,64},{16,80},{32,96},{48,112},{64,0},{80,16},{96,32},{112,48},{1... | collective-permute-start | bytes 417800 | tf_op jit(solution)/shard_map/ppermute | solution.py:294
  33.9 3.5 %tower.1 = (bf16[1280,2048]{1,0:T(8,128)(2,1)S(1)}, bf16[1024,256]{1,0:T(8,128)(2,1)S(1)}, bf16[256,256]{1,0:T(8,128)(2,1)S(1)}, bf16[1280,256]{1,0:T(8,128)(2,1...) custom-call(bf16[528,256]{1,0:T(8,128)(2,1)S(1)} %copy-done.3, ...), custom_call_target="tpu_custom_call" | custom-call | flops 2684354560 | bytes 10000000 | tf_op jit(solution)/shard_map/tower/pallas_call | solution.py:109
  37.4 4.2 %score.1 = (f32[8,256]{1,0:T(8,128)S(1)}, f32[8,256]{1,0:T(8,128)S(1)}, bf16[1024,2048]{1,0:T(8,128)(2,1)S(1)}) custom-call(s32[4]{0:T(128)S(1)} %pad_add_fusion.s_ref, bf16[1024,256]{1,0:T(8,128)(2,1)S(1)} %get-tuple-element.24.emb_ref, f32[1024,128]{1,0:T(8,128)S(1)} %get-tuple-element.25.nid_ref, f32[1024,128]{1,0:T(8,128)S(1)} %get-tuple-element.26.bias_ref, ...), custom_call_target="tpu_custom_call" | custom-call | flops 1073741824 | bytes 6000000 | tf_op jit(solution)/shard_map/score/pallas_call | solution.py:160
  41.6 2.2 %collective-permute-start.10 = (f32[8,256]{1,0:T(8,128)S(1)}, f32[8,256]{1,0:T(8,128)S(1)}, u32[]{:S(2)}, u32[]{:S(2)}) collective-permute-start(f32[8,256]{1,0:T(8,128)S(1)} %get-tuple-element.28), channel_id=1, source_target_pairs={{0,112},{16,96},{32,80},{48,64},{64,48},{80,32},{96,16},{112,0},{1... | collective-permute-start | bytes 24584 | tf_op jit(solution)/shard_map/ppermute | solution.py:294
  43.7 5.6 %collective-permute-start.9 = (f32[8,256]{1,0:T(8,128)S(1)}, f32[8,256]{1,0:T(8,128)S(1)}, u32[]{:S(2)}, u32[]{:S(2)}) collective-permute-start(f32[8,256]{1,0:T(8,128)S(1)} %get-tuple-element.28), channel_id=1, source_target_pairs={{0,96},{16,112},{32,64},{48,80},{64,32},{80,48},{96,0},{112,16},{1... | collective-permute-start | bytes 24584 | tf_op jit(solution)/shard_map/ppermute | solution.py:294
  52.5 2.8 %collective-permute-done.11 = f32[8,256]{1,0:T(8,128)S(1)} collective-permute-done((f32[8,256]{1,0:T(8,128)S(1)}, f32[8,256]{1,0:T(8,128)S(1)}, u32[]{:S(2)}, u32[]{:S(2)}) %collective-permute-start.11) | collective-permute-done | bytes 8224 | tf_op jit(solution)/shard_map/ppermute | solution.py:294
  55.3 4.1 %grads.1 = (bf16[8,256,256]{2,1,0:T(8,128)(2,1)}, bf16[1280,256]{1,0:T(8,128)(2,1)S(1)}, f32[256,256]{1,0:T(8,128)S(1)}) custom-call(s32[4]{0:T(128)S(1)} %pad_add_fusion.s_ref, f32[8,256]{1,0:T(8,128)S(1)} %add.57.tot_ref, f32[8,256]{1,0:T(8,128)S(1)} %get-tuple-element.29.tloc_ref, f32[1,256]{1,0:T(1,128)S(1)} %get-tuple-element.27.pexp_ref, ...), custom_call_target="tpu_custom_call" | custom-call | flops 2147483648 | bytes 8000000 | tf_op jit(solution)/shard_map/grads/pallas_call | solution.py:206
  59.4 5.1 %backward.1 = (bf16[4,4,128,256]{3,2,1,0:T(8,128)(2,1)S(1)}, bf16[4,4,128,256]{3,2,1,0:T(8,128)(2,1)S(1)}) custom-call(s32[4]{0:T(128)S(1)} %pad_add_fusion.s_ref, bf16[1280,256]{1,0:T(8,128)(2,1)S(1)} %get-tuple-element.34.g_ref, bf16[1280,256]{1,0:T(8,128)(2,1)S(1)} %get-tuple-element.35.feat_ref, bf16[2048,256]{1,0:T(8,128)(2,1)S(1)} %copy-done.2, ...), custom_call_target="tpu_custom_call" | custom-call | flops 4026531840 | bytes 10000000 | tf_op jit(solution)/shard_map/backward/pallas_call | solution.py:248
  64.6 10.0 %collective-permute-start.12 = (bf16[4,4,128,256]{3,2,1,0:T(8,128)(2,1)S(1)}, bf16[4,4,128,256]{3,2,1,0:T(8,128)(2,1)S(1)}, u32[]{:S(2)}, u32[]{:S(2)}) collective-permute-start(bf16[4,4,128,256]{3,2,1,0:T(8,128)(2,1)S(1)} %get-tuple-element.38), channel_id=1, source_target_pairs={{0,1},{1,0},{2,3},{3,2},{4,5},{5,4},{6,7},{7,6},{8,9},{9,8},{10,11... | collective-permute-start | bytes 3145736 | tf_op jit(solution)/shard_map/ppermute | solution.py:294
  74.6 2.3 %collective-permute-done.12 = bf16[4,4,128,256]{3,2,1,0:T(8,128)(2,1)S(1)} collective-permute-done((bf16[4,4,128,256]{3,2,1,0:T(8,128)(2,1)S(1)}, bf16[4,4,128,256]{3,2,1,0:T(8,128)(2,1)S(1)}, u32[]{:S(2)}, u32[]{:S(2)}) %collective-permute-start.12) | collective-permute-done | bytes 1048608 | tf_op jit(solution)/shard_map/ppermute | solution.py:294
  78.6 1.9 %collective-permute-start.15 = (bf16[4,128,256]{2,1,0:T(8,128)(2,1)S(1)}, bf16[4,128,256]{2,1,0:T(8,128)(2,1)S(1)}, u32[]{:S(2)}, u32[]{:S(2)}) collective-permute-start(bf16[4,128,256]{2,1,0:T(8,128)(2,1)S(1)} %get-tuple-element.42), channel_id=1, source_target_pairs={{0,136},{1,7},{2,138},{3,5},{4,140},{5,3},{6,142},{7,1},{128,8},{1... | collective-permute-start | bytes 786440 | tf_op jit(solution)/shard_map/ppermute | solution.py:311
  81.3 1.6 %collective-permute-done.13 = bf16[4,128,256]{2,1,0:T(8,128)(2,1)S(1)} collective-permute-done((bf16[4,128,256]{2,1,0:T(8,128)(2,1)S(1)}, bf16[4,128,256]{2,1,0:T(8,128)(2,1)S(1)}, u32[]{:S(2)}, u32[]{:S(2)}) %collective-permute-start.13) | collective-permute-done | bytes 262176 | tf_op jit(solution)/shard_map/ppermute | solution.py:311
  82.9 3.8 %collective-permute-done.15 = bf16[4,128,256]{2,1,0:T(8,128)(2,1)S(1)} collective-permute-done((bf16[4,128,256]{2,1,0:T(8,128)(2,1)S(1)}, bf16[4,128,256]{2,1,0:T(8,128)(2,1)S(1)}, u32[]{:S(2)}, u32[]{:S(2)}) %collective-permute-start.15) | collective-permute-done | bytes 262176 | tf_op jit(solution)/shard_map/ppermute | solution.py:311
  86.7 1.5 collective-permute-done.14
  88.4 2.5 %collective-permute-start.18 = (bf16[128,256]{1,0:T(8,128)(2,1)S(1)}, bf16[128,256]{1,0:T(8,128)(2,1)S(1)}, u32[]{:S(2)}, u32[]{:S(2)}) collective-permute-start(bf16[128,256]{1,0:T(8,128)(2,1)S(1)} %get-tuple-element.47), channel_id=1, source_target_pairs={{0,6},{1,137},{2,4},{3,139},{4,2},{5,141},{6,0},{7,143},{128,134},... | collective-permute-start | bytes 196616 | tf_op jit(solution)/shard_map/ppermute | solution.py:311
  92.8 2.7 %collective-permute-done.17 = bf16[128,256]{1,0:T(8,128)(2,1)S(1)} collective-permute-done((bf16[128,256]{1,0:T(8,128)(2,1)S(1)}, bf16[128,256]{1,0:T(8,128)(2,1)S(1)}, u32[]{:S(2)}, u32[]{:S(2)}) %collective-permute-start.17) | collective-permute-done | bytes 65568 | tf_op jit(solution)/shard_map/ppermute | solution.py:311
  96.5 2.3 %collective-permute-done.19 = bf16[128,256]{1,0:T(8,128)(2,1)S(1)} collective-permute-done((bf16[128,256]{1,0:T(8,128)(2,1)S(1)}, bf16[128,256]{1,0:T(8,128)(2,1)S(1)}, u32[]{:S(2)}, u32[]{:S(2)}) %collective-permute-start.19) | collective-permute-done | bytes 65568 | tf_op jit(solution)/shard_map/ppermute | solution.py:294
  98.8 2.0 %collective-permute-start.22 = (bf16[128,256]{1,0:T(8,128)(2,1)S(1)}, bf16[128,256]{1,0:T(8,128)(2,1)S(1)}, u32[]{:S(2)}, u32[]{:S(2)}) collective-permute-start(bf16[128,256]{1,0:T(8,128)(2,1)S(1)} %add_convert_fusion.2), channel_id=1, source_target_pairs={{0,96},{16,112},{32,64},{48,80},{64,32},{80,48},{96,0},{112,16},{1... | collective-permute-start | bytes 196616 | tf_op jit(solution)/shard_map/ppermute | solution.py:294
  100.8 2.5 %collective-permute-start.21 = (bf16[128,256]{1,0:T(8,128)(2,1)S(1)}, bf16[128,256]{1,0:T(8,128)(2,1)S(1)}, u32[]{:S(2)}, u32[]{:S(2)}) collective-permute-start(bf16[128,256]{1,0:T(8,128)(2,1)S(1)} %add_convert_fusion.2), channel_id=1, source_target_pairs={{0,64},{16,80},{32,96},{48,112},{64,0},{80,16},{96,32},{112,48},{1... | collective-permute-start | bytes 196616 | tf_op jit(solution)/shard_map/ppermute | solution.py:294
  104.5 3.4 %collective-permute-done.21 = bf16[128,256]{1,0:T(8,128)(2,1)S(1)} collective-permute-done((bf16[128,256]{1,0:T(8,128)(2,1)S(1)}, bf16[128,256]{1,0:T(8,128)(2,1)S(1)}, u32[]{:S(2)}, u32[]{:S(2)}) %collective-permute-start.21) | collective-permute-done | bytes 65568 | tf_op jit(solution)/shard_map/ppermute | solution.py:294
  110.4 2.4 %collective-permute-start.24 = (bf16[128,256]{1,0:T(8,128)(2,1)S(1)}, bf16[128,256]{1,0:T(8,128)(2,1)S(1)}, u32[]{:S(2)}, u32[]{:S(2)}) collective-permute-start(bf16[128,256]{1,0:T(8,128)(2,1)S(1)} %add_convert_fusion.1), channel_id=1, source_target_pairs={{0,4},{1,9},{2,6},{3,11},{4,0},{5,13},{6,2},{7,15},{128,132},{129,... | collective-permute-start | bytes 196616 | tf_op jit(solution)/shard_map/ppermute | solution.py:311
  116.3 2.9 %collective-permute-start.27 = (bf16[4,128,256]{2,1,0:T(8,128)(2,1)S(1)}, bf16[4,128,256]{2,1,0:T(8,128)(2,1)S(1)}, u32[]{:S(2)}, u32[]{:S(2)}) collective-permute-start(bf16[4,128,256]{2,1,0:T(8,128)(2,1)S(1)} %get-tuple-element.45), channel_id=1, source_target_pairs={{0,8},{1,5},{2,10},{3,7},{4,12},{5,1},{6,14},{7,3},{128,136},{129,... | collective-permute-start | bytes 786440 | tf_op jit(solution)/shard_map/ppermute | solution.py:311
  119.7 5.0 %collective-permute-done.27 = bf16[4,128,256]{2,1,0:T(8,128)(2,1)S(1)} collective-permute-done((bf16[4,128,256]{2,1,0:T(8,128)(2,1)S(1)}, bf16[4,128,256]{2,1,0:T(8,128)(2,1)S(1)}, u32[]{:S(2)}, u32[]{:S(2)}) %collective-permute-start.27) | collective-permute-done | bytes 262176 | tf_op jit(solution)/shard_map/ppermute | solution.py:311
  124.6 3.4 %collective-permute-done.26 = bf16[4,128,256]{2,1,0:T(8,128)(2,1)S(1)} collective-permute-done((bf16[4,128,256]{2,1,0:T(8,128)(2,1)S(1)}, bf16[4,128,256]{2,1,0:T(8,128)(2,1)S(1)}, u32[]{:S(2)}, u32[]{:S(2)}) %collective-permute-start.26) | collective-permute-done | bytes 262176 | tf_op jit(solution)/shard_map/ppermute | solution.py:311
  128.2 7.9 %collective-permute-start.29 = (bf16[4,4,128,256]{3,2,1,0:T(8,128)(2,1)S(1)}, bf16[4,4,128,256]{3,2,1,0:T(8,128)(2,1)S(1)}, u32[]{:S(2)}, u32[]{:S(2)}) collective-permute-start(bf16[4,4,128,256]{3,2,1,0:T(8,128)(2,1)S(1)} %pad_maximum_fusion.mine_ref), channel_id=1, source_target_pairs={{0,1},{1,0},{2,3},{3,2},{4,5},{5,4},{6,7},{7,6},{8,9},{9,8},{10,11... | collective-permute-start | bytes 3145736 | tf_op jit(solution)/shard_map/ppermute | solution.py:294
  136.1 1.6 %convert_add_fusion.1 = f32[256,256]{1,0:T(8,128)} fusion(f32[256,256]{1,0:T(8,128)S(1)} %get-tuple-element.33, bf16[1,256,256]{2,1,0:T(8,128)(2,1)} %reduce-scatter.2.cloned.1.call-done), kind=kLoop, calls=%fused_computation.11 | loop fusion | flops 131072 | bytes 655360 | tf_op jit(solution)/shard_map/add | solution.py:357
  138.4 3.0 %finish.1 = (f32[256,2048]{1,0:T(8,128)}, f32[2048,256]{1,0:T(8,128)}) custom-call(s32[4]{0:T(128)S(1)} %pad_add_fusion.s_ref, bf16[4,4,128,256]{3,2,1,0:T(8,128)(2,1)S(1)} %pad_maximum_fusion.mine_ref, bf16[4,4,128,256]{3,2,1,0:T(8,128)(2,1)S(1)} %collective-permute-done.29.other_ref), custom_call_target="tpu_custom_call" | custom-call | bytes 6000000 | tf_op jit(solution)/shard_map/finish/pallas_call | solution.py:275
  (64 shorter events, 26.2 us)
Async XLA Ops:
  7.2 128.9 %reduce-scatter.2.cloned.1.call-start = ((), (), s32[]{:S(2)}) async-start(), calls=%async_computation.1 | async-start | bytes 1179648 | tf_op jit(solution)/shard_map/reduce_scatter | solution.py:353
  9.0 17.7 %collective-permute-start = (bf16[528,256]{1,0:T(8,128)(2,1)}, bf16[528,256]{1,0:T(8,128)(2,1)S(1)}, u32[]{:S(2)}, u32[]{:S(2)}) collective-permute-start(bf16[528,256]{1,0:T(8,128)(2,1)} %get-tuple-element.22.near_ref), channel_id=1, source_target_pairs={{0,128},{128,0},{1,129},{129,1},{2,130},{130,2},{3,131},{131,3},{4... | collective-permute-start | bytes 811016 | tf_op jit(solution)/shard_map/ppermute | solution.py:294
  11.1 12.1 %collective-permute-start.7 = (bf16[272,256]{1,0:T(8,128)(2,1)}, bf16[272,256]{1,0:T(8,128)(2,1)S(1)}, u32[]{:S(2)}, u32[]{:S(2)}) collective-permute-start(bf16[272,256]{1,0:T(8,128)(2,1)} %get-tuple-element.23.mine_ref.rest_0_), channel_id=1, source_target_pairs={{0,112},{16,96},{32,80},{48,64},{64,48},{80,32},{96,16},{112,0},{1... | collective-permute-start | bytes 417800 | tf_op jit(solution)/shard_map/ppermute | solution.py:294
  16.6 9.3 %collective-permute-start.1 = (bf16[272,256]{1,0:T(8,128)(2,1)}, bf16[272,256]{1,0:T(8,128)(2,1)S(1)}, u32[]{:S(2)}, u32[]{:S(2)}) collective-permute-start(bf16[272,256]{1,0:T(8,128)(2,1)} %get-tuple-element.23.mine_ref.rest_0_), channel_id=1, source_target_pairs={{0,48},{16,32},{32,16},{48,0},{64,112},{80,96},{96,80},{112,64},{1... | collective-permute-start | bytes 417800 | tf_op jit(solution)/shard_map/ppermute | solution.py:294
  18.3 19.1 %collective-permute-start.6 = (bf16[272,256]{1,0:T(8,128)(2,1)}, bf16[272,256]{1,0:T(8,128)(2,1)S(1)}, u32[]{:S(2)}, u32[]{:S(2)}) collective-permute-start(bf16[272,256]{1,0:T(8,128)(2,1)} %get-tuple-element.23.mine_ref.rest_0_), channel_id=1, source_target_pairs={{0,96},{16,112},{32,64},{48,80},{64,32},{80,48},{96,0},{112,16},{1... | collective-permute-start | bytes 417800 | tf_op jit(solution)/shard_map/ppermute | solution.py:294
  18.3 19.1 %collective-permute-start.5 = (bf16[272,256]{1,0:T(8,128)(2,1)}, bf16[272,256]{1,0:T(8,128)(2,1)S(1)}, u32[]{:S(2)}, u32[]{:S(2)}) collective-permute-start(bf16[272,256]{1,0:T(8,128)(2,1)} %get-tuple-element.23.mine_ref.rest_0_), channel_id=1, source_target_pairs={{0,80},{16,64},{32,112},{48,96},{64,16},{80,0},{96,48},{112,32},{1... | collective-permute-start | bytes 417800 | tf_op jit(solution)/shard_map/ppermute | solution.py:294
  23.1 14.2 %collective-permute-start.4 = (bf16[272,256]{1,0:T(8,128)(2,1)}, bf16[272,256]{1,0:T(8,128)(2,1)S(1)}, u32[]{:S(2)}, u32[]{:S(2)}) collective-permute-start(bf16[272,256]{1,0:T(8,128)(2,1)} %get-tuple-element.23.mine_ref.rest_0_), channel_id=1, source_target_pairs={{0,64},{16,80},{32,96},{48,112},{64,0},{80,16},{96,32},{112,48},{1... | collective-permute-start | bytes 417800 | tf_op jit(solution)/shard_map/ppermute | solution.py:294
  25.9 11.4 %collective-permute-start.3 = (bf16[272,256]{1,0:T(8,128)(2,1)}, bf16[272,256]{1,0:T(8,128)(2,1)S(1)}, u32[]{:S(2)}, u32[]{:S(2)}) collective-permute-start(bf16[272,256]{1,0:T(8,128)(2,1)} %get-tuple-element.23.mine_ref.rest_0_), channel_id=1, source_target_pairs={{0,32},{16,48},{32,0},{48,16},{64,96},{80,112},{96,64},{112,80},{1... | collective-permute-start | bytes 417800 | tf_op jit(solution)/shard_map/ppermute | solution.py:294
  26.7 10.7 %collective-permute-start.2 = (bf16[272,256]{1,0:T(8,128)(2,1)}, bf16[272,256]{1,0:T(8,128)(2,1)S(1)}, u32[]{:S(2)}, u32[]{:S(2)}) collective-permute-start(bf16[272,256]{1,0:T(8,128)(2,1)} %get-tuple-element.23.mine_ref.rest_0_), channel_id=1, source_target_pairs={{0,16},{16,0},{32,48},{48,32},{64,80},{80,64},{96,112},{112,96},{1... | collective-permute-start | bytes 417800 | tf_op jit(solution)/shard_map/ppermute | solution.py:294
  41.6 7.8 %collective-permute-start.10 = (f32[8,256]{1,0:T(8,128)S(1)}, f32[8,256]{1,0:T(8,128)S(1)}, u32[]{:S(2)}, u32[]{:S(2)}) collective-permute-start(f32[8,256]{1,0:T(8,128)S(1)} %get-tuple-element.28), channel_id=1, source_target_pairs={{0,112},{16,96},{32,80},{48,64},{64,48},{80,32},{96,16},{112,0},{1... | collective-permute-start | bytes 24584 | tf_op jit(solution)/shard_map/ppermute | solution.py:294
  43.7 6.7 %collective-permute-start.9 = (f32[8,256]{1,0:T(8,128)S(1)}, f32[8,256]{1,0:T(8,128)S(1)}, u32[]{:S(2)}, u32[]{:S(2)}) collective-permute-start(f32[8,256]{1,0:T(8,128)S(1)} %get-tuple-element.28), channel_id=1, source_target_pairs={{0,96},{16,112},{32,64},{48,80},{64,32},{80,48},{96,0},{112,16},{1... | collective-permute-start | bytes 24584 | tf_op jit(solution)/shard_map/ppermute | solution.py:294
  49.3 2.5 %collective-permute-start.8 = (f32[8,256]{1,0:T(8,128)S(1)}, f32[8,256]{1,0:T(8,128)S(1)}, u32[]{:S(2)}, u32[]{:S(2)}) collective-permute-start(f32[8,256]{1,0:T(8,128)S(1)} %get-tuple-element.28), channel_id=1, source_target_pairs={{0,16},{16,0},{32,48},{48,32},{64,80},{80,64},{96,112},{112,96},{1... | collective-permute-start | bytes 24584 | tf_op jit(solution)/shard_map/ppermute | solution.py:294
  51.9 3.4 %collective-permute-start.11 = (f32[8,256]{1,0:T(8,128)S(1)}, f32[8,256]{1,0:T(8,128)S(1)}, u32[]{:S(2)}, u32[]{:S(2)}) collective-permute-start(f32[8,256]{1,0:T(8,128)S(1)} %add_add_fusion), channel_id=1, source_target_pairs={{0,32},{16,48},{32,0},{48,16},{64,96},{80,112},{96,64},{112,80},{1... | collective-permute-start | bytes 24584 | tf_op jit(solution)/shard_map/ppermute | solution.py:294
  55.3 4.2 %copy-start.2 = (bf16[2048,256]{1,0:T(8,128)(2,1)S(1)}, bf16[2048,256]{1,0:T(8,128)(2,1)}, u32[]{:S(2)}) copy-start(bf16[2048,256]{1,0:T(8,128)(2,1)} %w_out_ref.3) | copy-start | bytes 3145732
  64.6 12.3 %collective-permute-start.12 = (bf16[4,4,128,256]{3,2,1,0:T(8,128)(2,1)S(1)}, bf16[4,4,128,256]{3,2,1,0:T(8,128)(2,1)S(1)}, u32[]{:S(2)}, u32[]{:S(2)}) collective-permute-start(bf16[4,4,128,256]{3,2,1,0:T(8,128)(2,1)S(1)} %get-tuple-element.38), channel_id=1, source_target_pairs={{0,1},{1,0},{2,3},{3,2},{4,5},{5,4},{6,7},{7,6},{8,9},{9,8},{10,11... | collective-permute-start | bytes 3145736 | tf_op jit(solution)/shard_map/ppermute | solution.py:294
  77.2 5.6 %collective-permute-start.13 = (bf16[4,128,256]{2,1,0:T(8,128)(2,1)S(1)}, bf16[4,128,256]{2,1,0:T(8,128)(2,1)S(1)}, u32[]{:S(2)}, u32[]{:S(2)}) collective-permute-start(bf16[4,128,256]{2,1,0:T(8,128)(2,1)S(1)} %get-tuple-element.41), channel_id=1, source_target_pairs={{0,128},{1,3},{2,130},{3,1},{4,132},{5,7},{6,134},{7,5},{128,0},{1... | collective-permute-start | bytes 786440 | tf_op jit(solution)/shard_map/ppermute | solution.py:311
  78.6 8.0 %collective-permute-start.15 = (bf16[4,128,256]{2,1,0:T(8,128)(2,1)S(1)}, bf16[4,128,256]{2,1,0:T(8,128)(2,1)S(1)}, u32[]{:S(2)}, u32[]{:S(2)}) collective-permute-start(bf16[4,128,256]{2,1,0:T(8,128)(2,1)S(1)} %get-tuple-element.42), channel_id=1, source_target_pairs={{0,136},{1,7},{2,138},{3,5},{4,140},{5,3},{6,142},{7,1},{128,8},{1... | collective-permute-start | bytes 786440 | tf_op jit(solution)/shard_map/ppermute | solution.py:311
  80.5 7.6 %collective-permute-start.14 = (bf16[4,128,256]{2,1,0:T(8,128)(2,1)S(1)}, bf16[4,128,256]{2,1,0:T(8,128)(2,1)S(1)}, u32[]{:S(2)}, u32[]{:S(2)}) collective-permute-start(bf16[4,128,256]{2,1,0:T(8,128)(2,1)S(1)} %get-tuple-element.43), channel_id=1, source_target_pairs={{0,8},{1,5},{2,10},{3,7},{4,12},{5,1},{6,14},{7,3},{128,136},{129,... | collective-permute-start | bytes 786440 | tf_op jit(solution)/shard_map/ppermute | solution.py:311
  88.3 3.4 %collective-permute-start.16 = (bf16[128,256]{1,0:T(8,128)(2,1)S(1)}, bf16[128,256]{1,0:T(8,128)(2,1)S(1)}, u32[]{:S(2)}, u32[]{:S(2)}) collective-permute-start(bf16[128,256]{1,0:T(8,128)(2,1)S(1)} %get-tuple-element.46), channel_id=1, source_target_pairs={{0,2},{1,129},{2,0},{3,131},{4,6},{5,133},{6,4},{7,135},{128,130},... | collective-permute-start | bytes 196616 | tf_op jit(solution)/shard_map/ppermute | solution.py:311
  88.4 4.4 %collective-permute-start.18 = (bf16[128,256]{1,0:T(8,128)(2,1)S(1)}, bf16[128,256]{1,0:T(8,128)(2,1)S(1)}, u32[]{:S(2)}, u32[]{:S(2)}) collective-permute-start(bf16[128,256]{1,0:T(8,128)(2,1)S(1)} %get-tuple-element.47), channel_id=1, source_target_pairs={{0,6},{1,137},{2,4},{3,139},{4,2},{5,141},{6,0},{7,143},{128,134},... | collective-permute-start | bytes 196616 | tf_op jit(solution)/shard_map/ppermute | solution.py:311
  90.9 4.6 %collective-permute-start.17 = (bf16[128,256]{1,0:T(8,128)(2,1)S(1)}, bf16[128,256]{1,0:T(8,128)(2,1)S(1)}, u32[]{:S(2)}, u32[]{:S(2)}) collective-permute-start(bf16[128,256]{1,0:T(8,128)(2,1)S(1)} %get-tuple-element.48), channel_id=1, source_target_pairs={{0,4},{1,9},{2,6},{3,11},{4,0},{5,13},{6,2},{7,15},{128,132},{129,... | collective-permute-start | bytes 196616 | tf_op jit(solution)/shard_map/ppermute | solution.py:311
  95.5 3.2 %collective-permute-start.19 = (bf16[128,256]{1,0:T(8,128)(2,1)S(1)}, bf16[128,256]{1,0:T(8,128)(2,1)S(1)}, u32[]{:S(2)}, u32[]{:S(2)}) collective-permute-start(bf16[128,256]{1,0:T(8,128)(2,1)S(1)} %fusion.5), channel_id=1, source_target_pairs={{0,16},{16,0},{32,48},{48,32},{64,80},{80,64},{96,112},{112,96},{1... | collective-permute-start | bytes 196616 | tf_op jit(solution)/shard_map/ppermute | solution.py:294
  98.8 5.7 %collective-permute-start.22 = (bf16[128,256]{1,0:T(8,128)(2,1)S(1)}, bf16[128,256]{1,0:T(8,128)(2,1)S(1)}, u32[]{:S(2)}, u32[]{:S(2)}) collective-permute-start(bf16[128,256]{1,0:T(8,128)(2,1)S(1)} %add_convert_fusion.2), channel_id=1, source_target_pairs={{0,96},{16,112},{32,64},{48,80},{64,32},{80,48},{96,0},{112,16},{1... | collective-permute-start | bytes 196616 | tf_op jit(solution)/shard_map/ppermute | solution.py:294
  100.8 7.2 %collective-permute-start.21 = (bf16[128,256]{1,0:T(8,128)(2,1)S(1)}, bf16[128,256]{1,0:T(8,128)(2,1)S(1)}, u32[]{:S(2)}, u32[]{:S(2)}) collective-permute-start(bf16[128,256]{1,0:T(8,128)(2,1)S(1)} %add_convert_fusion.2), channel_id=1, source_target_pairs={{0,64},{16,80},{32,96},{48,112},{64,0},{80,16},{96,32},{112,48},{1... | collective-permute-start | bytes 196616 | tf_op jit(solution)/shard_map/ppermute | solution.py:294
  103.2 5.9 %collective-permute-start.20 = (bf16[128,256]{1,0:T(8,128)(2,1)S(1)}, bf16[128,256]{1,0:T(8,128)(2,1)S(1)}, u32[]{:S(2)}, u32[]{:S(2)}) collective-permute-start(bf16[128,256]{1,0:T(8,128)(2,1)S(1)} %add_convert_fusion.2), channel_id=1, source_target_pairs={{0,32},{16,48},{32,0},{48,16},{64,96},{80,112},{96,64},{112,80},{1... | collective-permute-start | bytes 196616 | tf_op jit(solution)/shard_map/ppermute | solution.py:294
  109.1 4.7 %collective-permute-start.25 = (bf16[128,256]{1,0:T(8,128)(2,1)S(1)}, bf16[128,256]{1,0:T(8,128)(2,1)S(1)}, u32[]{:S(2)}, u32[]{:S(2)}) collective-permute-start(bf16[128,256]{1,0:T(8,128)(2,1)S(1)} %add_convert_fusion.1), channel_id=1, source_target_pairs={{0,6},{1,137},{2,4},{3,139},{4,2},{5,141},{6,0},{7,143},{128,134},... | collective-permute-start | bytes 196616 | tf_op jit(solution)/shard_map/ppermute | solution.py:311
  110.4 4.9 %collective-permute-start.24 = (bf16[128,256]{1,0:T(8,128)(2,1)S(1)}, bf16[128,256]{1,0:T(8,128)(2,1)S(1)}, u32[]{:S(2)}, u32[]{:S(2)}) collective-permute-start(bf16[128,256]{1,0:T(8,128)(2,1)S(1)} %add_convert_fusion.1), channel_id=1, source_target_pairs={{0,4},{1,9},{2,6},{3,11},{4,0},{5,13},{6,2},{7,15},{128,132},{129,... | collective-permute-start | bytes 196616 | tf_op jit(solution)/shard_map/ppermute | solution.py:311
  112.8 3.5 %collective-permute-start.23 = (bf16[128,256]{1,0:T(8,128)(2,1)S(1)}, bf16[128,256]{1,0:T(8,128)(2,1)S(1)}, u32[]{:S(2)}, u32[]{:S(2)}) collective-permute-start(bf16[128,256]{1,0:T(8,128)(2,1)S(1)} %add_convert_fusion.1), channel_id=1, source_target_pairs={{0,2},{1,129},{2,0},{3,131},{4,6},{5,133},{6,4},{7,135},{128,130},... | collective-permute-start | bytes 196616 | tf_op jit(solution)/shard_map/ppermute | solution.py:311
  116.3 8.3 %collective-permute-start.27 = (bf16[4,128,256]{2,1,0:T(8,128)(2,1)S(1)}, bf16[4,128,256]{2,1,0:T(8,128)(2,1)S(1)}, u32[]{:S(2)}, u32[]{:S(2)}) collective-permute-start(bf16[4,128,256]{2,1,0:T(8,128)(2,1)S(1)} %get-tuple-element.45), channel_id=1, source_target_pairs={{0,8},{1,5},{2,10},{3,7},{4,12},{5,1},{6,14},{7,3},{128,136},{129,... | collective-permute-start | bytes 786440 | tf_op jit(solution)/shard_map/ppermute | solution.py:311
  119.2 8.8 %collective-permute-start.26 = (bf16[4,128,256]{2,1,0:T(8,128)(2,1)S(1)}, bf16[4,128,256]{2,1,0:T(8,128)(2,1)S(1)}, u32[]{:S(2)}, u32[]{:S(2)}) collective-permute-start(bf16[4,128,256]{2,1,0:T(8,128)(2,1)S(1)} %get-tuple-element.45), channel_id=1, source_target_pairs={{0,128},{1,3},{2,130},{3,1},{4,132},{5,7},{6,134},{7,5},{128,0},{1... | collective-permute-start | bytes 786440 | tf_op jit(solution)/shard_map/ppermute | solution.py:311
  119.7 8.4 %collective-permute-start.28 = (bf16[4,128,256]{2,1,0:T(8,128)(2,1)S(1)}, bf16[4,128,256]{2,1,0:T(8,128)(2,1)S(1)}, u32[]{:S(2)}, u32[]{:S(2)}) collective-permute-start(bf16[4,128,256]{2,1,0:T(8,128)(2,1)S(1)} %get-tuple-element.45), channel_id=1, source_target_pairs={{0,136},{1,7},{2,138},{3,5},{4,140},{5,3},{6,142},{7,1},{128,8},{1... | collective-permute-start | bytes 786440 | tf_op jit(solution)/shard_map/ppermute | solution.py:311
  128.2 10.2 %collective-permute-start.29 = (bf16[4,4,128,256]{3,2,1,0:T(8,128)(2,1)S(1)}, bf16[4,4,128,256]{3,2,1,0:T(8,128)(2,1)S(1)}, u32[]{:S(2)}, u32[]{:S(2)}) collective-permute-start(bf16[4,4,128,256]{3,2,1,0:T(8,128)(2,1)S(1)} %pad_maximum_fusion.mine_ref), channel_id=1, source_target_pairs={{0,1},{1,0},{2,3},{3,2},{4,5},{5,4},{6,7},{7,6},{8,9},{9,8},{10,11... | collective-permute-start | bytes 3145736 | tf_op jit(solution)/shard_map/ppermute | solution.py:294
  (6 other events, 5.9 us)
Sparse Core Ops, SparseCore 0:
  91.8 36.2 reduce-scatter.1

commit v3 on v2

--- a/solution.py
+++ b/solution.py
@@ -1,3 +1,5 @@
+import functools
+
 import jax
 import jax.numpy as jnp
 from jax import lax
@@ -16,7 +18,8 @@
 TILE = 256
 CHUNKS = H // TILE
 NZ = 8
-EARLY = 3
+OFFSETS = (0, -1, 1, -2, 2, -3, 3, 4)
+FIRST = 5
 VMEM_LIMIT = 24 * 1024 * 1024
 
 WIDE = 512
@@ -40,7 +43,20 @@
     return jnp.dot(a, b, preferred_element_type=F32)
 
 
-def pack_kernel(user_ref, pid_ref, feat_ref, nid_ref, bucket_ref, mine_ref, near_ref):
+def start(src, dst, sem):
+    copy = pltpu.make_async_copy(src, dst, sem)
+    copy.start()
+    return copy
+
+
+def pack_kernel(user_hbm, pid_hbm, feat_hbm, nid_hbm, bucket_hbm, mine_ref, near_ref, pid_ref, nid_ref, bucket_ref, sems):
+    copies = [
+        start(pid_hbm, pid_ref, sems.at[0]),
+        start(nid_hbm, nid_ref, sems.at[1]),
+        start(bucket_hbm, bucket_ref, sems.at[2]),
+        start(user_hbm, mine_ref.at[0:U], sems.at[3]),
+        start(feat_hbm, near_ref.at[0:N], sems.at[4]),
+    ]
     row = lax.broadcasted_iota(I32, (16, E), 0)
 
     def tail(digits):
@@ -53,44 +69,50 @@
         ids = [ids[:, i : i + 256] for i in range(0, ids.shape[1], 256)]
         return [i >> bits for i in ids] + [i & (2**bits - 1) for i in ids]
 
-    mine_ref[0:U] = user_ref[...]
+    for copy in copies[:3]:
+        copy.wait()
     mine_ref[U : U + 16] = tail(digits(pid_ref[...], 6))
-    near_ref[0:N] = feat_ref[...]
     near_ref[N : N + 16] = tail(digits(nid_ref[...], 6) + digits(bucket_ref[...], 5))
+    for copy in copies[3:]:
+        copy.wait()
 
 
 def pack(user_emb, pos_id, neg_feat, neg_id, neg_bucket):
     vm = pl.BlockSpec(memory_space=pltpu.VMEM)
     return pl.pallas_call(
         pack_kernel,
-        in_specs=[vm] * 5,
+        in_specs=[pl.BlockSpec(memory_space=pltpu.HBM)] * 5,
         out_specs=[vm] * 2,
         out_shape=[jax.ShapeDtypeStruct((U + 16, E), BF), jax.ShapeDtypeStruct((N + 16, E), BF)],
+        scratch_shapes=[
+            pltpu.VMEM((1, U), I32),
+            pltpu.VMEM((1, N), I32),
+            pltpu.VMEM((1, N), I32),
+            pltpu.SemaphoreType.DMA((5,)),
+        ],
         compiler_params=params(60 * 1024 * 1024),
         cost_estimate=cost(0, 1e6),
         name="pack",
     )(user_emb, pos_id.reshape(1, U), neg_feat, neg_id.reshape(1, N), neg_bucket.reshape(1, N))
 
 
-def tower_kernel(near_ref, far_ref, pos_ref, mine_ref, w_in_ref, w_out_ref, table_ref, early_ref, *outs):
-    del early_ref
-    hid_ref, emb_ref, pemb_ref, feat_ref, nid_ref, bias_ref, pexp_ref = outs
-    sources = [(near_ref, 0), (near_ref, 256), (far_ref, 0), (far_ref, 256), (pos_ref, 0)]
+def hidden(feat, w_in_ref):
+    return jnp.maximum(mm(feat, w_in_ref[...]), 0.0).astype(BF)
+
+
+def hidden_kernel(near_ref, pos_ref, w_in_ref, hid_ref):
+    for m, feat in enumerate((near_ref[0:TILE], near_ref[TILE:N], pos_ref[...])):
+        hid_ref[m * TILE : (m + 1) * TILE] = hidden(feat, w_in_ref)
+
+
+def embed_kernel(hid_ref, w_out_ref, emb_ref, pemb_ref):
+    for m, (ref, first) in enumerate([(emb_ref, 0), (emb_ref, TILE), (pemb_ref, 0)]):
+        hid = hid_ref[m * TILE : (m + 1) * TILE]
+        ref[first : first + TILE] = mm(hid, w_out_ref[...]).astype(BF)
+
+
+def far_kernel(near_ref, far_ref, w_in_ref, w_out_ref, table_ref, hid_ref, emb_ref, nid_ref, bias_ref):
     lane = lax.broadcasted_iota(I32, (TILE, 128), 1).astype(F32)
-    for m, (ref, start) in enumerate(sources):
-        rows = slice(m * TILE, (m + 1) * TILE)
-        feat = ref[start : start + TILE]
-        feat_ref[rows] = feat
-        hid = jnp.maximum(mm(feat, w_in_ref[...]), 0.0).astype(BF)
-        hid_ref[rows] = hid
-        emb = mm(hid, w_out_ref[...]).astype(BF)
-        if m < 4:
-            emb_ref[rows] = emb
-        else:
-            pemb_ref[...] = emb
-            prod = mine_ref[0:U].astype(F32) * emb.astype(F32)
-            prod = (prod[:, 0:128] + prod[:, 128:256]).T
-            pexp_ref[...] = jnp.exp(SCALE * jnp.sum(prod, axis=0, keepdims=True))
     for side, ref in enumerate((near_ref, far_ref)):
         tail = jnp.concatenate([ref[N : N + 16].astype(F32), jnp.zeros((112, E), F32)], axis=0).T
         for block in range(2):
@@ -102,45 +124,55 @@
             for b in range(8):
                 found = found + jnp.where(bucket == lane + 128.0 * b, table_ref[b : b + 1], 0.0)
             bias_ref[rows] = jnp.broadcast_to(jnp.sum(found, axis=1, keepdims=True), (TILE, 128))
-
-
-def tower(near, far, pos, mine, w_in, w_out, table, early):
+    for m in range(N // TILE):
+        rows = slice(m * TILE, (m + 1) * TILE)
+        hid = hidden(far_ref[rows], w_in_ref)
+        hid_ref[rows] = hid
+        emb_ref[rows] = mm(hid, w_out_ref[...]).astype(BF)
+
+
+def in_vmem(kernel, name, flops, outs, *args):
     vm = pl.BlockSpec(memory_space=pltpu.VMEM)
     return pl.pallas_call(
-        tower_kernel,
-        in_specs=[vm] * 7 + [pl.BlockSpec(memory_space=pl.ANY)],
-        out_specs=[vm] * 7,
-        out_shape=[
-            jax.ShapeDtypeStruct((ROWS, H), BF),
-            jax.ShapeDtypeStruct((NN, E), BF),
-            jax.ShapeDtypeStruct((U, E), BF),
-            jax.ShapeDtypeStruct((ROWS, E), BF),
-            jax.ShapeDtypeStruct((NN, 128), F32),
-            jax.ShapeDtypeStruct((NN, 128), F32),
-            jax.ShapeDtypeStruct((1, U), F32),
-        ],
+        kernel,
+        in_specs=[vm] * len(args),
+        out_specs=[vm] * len(outs),
+        out_shape=[jax.ShapeDtypeStruct(shape, dtype) for shape, dtype in outs],
         compiler_params=params(),
-        cost_estimate=cost(4 * ROWS * E * H, 10e6),
-        name="tower",
-    )(near, far, pos, mine, w_in, w_out, table, early)
+        cost_estimate=cost(flops, 4e6),
+        name=name,
+    )(*args)
 
 
 def twice(x):
     return jnp.concatenate([x, x], axis=1)
 
 
-def score_kernel(s_ref, emb_ref, nid_ref, bias_ref, pexp_ref, *rest):
-    users = rest[:NZ]
-    tloc_ref, tin_ref, kept_ref, kf = rest[NZ:]
+def home(z, k):
+    return (z + OFFSETS[k] + NZ) & (NZ - 1)
+
+
+def score_kernel(ks, s_ref, near_emb, far_emb, nid_ref, bias_ref, pemb_ref, tloc_in, tin_in, *rest):
+    users = rest[: len(ks)]
+    tloc_ref, tin_ref, pexp_ref, kept_ref, kf = rest[len(ks) :]
     z = s_ref[0]
-    for k in range(NZ):
-        u = (users[k][0:U].astype(F32) * SCALE).astype(BF)
-        tail = users[k][U : U + 16].astype(F32)
+    tloc_ref[...] = tloc_in[...]
+    tin_ref[...] = tin_in[...]
+    if ks[0] == 0:
+        prod = users[0][0:U].astype(F32) * pemb_ref[...].astype(F32)
+        prod = (prod[:, 0:128] + prod[:, 128:256]).T
+        pexp_ref[...] = jnp.exp(SCALE * jnp.sum(prod, axis=0, keepdims=True))
+    else:
+        pexp_ref[...] = jnp.zeros_like(pexp_ref)
+    for i, k in enumerate(ks):
+        u = (users[i][0:U].astype(F32) * SCALE).astype(BF)
+        tail = users[i][U : U + 16].astype(F32)
         pid = tail[0:1] * 64.0 + tail[1:2]
         total = jnp.zeros((8, U), F32)
         for m in range(NN // TILE):
             rows = slice(m * TILE, (m + 1) * TILE)
-            sc = lax.dot_general(emb_ref[rows], u, NT, preferred_element_type=F32) - twice(bias_ref[rows])
+            emb = near_emb[rows] if m < 2 else far_emb[(m - 2) * TILE : (m - 1) * TILE]
+            sc = lax.dot_general(emb, u, NT, preferred_element_type=F32) - twice(bias_ref[rows])
             kept = jnp.where(twice(nid_ref[rows]) != pid, jnp.exp(sc), 0.0)
             kf[rows] = kept
             total = total + jnp.sum(kept.reshape(TILE // 8, 8, U), axis=0)
@@ -149,31 +181,33 @@
         inv = jnp.where(t > 0.0, 1.0 / (t * shrink), 0.0)
         for m in range(NN // TILE):
             rows = slice(m * TILE, (m + 1) * TILE)
-            kept_ref[rows, k * U : (k + 1) * U] = ((kf[rows] * shrink) * inv).astype(BF)
-        row = pl.ds(jnp.bitwise_xor(z, k), 1)
+            kept_ref[rows, i * U : (i + 1) * U] = ((kf[rows] * shrink) * inv).astype(BF)
+        row = pl.ds(home(z, k), 1)
         tloc_ref[row, :] = t
         tin_ref[row, :] = t + pexp_ref[...] if k == 0 else t
 
 
-def score(scalars, emb, nid, bias, pexp, users):
+def score(ks, scalars, near_emb, far_emb, nid, bias, pemb, tloc, tin, users):
     vm = pl.BlockSpec(memory_space=pltpu.VMEM)
-    return pl.pallas_call(
-        score_kernel,
-        in_specs=[pl.BlockSpec(memory_space=pltpu.SMEM)] + [vm] * (4 + NZ),
-        out_specs=[vm] * 3,
+    n = len(ks)
+    return pl.pallas_call(
+        functools.partial(score_kernel, ks),
+        in_specs=[pl.BlockSpec(memory_space=pltpu.SMEM)] + [vm] * (7 + n),
+        out_specs=[vm] * 4,
         out_shape=[
             jax.ShapeDtypeStruct((NZ, U), F32),
             jax.ShapeDtypeStruct((NZ, U), F32),
-            jax.ShapeDtypeStruct((NN, NZ * U), BF),
+            jax.ShapeDtypeStruct((1, U), F32),
+            jax.ShapeDtypeStruct((NN, n * U), BF),
         ],
         scratch_shapes=[pltpu.VMEM((NN, U), F32)],
         compiler_params=params(),
-        cost_estimate=cost(2 * NZ * U * NN * E, 6e6, NZ * U * NN),
+        cost_estimate=cost(2 * n * U * NN * E, 5e6, n * U * NN),
         name="score",
-    )(scalars, emb, nid, bias, pexp, *users)
-
-
-def grad_kernel(s_ref, tot_ref, tloc_ref, pexp_ref, emb_ref, pemb_ref, kept_ref, *rest):
+    )(scalars, near_emb, far_emb, nid, bias, pemb, tloc, tin, *[users[k] for k in ks])
+
+
+def grad_kernel(s_ref, tot_ref, tloc_ref, pexp_ref, near_emb, far_emb, pemb_ref, kept_a, kept_b, *rest):
     users = rest[:NZ]
     ug_ref, g_ref, pterm_ref, wu, ratio, rel = rest[NZ:]
     z = s_ref[0]
@@ -185,27 +219,32 @@
     pprob = (pexp_ref[...] * shrink) * (1.0 / (own * shrink))
     rel[...] = jnp.zeros_like(rel)
     for k in range(NZ):
-        rel[k : k + 1] = SCALE * ratio[pl.ds(jnp.bitwise_xor(z, k), 1), :]
+        rel[k : k + 1] = SCALE * ratio[pl.ds(home(z, k), 1), :]
     rel[NZ : NZ + 1] = SCALE * (pprob - 1.0)
     cols = rel[...].T
     for k in range(NZ):
         wu[k * U : (k + 1) * U] = (users[k][0:U].astype(F32) * cols[:, k : k + 1]).astype(BF)
     coef = cols[:, NZ : NZ + 1]
-    g_ref[NN:ROWS] = (users[0][0:U].astype(F32) * coef).astype(BF)
+    g_ref[N : N + U] = (users[0][0:U].astype(F32) * coef).astype(BF)
     pterm_ref[...] = pemb_ref[...].astype(F32) * coef
     for k in range(NZ):
-        ug = lax.dot_general(kept_ref[:, k * U : (k + 1) * U], emb_ref[...], TN, preferred_element_type=F32)
-        ug_ref[jnp.bitwise_xor(z, k)] = (ug * cols[:, k : k + 1]).astype(BF)
+        kept, i = (kept_a, k) if k < FIRST else (kept_b, k - FIRST)
+        cols_k = slice(i * U, (i + 1) * U)
+        ug = lax.dot_general(kept[0:N, cols_k], near_emb[...], TN, preferred_element_type=F32)
+        ug = ug + lax.dot_general(kept[N:NN, cols_k], far_emb[...], TN, preferred_element_type=F32)
+        ug_ref[home(z, k)] = (ug * cols[:, k : k + 1]).astype(BF)
     for m in range(NN // TILE):
         rows = slice(m * TILE, (m + 1) * TILE)
-        g_ref[rows] = mm(kept_ref[rows], wu[...]).astype(BF)
-
-
-def grads(scalars, tot, tloc, pexp, emb, pemb, kept, users):
+        g = mm(kept_a[rows], wu[0 : FIRST * U]) + mm(kept_b[rows], wu[FIRST * U :])
+        first = m * TILE if m < 2 else m * TILE + U
+        g_ref[first : first + TILE] = g.astype(BF)
+
+
+def grads(scalars, tot, tloc, pexp, near_emb, far_emb, pemb, kept_a, kept_b, users):
     vm = pl.BlockSpec(memory_space=pltpu.VMEM)
     return pl.pallas_call(
         grad_kernel,
-        in_specs=[pl.BlockSpec(memory_space=pltpu.SMEM)] + [vm] * (6 + NZ),
+        in_specs=[pl.BlockSpec(memory_space=pltpu.SMEM)] + [vm] * (8 + NZ),
         out_specs=[vm, vm, vm],
         out_shape=[
             jax.ShapeDtypeStruct((NZ, U, E), BF),
@@ -220,17 +259,20 @@
         compiler_params=params(),
         cost_estimate=cost(4 * NZ * U * NN * E, 8e6),
         name="grads",
-    )(scalars, tot, tloc, pexp, emb, pemb, kept, *users)
-
-
-def back_kernel(s_ref, g_ref, feat_ref, w_out_ref, hid_ref, mine_ref, theirs_ref):
+    )(scalars, tot, tloc, pexp, near_emb, far_emb, pemb, kept_a, kept_b, *users)
+
+
+def back_kernel(s_ref, g_ref, near_ref, pos_ref, far_ref, w_out_ref, hid_ref, far_hid, mine_ref, theirs_ref, feat):
     first, second, core = s_ref[1], s_ref[2], s_ref[3]
+    feat[0:N] = near_ref[0:N]
+    feat[N : N + U] = pos_ref[...]
+    feat[N + U : ROWS] = far_ref[0:N]
     for c in range(H // WIDE):
         cols = slice(c * WIDE, (c + 1) * WIDE)
-        hid = hid_ref[:, cols]
+        hid = jnp.concatenate([hid_ref[:, cols], far_hid[:, cols]], axis=0)
         back = lax.dot_general(g_ref[...], w_out_ref[cols], NT, preferred_element_type=F32)
         back = jnp.where(hid > 0, back, 0.0).astype(BF)
-        w_in = lax.dot_general(feat_ref[...], back, TN, preferred_element_type=F32)
+        w_in = lax.dot_general(feat[...], back, TN, preferred_element_type=F32)
         w_out = lax.dot_general(hid, g_ref[...], TN, preferred_element_type=F32)
         to_mine, to_theirs = jnp.bitwise_xor(first, c), jnp.bitwise_xor(second, c)
         for t in range(WIDE // TILE):
@@ -243,17 +285,18 @@
                 theirs_ref[to_theirs, jnp.bitwise_xor(first, 2 * t + half)] = theirs[rows]
 
 
-def backward(scalars, g, feat, w_out, hid):
+def backward(scalars, g, near, pos, far, w_out, hid, far_hid):
     vm = pl.BlockSpec(memory_space=pltpu.VMEM)
     return pl.pallas_call(
         back_kernel,
-        in_specs=[pl.BlockSpec(memory_space=pltpu.SMEM)] + [vm] * 4,
+        in_specs=[pl.BlockSpec(memory_space=pltpu.SMEM)] + [vm] * 7,
         out_specs=[vm, vm],
         out_shape=[jax.ShapeDtypeStruct((4, 4, 128, TILE), BF)] * 2,
+        scratch_shapes=[pltpu.VMEM((ROWS, E), BF)],
         compiler_params=params(),
         cost_estimate=cost(6 * ROWS * E * H, 10e6),
         name="backward",
-    )(scalars, g, feat, w_out, hid)
+    )(scalars, g, near, pos, far, w_out, hid, far_hid)
 
 
 def finish_kernel(s_ref, mine_ref, other_ref, w_in_ref, w_out_ref):
@@ -294,6 +337,14 @@
     return lax.ppermute(x, axis, [(i, i ^ k) for i in range(SIZES[AXES.index(axis)])])
 
 
+def after(x, *needed):
+    return lax.optimization_barrier((x, *needed))[0]
+
+
+def shift(x, by):
+    return lax.ppermute(x, "z", [(i, (i + by) % NZ) for i in range(NZ)])
+
+
 def device(x_lo, z, x_hi, y, core):
     return (((x_lo * 8 + z) * 2 + x_hi) * 4 + y) * 2 + core
 
@@ -341,17 +392,37 @@
     scalars = jnp.stack([z, jnp.where(core == 0, xx, y), jnp.where(core == 0, y, xx), core]).astype(I32)
 
     mine, near = pack(user_emb, pos_id, neg_feat, neg_id, neg_bucket)
+    up, down = shift(mine, 1), shift(mine, -1)
     far = swap(near, "x_lo", 1)
-    users = [mine] + [swap(mine, "z", k) for k in range(1, NZ)]
-
-    hid, emb, pemb, feat, nid, bias, pexp = tower(
-        near, far, pos_feat, mine, w_in, w_out, logq_table.reshape(8, 128), users[EARLY]
+    users = [mine, up, down]
+    (hid,) = in_vmem(hidden_kernel, "hidden", 2 * (N + U) * E * H, [((N + U, H), BF)], near, pos_feat, w_in)
+    up, down = shift(after(up, hid), 1), shift(after(down, hid), -1)
+    users += [up, down]
+    near_emb, pemb = in_vmem(
+        embed_kernel, "embed", 2 * (N + U) * E * H, [((N, E), BF), ((U, E), BF)], hid, w_out
     )
-    tloc, tot, kept = score(scalars, emb, nid, bias, pexp, users)
+    up, down = shift(after(up, near_emb), 1), shift(after(down, near_emb), -1)
+    users += [up, down]
+    far_hid, far_emb, nid, bias = in_vmem(
+        far_kernel,
+        "far",
+        4 * N * E * H,
+        [((N, H), BF), ((N, E), BF), ((NN, 128), F32), ((NN, 128), F32)],
+        near,
+        far,
+        w_in,
+        w_out,
+        logq_table.reshape(8, 128),
+    )
+    users += [shift(after(up, far_emb), 1)]
+    none = jnp.zeros((NZ, U), F32)
+    ks = tuple(range(NZ))
+    tloc, tot, pexp, kept_a = score(ks[:FIRST], scalars, near_emb, far_emb, nid, bias, pemb, none, none, users)
+    tloc, tot, _, kept_b = score(ks[FIRST:], scalars, near_emb, far_emb, nid, bias, pemb, tloc, tot, users)
     tot = sum_over_z(tot, ((1, 6, 7), (2,)), F32)
-    ug, g, pterm = grads(scalars, tot, tloc, pexp, emb, pemb, kept, users)
+    ug, g, pterm = grads(scalars, tot, tloc, pexp, near_emb, far_emb, pemb, kept_a, kept_b, users)
     user_sum = lax.psum_scatter(ug, "z", scatter_dimension=0, tiled=False)
-    mine_g, theirs_g = backward(scalars, g, feat, w_out, hid)
+    mine_g, theirs_g = backward(scalars, g, near, pos_feat, far, w_out, hid, far_hid)
     half, other = all_reduce(mine_g, theirs_g)
     w_in_grad, w_out_grad = finish(scalars, half, other)
     user_grad = user_sum.astype(F32) + pterm

time: 149 us -> 145 us (0.973)
  starting transfers between devices: 65.5 us -> 55.9 us
  Pallas kernels: 21.7 us -> 25.4 us
  local copies, waits for them, and re-layouts: 5.97 us -> 8.47 us
    ppermute x18 -> x11, starting transfers between devices: 51.1 us -> 29.9 us  [swap(): lax.ppermute(x, axis, [(i, i ^ k) for i in range(SIZES[AXES.index(axis)])])]
    ppermute x0 -> x7, starting transfers between devices: none -> 12 us  [shift(): return lax.ppermute(x, 'z', [(i, (i + by) % NZ) for i in range(NZ)])]
    pallas_call x3 -> x6, Pallas kernels: 9.44 us -> 12.3 us  [the longest x2 5.68 us: score(): pl.pallas_call(functools.partial(score_kernel, ks), in_specs=[pl.BlockSpe...]
    unnamed x14 -> x42, local copies, waits for them, and re-layouts: 5.9 us -> 8.4 us
    ppermute x0 -> x7, waiting for transfers between devices: none -> 1.88 us  [shift(): return lax.ppermute(x, 'z', [(i, (i + by) % NZ) for i in range(NZ)])]
    ppermute x12, waiting for transfers between devices: 22.6 us -> 20.7 us  [plane_swap(): return lax.ppermute(x, AXES, pairs)]
    ppermute x18 -> x11, waiting for transfers between devices: 15.8 us -> 14.9 us  [swap(): lax.ppermute(x, axis, [(i, i ^ k) for i in range(SIZES[AXES.index(axis)])])]
  transfers between devices with their start and end apart: 31 -> 31, of which waited for: 19 -> 20; matrix products, arithmetic and copies ran while one was open for 1% -> 1% of each run, Pallas kernels for 2% -> 6%
where the time goes in v3:
time: 145 us; the launch traced here: 144 us
  starting transfers between devices  55.9 us (39%)
  waiting for transfers between devices  37.5 us (26%)
  Pallas kernels  25.4 us (18%)
  between operations  14.3 us (10%)
  local copies, waits for them, and re-layouts  8.47 us (6%)
  other arithmetic  2.46 us (2%)
    ppermute x11, starting transfers between devices, swap(): lax.ppermute(x, axis, [(i, i ^ k) for i in range(SIZES[AXES.index(axis)])])  29.9 us
    ppermute x12, waiting for transfers between devices, plane_swap(): return lax.ppermute(x, AXES, pairs)  20.7 us
    ppermute x11, waiting for transfers between devices, swap(): lax.ppermute(x, axis, [(i, i ^ k) for i in range(SIZES[AXES.index(axis)])])  14.9 us
    ppermute x12, starting transfers between devices, plane_swap(): return lax.ppermute(x, AXES, pairs)  14 us
    ppermute x7, starting transfers between devices, shift(): return lax.ppermute(x, 'z', [(i, (i + by) % NZ) for i in range(NZ)])  12 us
    unnamed x42, local copies, waits for them, and re-layouts  8.4 us
    pallas_call x1, Pallas kernels, backward(): pl.pallas_call(back_kernel, in_specs=[pl.BlockSpec(memory_space=pltpu.SME...  5.69 us
    pallas_call x2, Pallas kernels, score(): pl.pallas_call(functools.partial(score_kernel, ks), in_specs=[pl.BlockSpe...  5.68 us
  transfers between devices with their start and end apart: 31, of which 20 were waited for; matrix products, arithmetic and copies ran while one was open for 1% of the time, Pallas kernels for 6%

profile of v3, /device:TPU:1, one launch (start us, length us, event | category | flops | bytes accessed | tf_op | source)
XLA Modules:
  0.0 144.1 jit_solution(10143812289067294883)
XLA Ops:
  7.2 1.9 %pack.1 = (bf16[272,256]{1,0:T(8,128)(2,1)}, bf16[528,256]{1,0:T(8,128)(2,1)}) custom-call(bf16[256,256]{1,0:T(8,128)(2,1)} %user_hbm.1, s32[1,256]{1,0:T(1,128)} %bitcast.52, bf16[512,256]{1,0:T(8,128)(2,1)} %feat_hbm.1, s32[1,512]{1,0:T(1,128)} %bitcast.50, s32[1,512]{1,0:T(1,128)} %bitcast.51), custom_call_target="tpu_custom_call" | custom-call | bytes 1000000 | tf_op jit(solution)/shard_map/pack/pallas_call | solution.py:82
  9.1 2.5 %collective-permute-start.1 = (bf16[272,256]{1,0:T(8,128)(2,1)}, bf16[272,256]{1,0:T(8,128)(2,1)S(1)}, u32[]{:S(2)}, u32[]{:S(2)}) collective-permute-start(bf16[272,256]{1,0:T(8,128)(2,1)} %get-tuple-element.36.rest_0_), channel_id=1, source_target_pairs={{0,16},{16,32},{32,48},{48,64},{64,80},{80,96},{96,112},{112,0},{1... | collective-permute-start | bytes 417800 | tf_op jit(solution)/shard_map/ppermute | solution.py:345
  12.8 4.0 %collective-permute-start.2 = (bf16[272,256]{1,0:T(8,128)(2,1)}, bf16[272,256]{1,0:T(8,128)(2,1)}, u32[]{:S(2)}, u32[]{:S(2)}) collective-permute-start(bf16[272,256]{1,0:T(8,128)(2,1)} %get-tuple-element.36.rest_0_), channel_id=1, source_target_pairs={{0,112},{16,0},{32,16},{48,32},{64,48},{80,64},{96,80},{112,96},{1... | collective-permute-start | bytes 417800 | tf_op jit(solution)/shard_map/ppermute | solution.py:345
  23.6 2.6 %collective-permute-start.4 = (bf16[272,256]{1,0:T(8,128)(2,1)}, bf16[272,256]{1,0:T(8,128)(2,1)}, u32[]{:S(2)}, u32[]{:S(2)}) collective-permute-start(bf16[272,256]{1,0:T(8,128)(2,1)} %collective-permute-done.2.rest_2_), channel_id=1, source_target_pairs={{0,112},{16,0},{32,16},{48,32},{64,48},{80,64},{96,80},{112,96},{1... | collective-permute-start | bytes 417800 | tf_op jit(solution)/shard_map/ppermute | solution.py:345
  29.5 2.8 %far.1 = (bf16[512,2048]{1,0:T(8,128)(2,1)S(1)}, bf16[512,256]{1,0:T(8,128)(2,1)S(1)}, f32[1024,128]{1,0:T(8,128)S(1)}, f32[1024,128]{1,0:T(8,128)S(1)}) custom-call(bf16[528,256]{1,0:T(8,128)(2,1)S(1)} %copy-done.6, bf16[528,256]{1,0:T(8,128)(2,1)} %collective-permute-done.far_ref, bf16[256,2048]{1,0:T(8,128)(2,1)S(1)} %copy-done.1, ...), custom_call_target="tpu_custom_call" | custom-call | flops 1073741824 | bytes 4000000 | tf_op jit(solution)/shard_map/far/pallas_call | solution.py:136
  32.2 2.7 %collective-permute-start.6 = (bf16[272,256]{1,0:T(8,128)(2,1)}, bf16[272,256]{1,0:T(8,128)(2,1)S(1)}, u32[]{:S(2)}, u32[]{:S(2)}) collective-permute-start(bf16[272,256]{1,0:T(8,128)(2,1)} %collective-permute-done.4.rest_4_), channel_id=1, source_target_pairs={{0,112},{16,0},{32,16},{48,32},{64,48},{80,64},{96,80},{112,96},{1... | collective-permute-start | bytes 417800 | tf_op jit(solution)/shard_map/ppermute | solution.py:345
  35.1 3.3 %score.2 = (f32[8,256]{1,0:T(8,128)S(1)}, f32[8,256]{1,0:T(8,128)S(1)}, f32[1,256]{1,0:T(1,128)S(1)}, bf16[1024,1280]{1,0:T(8,128)(2,1)S(1)}) custom-call(s32[4]{0:T(128)S(1)} %pad_add_fusion.s_ref, bf16[512,256]{1,0:T(8,128)(2,1)S(1)} %copy-done.8, bf16[512,256]{1,0:T(8,128)(2,1)S(1)} %get-tuple-element.32.far_emb, ...), custom_call_target="tpu_custom_call" | custom-call | flops 671088640 | bytes 5000000 | tf_op jit(solution)/shard_map/score/pallas_call | solution.py:193
  38.4 1.7 %collective-permute-done.7.rest_2_.rest_7_ = bf16[272,256]{1,0:T(8,128)(2,1)S(1)} collective-permute-done((bf16[272,256]{1,0:T(8,128)(2,1)S(1)}, bf16[272,256]{1,0:T(8,128)(2,1)S(1)}, u32[]{:S(2)}, u32[]{:S(2)}) %collective-permute-start.7) | collective-permute-done | bytes 139296 | tf_op jit(solution)/shard_map/ppermute | solution.py:345
  40.1 2.4 %score.3 = (f32[8,256]{1,0:T(8,128)S(1)}, f32[8,256]{1,0:T(8,128)S(1)}, f32[1,256]{1,0:T(1,128)}, bf16[1024,768]{1,0:T(8,128)(2,1)S(1)}) custom-call(s32[4]{0:T(128)S(1)} %pad_add_fusion.s_ref, bf16[512,256]{1,0:T(8,128)(2,1)S(1)} %copy-done.8, bf16[512,256]{1,0:T(8,128)(2,1)S(1)} %get-tuple-element.32.far_emb, f32[1024,128]{1,0:T(8,128)S(1)} %get-tuple-element.33.nid_ref, ...), custom_call_target="tpu_custom_call" | custom-call | flops 402653184 | bytes 5000000 | tf_op jit(solution)/shard_map/score/pallas_call | solution.py:193
  46.4 1.7 %collective-permute-done.9 = f32[8,256]{1,0:T(8,128)S(1)} collective-permute-done((f32[8,256]{1,0:T(8,128)S(1)}, f32[8,256]{1,0:T(8,128)S(1)}, u32[]{:S(2)}, u32[]{:S(2)}) %collective-permute-start.9) | collective-permute-done | bytes 8224 | tf_op jit(solution)/shard_map/ppermute | solution.py:337
  48.1 2.1 %collective-permute-start.11 = (f32[8,256]{1,0:T(8,128)S(1)}, f32[8,256]{1,0:T(8,128)S(1)}, u32[]{:S(2)}, u32[]{:S(2)}) collective-permute-start(f32[8,256]{1,0:T(8,128)S(1)} %add_add_fusion), channel_id=1, source_target_pairs={{0,32},{16,48},{32,0},{48,16},{64,96},{80,112},{96,64},{112,80},{1... | collective-permute-start | bytes 24584 | tf_op jit(solution)/shard_map/ppermute | solution.py:337
  50.2 1.7 %collective-permute-done.11 = f32[8,256]{1,0:T(8,128)S(1)} collective-permute-done((f32[8,256]{1,0:T(8,128)S(1)}, f32[8,256]{1,0:T(8,128)S(1)}, u32[]{:S(2)}, u32[]{:S(2)}) %collective-permute-start.11) | collective-permute-done | bytes 8224 | tf_op jit(solution)/shard_map/ppermute | solution.py:337
  51.9 4.4 %grads.1 = (bf16[8,256,256]{2,1,0:T(8,128)(2,1)}, bf16[1280,256]{1,0:T(8,128)(2,1)S(1)}, f32[256,256]{1,0:T(8,128)S(1)}) custom-call(s32[4]{0:T(128)S(1)} %pad_add_fusion.s_ref, f32[8,256]{1,0:T(8,128)S(1)} %add.57.tot_ref, f32[8,256]{1,0:T(8,128)S(1)} %get-tuple-element.45.tloc_ref, f32[1,256]{1,0:T(1,128)S(1)} %get-tuple-element.46.pexp_ref, ...), custom_call_target="tpu_custom_call" | custom-call | flops 2147483648 | bytes 8000000 | tf_op jit(solution)/shard_map/grads/pallas_call | solution.py:245
  57.0 5.7 %backward.1 = (bf16[4,4,128,256]{3,2,1,0:T(8,128)(2,1)S(1)}, bf16[4,4,128,256]{3,2,1,0:T(8,128)(2,1)S(1)}) custom-call(s32[4]{0:T(128)S(1)} %pad_add_fusion.s_ref, bf16[1280,256]{1,0:T(8,128)(2,1)S(1)} %get-tuple-element.51.g_ref, bf16[528,256]{1,0:T(8,128)(2,1)S(1)} %copy-done.6, bf16[256,256]{1,0:T(8,128)(2,1)S(1)} %copy-done.12, ...), custom_call_target="tpu_custom_call" | custom-call | flops 4026531840 | bytes 10000000 | tf_op jit(solution)/shard_map/backward/pallas_call | solution.py:290
  62.7 5.8 %collective-permute-start.12 = (bf16[4,4,128,256]{3,2,1,0:T(8,128)(2,1)S(1)}, bf16[4,4,128,256]{3,2,1,0:T(8,128)(2,1)S(1)}, u32[]{:S(2)}, u32[]{:S(2)}) collective-permute-start(bf16[4,4,128,256]{3,2,1,0:T(8,128)(2,1)S(1)} %get-tuple-element.54), channel_id=1, source_target_pairs={{0,1},{1,0},{2,3},{3,2},{4,5},{5,4},{6,7},{7,6},{8,9},{9,8},{10,11... | collective-permute-start | bytes 3145736 | tf_op jit(solution)/shard_map/ppermute | solution.py:337
  68.5 2.3 %collective-permute-done.12 = bf16[4,4,128,256]{3,2,1,0:T(8,128)(2,1)S(1)} collective-permute-done((bf16[4,4,128,256]{3,2,1,0:T(8,128)(2,1)S(1)}, bf16[4,4,128,256]{3,2,1,0:T(8,128)(2,1)S(1)}, u32[]{:S(2)}, u32[]{:S(2)}) %collective-permute-start.12) | collective-permute-done | bytes 1048608 | tf_op jit(solution)/shard_map/ppermute | solution.py:337
  72.6 1.9 %collective-permute-start.15 = (bf16[4,128,256]{2,1,0:T(8,128)(2,1)S(1)}, bf16[4,128,256]{2,1,0:T(8,128)(2,1)S(1)}, u32[]{:S(2)}, u32[]{:S(2)}) collective-permute-start(bf16[4,128,256]{2,1,0:T(8,128)(2,1)S(1)} %get-tuple-element.58), channel_id=1, source_target_pairs={{0,136},{1,7},{2,138},{3,5},{4,140},{5,3},{6,142},{7,1},{128,8},{1... | collective-permute-start | bytes 786440 | tf_op jit(solution)/shard_map/ppermute | solution.py:362
  76.8 3.8 %collective-permute-done.15 = bf16[4,128,256]{2,1,0:T(8,128)(2,1)S(1)} collective-permute-done((bf16[4,128,256]{2,1,0:T(8,128)(2,1)S(1)}, bf16[4,128,256]{2,1,0:T(8,128)(2,1)S(1)}, u32[]{:S(2)}, u32[]{:S(2)}) %collective-permute-start.15) | collective-permute-done | bytes 262176 | tf_op jit(solution)/shard_map/ppermute | solution.py:362
  82.3 2.5 %collective-permute-start.18 = (bf16[128,256]{1,0:T(8,128)(2,1)S(1)}, bf16[128,256]{1,0:T(8,128)(2,1)S(1)}, u32[]{:S(2)}, u32[]{:S(2)}) collective-permute-start(bf16[128,256]{1,0:T(8,128)(2,1)S(1)} %get-tuple-element.63), channel_id=1, source_target_pairs={{0,6},{1,137},{2,4},{3,139},{4,2},{5,141},{6,0},{7,143},{128,134},... | collective-permute-start | bytes 196616 | tf_op jit(solution)/shard_map/ppermute | solution.py:362
  86.7 2.7 %collective-permute-done.17 = bf16[128,256]{1,0:T(8,128)(2,1)S(1)} collective-permute-done((bf16[128,256]{1,0:T(8,128)(2,1)S(1)}, bf16[128,256]{1,0:T(8,128)(2,1)S(1)}, u32[]{:S(2)}, u32[]{:S(2)}) %collective-permute-start.17) | collective-permute-done | bytes 65568 | tf_op jit(solution)/shard_map/ppermute | solution.py:362
  89.4 1.9 %collective-permute-start.19 = (bf16[128,256]{1,0:T(8,128)(2,1)S(1)}, bf16[128,256]{1,0:T(8,128)(2,1)S(1)}, u32[]{:S(2)}, u32[]{:S(2)}) collective-permute-start(bf16[128,256]{1,0:T(8,128)(2,1)S(1)} %fusion.5), channel_id=1, source_target_pairs={{0,16},{16,0},{32,48},{48,32},{64,80},{80,64},{96,112},{112,96},{1... | collective-permute-start | bytes 196616 | tf_op jit(solution)/shard_map/ppermute | solution.py:337
  91.4 1.7 %collective-permute-done.19 = bf16[128,256]{1,0:T(8,128)(2,1)S(1)} collective-permute-done((bf16[128,256]{1,0:T(8,128)(2,1)S(1)}, bf16[128,256]{1,0:T(8,128)(2,1)S(1)}, u32[]{:S(2)}, u32[]{:S(2)}) %collective-permute-start.19) | collective-permute-done | bytes 65568 | tf_op jit(solution)/shard_map/ppermute | solution.py:337
  93.1 2.1 %collective-permute-start.22 = (bf16[128,256]{1,0:T(8,128)(2,1)S(1)}, bf16[128,256]{1,0:T(8,128)(2,1)S(1)}, u32[]{:S(2)}, u32[]{:S(2)}) collective-permute-start(bf16[128,256]{1,0:T(8,128)(2,1)S(1)} %add_convert_fusion.2), channel_id=1, source_target_pairs={{0,96},{16,112},{32,64},{48,80},{64,32},{80,48},{96,0},{112,16},{1... | collective-permute-start | bytes 196616 | tf_op jit(solution)/shard_map/ppermute | solution.py:337
  95.1 4.2 %collective-permute-start.21 = (bf16[128,256]{1,0:T(8,128)(2,1)S(1)}, bf16[128,256]{1,0:T(8,128)(2,1)S(1)}, u32[]{:S(2)}, u32[]{:S(2)}) collective-permute-start(bf16[128,256]{1,0:T(8,128)(2,1)S(1)} %add_convert_fusion.2), channel_id=1, source_target_pairs={{0,64},{16,80},{32,96},{48,112},{64,0},{80,16},{96,32},{112,48},{1... | collective-permute-start | bytes 196616 | tf_op jit(solution)/shard_map/ppermute | solution.py:337
  99.3 3.1 %collective-permute-done.21 = bf16[128,256]{1,0:T(8,128)(2,1)S(1)} collective-permute-done((bf16[128,256]{1,0:T(8,128)(2,1)S(1)}, bf16[128,256]{1,0:T(8,128)(2,1)S(1)}, u32[]{:S(2)}, u32[]{:S(2)}) %collective-permute-start.21) | collective-permute-done | bytes 65568 | tf_op jit(solution)/shard_map/ppermute | solution.py:337
  102.4 3.8 %collective-permute-done.20 = bf16[128,256]{1,0:T(8,128)(2,1)S(1)} collective-permute-done((bf16[128,256]{1,0:T(8,128)(2,1)S(1)}, bf16[128,256]{1,0:T(8,128)(2,1)S(1)}, u32[]{:S(2)}, u32[]{:S(2)}) %collective-permute-start.20) | collective-permute-done | bytes 65568 | tf_op jit(solution)/shard_map/ppermute | solution.py:337
  107.7 1.9 %collective-permute-start.23 = (bf16[128,256]{1,0:T(8,128)(2,1)S(1)}, bf16[128,256]{1,0:T(8,128)(2,1)S(1)}, u32[]{:S(2)}, u32[]{:S(2)}) collective-permute-start(bf16[128,256]{1,0:T(8,128)(2,1)S(1)} %add_convert_fusion.1), channel_id=1, source_target_pairs={{0,2},{1,129},{2,0},{3,131},{4,6},{5,133},{6,4},{7,135},{128,130},... | collective-permute-start | bytes 196616 | tf_op jit(solution)/shard_map/ppermute | solution.py:362
  115.7 5.0 %collective-permute-done.27 = bf16[4,128,256]{2,1,0:T(8,128)(2,1)S(1)} collective-permute-done((bf16[4,128,256]{2,1,0:T(8,128)(2,1)S(1)}, bf16[4,128,256]{2,1,0:T(8,128)(2,1)S(1)}, u32[]{:S(2)}, u32[]{:S(2)}) %collective-permute-start.27) | collective-permute-done | bytes 262176 | tf_op jit(solution)/shard_map/ppermute | solution.py:362
  120.7 1.8 %collective-permute-done.26 = bf16[4,128,256]{2,1,0:T(8,128)(2,1)S(1)} collective-permute-done((bf16[4,128,256]{2,1,0:T(8,128)(2,1)S(1)}, bf16[4,128,256]{2,1,0:T(8,128)(2,1)S(1)}, u32[]{:S(2)}, u32[]{:S(2)}) %collective-permute-start.26) | collective-permute-done | bytes 262176 | tf_op jit(solution)/shard_map/ppermute | solution.py:362
  123.2 8.8 %collective-permute-start.29 = (bf16[4,4,128,256]{3,2,1,0:T(8,128)(2,1)S(1)}, bf16[4,4,128,256]{3,2,1,0:T(8,128)(2,1)S(1)}, u32[]{:S(2)}, u32[]{:S(2)}) collective-permute-start(bf16[4,4,128,256]{3,2,1,0:T(8,128)(2,1)S(1)} %pad_maximum_fusion.mine_ref), channel_id=1, source_target_pairs={{0,1},{1,0},{2,3},{3,2},{4,5},{5,4},{6,7},{7,6},{8,9},{9,8},{10,11... | collective-permute-start | bytes 3145736 | tf_op jit(solution)/shard_map/ppermute | solution.py:337
  132.0 1.6 %convert_add_fusion.1 = f32[256,256]{1,0:T(8,128)} fusion(f32[256,256]{1,0:T(8,128)S(1)} %copy-done.10, bf16[1,256,256]{2,1,0:T(8,128)(2,1)} %reduce-scatter.2.cloned.1.call-done), kind=kLoop, calls=%fused_computation.11 | loop fusion | flops 131072 | bytes 655360 | tf_op jit(solution)/shard_map/add | solution.py:428
  134.3 3.0 %finish.1 = (f32[256,2048]{1,0:T(8,128)}, f32[2048,256]{1,0:T(8,128)}) custom-call(s32[4]{0:T(128)S(1)} %copy-done.16, bf16[4,4,128,256]{3,2,1,0:T(8,128)(2,1)S(1)} %pad_maximum_fusion.mine_ref, bf16[4,4,128,256]{3,2,1,0:T(8,128)(2,1)S(1)} %collective-permute-done.29.other_ref), custom_call_target="tpu_custom_call" | custom-call | bytes 6000000 | tf_op jit(solution)/shard_map/finish/pallas_call | solution.py:318
  (96 shorter events, 32.6 us)
Async XLA Ops:
  7.2 124.8 %reduce-scatter.2.cloned.1.call-start = ((), (), s32[]{:S(2)}) async-start(), calls=%async_computation.1 | async-start | bytes 1179648 | tf_op jit(solution)/shard_map/reduce_scatter | solution.py:424
  9.1 11.9 %collective-permute-start.1 = (bf16[272,256]{1,0:T(8,128)(2,1)}, bf16[272,256]{1,0:T(8,128)(2,1)S(1)}, u32[]{:S(2)}, u32[]{:S(2)}) collective-permute-start(bf16[272,256]{1,0:T(8,128)(2,1)} %get-tuple-element.36.rest_0_), channel_id=1, source_target_pairs={{0,16},{16,32},{32,48},{48,64},{64,80},{80,96},{96,112},{112,0},{1... | collective-permute-start | bytes 417800 | tf_op jit(solution)/shard_map/ppermute | solution.py:345
  11.6 14.7 %collective-permute-start = (bf16[528,256]{1,0:T(8,128)(2,1)}, bf16[528,256]{1,0:T(8,128)(2,1)}, u32[]{:S(2)}, u32[]{:S(2)}) collective-permute-start(bf16[528,256]{1,0:T(8,128)(2,1)} %get-tuple-element.30.near_ref), channel_id=1, source_target_pairs={{0,128},{128,0},{1,129},{129,1},{2,130},{130,2},{3,131},{131,3},{4... | collective-permute-start | bytes 811016 | tf_op jit(solution)/shard_map/ppermute | solution.py:337
  12.8 10.7 %collective-permute-start.2 = (bf16[272,256]{1,0:T(8,128)(2,1)}, bf16[272,256]{1,0:T(8,128)(2,1)}, u32[]{:S(2)}, u32[]{:S(2)}) collective-permute-start(bf16[272,256]{1,0:T(8,128)(2,1)} %get-tuple-element.36.rest_0_), channel_id=1, source_target_pairs={{0,112},{16,0},{32,16},{48,32},{64,48},{80,64},{96,80},{112,96},{1... | collective-permute-start | bytes 417800 | tf_op jit(solution)/shard_map/ppermute | solution.py:345
  21.0 5.3 %collective-permute-start.3 = (bf16[272,256]{1,0:T(8,128)(2,1)S(1)}, bf16[272,256]{1,0:T(8,128)(2,1)}, u32[]{:S(2)}, u32[]{:S(2)}) collective-permute-start(bf16[272,256]{1,0:T(8,128)(2,1)S(1)} %collective-permute-done.1.rest_1_), channel_id=1, source_target_pairs={{0,16},{16,32},{32,48},{48,64},{64,80},{80,96},{96,112},{112,0},{1... | collective-permute-start | bytes 417800 | tf_op jit(solution)/shard_map/ppermute | solution.py:345
  23.6 8.7 %collective-permute-start.4 = (bf16[272,256]{1,0:T(8,128)(2,1)}, bf16[272,256]{1,0:T(8,128)(2,1)}, u32[]{:S(2)}, u32[]{:S(2)}) collective-permute-start(bf16[272,256]{1,0:T(8,128)(2,1)} %collective-permute-done.2.rest_2_), channel_id=1, source_target_pairs={{0,112},{16,0},{32,16},{48,32},{64,48},{80,64},{96,80},{112,96},{1... | collective-permute-start | bytes 417800 | tf_op jit(solution)/shard_map/ppermute | solution.py:345
  26.3 8.7 %collective-permute-start.5 = (bf16[272,256]{1,0:T(8,128)(2,1)}, bf16[272,256]{1,0:T(8,128)(2,1)S(1)}, u32[]{:S(2)}, u32[]{:S(2)}) collective-permute-start(bf16[272,256]{1,0:T(8,128)(2,1)} %collective-permute-done.3.rest_3_), channel_id=1, source_target_pairs={{0,16},{16,32},{32,48},{48,64},{64,80},{80,96},{96,112},{112,0},{1... | collective-permute-start | bytes 417800 | tf_op jit(solution)/shard_map/ppermute | solution.py:345
  32.2 6.2 %collective-permute-start.6 = (bf16[272,256]{1,0:T(8,128)(2,1)}, bf16[272,256]{1,0:T(8,128)(2,1)S(1)}, u32[]{:S(2)}, u32[]{:S(2)}) collective-permute-start(bf16[272,256]{1,0:T(8,128)(2,1)} %collective-permute-done.4.rest_4_), channel_id=1, source_target_pairs={{0,112},{16,0},{32,16},{48,32},{64,48},{80,64},{96,80},{112,96},{1... | collective-permute-start | bytes 417800 | tf_op jit(solution)/shard_map/ppermute | solution.py:345
  35.0 5.1 %collective-permute-start.7 = (bf16[272,256]{1,0:T(8,128)(2,1)S(1)}, bf16[272,256]{1,0:T(8,128)(2,1)S(1)}, u32[]{:S(2)}, u32[]{:S(2)}) collective-permute-start(bf16[272,256]{1,0:T(8,128)(2,1)S(1)} %collective-permute-done.5.rest_0_.rest_5_), channel_id=1, source_target_pairs={{0,16},{16,32},{32,48},{48,64},{64,80},{80,96},{96,112},{112,0},{1... | collective-permute-start | bytes 417800 | tf_op jit(solution)/shard_map/ppermute | solution.py:345
  42.5 3.9 %collective-permute-start.10 = (f32[8,256]{1,0:T(8,128)S(1)}, f32[8,256]{1,0:T(8,128)S(1)}, u32[]{:S(2)}, u32[]{:S(2)}) collective-permute-start(f32[8,256]{1,0:T(8,128)S(1)} %get-tuple-element.44), channel_id=1, source_target_pairs={{0,112},{16,96},{32,80},{48,64},{64,48},{80,32},{96,16},{112,0},{1... | collective-permute-start | bytes 24584 | tf_op jit(solution)/shard_map/ppermute | solution.py:337
  43.5 4.6 %collective-permute-start.9 = (f32[8,256]{1,0:T(8,128)S(1)}, f32[8,256]{1,0:T(8,128)S(1)}, u32[]{:S(2)}, u32[]{:S(2)}) collective-permute-start(f32[8,256]{1,0:T(8,128)S(1)} %get-tuple-element.44), channel_id=1, source_target_pairs={{0,96},{16,112},{32,64},{48,80},{64,32},{80,48},{96,0},{112,16},{1... | collective-permute-start | bytes 24584 | tf_op jit(solution)/shard_map/ppermute | solution.py:337
  44.9 3.2 %collective-permute-start.8 = (f32[8,256]{1,0:T(8,128)S(1)}, f32[8,256]{1,0:T(8,128)S(1)}, u32[]{:S(2)}, u32[]{:S(2)}) collective-permute-start(f32[8,256]{1,0:T(8,128)S(1)} %get-tuple-element.44), channel_id=1, source_target_pairs={{0,16},{16,0},{32,48},{48,32},{64,80},{80,64},{96,112},{112,96},{1... | collective-permute-start | bytes 24584 | tf_op jit(solution)/shard_map/ppermute | solution.py:337
  48.1 3.8 %collective-permute-start.11 = (f32[8,256]{1,0:T(8,128)S(1)}, f32[8,256]{1,0:T(8,128)S(1)}, u32[]{:S(2)}, u32[]{:S(2)}) collective-permute-start(f32[8,256]{1,0:T(8,128)S(1)} %add_add_fusion), channel_id=1, source_target_pairs={{0,32},{16,48},{32,0},{48,16},{64,96},{80,112},{96,64},{112,80},{1... | collective-permute-start | bytes 24584 | tf_op jit(solution)/shard_map/ppermute | solution.py:337
  62.7 8.0 %collective-permute-start.12 = (bf16[4,4,128,256]{3,2,1,0:T(8,128)(2,1)S(1)}, bf16[4,4,128,256]{3,2,1,0:T(8,128)(2,1)S(1)}, u32[]{:S(2)}, u32[]{:S(2)}) collective-permute-start(bf16[4,4,128,256]{3,2,1,0:T(8,128)(2,1)S(1)} %get-tuple-element.54), channel_id=1, source_target_pairs={{0,1},{1,0},{2,3},{3,2},{4,5},{5,4},{6,7},{7,6},{8,9},{9,8},{10,11... | collective-permute-start | bytes 3145736 | tf_op jit(solution)/shard_map/ppermute | solution.py:337
  71.2 5.6 %collective-permute-start.13 = (bf16[4,128,256]{2,1,0:T(8,128)(2,1)S(1)}, bf16[4,128,256]{2,1,0:T(8,128)(2,1)S(1)}, u32[]{:S(2)}, u32[]{:S(2)}) collective-permute-start(bf16[4,128,256]{2,1,0:T(8,128)(2,1)S(1)} %get-tuple-element.57), channel_id=1, source_target_pairs={{0,128},{1,3},{2,130},{3,1},{4,132},{5,7},{6,134},{7,5},{128,0},{1... | collective-permute-start | bytes 786440 | tf_op jit(solution)/shard_map/ppermute | solution.py:362
  72.6 8.0 %collective-permute-start.15 = (bf16[4,128,256]{2,1,0:T(8,128)(2,1)S(1)}, bf16[4,128,256]{2,1,0:T(8,128)(2,1)S(1)}, u32[]{:S(2)}, u32[]{:S(2)}) collective-permute-start(bf16[4,128,256]{2,1,0:T(8,128)(2,1)S(1)} %get-tuple-element.58), channel_id=1, source_target_pairs={{0,136},{1,7},{2,138},{3,5},{4,140},{5,3},{6,142},{7,1},{128,8},{1... | collective-permute-start | bytes 786440 | tf_op jit(solution)/shard_map/ppermute | solution.py:362
  74.5 7.6 %collective-permute-start.14 = (bf16[4,128,256]{2,1,0:T(8,128)(2,1)S(1)}, bf16[4,128,256]{2,1,0:T(8,128)(2,1)S(1)}, u32[]{:S(2)}, u32[]{:S(2)}) collective-permute-start(bf16[4,128,256]{2,1,0:T(8,128)(2,1)S(1)} %get-tuple-element.59), channel_id=1, source_target_pairs={{0,8},{1,5},{2,10},{3,7},{4,12},{5,1},{6,14},{7,3},{128,136},{129,... | collective-permute-start | bytes 786440 | tf_op jit(solution)/shard_map/ppermute | solution.py:362
  82.2 3.4 %collective-permute-start.16 = (bf16[128,256]{1,0:T(8,128)(2,1)S(1)}, bf16[128,256]{1,0:T(8,128)(2,1)S(1)}, u32[]{:S(2)}, u32[]{:S(2)}) collective-permute-start(bf16[128,256]{1,0:T(8,128)(2,1)S(1)} %get-tuple-element.62), channel_id=1, source_target_pairs={{0,2},{1,129},{2,0},{3,131},{4,6},{5,133},{6,4},{7,135},{128,130},... | collective-permute-start | bytes 196616 | tf_op jit(solution)/shard_map/ppermute | solution.py:362
  82.3 4.4 %collective-permute-start.18 = (bf16[128,256]{1,0:T(8,128)(2,1)S(1)}, bf16[128,256]{1,0:T(8,128)(2,1)S(1)}, u32[]{:S(2)}, u32[]{:S(2)}) collective-permute-start(bf16[128,256]{1,0:T(8,128)(2,1)S(1)} %get-tuple-element.63), channel_id=1, source_target_pairs={{0,6},{1,137},{2,4},{3,139},{4,2},{5,141},{6,0},{7,143},{128,134},... | collective-permute-start | bytes 196616 | tf_op jit(solution)/shard_map/ppermute | solution.py:362
  84.8 4.6 %collective-permute-start.17 = (bf16[128,256]{1,0:T(8,128)(2,1)S(1)}, bf16[128,256]{1,0:T(8,128)(2,1)S(1)}, u32[]{:S(2)}, u32[]{:S(2)}) collective-permute-start(bf16[128,256]{1,0:T(8,128)(2,1)S(1)} %get-tuple-element.64), channel_id=1, source_target_pairs={{0,4},{1,9},{2,6},{3,11},{4,0},{5,13},{6,2},{7,15},{128,132},{129,... | collective-permute-start | bytes 196616 | tf_op jit(solution)/shard_map/ppermute | solution.py:362
  85.6 46.4 %copy-start.10 = (f32[256,256]{1,0:T(8,128)S(1)}, f32[256,256]{1,0:T(8,128)}, u32[]{:S(2)}) copy-start(f32[256,256]{1,0:T(8,128)} %copy-done.9) | copy-start | bytes 786436
  89.4 3.6 %collective-permute-start.19 = (bf16[128,256]{1,0:T(8,128)(2,1)S(1)}, bf16[128,256]{1,0:T(8,128)(2,1)S(1)}, u32[]{:S(2)}, u32[]{:S(2)}) collective-permute-start(bf16[128,256]{1,0:T(8,128)(2,1)S(1)} %fusion.5), channel_id=1, source_target_pairs={{0,16},{16,0},{32,48},{48,32},{64,80},{80,64},{96,112},{112,96},{1... | collective-permute-start | bytes 196616 | tf_op jit(solution)/shard_map/ppermute | solution.py:337
  93.1 6.2 %collective-permute-start.22 = (bf16[128,256]{1,0:T(8,128)(2,1)S(1)}, bf16[128,256]{1,0:T(8,128)(2,1)S(1)}, u32[]{:S(2)}, u32[]{:S(2)}) collective-permute-start(bf16[128,256]{1,0:T(8,128)(2,1)S(1)} %add_convert_fusion.2), channel_id=1, source_target_pairs={{0,96},{16,112},{32,64},{48,80},{64,32},{80,48},{96,0},{112,16},{1... | collective-permute-start | bytes 196616 | tf_op jit(solution)/shard_map/ppermute | solution.py:337
  95.1 7.3 %collective-permute-start.21 = (bf16[128,256]{1,0:T(8,128)(2,1)S(1)}, bf16[128,256]{1,0:T(8,128)(2,1)S(1)}, u32[]{:S(2)}, u32[]{:S(2)}) collective-permute-start(bf16[128,256]{1,0:T(8,128)(2,1)S(1)} %add_convert_fusion.2), channel_id=1, source_target_pairs={{0,64},{16,80},{32,96},{48,112},{64,0},{80,16},{96,32},{112,48},{1... | collective-permute-start | bytes 196616 | tf_op jit(solution)/shard_map/ppermute | solution.py:337
  99.3 6.9 %collective-permute-start.20 = (bf16[128,256]{1,0:T(8,128)(2,1)S(1)}, bf16[128,256]{1,0:T(8,128)(2,1)S(1)}, u32[]{:S(2)}, u32[]{:S(2)}) collective-permute-start(bf16[128,256]{1,0:T(8,128)(2,1)S(1)} %add_convert_fusion.2), channel_id=1, source_target_pairs={{0,32},{16,48},{32,0},{48,16},{64,96},{80,112},{96,64},{112,80},{1... | collective-permute-start | bytes 196616 | tf_op jit(solution)/shard_map/ppermute | solution.py:337
  106.2 4.7 %collective-permute-start.25 = (bf16[128,256]{1,0:T(8,128)(2,1)S(1)}, bf16[128,256]{1,0:T(8,128)(2,1)S(1)}, u32[]{:S(2)}, u32[]{:S(2)}) collective-permute-start(bf16[128,256]{1,0:T(8,128)(2,1)S(1)} %add_convert_fusion.1), channel_id=1, source_target_pairs={{0,6},{1,137},{2,4},{3,139},{4,2},{5,141},{6,0},{7,143},{128,134},... | collective-permute-start | bytes 196616 | tf_op jit(solution)/shard_map/ppermute | solution.py:362
  107.1 4.6 %collective-permute-start.24 = (bf16[128,256]{1,0:T(8,128)(2,1)S(1)}, bf16[128,256]{1,0:T(8,128)(2,1)S(1)}, u32[]{:S(2)}, u32[]{:S(2)}) collective-permute-start(bf16[128,256]{1,0:T(8,128)(2,1)S(1)} %add_convert_fusion.1), channel_id=1, source_target_pairs={{0,4},{1,9},{2,6},{3,11},{4,0},{5,13},{6,2},{7,15},{128,132},{129,... | collective-permute-start | bytes 196616 | tf_op jit(solution)/shard_map/ppermute | solution.py:362
  107.7 4.7 %collective-permute-start.23 = (bf16[128,256]{1,0:T(8,128)(2,1)S(1)}, bf16[128,256]{1,0:T(8,128)(2,1)S(1)}, u32[]{:S(2)}, u32[]{:S(2)}) collective-permute-start(bf16[128,256]{1,0:T(8,128)(2,1)S(1)} %add_convert_fusion.1), channel_id=1, source_target_pairs={{0,2},{1,129},{2,0},{3,131},{4,6},{5,133},{6,4},{7,135},{128,130},... | collective-permute-start | bytes 196616 | tf_op jit(solution)/shard_map/ppermute | solution.py:362
  112.4 8.3 %collective-permute-start.27 = (bf16[4,128,256]{2,1,0:T(8,128)(2,1)S(1)}, bf16[4,128,256]{2,1,0:T(8,128)(2,1)S(1)}, u32[]{:S(2)}, u32[]{:S(2)}) collective-permute-start(bf16[4,128,256]{2,1,0:T(8,128)(2,1)S(1)} %get-tuple-element.61), channel_id=1, source_target_pairs={{0,8},{1,5},{2,10},{3,7},{4,12},{5,1},{6,14},{7,3},{128,136},{129,... | collective-permute-start | bytes 786440 | tf_op jit(solution)/shard_map/ppermute | solution.py:362
  113.8 8.6 %collective-permute-start.26 = (bf16[4,128,256]{2,1,0:T(8,128)(2,1)S(1)}, bf16[4,128,256]{2,1,0:T(8,128)(2,1)S(1)}, u32[]{:S(2)}, u32[]{:S(2)}) collective-permute-start(bf16[4,128,256]{2,1,0:T(8,128)(2,1)S(1)} %get-tuple-element.61), channel_id=1, source_target_pairs={{0,128},{1,3},{2,130},{3,1},{4,132},{5,7},{6,134},{7,5},{128,0},{1... | collective-permute-start | bytes 786440 | tf_op jit(solution)/shard_map/ppermute | solution.py:362
  115.0 8.0 %collective-permute-start.28 = (bf16[4,128,256]{2,1,0:T(8,128)(2,1)S(1)}, bf16[4,128,256]{2,1,0:T(8,128)(2,1)S(1)}, u32[]{:S(2)}, u32[]{:S(2)}) collective-permute-start(bf16[4,128,256]{2,1,0:T(8,128)(2,1)S(1)} %get-tuple-element.61), channel_id=1, source_target_pairs={{0,136},{1,7},{2,138},{3,5},{4,140},{5,3},{6,142},{7,1},{128,8},{1... | collective-permute-start | bytes 786440 | tf_op jit(solution)/shard_map/ppermute | solution.py:362
  123.2 11.1 %collective-permute-start.29 = (bf16[4,4,128,256]{3,2,1,0:T(8,128)(2,1)S(1)}, bf16[4,4,128,256]{3,2,1,0:T(8,128)(2,1)S(1)}, u32[]{:S(2)}, u32[]{:S(2)}) collective-permute-start(bf16[4,4,128,256]{3,2,1,0:T(8,128)(2,1)S(1)} %pad_maximum_fusion.mine_ref), channel_id=1, source_target_pairs={{0,1},{1,0},{2,3},{3,2},{4,5},{5,4},{6,7},{7,6},{8,9},{9,8},{10,11... | collective-permute-start | bytes 3145736 | tf_op jit(solution)/shard_map/ppermute | solution.py:337
  (20 other events, 115.6 us)
Sparse Core Ops, SparseCore 0:
  85.7 38.5 reduce-scatter.1

commit v4 on v3

--- a/solution.py
+++ b/solution.py
@@ -49,7 +49,8 @@
     return copy
 
 
-def pack_kernel(user_hbm, pid_hbm, feat_hbm, nid_hbm, bucket_hbm, mine_ref, near_ref, pid_ref, nid_ref, bucket_ref, sems):
+def pack_kernel(s_ref, user_hbm, pid_hbm, feat_hbm, nid_hbm, bucket_hbm, mine_ref, near_ref, pid_ref, nid_ref, bucket_ref, sems):
+    del s_ref
     copies = [
         start(pid_hbm, pid_ref, sems.at[0]),
         start(nid_hbm, nid_ref, sems.at[1]),
@@ -77,11 +78,11 @@
         copy.wait()
 
 
-def pack(user_emb, pos_id, neg_feat, neg_id, neg_bucket):
+def pack(scalars, user_emb, pos_id, neg_feat, neg_id, neg_bucket):
     vm = pl.BlockSpec(memory_space=pltpu.VMEM)
     return pl.pallas_call(
         pack_kernel,
-        in_specs=[pl.BlockSpec(memory_space=pltpu.HBM)] * 5,
+        in_specs=[pl.BlockSpec(memory_space=pltpu.SMEM)] + [pl.BlockSpec(memory_space=pltpu.HBM)] * 5,
         out_specs=[vm] * 2,
         out_shape=[jax.ShapeDtypeStruct((U + 16, E), BF), jax.ShapeDtypeStruct((N + 16, E), BF)],
         scratch_shapes=[
@@ -93,28 +94,33 @@
         compiler_params=params(60 * 1024 * 1024),
         cost_estimate=cost(0, 1e6),
         name="pack",
-    )(user_emb, pos_id.reshape(1, U), neg_feat, neg_id.reshape(1, N), neg_bucket.reshape(1, N))
+    )(scalars, user_emb, pos_id.reshape(1, U), neg_feat, neg_id.reshape(1, N), neg_bucket.reshape(1, N))
 
 
 def hidden(feat, w_in_ref):
     return jnp.maximum(mm(feat, w_in_ref[...]), 0.0).astype(BF)
 
 
-def hidden_kernel(near_ref, pos_ref, w_in_ref, hid_ref):
+def hidden_kernel(near_ref, pos_ref, w_in_ref, hid_ref, feat_ref, tail_ref, w_in_out):
     for m, feat in enumerate((near_ref[0:TILE], near_ref[TILE:N], pos_ref[...])):
-        hid_ref[m * TILE : (m + 1) * TILE] = hidden(feat, w_in_ref)
-
-
-def embed_kernel(hid_ref, w_out_ref, emb_ref, pemb_ref):
+        rows = slice(m * TILE, (m + 1) * TILE)
+        feat_ref[rows] = feat
+        hid_ref[rows] = hidden(feat, w_in_ref)
+    tail_ref[...] = near_ref[N : N + 16]
+    w_in_out[...] = w_in_ref[...]
+
+
+def embed_kernel(hid_ref, w_out_ref, emb_ref, pemb_ref, w_out_out):
+    w_out_out[...] = w_out_ref[...]
     for m, (ref, first) in enumerate([(emb_ref, 0), (emb_ref, TILE), (pemb_ref, 0)]):
         hid = hid_ref[m * TILE : (m + 1) * TILE]
         ref[first : first + TILE] = mm(hid, w_out_ref[...]).astype(BF)
 
 
-def far_kernel(near_ref, far_ref, w_in_ref, w_out_ref, table_ref, hid_ref, emb_ref, nid_ref, bias_ref):
+def far_kernel(near_tail, far_ref, w_in_ref, w_out_ref, table_ref, hid_ref, emb_ref, nid_ref, bias_ref):
     lane = lax.broadcasted_iota(I32, (TILE, 128), 1).astype(F32)
-    for side, ref in enumerate((near_ref, far_ref)):
-        tail = jnp.concatenate([ref[N : N + 16].astype(F32), jnp.zeros((112, E), F32)], axis=0).T
+    for side, tail in enumerate((near_tail[...], far_ref[N : N + 16])):
+        tail = jnp.concatenate([tail.astype(F32), jnp.zeros((112, E), F32)], axis=0).T
         for block in range(2):
             rows = slice((2 * side + block) * TILE, (2 * side + block + 1) * TILE)
             nid = tail[:, block : block + 1] * 64.0 + tail[:, block + 2 : block + 3]
@@ -138,7 +144,7 @@
         in_specs=[vm] * len(args),
         out_specs=[vm] * len(outs),
         out_shape=[jax.ShapeDtypeStruct(shape, dtype) for shape, dtype in outs],
-        compiler_params=params(),
+        compiler_params=params(14 * 1024 * 1024),
         cost_estimate=cost(flops, 4e6),
         name=name,
     )(*args)
@@ -201,7 +207,7 @@
             jax.ShapeDtypeStruct((NN, n * U), BF),
         ],
         scratch_shapes=[pltpu.VMEM((NN, U), F32)],
-        compiler_params=params(),
+        compiler_params=params(14 * 1024 * 1024),
         cost_estimate=cost(2 * n * U * NN * E, 5e6, n * U * NN),
         name="score",
     )(scalars, near_emb, far_emb, nid, bias, pemb, tloc, tin, *[users[k] for k in ks])
@@ -209,7 +215,7 @@
 
 def grad_kernel(s_ref, tot_ref, tloc_ref, pexp_ref, near_emb, far_emb, pemb_ref, kept_a, kept_b, *rest):
     users = rest[:NZ]
-    ug_ref, g_ref, pterm_ref, wu, ratio, rel = rest[NZ:]
+    keep_ref, send_ref, g_ref, pterm_ref, wu, ratio, rel = rest[NZ:]
     z = s_ref[0]
     tot = tot_ref[...]
     shrink = jnp.where(tot > 1.0, SMALL, 1.0)
@@ -232,7 +238,9 @@
         cols_k = slice(i * U, (i + 1) * U)
         ug = lax.dot_general(kept[0:N, cols_k], near_emb[...], TN, preferred_element_type=F32)
         ug = ug + lax.dot_general(kept[N:NN, cols_k], far_emb[...], TN, preferred_element_type=F32)
-        ug_ref[home(z, k)] = (ug * cols[:, k : k + 1]).astype(BF)
+        apart = jnp.bitwise_xor(home(z, k), z)
+        place = (apart & 2) + (apart >> 2)
+        (send_ref if OFFSETS[k] % 2 else keep_ref)[place] = (ug * cols[:, k : k + 1]).astype(BF)
     for m in range(NN // TILE):
         rows = slice(m * TILE, (m + 1) * TILE)
         g = mm(kept_a[rows], wu[0 : FIRST * U]) + mm(kept_b[rows], wu[FIRST * U :])
@@ -245,9 +253,10 @@
     return pl.pallas_call(
         grad_kernel,
         in_specs=[pl.BlockSpec(memory_space=pltpu.SMEM)] + [vm] * (8 + NZ),
-        out_specs=[vm, vm, vm],
+        out_specs=[vm] * 4,
         out_shape=[
-            jax.ShapeDtypeStruct((NZ, U, E), BF),
+            jax.ShapeDtypeStruct((NZ // 2, U, E), BF),
+            jax.ShapeDtypeStruct((NZ // 2, U, E), BF),
             jax.ShapeDtypeStruct((ROWS, E), BF),
             jax.ShapeDtypeStruct((U, E), F32),
         ],
@@ -262,10 +271,9 @@
     )(scalars, tot, tloc, pexp, near_emb, far_emb, pemb, kept_a, kept_b, *users)
 
 
-def back_kernel(s_ref, g_ref, near_ref, pos_ref, far_ref, w_out_ref, hid_ref, far_hid, mine_ref, theirs_ref, feat):
+def back_kernel(s_ref, g_ref, feat_ref, far_ref, w_out_ref, hid_ref, far_hid, mine_ref, theirs_ref, feat):
     first, second, core = s_ref[1], s_ref[2], s_ref[3]
-    feat[0:N] = near_ref[0:N]
-    feat[N : N + U] = pos_ref[...]
+    feat[0 : N + U] = feat_ref[...]
     feat[N + U : ROWS] = far_ref[0:N]
     for c in range(H // WIDE):
         cols = slice(c * WIDE, (c + 1) * WIDE)
@@ -285,18 +293,18 @@
                 theirs_ref[to_theirs, jnp.bitwise_xor(first, 2 * t + half)] = theirs[rows]
 
 
-def backward(scalars, g, near, pos, far, w_out, hid, far_hid):
+def backward(scalars, g, feat, far, w_out, hid, far_hid):
     vm = pl.BlockSpec(memory_space=pltpu.VMEM)
     return pl.pallas_call(
         back_kernel,
-        in_specs=[pl.BlockSpec(memory_space=pltpu.SMEM)] + [vm] * 7,
+        in_specs=[pl.BlockSpec(memory_space=pltpu.SMEM)] + [vm] * 6,
         out_specs=[vm, vm],
         out_shape=[jax.ShapeDtypeStruct((4, 4, 128, TILE), BF)] * 2,
         scratch_shapes=[pltpu.VMEM((ROWS, E), BF)],
         compiler_params=params(),
         cost_estimate=cost(6 * ROWS * E * H, 10e6),
         name="backward",
-    )(scalars, g, near, pos, far, w_out, hid, far_hid)
+    )(scalars, g, feat, far, w_out, hid, far_hid)
 
 
 def finish_kernel(s_ref, mine_ref, other_ref, w_in_ref, w_out_ref):
@@ -376,14 +384,27 @@
     return x
 
 
-def all_reduce(mine, theirs):
+def halve(keep, send, k):
+    total = add(keep, swap(send, "z", k)).astype(BF)
+    half = total.shape[0] // 2
+    return (total[:half], total[half:]) if half else total[0]
+
+
+def all_reduce(mine, theirs, keep, send):
     half = add(mine, swap(theirs, "core", 1)).astype(BF)
     quarter = add(half[0], *[plane_swap(half[k], k, 0) for k in (1, 2, 3)]).astype(BF)
+    keep, send = halve(keep, send, 1)
+    quarter, keep, send = lax.optimization_barrier((quarter, keep, send))
     part = add(quarter[0], *[plane_swap(quarter[k], k, 1) for k in (1, 2, 3)])
+    keep, send = halve(keep, send, 2)
+    part, keep, send = lax.optimization_barrier((part, keep, send))
     part = sum_over_z(part, ((1,), (2, 4, 6)), BF).astype(BF)
+    part, keep, send = lax.optimization_barrier((part, keep, send))
     quarter = jnp.stack([part] + [plane_swap(part, k, 1) for k in (1, 2, 3)])
+    user = halve(keep, send, 4)
+    quarter, user = lax.optimization_barrier((quarter, user))
     half = jnp.stack([quarter] + [plane_swap(quarter, k, 0) for k in (1, 2, 3)])
-    return half, swap(half, "core", 1)
+    return half, swap(half, "core", 1), user
 
 
 def on_device(user_emb, pos_feat, pos_id, neg_feat, neg_id, neg_bucket, logq_table, w_in, w_out):
@@ -391,15 +412,23 @@
     xx = x_hi * 2 + x_lo
     scalars = jnp.stack([z, jnp.where(core == 0, xx, y), jnp.where(core == 0, y, xx), core]).astype(I32)
 
-    mine, near = pack(user_emb, pos_id, neg_feat, neg_id, neg_bucket)
+    mine, near = pack(scalars, user_emb, pos_id, neg_feat, neg_id, neg_bucket)
     up, down = shift(mine, 1), shift(mine, -1)
     far = swap(near, "x_lo", 1)
     users = [mine, up, down]
-    (hid,) = in_vmem(hidden_kernel, "hidden", 2 * (N + U) * E * H, [((N + U, H), BF)], near, pos_feat, w_in)
+    hid, feat, tail, w_in = in_vmem(
+        hidden_kernel,
+        "hidden",
+        2 * (N + U) * E * H,
+        [((N + U, H), BF), ((N + U, E), BF), ((16, E), BF), ((E, H), BF)],
+        near,
+        pos_feat,
+        w_in,
+    )
     up, down = shift(after(up, hid), 1), shift(after(down, hid), -1)
     users += [up, down]
-    near_emb, pemb = in_vmem(
-        embed_kernel, "embed", 2 * (N + U) * E * H, [((N, E), BF), ((U, E), BF)], hid, w_out
+    near_emb, pemb, w_out = in_vmem(
+        embed_kernel, "embed", 2 * (N + U) * E * H, [((N, E), BF), ((U, E), BF), ((H, E), BF)], hid, w_out
     )
     up, down = shift(after(up, near_emb), 1), shift(after(down, near_emb), -1)
     users += [up, down]
@@ -408,7 +437,7 @@
         "far",
         4 * N * E * H,
         [((N, H), BF), ((N, E), BF), ((NN, 128), F32), ((NN, 128), F32)],
-        near,
+        tail,
         far,
         w_in,
         w_out,
@@ -420,13 +449,13 @@
     tloc, tot, pexp, kept_a = score(ks[:FIRST], scalars, near_emb, far_emb, nid, bias, pemb, none, none, users)
     tloc, tot, _, kept_b = score(ks[FIRST:], scalars, near_emb, far_emb, nid, bias, pemb, tloc, tot, users)
     tot = sum_over_z(tot, ((1, 6, 7), (2,)), F32)
-    ug, g, pterm = grads(scalars, tot, tloc, pexp, near_emb, far_emb, pemb, kept_a, kept_b, users)
-    user_sum = lax.psum_scatter(ug, "z", scatter_dimension=0, tiled=False)
-    mine_g, theirs_g = backward(scalars, g, near, pos_feat, far, w_out, hid, far_hid)
-    half, other = all_reduce(mine_g, theirs_g)
+    keep, send, g, pterm = grads(
+        scalars, tot, tloc, pexp, near_emb, far_emb, pemb, kept_a, kept_b, users
+    )
+    mine_g, theirs_g = backward(scalars, g, feat, far, w_out, hid, far_hid)
+    half, other, user = all_reduce(mine_g, theirs_g, keep, send)
     w_in_grad, w_out_grad = finish(scalars, half, other)
-    user_grad = user_sum.astype(F32) + pterm
-    return user_grad, w_in_grad, w_out_grad
+    return user.astype(F32) + pterm, w_in_grad, w_out_grad
 
 
 def solution(mesh):

time: 145 us -> 140 us (0.966)
  between operations: 14.3 us -> 0.92 us
  waiting for transfers between devices: 37.5 us -> 50.5 us
  local copies, waits for them, and re-layouts: 8.47 us -> 3.23 us
  starting transfers between devices: 55.9 us -> 59.4 us
  Pallas kernels: 25.4 us -> 23.1 us
    ppermute x11 -> x14, waiting for transfers between devices: 14.9 us -> 35.8 us  [swap(): lax.ppermute(x, axis, [(i, i ^ k) for i in range(SIZES[AXES.index(axis)])])]
    ppermute x12, waiting for transfers between devices: 20.7 us -> 10.5 us  [plane_swap(): return lax.ppermute(x, AXES, pairs)]
    unnamed x42 -> x14, local copies, waits for them, and re-layouts: 8.4 us -> 3.1 us
    ppermute x11 -> x14, starting transfers between devices: 29.9 us -> 33.1 us  [swap(): lax.ppermute(x, axis, [(i, i ^ k) for i in range(SIZES[AXES.index(axis)])])]
    ppermute x7, waiting for transfers between devices: 1.88 us -> 4.22 us  [shift(): return lax.ppermute(x, 'z', [(i, (i + by) % NZ) for i in range(NZ)])]
  transfers between devices with their start and end apart: 31 -> 33, of which waited for: 20 -> 19; matrix products, arithmetic and copies ran while one was open for 1% -> 1% of each run, Pallas kernels for 6% -> 5%
where the time goes in v4:
time: 140 us; the launch traced here: 139 us
  starting transfers between devices  59.4 us (42%)
  waiting for transfers between devices  50.5 us (36%)
  Pallas kernels  23.1 us (16%)
  local copies, waits for them, and re-layouts  3.23 us (2%)
  other arithmetic  2.29 us (2%)
    ppermute x14, waiting for transfers between devices, swap(): lax.ppermute(x, axis, [(i, i ^ k) for i in range(SIZES[AXES.index(axis)])])  35.8 us
    ppermute x14, starting transfers between devices, swap(): lax.ppermute(x, axis, [(i, i ^ k) for i in range(SIZES[AXES.index(axis)])])  33.1 us
    ppermute x12, starting transfers between devices, plane_swap(): return lax.ppermute(x, AXES, pairs)  14.2 us
    ppermute x7, starting transfers between devices, shift(): return lax.ppermute(x, 'z', [(i, (i + by) % NZ) for i in range(NZ)])  12.1 us
    ppermute x12, waiting for transfers between devices, plane_swap(): return lax.ppermute(x, AXES, pairs)  10.5 us
    pallas_call x1, Pallas kernels, backward(): pl.pallas_call(back_kernel, in_specs=[pl.BlockSpec(memory_space=pltpu.SME...  5.38 us
    pallas_call x2, Pallas kernels, score(): pl.pallas_call(functools.partial(score_kernel, ks), in_specs=[pl.BlockSpe...  5.2 us
    ppermute x7, waiting for transfers between devices, shift(): return lax.ppermute(x, 'z', [(i, (i + by) % NZ) for i in range(NZ)])  4.22 us
  transfers between devices with their start and end apart: 33, of which 19 were waited for; matrix products, arithmetic and copies ran while one was open for 1% of the time, Pallas kernels for 5%

profile of v4, /device:TPU:1, one launch (start us, length us, event | category | flops | bytes accessed | tf_op | source)
XLA Modules:
  0.0 139.5 jit_solution(11541825614063995310)
XLA Ops:
  1.2 2.5 %pack.1 = (bf16[272,256]{1,0:T(8,128)(2,1)}, bf16[528,256]{1,0:T(8,128)(2,1)}) custom-call(s32[4]{0:T(128)} %pad_add_fusion.s_ref, bf16[256,256]{1,0:T(8,128)(2,1)} %user_hbm.1, s32[1,256]{1,0:T(1,128)} %bitcast.49, bf16[512,256]{1,0:T(8,128)(2,1)} %feat_hbm.1, s32[1,512]{1,0:T(1,128)} %bitcast.47, s32[1,512]{1,0:T(1,128)} %bitcast.48), custom_call_target="tpu_custom_call" | custom-call | bytes 1000000 | tf_op jit(solution)/shard_map/pack/pallas_call | solution.py:83
  3.8 2.5 %collective-permute-start.1 = (bf16[272,256]{1,0:T(8,128)(2,1)}, bf16[272,256]{1,0:T(8,128)(2,1)S(1)}, u32[]{:S(2)}, u32[]{:S(2)}) collective-permute-start(bf16[272,256]{1,0:T(8,128)(2,1)} %get-tuple-element.57.rest_0_), channel_id=1, source_target_pairs={{0,16},{16,32},{32,48},{48,64},{64,80},{80,96},{96,112},{112,0},{1... | collective-permute-start | bytes 417800 | tf_op jit(solution)/shard_map/ppermute | solution.py:353
  7.5 4.0 %collective-permute-start.2 = (bf16[272,256]{1,0:T(8,128)(2,1)}, bf16[272,256]{1,0:T(8,128)(2,1)S(1)}, u32[]{:S(2)}, u32[]{:S(2)}) collective-permute-start(bf16[272,256]{1,0:T(8,128)(2,1)} %get-tuple-element.57.rest_0_), channel_id=1, source_target_pairs={{0,112},{16,0},{32,16},{48,32},{64,48},{80,64},{96,80},{112,96},{1... | collective-permute-start | bytes 417800 | tf_op jit(solution)/shard_map/ppermute | solution.py:353
  16.9 2.7 %collective-permute-start.4 = (bf16[272,256]{1,0:T(8,128)(2,1)S(1)}, bf16[272,256]{1,0:T(8,128)(2,1)S(1)}, u32[]{:S(2)}, u32[]{:S(2)}) collective-permute-start(bf16[272,256]{1,0:T(8,128)(2,1)S(1)} %collective-permute-done.2.rest_2_), channel_id=1, source_target_pairs={{0,112},{16,0},{32,16},{48,32},{64,48},{80,64},{96,80},{112,96},{1... | collective-permute-start | bytes 417800 | tf_op jit(solution)/shard_map/ppermute | solution.py:353
  20.9 1.7 %far.1 = (bf16[512,2048]{1,0:T(8,128)(2,1)S(1)}, bf16[512,256]{1,0:T(8,128)(2,1)S(1)}, f32[1024,128]{1,0:T(8,128)S(1)}, f32[1024,128]{1,0:T(8,128)S(1)}) custom-call(bf16[16,256]{1,0:T(8,128)(2,1)S(1)} %get-tuple-element.50.near_tail, bf16[528,256]{1,0:T(8,128)(2,1)S(1)} %collective-permute-done.far_ref, bf16[256,2048]{1,0:T(8,128)(2,1)S(1)} %get-tuple-element.51.w_in_ref, ...), custom_call_target="tpu_custom_call" | custom-call | flops 1073741824 | bytes 4000000 | tf_op jit(solution)/shard_map/far/pallas_call | solution.py:142
  22.6 2.7 %collective-permute-start.6 = (bf16[272,256]{1,0:T(8,128)(2,1)S(1)}, bf16[272,256]{1,0:T(8,128)(2,1)S(1)}, u32[]{:S(2)}, u32[]{:S(2)}) collective-permute-start(bf16[272,256]{1,0:T(8,128)(2,1)S(1)} %collective-permute-done.4.rest_4_), channel_id=1, source_target_pairs={{0,112},{16,0},{32,16},{48,32},{64,48},{80,64},{96,80},{112,96},{1... | collective-permute-start | bytes 417800 | tf_op jit(solution)/shard_map/ppermute | solution.py:353
  26.0 2.8 %score.2 = (f32[8,256]{1,0:T(8,128)S(1)}, f32[8,256]{1,0:T(8,128)S(1)}, f32[1,256]{1,0:T(1,128)S(1)}, bf16[1024,1280]{1,0:T(8,128)(2,1)S(1)}) custom-call(s32[4]{0:T(128)S(1)} %copy-done.1, bf16[512,256]{1,0:T(8,128)(2,1)S(1)} %get-tuple-element.49.near_emb, bf16[512,256]{1,0:T(8,128)(2,1)S(1)} %get-tuple-element.53.far_emb, ...), custom_call_target="tpu_custom_call" | custom-call | flops 671088640 | bytes 5000000 | tf_op jit(solution)/shard_map/score/pallas_call | solution.py:199
  28.8 2.3 %collective-permute-done.7.rest_2_.rest_7_ = bf16[272,256]{1,0:T(8,128)(2,1)S(1)} collective-permute-done((bf16[272,256]{1,0:T(8,128)(2,1)S(1)}, bf16[272,256]{1,0:T(8,128)(2,1)S(1)}, u32[]{:S(2)}, u32[]{:S(2)}) %collective-permute-start.7) | collective-permute-done | bytes 139296 | tf_op jit(solution)/shard_map/ppermute | solution.py:353
  31.1 2.4 %score.3 = (f32[8,256]{1,0:T(8,128)S(1)}, f32[8,256]{1,0:T(8,128)S(1)}, f32[1,256]{1,0:T(1,128)}, bf16[1024,768]{1,0:T(8,128)(2,1)S(1)}) custom-call(s32[4]{0:T(128)S(1)} %copy-done.1, bf16[512,256]{1,0:T(8,128)(2,1)S(1)} %get-tuple-element.49.near_emb, bf16[512,256]{1,0:T(8,128)(2,1)S(1)} %get-tuple-element.53.far_emb, ...), custom_call_target="tpu_custom_call" | custom-call | flops 402653184 | bytes 5000000 | tf_op jit(solution)/shard_map/score/pallas_call | solution.py:199
  33.9 1.7 %collective-permute-start.9 = (f32[8,256]{1,0:T(8,128)S(1)}, f32[8,256]{1,0:T(8,128)S(1)}, u32[]{:S(2)}, u32[]{:S(2)}) collective-permute-start(f32[8,256]{1,0:T(8,128)S(1)} %get-tuple-element.65), channel_id=1, source_target_pairs={{0,96},{16,112},{32,64},{48,80},{64,32},{80,48},{96,0},{112,16},{1... | collective-permute-start | bytes 24584 | tf_op jit(solution)/shard_map/ppermute | solution.py:345
  35.6 1.8 %collective-permute-start.8 = (f32[8,256]{1,0:T(8,128)S(1)}, f32[8,256]{1,0:T(8,128)S(1)}, u32[]{:S(2)}, u32[]{:S(2)}) collective-permute-start(f32[8,256]{1,0:T(8,128)S(1)} %get-tuple-element.65), channel_id=1, source_target_pairs={{0,16},{16,0},{32,48},{48,32},{64,80},{80,64},{96,112},{112,96},{1... | collective-permute-start | bytes 24584 | tf_op jit(solution)/shard_map/ppermute | solution.py:345
  38.5 2.4 %collective-permute-start.11 = (f32[8,256]{1,0:T(8,128)S(1)}, f32[8,256]{1,0:T(8,128)S(1)}, u32[]{:S(2)}, u32[]{:S(2)}) collective-permute-start(f32[8,256]{1,0:T(8,128)S(1)} %add_add_fusion), channel_id=1, source_target_pairs={{0,32},{16,48},{32,0},{48,16},{64,96},{80,112},{96,64},{112,80},{1... | collective-permute-start | bytes 24584 | tf_op jit(solution)/shard_map/ppermute | solution.py:345
  42.0 3.3 %grads.1 = (bf16[4,256,256]{2,1,0:T(8,128)(2,1)S(1)}, bf16[4,256,256]{2,1,0:T(8,128)(2,1)S(1)}, bf16[1280,256]{1,0:T(8,128)(2,1)S(1)}, f32[256,256]{1,0:T(8,128)S(1)}) custom-call(s32[4]{0:T(128)S(1)} %copy-done.1, f32[8,256]{1,0:T(8,128)S(1)} %add.64.tot_ref, f32[8,256]{1,0:T(8,128)S(1)} %get-tuple-element.66.tloc_ref, ...), custom_call_target="tpu_custom_call" | custom-call | flops 2147483648 | bytes 8000000 | tf_op jit(solution)/shard_map/grads/pallas_call | solution.py:253
  45.3 5.4 %backward.1 = (bf16[4,4,128,256]{3,2,1,0:T(8,128)(2,1)S(1)}, bf16[4,4,128,256]{3,2,1,0:T(8,128)(2,1)S(1)}) custom-call(s32[4]{0:T(128)S(1)} %copy-done.1, bf16[1280,256]{1,0:T(8,128)(2,1)S(1)} %get-tuple-element.70.g_ref, bf16[768,256]{1,0:T(8,128)(2,1)S(1)} %get-tuple-element.71.feat_ref, bf16[528,256]{1,0:T(8,128)(2,1)S(1)} %collective-permute-done.far_ref, ...), custom_call_target="tpu_custom_call" | custom-call | flops 4026531840 | bytes 10000000 | tf_op jit(solution)/shard_map/backward/pallas_call | solution.py:298
  50.7 7.3 %collective-permute-start.12 = (bf16[4,4,128,256]{3,2,1,0:T(8,128)(2,1)S(1)}, bf16[4,4,128,256]{3,2,1,0:T(8,128)(2,1)S(1)}, u32[]{:S(2)}, u32[]{:S(2)}) collective-permute-start(bf16[4,4,128,256]{3,2,1,0:T(8,128)(2,1)S(1)} %get-tuple-element.74), channel_id=1, source_target_pairs={{0,1},{1,0},{2,3},{3,2},{4,5},{5,4},{6,7},{7,6},{8,9},{9,8},{10,11... | collective-permute-start | bytes 3145736 | tf_op jit(solution)/shard_map/ppermute | solution.py:345
  57.9 1.9 %collective-permute-start.16 = (bf16[4,256,256]{2,1,0:T(8,128)(2,1)S(1)}, bf16[4,256,256]{2,1,0:T(8,128)(2,1)S(1)}, u32[]{:S(2)}, u32[]{:S(2)}) collective-permute-start(bf16[4,256,256]{2,1,0:T(8,128)(2,1)S(1)} %get-tuple-element.76), channel_id=1, source_target_pairs={{0,16},{16,0},{32,48},{48,32},{64,80},{80,64},{96,112},{112,96},{1... | collective-permute-start | bytes 1572872 | tf_op jit(solution)/shard_map/ppermute | solution.py:345
  62.0 1.9 %collective-permute-start.15 = (bf16[4,128,256]{2,1,0:T(8,128)(2,1)S(1)}, bf16[4,128,256]{2,1,0:T(8,128)(2,1)S(1)}, u32[]{:S(2)}, u32[]{:S(2)}) collective-permute-start(bf16[4,128,256]{2,1,0:T(8,128)(2,1)S(1)} %get-tuple-element.92), channel_id=1, source_target_pairs={{0,136},{1,7},{2,138},{3,5},{4,140},{5,3},{6,142},{7,1},{128,8},{1... | collective-permute-start | bytes 786440 | tf_op jit(solution)/shard_map/ppermute | solution.py:370
  64.7 7.3 %collective-permute-done.16 = bf16[4,256,256]{2,1,0:T(8,128)(2,1)S(1)} collective-permute-done((bf16[4,256,256]{2,1,0:T(8,128)(2,1)S(1)}, bf16[4,256,256]{2,1,0:T(8,128)(2,1)S(1)}, u32[]{:S(2)}, u32[]{:S(2)}) %collective-permute-start.16) | collective-permute-done | bytes 524320 | tf_op jit(solution)/shard_map/ppermute | solution.py:345
  72.7 2.5 %collective-permute-start.19 = (bf16[128,256]{1,0:T(8,128)(2,1)S(1)}, bf16[128,256]{1,0:T(8,128)(2,1)S(1)}, u32[]{:S(2)}, u32[]{:S(2)}) collective-permute-start(bf16[128,256]{1,0:T(8,128)(2,1)S(1)} %get-tuple-element.99), channel_id=1, source_target_pairs={{0,6},{1,137},{2,4},{3,139},{4,2},{5,141},{6,0},{7,143},{128,134},... | collective-permute-start | bytes 196616 | tf_op jit(solution)/shard_map/ppermute | solution.py:370
  75.7 2.6 %collective-permute-start.20 = (bf16[2,256,256]{2,1,0:T(8,128)(2,1)S(1)}, bf16[2,256,256]{2,1,0:T(8,128)(2,1)S(1)}, u32[]{:S(2)}, u32[]{:S(2)}) collective-permute-start(bf16[2,256,256]{2,1,0:T(8,128)(2,1)S(1)} %get-tuple-element.79), channel_id=1, source_target_pairs={{0,32},{16,48},{32,0},{48,16},{64,96},{80,112},{96,64},{112,80},{1... | collective-permute-start | bytes 786440 | tf_op jit(solution)/shard_map/ppermute | solution.py:345
  79.8 9.8 %collective-permute-done.20 = bf16[2,256,256]{2,1,0:T(8,128)(2,1)S(1)} collective-permute-done((bf16[2,256,256]{2,1,0:T(8,128)(2,1)S(1)}, bf16[2,256,256]{2,1,0:T(8,128)(2,1)S(1)}, u32[]{:S(2)}, u32[]{:S(2)}) %collective-permute-start.20) | collective-permute-done | bytes 262176 | tf_op jit(solution)/shard_map/ppermute | solution.py:345
  93.0 2.9 %collective-permute-start.24 = (bf16[128,256]{1,0:T(8,128)(2,1)S(1)}, bf16[128,256]{1,0:T(8,128)(2,1)S(1)}, u32[]{:S(2)}, u32[]{:S(2)}) collective-permute-start(bf16[128,256]{1,0:T(8,128)(2,1)S(1)} %add_convert_fusion.5), channel_id=1, source_target_pairs={{0,96},{16,112},{32,64},{48,80},{64,32},{80,48},{96,0},{112,16},{1... | collective-permute-start | bytes 196616 | tf_op jit(solution)/shard_map/ppermute | solution.py:345
  95.9 4.0 %collective-permute-start.23 = (bf16[128,256]{1,0:T(8,128)(2,1)S(1)}, bf16[128,256]{1,0:T(8,128)(2,1)S(1)}, u32[]{:S(2)}, u32[]{:S(2)}) collective-permute-start(bf16[128,256]{1,0:T(8,128)(2,1)S(1)} %add_convert_fusion.5), channel_id=1, source_target_pairs={{0,64},{16,80},{32,96},{48,112},{64,0},{80,16},{96,32},{112,48},{1... | collective-permute-start | bytes 196616 | tf_op jit(solution)/shard_map/ppermute | solution.py:345
  99.9 4.8 %collective-permute-done.23 = bf16[128,256]{1,0:T(8,128)(2,1)S(1)} collective-permute-done((bf16[128,256]{1,0:T(8,128)(2,1)S(1)}, bf16[128,256]{1,0:T(8,128)(2,1)S(1)}, u32[]{:S(2)}, u32[]{:S(2)}) %collective-permute-start.23) | collective-permute-done | bytes 65568 | tf_op jit(solution)/shard_map/ppermute | solution.py:345
  104.6 3.5 %collective-permute-done.22 = bf16[128,256]{1,0:T(8,128)(2,1)S(1)} collective-permute-done((bf16[128,256]{1,0:T(8,128)(2,1)S(1)}, bf16[128,256]{1,0:T(8,128)(2,1)S(1)}, u32[]{:S(2)}, u32[]{:S(2)}) %collective-permute-start.22) | collective-permute-done | bytes 65568 | tf_op jit(solution)/shard_map/ppermute | solution.py:345
  108.2 1.9 %collective-permute-start.27 = (bf16[128,256]{1,0:T(8,128)(2,1)S(1)}, bf16[128,256]{1,0:T(8,128)(2,1)S(1)}, u32[]{:S(2)}, u32[]{:S(2)}) collective-permute-start(bf16[128,256]{1,0:T(8,128)(2,1)S(1)} %add_convert_fusion.4), channel_id=1, source_target_pairs={{0,6},{1,137},{2,4},{3,139},{4,2},{5,141},{6,0},{7,143},{128,134},... | collective-permute-start | bytes 196616 | tf_op jit(solution)/shard_map/ppermute | solution.py:370
  112.6 2.1 %collective-permute-done.26 = bf16[128,256]{1,0:T(8,128)(2,1)S(1)} collective-permute-done((bf16[128,256]{1,0:T(8,128)(2,1)S(1)}, bf16[128,256]{1,0:T(8,128)(2,1)S(1)}, u32[]{:S(2)}, u32[]{:S(2)}) %collective-permute-start.26) | collective-permute-done | bytes 65568 | tf_op jit(solution)/shard_map/ppermute | solution.py:370
  114.7 4.6 %collective-permute-done.28 = bf16[1,256,256]{2,1,0:T(8,128)(2,1)S(1)} collective-permute-done((bf16[1,256,256]{2,1,0:T(8,128)(2,1)S(1)}, bf16[1,256,256]{2,1,0:T(8,128)(2,1)S(1)}, u32[]{:S(2)}, u32[]{:S(2)}) %collective-permute-start.28) | collective-permute-done | bytes 131104 | tf_op jit(solution)/shard_map/ppermute | solution.py:345
  119.4 2.8 %collective-permute-start.31 = (bf16[4,128,256]{2,1,0:T(8,128)(2,1)S(1)}, bf16[4,128,256]{2,1,0:T(8,128)(2,1)S(1)}, u32[]{:S(2)}, u32[]{:S(2)}) collective-permute-start(bf16[4,128,256]{2,1,0:T(8,128)(2,1)S(1)} %pad_maximum_fusion.1), channel_id=1, source_target_pairs={{0,136},{1,7},{2,138},{3,5},{4,140},{5,3},{6,142},{7,1},{128,8},{1... | collective-permute-start | bytes 786440 | tf_op jit(solution)/shard_map/ppermute | solution.py:370
  122.8 5.4 %collective-permute-done.31 = bf16[4,128,256]{2,1,0:T(8,128)(2,1)S(1)} collective-permute-done((bf16[4,128,256]{2,1,0:T(8,128)(2,1)S(1)}, bf16[4,128,256]{2,1,0:T(8,128)(2,1)S(1)}, u32[]{:S(2)}, u32[]{:S(2)}) %collective-permute-start.31) | collective-permute-done | bytes 262176 | tf_op jit(solution)/shard_map/ppermute | solution.py:370
  129.9 4.3 %collective-permute-start.32 = (bf16[4,4,128,256]{3,2,1,0:T(8,128)(2,1)S(1)}, bf16[4,4,128,256]{3,2,1,0:T(8,128)(2,1)S(1)}, u32[]{:S(2)}, u32[]{:S(2)}) collective-permute-start(bf16[4,4,128,256]{3,2,1,0:T(8,128)(2,1)S(1)} %pad_maximum_fusion.mine_ref), channel_id=1, source_target_pairs={{0,1},{1,0},{2,3},{3,2},{4,5},{5,4},{6,7},{7,6},{8,9},{9,8},{10,11... | collective-permute-start | bytes 3145736 | tf_op jit(solution)/shard_map/ppermute | solution.py:345
  136.5 3.0 %finish.1 = (f32[256,2048]{1,0:T(8,128)}, f32[2048,256]{1,0:T(8,128)}) custom-call(s32[4]{0:T(128)S(1)} %copy-done.1, bf16[4,4,128,256]{3,2,1,0:T(8,128)(2,1)S(1)} %pad_maximum_fusion.mine_ref, bf16[4,4,128,256]{3,2,1,0:T(8,128)(2,1)S(1)} %collective-permute-done.32.other_ref), custom_call_target="tpu_custom_call" | custom-call | bytes 6000000 | tf_op jit(solution)/shard_map/finish/pallas_call | solution.py:326
  (76 shorter events, 27.6 us)
Async XLA Ops:
  3.8 11.9 %collective-permute-start.1 = (bf16[272,256]{1,0:T(8,128)(2,1)}, bf16[272,256]{1,0:T(8,128)(2,1)S(1)}, u32[]{:S(2)}, u32[]{:S(2)}) collective-permute-start(bf16[272,256]{1,0:T(8,128)(2,1)} %get-tuple-element.57.rest_0_), channel_id=1, source_target_pairs={{0,16},{16,32},{32,48},{48,64},{64,80},{80,96},{96,112},{112,0},{1... | collective-permute-start | bytes 417800 | tf_op jit(solution)/shard_map/ppermute | solution.py:353
  6.3 14.6 %collective-permute-start = (bf16[528,256]{1,0:T(8,128)(2,1)}, bf16[528,256]{1,0:T(8,128)(2,1)S(1)}, u32[]{:S(2)}, u32[]{:S(2)}) collective-permute-start(bf16[528,256]{1,0:T(8,128)(2,1)} %get-tuple-element.47.near_ref), channel_id=1, source_target_pairs={{0,128},{128,0},{1,129},{129,1},{2,130},{130,2},{3,131},{131,3},{4... | collective-permute-start | bytes 811016 | tf_op jit(solution)/shard_map/ppermute | solution.py:345
  7.5 9.3 %collective-permute-start.2 = (bf16[272,256]{1,0:T(8,128)(2,1)}, bf16[272,256]{1,0:T(8,128)(2,1)S(1)}, u32[]{:S(2)}, u32[]{:S(2)}) collective-permute-start(bf16[272,256]{1,0:T(8,128)(2,1)} %get-tuple-element.57.rest_0_), channel_id=1, source_target_pairs={{0,112},{16,0},{32,16},{48,32},{64,48},{80,64},{96,80},{112,96},{1... | collective-permute-start | bytes 417800 | tf_op jit(solution)/shard_map/ppermute | solution.py:353
  15.7 5.2 %collective-permute-start.3 = (bf16[272,256]{1,0:T(8,128)(2,1)S(1)}, bf16[272,256]{1,0:T(8,128)(2,1)S(1)}, u32[]{:S(2)}, u32[]{:S(2)}) collective-permute-start(bf16[272,256]{1,0:T(8,128)(2,1)S(1)} %collective-permute-done.1.rest_1_), channel_id=1, source_target_pairs={{0,16},{16,32},{32,48},{48,64},{64,80},{80,96},{96,112},{112,0},{1... | collective-permute-start | bytes 417800 | tf_op jit(solution)/shard_map/ppermute | solution.py:353
  16.9 5.7 %collective-permute-start.4 = (bf16[272,256]{1,0:T(8,128)(2,1)S(1)}, bf16[272,256]{1,0:T(8,128)(2,1)S(1)}, u32[]{:S(2)}, u32[]{:S(2)}) collective-permute-start(bf16[272,256]{1,0:T(8,128)(2,1)S(1)} %collective-permute-done.2.rest_2_), channel_id=1, source_target_pairs={{0,112},{16,0},{32,16},{48,32},{64,48},{80,64},{96,80},{112,96},{1... | collective-permute-start | bytes 417800 | tf_op jit(solution)/shard_map/ppermute | solution.py:353
  20.9 5.1 %collective-permute-start.5 = (bf16[272,256]{1,0:T(8,128)(2,1)S(1)}, bf16[272,256]{1,0:T(8,128)(2,1)S(1)}, u32[]{:S(2)}, u32[]{:S(2)}) collective-permute-start(bf16[272,256]{1,0:T(8,128)(2,1)S(1)} %collective-permute-done.3.rest_3_), channel_id=1, source_target_pairs={{0,16},{16,32},{32,48},{48,64},{64,80},{80,96},{96,112},{112,0},{1... | collective-permute-start | bytes 417800 | tf_op jit(solution)/shard_map/ppermute | solution.py:353
  22.6 6.2 %collective-permute-start.6 = (bf16[272,256]{1,0:T(8,128)(2,1)S(1)}, bf16[272,256]{1,0:T(8,128)(2,1)S(1)}, u32[]{:S(2)}, u32[]{:S(2)}) collective-permute-start(bf16[272,256]{1,0:T(8,128)(2,1)S(1)} %collective-permute-done.4.rest_4_), channel_id=1, source_target_pairs={{0,112},{16,0},{32,16},{48,32},{64,48},{80,64},{96,80},{112,96},{1... | collective-permute-start | bytes 417800 | tf_op jit(solution)/shard_map/ppermute | solution.py:353
  26.0 5.1 %collective-permute-start.7 = (bf16[272,256]{1,0:T(8,128)(2,1)S(1)}, bf16[272,256]{1,0:T(8,128)(2,1)S(1)}, u32[]{:S(2)}, u32[]{:S(2)}) collective-permute-start(bf16[272,256]{1,0:T(8,128)(2,1)S(1)} %collective-permute-done.5.rest_0_.rest_5_), channel_id=1, source_target_pairs={{0,16},{16,32},{32,48},{48,64},{64,80},{80,96},{96,112},{112,0},{1... | collective-permute-start | bytes 417800 | tf_op jit(solution)/shard_map/ppermute | solution.py:353
  33.5 3.9 %collective-permute-start.10 = (f32[8,256]{1,0:T(8,128)S(1)}, f32[8,256]{1,0:T(8,128)S(1)}, u32[]{:S(2)}, u32[]{:S(2)}) collective-permute-start(f32[8,256]{1,0:T(8,128)S(1)} %get-tuple-element.65), channel_id=1, source_target_pairs={{0,112},{16,96},{32,80},{48,64},{64,48},{80,32},{96,16},{112,0},{1... | collective-permute-start | bytes 24584 | tf_op jit(solution)/shard_map/ppermute | solution.py:345
  33.9 4.6 %collective-permute-start.9 = (f32[8,256]{1,0:T(8,128)S(1)}, f32[8,256]{1,0:T(8,128)S(1)}, u32[]{:S(2)}, u32[]{:S(2)}) collective-permute-start(f32[8,256]{1,0:T(8,128)S(1)} %get-tuple-element.65), channel_id=1, source_target_pairs={{0,96},{16,112},{32,64},{48,80},{64,32},{80,48},{96,0},{112,16},{1... | collective-permute-start | bytes 24584 | tf_op jit(solution)/shard_map/ppermute | solution.py:345
  38.5 3.5 %collective-permute-start.11 = (f32[8,256]{1,0:T(8,128)S(1)}, f32[8,256]{1,0:T(8,128)S(1)}, u32[]{:S(2)}, u32[]{:S(2)}) collective-permute-start(f32[8,256]{1,0:T(8,128)S(1)} %add_add_fusion), channel_id=1, source_target_pairs={{0,32},{16,48},{32,0},{48,16},{64,96},{80,112},{96,64},{112,80},{1... | collective-permute-start | bytes 24584 | tf_op jit(solution)/shard_map/ppermute | solution.py:345
  50.7 9.6 %collective-permute-start.12 = (bf16[4,4,128,256]{3,2,1,0:T(8,128)(2,1)S(1)}, bf16[4,4,128,256]{3,2,1,0:T(8,128)(2,1)S(1)}, u32[]{:S(2)}, u32[]{:S(2)}) collective-permute-start(bf16[4,4,128,256]{3,2,1,0:T(8,128)(2,1)S(1)} %get-tuple-element.74), channel_id=1, source_target_pairs={{0,1},{1,0},{2,3},{3,2},{4,5},{5,4},{6,7},{7,6},{8,9},{9,8},{10,11... | collective-permute-start | bytes 3145736 | tf_op jit(solution)/shard_map/ppermute | solution.py:345
  57.9 14.0 %collective-permute-start.16 = (bf16[4,256,256]{2,1,0:T(8,128)(2,1)S(1)}, bf16[4,256,256]{2,1,0:T(8,128)(2,1)S(1)}, u32[]{:S(2)}, u32[]{:S(2)}) collective-permute-start(bf16[4,256,256]{2,1,0:T(8,128)(2,1)S(1)} %get-tuple-element.76), channel_id=1, source_target_pairs={{0,16},{16,0},{32,48},{48,32},{64,80},{80,64},{96,112},{112,96},{1... | collective-permute-start | bytes 1572872 | tf_op jit(solution)/shard_map/ppermute | solution.py:345
  60.6 11.5 %collective-permute-start.13 = (bf16[4,128,256]{2,1,0:T(8,128)(2,1)S(1)}, bf16[4,128,256]{2,1,0:T(8,128)(2,1)S(1)}, u32[]{:S(2)}, u32[]{:S(2)}) collective-permute-start(bf16[4,128,256]{2,1,0:T(8,128)(2,1)S(1)} %get-tuple-element.91), channel_id=1, source_target_pairs={{0,128},{1,3},{2,130},{3,1},{4,132},{5,7},{6,134},{7,5},{128,0},{1... | collective-permute-start | bytes 786440 | tf_op jit(solution)/shard_map/ppermute | solution.py:370
  62.0 10.2 %collective-permute-start.15 = (bf16[4,128,256]{2,1,0:T(8,128)(2,1)S(1)}, bf16[4,128,256]{2,1,0:T(8,128)(2,1)S(1)}, u32[]{:S(2)}, u32[]{:S(2)}) collective-permute-start(bf16[4,128,256]{2,1,0:T(8,128)(2,1)S(1)} %get-tuple-element.92), channel_id=1, source_target_pairs={{0,136},{1,7},{2,138},{3,5},{4,140},{5,3},{6,142},{7,1},{128,8},{1... | collective-permute-start | bytes 786440 | tf_op jit(solution)/shard_map/ppermute | solution.py:370
  63.9 8.3 %collective-permute-start.14 = (bf16[4,128,256]{2,1,0:T(8,128)(2,1)S(1)}, bf16[4,128,256]{2,1,0:T(8,128)(2,1)S(1)}, u32[]{:S(2)}, u32[]{:S(2)}) collective-permute-start(bf16[4,128,256]{2,1,0:T(8,128)(2,1)S(1)} %get-tuple-element.93), channel_id=1, source_target_pairs={{0,8},{1,5},{2,10},{3,7},{4,12},{5,1},{6,14},{7,3},{128,136},{129,... | collective-permute-start | bytes 786440 | tf_op jit(solution)/shard_map/ppermute | solution.py:370
  72.4 6.0 %collective-permute-start.17 = (bf16[128,256]{1,0:T(8,128)(2,1)S(1)}, bf16[128,256]{1,0:T(8,128)(2,1)S(1)}, u32[]{:S(2)}, u32[]{:S(2)}) collective-permute-start(bf16[128,256]{1,0:T(8,128)(2,1)S(1)} %get-tuple-element.98), channel_id=1, source_target_pairs={{0,2},{1,129},{2,0},{3,131},{4,6},{5,133},{6,4},{7,135},{128,130},... | collective-permute-start | bytes 196616 | tf_op jit(solution)/shard_map/ppermute | solution.py:370
  72.7 5.6 %collective-permute-start.19 = (bf16[128,256]{1,0:T(8,128)(2,1)S(1)}, bf16[128,256]{1,0:T(8,128)(2,1)S(1)}, u32[]{:S(2)}, u32[]{:S(2)}) collective-permute-start(bf16[128,256]{1,0:T(8,128)(2,1)S(1)} %get-tuple-element.99), channel_id=1, source_target_pairs={{0,6},{1,137},{2,4},{3,139},{4,2},{5,141},{6,0},{7,143},{128,134},... | collective-permute-start | bytes 196616 | tf_op jit(solution)/shard_map/ppermute | solution.py:370
  75.2 4.6 %collective-permute-start.18 = (bf16[128,256]{1,0:T(8,128)(2,1)S(1)}, bf16[128,256]{1,0:T(8,128)(2,1)S(1)}, u32[]{:S(2)}, u32[]{:S(2)}) collective-permute-start(bf16[128,256]{1,0:T(8,128)(2,1)S(1)} %get-tuple-element.100), channel_id=1, source_target_pairs={{0,4},{1,9},{2,6},{3,11},{4,0},{5,13},{6,2},{7,15},{128,132},{129,... | collective-permute-start | bytes 196616 | tf_op jit(solution)/shard_map/ppermute | solution.py:370
  75.7 13.9 %collective-permute-start.20 = (bf16[2,256,256]{2,1,0:T(8,128)(2,1)S(1)}, bf16[2,256,256]{2,1,0:T(8,128)(2,1)S(1)}, u32[]{:S(2)}, u32[]{:S(2)}) collective-permute-start(bf16[2,256,256]{2,1,0:T(8,128)(2,1)S(1)} %get-tuple-element.79), channel_id=1, source_target_pairs={{0,32},{16,48},{32,0},{48,16},{64,96},{80,112},{96,64},{112,80},{1... | collective-permute-start | bytes 786440 | tf_op jit(solution)/shard_map/ppermute | solution.py:345
  89.7 3.3 %collective-permute-start.21 = (bf16[128,256]{1,0:T(8,128)(2,1)S(1)}, bf16[128,256]{1,0:T(8,128)(2,1)S(1)}, u32[]{:S(2)}, u32[]{:S(2)}) collective-permute-start(bf16[128,256]{1,0:T(8,128)(2,1)S(1)} %fusion.5), channel_id=1, source_target_pairs={{0,16},{16,0},{32,48},{48,32},{64,80},{80,64},{96,112},{112,96},{1... | collective-permute-start | bytes 196616 | tf_op jit(solution)/shard_map/ppermute | solution.py:345
  93.0 6.9 %collective-permute-start.24 = (bf16[128,256]{1,0:T(8,128)(2,1)S(1)}, bf16[128,256]{1,0:T(8,128)(2,1)S(1)}, u32[]{:S(2)}, u32[]{:S(2)}) collective-permute-start(bf16[128,256]{1,0:T(8,128)(2,1)S(1)} %add_convert_fusion.5), channel_id=1, source_target_pairs={{0,96},{16,112},{32,64},{48,80},{64,32},{80,48},{96,0},{112,16},{1... | collective-permute-start | bytes 196616 | tf_op jit(solution)/shard_map/ppermute | solution.py:345
  95.9 8.7 %collective-permute-start.23 = (bf16[128,256]{1,0:T(8,128)(2,1)S(1)}, bf16[128,256]{1,0:T(8,128)(2,1)S(1)}, u32[]{:S(2)}, u32[]{:S(2)}) collective-permute-start(bf16[128,256]{1,0:T(8,128)(2,1)S(1)} %add_convert_fusion.5), channel_id=1, source_target_pairs={{0,64},{16,80},{32,96},{48,112},{64,0},{80,16},{96,32},{112,48},{1... | collective-permute-start | bytes 196616 | tf_op jit(solution)/shard_map/ppermute | solution.py:345
  99.9 8.3 %collective-permute-start.22 = (bf16[128,256]{1,0:T(8,128)(2,1)S(1)}, bf16[128,256]{1,0:T(8,128)(2,1)S(1)}, u32[]{:S(2)}, u32[]{:S(2)}) collective-permute-start(bf16[128,256]{1,0:T(8,128)(2,1)S(1)} %add_convert_fusion.5), channel_id=1, source_target_pairs={{0,32},{16,48},{32,0},{48,16},{64,96},{80,112},{96,64},{112,80},{1... | collective-permute-start | bytes 196616 | tf_op jit(solution)/shard_map/ppermute | solution.py:345
  108.2 4.4 %collective-permute-start.27 = (bf16[128,256]{1,0:T(8,128)(2,1)S(1)}, bf16[128,256]{1,0:T(8,128)(2,1)S(1)}, u32[]{:S(2)}, u32[]{:S(2)}) collective-permute-start(bf16[128,256]{1,0:T(8,128)(2,1)S(1)} %add_convert_fusion.4), channel_id=1, source_target_pairs={{0,6},{1,137},{2,4},{3,139},{4,2},{5,141},{6,0},{7,143},{128,134},... | collective-permute-start | bytes 196616 | tf_op jit(solution)/shard_map/ppermute | solution.py:370
  110.1 4.6 %collective-permute-start.26 = (bf16[128,256]{1,0:T(8,128)(2,1)S(1)}, bf16[128,256]{1,0:T(8,128)(2,1)S(1)}, u32[]{:S(2)}, u32[]{:S(2)}) collective-permute-start(bf16[128,256]{1,0:T(8,128)(2,1)S(1)} %add_convert_fusion.4), channel_id=1, source_target_pairs={{0,4},{1,9},{2,6},{3,11},{4,0},{5,13},{6,2},{7,15},{128,132},{129,... | collective-permute-start | bytes 196616 | tf_op jit(solution)/shard_map/ppermute | solution.py:370
  110.8 3.9 %collective-permute-start.25 = (bf16[128,256]{1,0:T(8,128)(2,1)S(1)}, bf16[128,256]{1,0:T(8,128)(2,1)S(1)}, u32[]{:S(2)}, u32[]{:S(2)}) collective-permute-start(bf16[128,256]{1,0:T(8,128)(2,1)S(1)} %add_convert_fusion.4), channel_id=1, source_target_pairs={{0,2},{1,129},{2,0},{3,131},{4,6},{5,133},{6,4},{7,135},{128,130},... | collective-permute-start | bytes 196616 | tf_op jit(solution)/shard_map/ppermute | solution.py:370
  111.5 7.8 %collective-permute-start.28 = (bf16[1,256,256]{2,1,0:T(8,128)(2,1)S(1)}, bf16[1,256,256]{2,1,0:T(8,128)(2,1)S(1)}, u32[]{:S(2)}, u32[]{:S(2)}) collective-permute-start(bf16[1,256,256]{2,1,0:T(8,128)(2,1)S(1)} %get-tuple-element.85), channel_id=1, source_target_pairs={{0,64},{16,80},{32,96},{48,112},{64,0},{80,16},{96,32},{112,48},{1... | collective-permute-start | bytes 393224 | tf_op jit(solution)/shard_map/ppermute | solution.py:345
  119.4 8.9 %collective-permute-start.31 = (bf16[4,128,256]{2,1,0:T(8,128)(2,1)S(1)}, bf16[4,128,256]{2,1,0:T(8,128)(2,1)S(1)}, u32[]{:S(2)}, u32[]{:S(2)}) collective-permute-start(bf16[4,128,256]{2,1,0:T(8,128)(2,1)S(1)} %pad_maximum_fusion.1), channel_id=1, source_target_pairs={{0,136},{1,7},{2,138},{3,5},{4,140},{5,3},{6,142},{7,1},{128,8},{1... | collective-permute-start | bytes 786440 | tf_op jit(solution)/shard_map/ppermute | solution.py:370
  122.2 6.7 %collective-permute-start.30 = (bf16[4,128,256]{2,1,0:T(8,128)(2,1)S(1)}, bf16[4,128,256]{2,1,0:T(8,128)(2,1)S(1)}, u32[]{:S(2)}, u32[]{:S(2)}) collective-permute-start(bf16[4,128,256]{2,1,0:T(8,128)(2,1)S(1)} %pad_maximum_fusion.1), channel_id=1, source_target_pairs={{0,8},{1,5},{2,10},{3,7},{4,12},{5,1},{6,14},{7,3},{128,136},{129,... | collective-permute-start | bytes 786440 | tf_op jit(solution)/shard_map/ppermute | solution.py:370
  122.5 7.2 %collective-permute-start.29 = (bf16[4,128,256]{2,1,0:T(8,128)(2,1)S(1)}, bf16[4,128,256]{2,1,0:T(8,128)(2,1)S(1)}, u32[]{:S(2)}, u32[]{:S(2)}) collective-permute-start(bf16[4,128,256]{2,1,0:T(8,128)(2,1)S(1)} %pad_maximum_fusion.1), channel_id=1, source_target_pairs={{0,128},{1,3},{2,130},{3,1},{4,132},{5,7},{6,134},{7,5},{128,0},{1... | collective-permute-start | bytes 786440 | tf_op jit(solution)/shard_map/ppermute | solution.py:370
  129.9 6.6 %collective-permute-start.32 = (bf16[4,4,128,256]{3,2,1,0:T(8,128)(2,1)S(1)}, bf16[4,4,128,256]{3,2,1,0:T(8,128)(2,1)S(1)}, u32[]{:S(2)}, u32[]{:S(2)}) collective-permute-start(bf16[4,4,128,256]{3,2,1,0:T(8,128)(2,1)S(1)} %pad_maximum_fusion.mine_ref), channel_id=1, source_target_pairs={{0,1},{1,0},{2,3},{3,2},{4,5},{5,4},{6,7},{7,6},{8,9},{9,8},{10,11... | collective-permute-start | bytes 3145736 | tf_op jit(solution)/shard_map/ppermute | solution.py:345
  (8 other events, 44.6 us)

commit v5 on v4

--- a/solution.py
+++ b/solution.py
@@ -49,8 +49,7 @@
     return copy
 
 
-def pack_kernel(s_ref, user_hbm, pid_hbm, feat_hbm, nid_hbm, bucket_hbm, mine_ref, near_ref, pid_ref, nid_ref, bucket_ref, sems):
-    del s_ref
+def pack_kernel(user_hbm, pid_hbm, feat_hbm, nid_hbm, bucket_hbm, mine_ref, near_ref, pid_ref, nid_ref, bucket_ref, sems):
     copies = [
         start(pid_hbm, pid_ref, sems.at[0]),
         start(nid_hbm, nid_ref, sems.at[1]),
@@ -78,11 +77,11 @@
         copy.wait()
 
 
-def pack(scalars, user_emb, pos_id, neg_feat, neg_id, neg_bucket):
+def pack(user_emb, pos_id, neg_feat, neg_id, neg_bucket):
     vm = pl.BlockSpec(memory_space=pltpu.VMEM)
     return pl.pallas_call(
         pack_kernel,
-        in_specs=[pl.BlockSpec(memory_space=pltpu.SMEM)] + [pl.BlockSpec(memory_space=pltpu.HBM)] * 5,
+        in_specs=[pl.BlockSpec(memory_space=pltpu.HBM)] * 5,
         out_specs=[vm] * 2,
         out_shape=[jax.ShapeDtypeStruct((U + 16, E), BF), jax.ShapeDtypeStruct((N + 16, E), BF)],
         scratch_shapes=[
@@ -94,7 +93,7 @@
         compiler_params=params(60 * 1024 * 1024),
         cost_estimate=cost(0, 1e6),
         name="pack",
-    )(scalars, user_emb, pos_id.reshape(1, U), neg_feat, neg_id.reshape(1, N), neg_bucket.reshape(1, N))
+    )(user_emb, pos_id.reshape(1, U), neg_feat, neg_id.reshape(1, N), neg_bucket.reshape(1, N))
 
 
 def hidden(feat, w_in_ref):
@@ -158,10 +157,10 @@
     return (z + OFFSETS[k] + NZ) & (NZ - 1)
 
 
-def score_kernel(ks, s_ref, near_emb, far_emb, nid_ref, bias_ref, pemb_ref, tloc_in, tin_in, *rest):
+def score_kernel(ks, near_emb, far_emb, nid_ref, bias_ref, pemb_ref, tloc_in, tin_in, *rest):
     users = rest[: len(ks)]
     tloc_ref, tin_ref, pexp_ref, kept_ref, kf = rest[len(ks) :]
-    z = s_ref[0]
+    z = lax.axis_index("z")
     tloc_ref[...] = tloc_in[...]
     tin_ref[...] = tin_in[...]
     if ks[0] == 0:
@@ -193,12 +192,12 @@
         tin_ref[row, :] = t + pexp_ref[...] if k == 0 else t
 
 
-def score(ks, scalars, near_emb, far_emb, nid, bias, pemb, tloc, tin, users):
+def score(ks, near_emb, far_emb, nid, bias, pemb, tloc, tin, users):
     vm = pl.BlockSpec(memory_space=pltpu.VMEM)
     n = len(ks)
     return pl.pallas_call(
         functools.partial(score_kernel, ks),
-        in_specs=[pl.BlockSpec(memory_space=pltpu.SMEM)] + [vm] * (7 + n),
+        in_specs=[vm] * (7 + n),
         out_specs=[vm] * 4,
         out_shape=[
             jax.ShapeDtypeStruct((NZ, U), F32),
@@ -210,13 +209,13 @@
         compiler_params=params(14 * 1024 * 1024),
         cost_estimate=cost(2 * n * U * NN * E, 5e6, n * U * NN),
         name="score",
-    )(scalars, near_emb, far_emb, nid, bias, pemb, tloc, tin, *[users[k] for k in ks])
-
-
-def grad_kernel(s_ref, tot_ref, tloc_ref, pexp_ref, near_emb, far_emb, pemb_ref, kept_a, kept_b, *rest):
+    )(near_emb, far_emb, nid, bias, pemb, tloc, tin, *[users[k] for k in ks])
+
+
+def grad_kernel(tot_ref, tloc_ref, pexp_ref, near_emb, far_emb, pemb_ref, kept_a, kept_b, *rest):
     users = rest[:NZ]
     keep_ref, send_ref, g_ref, pterm_ref, wu, ratio, rel = rest[NZ:]
-    z = s_ref[0]
+    z = lax.axis_index("z")
     tot = tot_ref[...]
     shrink = jnp.where(tot > 1.0, SMALL, 1.0)
     ratio[...] = (tloc_ref[...] * shrink) * (1.0 / (tot * shrink))
@@ -248,11 +247,11 @@
         g_ref[first : first + TILE] = g.astype(BF)
 
 
-def grads(scalars, tot, tloc, pexp, near_emb, far_emb, pemb, kept_a, kept_b, users):
+def grads(tot, tloc, pexp, near_emb, far_emb, pemb, kept_a, kept_b, users):
     vm = pl.BlockSpec(memory_space=pltpu.VMEM)
     return pl.pallas_call(
         grad_kernel,
-        in_specs=[pl.BlockSpec(memory_space=pltpu.SMEM)] + [vm] * (8 + NZ),
+        in_specs=[vm] * (8 + NZ),
         out_specs=[vm] * 4,
         out_shape=[
             jax.ShapeDtypeStruct((NZ // 2, U, E), BF),
@@ -268,77 +267,85 @@
         compiler_params=params(),
         cost_estimate=cost(4 * NZ * U * NN * E, 8e6),
         name="grads",
-    )(scalars, tot, tloc, pexp, near_emb, far_emb, pemb, kept_a, kept_b, *users)
-
-
-def back_kernel(s_ref, g_ref, feat_ref, far_ref, w_out_ref, hid_ref, far_hid, mine_ref, theirs_ref, feat):
-    first, second, core = s_ref[1], s_ref[2], s_ref[3]
-    feat[0 : N + U] = feat_ref[...]
-    feat[N + U : ROWS] = far_ref[0:N]
-    for c in range(H // WIDE):
-        cols = slice(c * WIDE, (c + 1) * WIDE)
-        hid = jnp.concatenate([hid_ref[:, cols], far_hid[:, cols]], axis=0)
-        back = lax.dot_general(g_ref[...], w_out_ref[cols], NT, preferred_element_type=F32)
-        back = jnp.where(hid > 0, back, 0.0).astype(BF)
-        w_in = lax.dot_general(feat[...], back, TN, preferred_element_type=F32)
-        w_out = lax.dot_general(hid, g_ref[...], TN, preferred_element_type=F32)
-        to_mine, to_theirs = jnp.bitwise_xor(first, c), jnp.bitwise_xor(second, c)
-        for t in range(WIDE // TILE):
-            a, b = w_in[:, t * TILE : (t + 1) * TILE], w_out[t * TILE : (t + 1) * TILE]
-            mine = jnp.where(core == 0, a, b).astype(BF)
-            theirs = jnp.where(core == 0, b, a).astype(BF)
+    )(tot, tloc, pexp, near_emb, far_emb, pemb, kept_a, kept_b, *users)
+
+
+def order():
+    core = lax.axis_index("core")
+    xx, y = lax.axis_index("x_hi") * 2 + lax.axis_index("x_lo"), lax.axis_index("y")
+    return core, jnp.where(core == 0, xx, y), jnp.where(core == 0, y, xx)
+
+
+def back_kernel(mine, g_ref, feat_ref, far_ref, w_out_ref, hid_ref, far_hid, out_ref):
+    core, first, second = order()
+    if not mine:
+        core, first, second = 1 - core, second, first
+    for c in range(2):
+        cols = pl.ds(pl.multiple_of(core * (H // 2) + c * WIDE, WIDE), WIDE)
+        w_in = w_out = 0.0
+        for rows, feat, hid in ((slice(0, N + U), feat_ref, hid_ref), (slice(N + U, ROWS), far_ref, far_hid)):
+            hid = hid[:, cols]
+            g = g_ref[rows]
+            back = lax.dot_general(g, w_out_ref[cols], NT, preferred_element_type=F32)
+            back = jnp.where(hid > 0, back, 0.0).astype(BF)
+            w_in += lax.dot_general(feat[0 : g.shape[0]], back, TN, preferred_element_type=F32)
+            w_out += lax.dot_general(hid, g, TN, preferred_element_type=F32)
+        w_in, w_out = w_in.astype(BF), w_out.astype(BF)
+        for t in range(2):
             for half in range(2):
+                inner = jnp.bitwise_xor(second, 2 * t + half)
                 rows = slice(half * 128, (half + 1) * 128)
-                mine_ref[to_mine, jnp.bitwise_xor(second, 2 * t + half)] = mine[rows]
-                theirs_ref[to_theirs, jnp.bitwise_xor(first, 2 * t + half)] = theirs[rows]
-
-
-def backward(scalars, g, feat, far, w_out, hid, far_hid):
-    vm = pl.BlockSpec(memory_space=pltpu.VMEM)
+                out_ref[jnp.bitwise_xor(first, c), inner] = w_in[rows, t * TILE : (t + 1) * TILE]
+                rows = slice(t * TILE + half * 128, t * TILE + (half + 1) * 128)
+                out_ref[jnp.bitwise_xor(first, 2 + c), inner] = w_out[rows]
+
+
+def backward(mine, *args):
+    return in_vmem(
+        functools.partial(back_kernel, mine), "backward", 3 * ROWS * E * H, [((4, 4, 128, TILE), BF)], *args
+    )[0]
+
+
+def finish_kernel(mine, x_ref, *rest):
+    w_in_hbm, w_out_hbm, a, b, sems = rest[-5:]
+    core, first, second = order()
+    if not mine:
+        core, first, second = 1 - core, second, first
+    copies = []
+    for c in range(2):
+        for t in range(2):
+            for half in range(2):
+                inner = jnp.bitwise_xor(second, 2 * t + half)
+                start_t = c * WIDE + t * TILE
+                cols = slice(start_t, start_t + TILE)
+                a[half * 128 : (half + 1) * 128, cols] = x_ref[jnp.bitwise_xor(first, c), inner].astype(F32)
+                rows = slice(start_t + half * 128, start_t + (half + 1) * 128)
+                b[rows] = x_ref[jnp.bitwise_xor(first, 2 + c), inner].astype(F32)
+        here = pl.ds(c * WIDE, WIDE)
+        there = pl.ds(pl.multiple_of(core * (H // 2) + c * WIDE, WIDE), WIDE)
+        copies.append(start(a.at[:, here], w_in_hbm.at[:, there], sems.at[2 * c]))
+        copies.append(start(b.at[here], w_out_hbm.at[there], sems.at[2 * c + 1]))
+    for copy in copies:
+        copy.wait()
+
+
+def finish(mine, x, *outs):
+    vm, hbm = pl.BlockSpec(memory_space=pltpu.VMEM), pl.BlockSpec(memory_space=pl.ANY)
     return pl.pallas_call(
-        back_kernel,
-        in_specs=[pl.BlockSpec(memory_space=pltpu.SMEM)] + [vm] * 6,
-        out_specs=[vm, vm],
-        out_shape=[jax.ShapeDtypeStruct((4, 4, 128, TILE), BF)] * 2,
-        scratch_shapes=[pltpu.VMEM((ROWS, E), BF)],
-        compiler_params=params(),
-        cost_estimate=cost(6 * ROWS * E * H, 10e6),
-        name="backward",
-    )(scalars, g, feat, far, w_out, hid, far_hid)
-
-
-def finish_kernel(s_ref, mine_ref, other_ref, w_in_ref, w_out_ref):
-    first, second, core = s_ref[1], s_ref[2], s_ref[3]
-    for t in range(2):
-        for half in range(2):
-            rows = slice(half * 128, (half + 1) * 128)
-            mine = mine_ref[0, jnp.bitwise_xor(second, 2 * t + half)].astype(F32)
-            other = other_ref[0, jnp.bitwise_xor(first, 2 * t + half)].astype(F32)
-            w_in_ref[rows, t * TILE : (t + 1) * TILE] = jnp.where(core == 0, mine, other)
-            start = t * TILE + half * 128
-            w_out_ref[start : start + 128] = jnp.where(core == 0, other, mine)
-
-
-def finish(scalars, mine, other):
-    def place(outer):
-        return pl.BlockSpec((1, 4, 128, TILE), lambda j, s: (jnp.bitwise_xor(j, s[outer]), 0, 0, 0))
-
-    return pl.pallas_call(
-        finish_kernel,
-        grid_spec=pltpu.PrefetchScalarGridSpec(
-            num_scalar_prefetch=1,
-            grid=(4,),
-            in_specs=[place(1), place(2)],
-            out_specs=[
-                pl.BlockSpec((E, 512), lambda j, s: (0, j)),
-                pl.BlockSpec((512, E), lambda j, s: (j, 0)),
-            ],
-        ),
+        functools.partial(finish_kernel, mine),
+        in_specs=[vm] + [hbm] * len(outs),
+        out_specs=[hbm, hbm],
         out_shape=[jax.ShapeDtypeStruct((E, H), F32), jax.ShapeDtypeStruct((H, E), F32)],
-        compiler_params=params(),
-        cost_estimate=cost(0, 6e6),
+        scratch_shapes=[
+            pltpu.VMEM((E, H // 2), F32),
+            pltpu.VMEM((H // 2, E), F32),
+            pltpu.SemaphoreType.DMA((4,)),
+        ],
+        input_output_aliases={1: 0, 2: 1} if outs else {},
+        compiler_params=params(14 * 1024 * 1024),
+        cost_estimate=cost(0, 3e6),
         name="finish",
-    )(scalars, mine, other)
+    )(x, *outs)
 
 
 def swap(x, axis, k):
@@ -384,35 +391,24 @@
     return x
 
 
-def halve(keep, send, k):
-    total = add(keep, swap(send, "z", k)).astype(BF)
-    half = total.shape[0] // 2
-    return (total[:half], total[half:]) if half else total[0]
-
-
 def all_reduce(mine, theirs, keep, send):
     half = add(mine, swap(theirs, "core", 1)).astype(BF)
     quarter = add(half[0], *[plane_swap(half[k], k, 0) for k in (1, 2, 3)]).astype(BF)
-    keep, send = halve(keep, send, 1)
-    quarter, keep, send = lax.optimization_barrier((quarter, keep, send))
+    keep = add(keep, swap(send, "z", 1)).astype(BF)
+    quarter, keep = lax.optimization_barrier((quarter, keep))
     part = add(quarter[0], *[plane_swap(quarter[k], k, 1) for k in (1, 2, 3)])
-    keep, send = halve(keep, send, 2)
-    part, keep, send = lax.optimization_barrier((part, keep, send))
     part = sum_over_z(part, ((1,), (2, 4, 6)), BF).astype(BF)
-    part, keep, send = lax.optimization_barrier((part, keep, send))
+    part, keep = lax.optimization_barrier((part, keep))
     quarter = jnp.stack([part] + [plane_swap(part, k, 1) for k in (1, 2, 3)])
-    user = halve(keep, send, 4)
-    quarter, user = lax.optimization_barrier((quarter, user))
-    half = jnp.stack([quarter] + [plane_swap(quarter, k, 0) for k in (1, 2, 3)])
+    user = add(keep[0], *[swap(keep[i], "z", k) for i, k in ((1, 4), (2, 2), (3, 6))])
+    others = [plane_swap(quarter, k, 0) for k in (1, 2, 3)]
+    others, user = lax.optimization_barrier((others, user))
+    half = jnp.stack([quarter] + others)
     return half, swap(half, "core", 1), user
 
 
 def on_device(user_emb, pos_feat, pos_id, neg_feat, neg_id, neg_bucket, logq_table, w_in, w_out):
-    x_lo, z, x_hi, y, core = [lax.axis_index(a) for a in AXES]
-    xx = x_hi * 2 + x_lo
-    scalars = jnp.stack([z, jnp.where(core == 0, xx, y), jnp.where(core == 0, y, xx), core]).astype(I32)
-
-    mine, near = pack(scalars, user_emb, pos_id, neg_feat, neg_id, neg_bucket)
+    mine, near = pack(user_emb, pos_id, neg_feat, neg_id, neg_bucket)
     up, down = shift(mine, 1), shift(mine, -1)
     far = swap(near, "x_lo", 1)
     users = [mine, up, down]
@@ -446,16 +442,15 @@
     users += [shift(after(up, far_emb), 1)]
     none = jnp.zeros((NZ, U), F32)
     ks = tuple(range(NZ))
-    tloc, tot, pexp, kept_a = score(ks[:FIRST], scalars, near_emb, far_emb, nid, bias, pemb, none, none, users)
-    tloc, tot, _, kept_b = score(ks[FIRST:], scalars, near_emb, far_emb, nid, bias, pemb, tloc, tot, users)
+    tloc, tot, pexp, kept_a = score(ks[:FIRST], near_emb, far_emb, nid, bias, pemb, none, none, users)
+    tloc, tot, _, kept_b = score(ks[FIRST:], near_emb, far_emb, nid, bias, pemb, tloc, tot, users)
     tot = sum_over_z(tot, ((1, 6, 7), (2,)), F32)
-    keep, send, g, pterm = grads(
-        scalars, tot, tloc, pexp, near_emb, far_emb, pemb, kept_a, kept_b, users
-    )
-    mine_g, theirs_g = backward(scalars, g, feat, far, w_out, hid, far_hid)
-    half, other, user = all_reduce(mine_g, theirs_g, keep, send)
-    w_in_grad, w_out_grad = finish(scalars, half, other)
-    return user.astype(F32) + pterm, w_in_grad, w_out_grad
+    keep, send, g, pterm = grads(tot, tloc, pexp, near_emb, far_emb, pemb, kept_a, kept_b, users)
+    args = (g, feat, far, w_out, hid, far_hid)
+    theirs_g = backward(False, *args)
+    half, other, user = all_reduce(backward(True, *args), theirs_g, keep, send)
+    w_in_grad, w_out_grad = finish(False, other, *finish(True, half))
+    return user + pterm, w_in_grad, w_out_grad
 
 
 def solution(mesh):

time: 140 us -> 124 us (0.89)
  waiting for transfers between devices: 50.5 us -> 32 us
  starting transfers between devices: 59.4 us -> 64.5 us
  Pallas kernels: 23.1 us -> 21.6 us
    ppermute x14 -> x15, waiting for transfers between devices: 35.8 us -> 16.3 us  [swap(): lax.ppermute(x, axis, [(i, i ^ k) for i in range(SIZES[AXES.index(axis)])])]
    pallas_call x6, Pallas kernels: 19.4 us -> 11.5 us  [the longest x2 4.09 us: score(): pl.pallas_call(functools.partial(score_kernel, ks), in_specs=[vm] * (7 +...]
    pallas_call x3 -> x5, Pallas kernels: 3.75 us -> 10.1 us  [in_vmem(): pl.pallas_call(kernel, in_specs=[vm] * len(args), out_specs=[vm] * len(ou...]
    ppermute x14 -> x15, starting transfers between devices: 33.1 us -> 38.3 us  [swap(): lax.ppermute(x, axis, [(i, i ^ k) for i in range(SIZES[AXES.index(axis)])])]
    unnamed x14 -> x12, local copies, waits for them, and re-layouts: 3.1 us -> 3.1 us
  transfers between devices with their start and end apart: 33 -> 34, of which waited for: 19 -> 19; matrix products, arithmetic and copies ran while one was open for 1% -> 1% of each run, Pallas kernels for 5% -> 8%
where the time goes in v5:
time: 124 us
  starting transfers between devices  64.5 us (52%)
  waiting for transfers between devices  32 us (26%)
  Pallas kernels  21.6 us (17%)
  local copies, waits for them, and re-layouts  3.19 us (3%)
  other arithmetic  1.72 us (1%)
    ppermute x15, starting transfers between devices, swap(): lax.ppermute(x, axis, [(i, i ^ k) for i in range(SIZES[AXES.index(axis)])])  38.3 us
    ppermute x15, waiting for transfers between devices, swap(): lax.ppermute(x, axis, [(i, i ^ k) for i in range(SIZES[AXES.index(axis)])])  16.3 us
    ppermute x12, starting transfers between devices, plane_swap(): return lax.ppermute(x, AXES, pairs)  14 us
    ppermute x7, starting transfers between devices, shift(): return lax.ppermute(x, 'z', [(i, (i + by) % NZ) for i in range(NZ)])  12.1 us
    ppermute x12, waiting for transfers between devices, plane_swap(): return lax.ppermute(x, AXES, pairs)  11 us
    pallas_call x5, Pallas kernels, in_vmem(): pl.pallas_call(kernel, in_specs=[vm] * len(args), out_specs=[vm] * len(ou...  10.1 us
    ppermute x7, waiting for transfers between devices, shift(): return lax.ppermute(x, 'z', [(i, (i + by) % NZ) for i in range(NZ)])  4.77 us
    pallas_call x2, Pallas kernels, score(): pl.pallas_call(functools.partial(score_kernel, ks), in_specs=[vm] * (7 +...  4.09 us
  transfers between devices with their start and end apart: 34, of which 19 were waited for; matrix products, arithmetic and copies ran while one was open for 1% of the time, Pallas kernels for 8%

profile of v5, /device:TPU:1, one launch (start us, length us, event | category | flops | bytes accessed | tf_op | source)
XLA Modules:
  0.0 124.1 jit_solution(14684719784990542691)
XLA Ops:
  0.6 1.9 %pack.1 = (bf16[272,256]{1,0:T(8,128)(2,1)}, bf16[528,256]{1,0:T(8,128)(2,1)}) custom-call(bf16[256,256]{1,0:T(8,128)(2,1)} %user_hbm.1, s32[1,256]{1,0:T(1,128)} %bitcast.52, bf16[512,256]{1,0:T(8,128)(2,1)} %feat_hbm.1, s32[1,512]{1,0:T(1,128)} %bitcast.50, s32[1,512]{1,0:T(1,128)} %bitcast.51), custom_call_target="tpu_custom_call" | custom-call | bytes 1000000 | tf_op jit(solution)/shard_map/pack/pallas_call | solution.py:82
  2.6 2.5 %collective-permute-start.1 = (bf16[272,256]{1,0:T(8,128)(2,1)}, bf16[272,256]{1,0:T(8,128)(2,1)S(1)}, u32[]{:S(2)}, u32[]{:S(2)}) collective-permute-start(bf16[272,256]{1,0:T(8,128)(2,1)} %get-tuple-element.54.rest_0_), channel_id=1, source_target_pairs={{0,16},{16,32},{32,48},{48,64},{64,80},{80,96},{96,112},{112,0},{1... | collective-permute-start | bytes 417800 | tf_op jit(solution)/shard_map/ppermute | solution.py:360
  6.3 4.0 %collective-permute-start.2 = (bf16[272,256]{1,0:T(8,128)(2,1)}, bf16[272,256]{1,0:T(8,128)(2,1)S(1)}, u32[]{:S(2)}, u32[]{:S(2)}) collective-permute-start(bf16[272,256]{1,0:T(8,128)(2,1)} %get-tuple-element.54.rest_0_), channel_id=1, source_target_pairs={{0,112},{16,0},{32,16},{48,32},{64,48},{80,64},{96,80},{112,96},{1... | collective-permute-start | bytes 417800 | tf_op jit(solution)/shard_map/ppermute | solution.py:360
  15.7 2.7 %collective-permute-start.4 = (bf16[272,256]{1,0:T(8,128)(2,1)S(1)}, bf16[272,256]{1,0:T(8,128)(2,1)S(1)}, u32[]{:S(2)}, u32[]{:S(2)}) collective-permute-start(bf16[272,256]{1,0:T(8,128)(2,1)S(1)} %collective-permute-done.2.rest_2_), channel_id=1, source_target_pairs={{0,112},{16,0},{32,16},{48,32},{64,48},{80,64},{96,80},{112,96},{1... | collective-permute-start | bytes 417800 | tf_op jit(solution)/shard_map/ppermute | solution.py:360
  19.7 1.7 %far.1 = (bf16[512,2048]{1,0:T(8,128)(2,1)S(1)}, bf16[512,256]{1,0:T(8,128)(2,1)S(1)}, f32[1024,128]{1,0:T(8,128)S(1)}, f32[1024,128]{1,0:T(8,128)S(1)}) custom-call(bf16[16,256]{1,0:T(8,128)(2,1)S(1)} %get-tuple-element.47.near_tail, bf16[528,256]{1,0:T(8,128)(2,1)S(1)} %collective-permute-done.far_ref, bf16[256,2048]{1,0:T(8,128)(2,1)S(1)} %get-tuple-element.48.w_in_ref, ...), custom_call_target="tpu_custom_call" | custom-call | flops 1073741824 | bytes 4000000 | tf_op jit(solution)/shard_map/far/pallas_call | solution.py:141
  21.5 2.7 %collective-permute-start.6 = (bf16[272,256]{1,0:T(8,128)(2,1)S(1)}, bf16[272,256]{1,0:T(8,128)(2,1)S(1)}, u32[]{:S(2)}, u32[]{:S(2)}) collective-permute-start(bf16[272,256]{1,0:T(8,128)(2,1)S(1)} %collective-permute-done.4.rest_4_), channel_id=1, source_target_pairs={{0,112},{16,0},{32,16},{48,32},{64,48},{80,64},{96,80},{112,96},{1... | collective-permute-start | bytes 417800 | tf_op jit(solution)/shard_map/ppermute | solution.py:360
  24.8 2.2 %score.2 = (f32[8,256]{1,0:T(8,128)S(1)}, f32[8,256]{1,0:T(8,128)S(1)}, f32[1,256]{1,0:T(1,128)S(1)}, bf16[1024,1280]{1,0:T(8,128)(2,1)S(1)}) custom-call(bf16[512,256]{1,0:T(8,128)(2,1)S(1)} %get-tuple-element.46.near_emb, bf16[512,256]{1,0:T(8,128)(2,1)S(1)} %get-tuple-element.50.far_emb, f32[1024,128]{1,0:T(8,128)S(1)} %get-tuple-element.51.nid_ref, ...), custom_call_target="tpu_custom_call" | custom-call | flops 671088640 | bytes 5000000 | tf_op jit(solution)/shard_map/score/pallas_call | solution.py:198
  27.1 2.9 %collective-permute-done.7.rest_2_.rest_7_ = bf16[272,256]{1,0:T(8,128)(2,1)S(1)} collective-permute-done((bf16[272,256]{1,0:T(8,128)(2,1)S(1)}, bf16[272,256]{1,0:T(8,128)(2,1)S(1)}, u32[]{:S(2)}, u32[]{:S(2)}) %collective-permute-start.7) | collective-permute-done | bytes 139296 | tf_op jit(solution)/shard_map/ppermute | solution.py:360
  29.9 1.9 %score.3 = (f32[8,256]{1,0:T(8,128)S(1)}, f32[8,256]{1,0:T(8,128)S(1)}, f32[1,256]{1,0:T(1,128)}, bf16[1024,768]{1,0:T(8,128)(2,1)S(1)}) custom-call(bf16[512,256]{1,0:T(8,128)(2,1)S(1)} %get-tuple-element.46.near_emb, bf16[512,256]{1,0:T(8,128)(2,1)S(1)} %get-tuple-element.50.far_emb, f32[1024,128]{1,0:T(8,128)S(1)} %get-tuple-element.51.nid_ref, ...), custom_call_target="tpu_custom_call" | custom-call | flops 402653184 | bytes 5000000 | tf_op jit(solution)/shard_map/score/pallas_call | solution.py:198
  31.8 2.1 %collective-permute-start.9 = (f32[8,256]{1,0:T(8,128)S(1)}, f32[8,256]{1,0:T(8,128)S(1)}, u32[]{:S(2)}, u32[]{:S(2)}) collective-permute-start(f32[8,256]{1,0:T(8,128)S(1)} %get-tuple-element.62), channel_id=1, source_target_pairs={{0,96},{16,112},{32,64},{48,80},{64,32},{80,48},{96,0},{112,16},{1... | collective-permute-start | bytes 24584 | tf_op jit(solution)/shard_map/ppermute | solution.py:352
  33.9 1.7 %collective-permute-start.8 = (f32[8,256]{1,0:T(8,128)S(1)}, f32[8,256]{1,0:T(8,128)S(1)}, u32[]{:S(2)}, u32[]{:S(2)}) collective-permute-start(f32[8,256]{1,0:T(8,128)S(1)} %get-tuple-element.62), channel_id=1, source_target_pairs={{0,16},{16,0},{32,48},{48,32},{64,80},{80,64},{96,112},{112,96},{1... | collective-permute-start | bytes 24584 | tf_op jit(solution)/shard_map/ppermute | solution.py:352
  36.8 2.4 %collective-permute-start.11 = (f32[8,256]{1,0:T(8,128)S(1)}, f32[8,256]{1,0:T(8,128)S(1)}, u32[]{:S(2)}, u32[]{:S(2)}) collective-permute-start(f32[8,256]{1,0:T(8,128)S(1)} %add_add_fusion), channel_id=1, source_target_pairs={{0,32},{16,48},{32,0},{48,16},{64,96},{80,112},{96,64},{112,80},{1... | collective-permute-start | bytes 24584 | tf_op jit(solution)/shard_map/ppermute | solution.py:352
  40.2 2.7 %grads.1 = (bf16[4,256,256]{2,1,0:T(8,128)(2,1)S(1)}, bf16[4,256,256]{2,1,0:T(8,128)(2,1)S(1)}, bf16[1280,256]{1,0:T(8,128)(2,1)S(1)}, f32[256,256]{1,0:T(8,128)S(1)}) custom-call(f32[8,256]{1,0:T(8,128)S(1)} %add.63.tot_ref, f32[8,256]{1,0:T(8,128)S(1)} %get-tuple-element.63.tloc_ref, f32[1,256]{1,0:T(1,128)S(1)} %get-tuple-element.64.pexp_ref, ...), custom_call_target="tpu_custom_call" | custom-call | flops 2147483648 | bytes 8000000 | tf_op jit(solution)/shard_map/grads/pallas_call | solution.py:252
  43.0 3.1 %backward.3 = bf16[4,4,128,256]{3,2,1,0:T(8,128)(2,1)S(1)} custom-call(bf16[1280,256]{1,0:T(8,128)(2,1)S(1)} %get-tuple-element.67.g_ref, bf16[768,256]{1,0:T(8,128)(2,1)S(1)} %get-tuple-element.68.feat_ref, bf16[528,256]{1,0:T(8,128)(2,1)S(1)} %collective-permute-done.far_ref, bf16[2048,256]{1,0:T(8,128)(2,1)S(1)} %get-tuple-element.49.w_out_ref, ...), custom_call_target="tpu_custom_call" | custom-call | flops 2013265920 | bytes 4000000 | tf_op jit(solution)/shard_map/backward/pallas_call | solution.py:141
  46.1 7.3 %collective-permute-start.12 = (bf16[4,4,128,256]{3,2,1,0:T(8,128)(2,1)S(1)}, bf16[4,4,128,256]{3,2,1,0:T(8,128)(2,1)S(1)}, u32[]{:S(2)}, u32[]{:S(2)}) collective-permute-start(bf16[4,4,128,256]{3,2,1,0:T(8,128)(2,1)S(1)} %backward.3), channel_id=1, source_target_pairs={{0,1},{1,0},{2,3},{3,2},{4,5},{5,4},{6,7},{7,6},{8,9},{9,8},{10,11... | collective-permute-start | bytes 3145736 | tf_op jit(solution)/shard_map/ppermute | solution.py:352
  53.4 1.8 %collective-permute-start.16 = (bf16[4,256,256]{2,1,0:T(8,128)(2,1)S(1)}, bf16[4,256,256]{2,1,0:T(8,128)(2,1)S(1)}, u32[]{:S(2)}, u32[]{:S(2)}) collective-permute-start(bf16[4,256,256]{2,1,0:T(8,128)(2,1)S(1)} %get-tuple-element.71), channel_id=1, source_target_pairs={{0,16},{16,0},{32,48},{48,32},{64,80},{80,64},{96,112},{112,96},{1... | collective-permute-start | bytes 1572872 | tf_op jit(solution)/shard_map/ppermute | solution.py:352
  55.3 3.1 %backward.2 = bf16[4,4,128,256]{3,2,1,0:T(8,128)(2,1)S(1)} custom-call(bf16[1280,256]{1,0:T(8,128)(2,1)S(1)} %get-tuple-element.67.g_ref, bf16[768,256]{1,0:T(8,128)(2,1)S(1)} %get-tuple-element.68.feat_ref, bf16[528,256]{1,0:T(8,128)(2,1)S(1)} %collective-permute-done.far_ref, bf16[2048,256]{1,0:T(8,128)(2,1)S(1)} %get-tuple-element.49.w_out_ref, ...), custom_call_target="tpu_custom_call" | custom-call | flops 2013265920 | bytes 4000000 | tf_op jit(solution)/shard_map/backward/pallas_call | solution.py:141
  60.2 1.9 %collective-permute-start.15 = (bf16[4,128,256]{2,1,0:T(8,128)(2,1)S(1)}, bf16[4,128,256]{2,1,0:T(8,128)(2,1)S(1)}, u32[]{:S(2)}, u32[]{:S(2)}) collective-permute-start(bf16[4,128,256]{2,1,0:T(8,128)(2,1)S(1)} %get-tuple-element.86), channel_id=1, source_target_pairs={{0,136},{1,7},{2,138},{3,5},{4,140},{5,3},{6,142},{7,1},{128,8},{1... | collective-permute-start | bytes 786440 | tf_op jit(solution)/shard_map/ppermute | solution.py:377
  62.9 4.5 %collective-permute-done.16 = bf16[4,256,256]{2,1,0:T(8,128)(2,1)S(1)} collective-permute-done((bf16[4,256,256]{2,1,0:T(8,128)(2,1)S(1)}, bf16[4,256,256]{2,1,0:T(8,128)(2,1)S(1)}, u32[]{:S(2)}, u32[]{:S(2)}) %collective-permute-start.16) | collective-permute-done | bytes 524320 | tf_op jit(solution)/shard_map/ppermute | solution.py:352
  70.0 2.5 %collective-permute-start.19 = (bf16[128,256]{1,0:T(8,128)(2,1)S(1)}, bf16[128,256]{1,0:T(8,128)(2,1)S(1)}, u32[]{:S(2)}, u32[]{:S(2)}) collective-permute-start(bf16[128,256]{1,0:T(8,128)(2,1)S(1)} %get-tuple-element.94), channel_id=1, source_target_pairs={{0,6},{1,137},{2,4},{3,139},{4,2},{5,141},{6,0},{7,143},{128,134},... | collective-permute-start | bytes 196616 | tf_op jit(solution)/shard_map/ppermute | solution.py:377
  74.4 2.7 %collective-permute-done.18 = bf16[128,256]{1,0:T(8,128)(2,1)S(1)} collective-permute-done((bf16[128,256]{1,0:T(8,128)(2,1)S(1)}, bf16[128,256]{1,0:T(8,128)(2,1)S(1)}, u32[]{:S(2)}, u32[]{:S(2)}) %collective-permute-start.18) | collective-permute-done | bytes 65568 | tf_op jit(solution)/shard_map/ppermute | solution.py:377
  77.2 3.1 %collective-permute-done.20 = bf16[128,256]{1,0:T(8,128)(2,1)S(1)} collective-permute-done((bf16[128,256]{1,0:T(8,128)(2,1)S(1)}, bf16[128,256]{1,0:T(8,128)(2,1)S(1)}, u32[]{:S(2)}, u32[]{:S(2)}) %collective-permute-start.20) | collective-permute-done | bytes 65568 | tf_op jit(solution)/shard_map/ppermute | solution.py:352
  80.3 1.8 %collective-permute-start.23 = (bf16[128,256]{1,0:T(8,128)(2,1)S(1)}, bf16[128,256]{1,0:T(8,128)(2,1)S(1)}, u32[]{:S(2)}, u32[]{:S(2)}) collective-permute-start(bf16[128,256]{1,0:T(8,128)(2,1)S(1)} %add_convert_fusion.3), channel_id=1, source_target_pairs={{0,96},{16,112},{32,64},{48,80},{64,32},{80,48},{96,0},{112,16},{1... | collective-permute-start | bytes 196616 | tf_op jit(solution)/shard_map/ppermute | solution.py:352
  82.2 4.2 %collective-permute-start.22 = (bf16[128,256]{1,0:T(8,128)(2,1)S(1)}, bf16[128,256]{1,0:T(8,128)(2,1)S(1)}, u32[]{:S(2)}, u32[]{:S(2)}) collective-permute-start(bf16[128,256]{1,0:T(8,128)(2,1)S(1)} %add_convert_fusion.3), channel_id=1, source_target_pairs={{0,64},{16,80},{32,96},{48,112},{64,0},{80,16},{96,32},{112,48},{1... | collective-permute-start | bytes 196616 | tf_op jit(solution)/shard_map/ppermute | solution.py:352
  86.4 2.9 %collective-permute-done.22 = bf16[128,256]{1,0:T(8,128)(2,1)S(1)} collective-permute-done((bf16[128,256]{1,0:T(8,128)(2,1)S(1)}, bf16[128,256]{1,0:T(8,128)(2,1)S(1)}, u32[]{:S(2)}, u32[]{:S(2)}) %collective-permute-start.22) | collective-permute-done | bytes 65568 | tf_op jit(solution)/shard_map/ppermute | solution.py:352
  89.3 1.8 %collective-permute-done.21 = bf16[128,256]{1,0:T(8,128)(2,1)S(1)} collective-permute-done((bf16[128,256]{1,0:T(8,128)(2,1)S(1)}, bf16[128,256]{1,0:T(8,128)(2,1)S(1)}, u32[]{:S(2)}, u32[]{:S(2)}) %collective-permute-start.21) | collective-permute-done | bytes 65568 | tf_op jit(solution)/shard_map/ppermute | solution.py:352
  91.7 1.5 %collective-permute-start.25 = (bf16[128,256]{1,0:T(8,128)(2,1)S(1)}, bf16[128,256]{1,0:T(8,128)(2,1)S(1)}, u32[]{:S(2)}, u32[]{:S(2)}) collective-permute-start(bf16[128,256]{1,0:T(8,128)(2,1)S(1)} %add_convert_fusion.2), channel_id=1, source_target_pairs={{0,4},{1,9},{2,6},{3,11},{4,0},{5,13},{6,2},{7,15},{128,132},{129,... | collective-permute-start | bytes 196616 | tf_op jit(solution)/shard_map/ppermute | solution.py:377
  94.5 2.5 %collective-permute-start.30 = (bf16[256,256]{1,0:T(8,128)(2,1)S(1)}, bf16[256,256]{1,0:T(8,128)(2,1)S(1)}, u32[]{:S(2)}, u32[]{:S(2)}) collective-permute-start(bf16[256,256]{1,0:T(8,128)(2,1)S(1)} %get-tuple-element.88), channel_id=1, source_target_pairs={{0,64},{16,80},{32,96},{48,112},{64,0},{80,16},{96,32},{112,48},{1... | collective-permute-start | bytes 393224 | tf_op jit(solution)/shard_map/ppermute | solution.py:352
  97.1 1.8 %collective-permute-start.32 = (bf16[256,256]{1,0:T(8,128)(2,1)S(1)}, bf16[256,256]{1,0:T(8,128)(2,1)S(1)}, u32[]{:S(2)}, u32[]{:S(2)}) collective-permute-start(bf16[256,256]{1,0:T(8,128)(2,1)S(1)} %get-tuple-element.89), channel_id=1, source_target_pairs={{0,96},{16,112},{32,64},{48,80},{64,32},{80,48},{96,0},{112,16},{1... | collective-permute-start | bytes 393224 | tf_op jit(solution)/shard_map/ppermute | solution.py:352
  100.3 2.4 %collective-permute-start.29 = (bf16[4,128,256]{2,1,0:T(8,128)(2,1)S(1)}, bf16[4,128,256]{2,1,0:T(8,128)(2,1)S(1)}, u32[]{:S(2)}, u32[]{:S(2)}) collective-permute-start(bf16[4,128,256]{2,1,0:T(8,128)(2,1)S(1)} %get-tuple-element.92), channel_id=1, source_target_pairs={{0,136},{1,7},{2,138},{3,5},{4,140},{5,3},{6,142},{7,1},{128,8},{1... | collective-permute-start | bytes 786440 | tf_op jit(solution)/shard_map/ppermute | solution.py:377
  105.4 4.2 %collective-permute-done.29 = bf16[4,128,256]{2,1,0:T(8,128)(2,1)S(1)} collective-permute-done((bf16[4,128,256]{2,1,0:T(8,128)(2,1)S(1)}, bf16[4,128,256]{2,1,0:T(8,128)(2,1)S(1)}, u32[]{:S(2)}, u32[]{:S(2)}) %collective-permute-start.29) | collective-permute-done | bytes 262176 | tf_op jit(solution)/shard_map/ppermute | solution.py:377
  110.4 9.8 %collective-permute-start.33 = (bf16[4,4,128,256]{3,2,1,0:T(8,128)(2,1)S(1)}, bf16[4,4,128,256]{3,2,1,0:T(8,128)(2,1)S(1)}, u32[]{:S(2)}, u32[]{:S(2)}) collective-permute-start(bf16[4,4,128,256]{3,2,1,0:T(8,128)(2,1)S(1)} %pad_maximum_fusion.x_ref), channel_id=1, source_target_pairs={{0,1},{1,0},{2,3},{3,2},{4,5},{5,4},{6,7},{7,6},{8,9},{9,8},{10,11... | collective-permute-start | bytes 3145736 | tf_op jit(solution)/shard_map/ppermute | solution.py:352
  (75 shorter events, 28.1 us)
Async XLA Ops:
  2.6 11.9 %collective-permute-start.1 = (bf16[272,256]{1,0:T(8,128)(2,1)}, bf16[272,256]{1,0:T(8,128)(2,1)S(1)}, u32[]{:S(2)}, u32[]{:S(2)}) collective-permute-start(bf16[272,256]{1,0:T(8,128)(2,1)} %get-tuple-element.54.rest_0_), channel_id=1, source_target_pairs={{0,16},{16,32},{32,48},{48,64},{64,80},{80,96},{96,112},{112,0},{1... | collective-permute-start | bytes 417800 | tf_op jit(solution)/shard_map/ppermute | solution.py:360
  5.1 14.6 %collective-permute-start = (bf16[528,256]{1,0:T(8,128)(2,1)}, bf16[528,256]{1,0:T(8,128)(2,1)S(1)}, u32[]{:S(2)}, u32[]{:S(2)}) collective-permute-start(bf16[528,256]{1,0:T(8,128)(2,1)} %get-tuple-element.44.near_ref), channel_id=1, source_target_pairs={{0,128},{128,0},{1,129},{129,1},{2,130},{130,2},{3,131},{131,3},{4... | collective-permute-start | bytes 811016 | tf_op jit(solution)/shard_map/ppermute | solution.py:352
  6.3 9.3 %collective-permute-start.2 = (bf16[272,256]{1,0:T(8,128)(2,1)}, bf16[272,256]{1,0:T(8,128)(2,1)S(1)}, u32[]{:S(2)}, u32[]{:S(2)}) collective-permute-start(bf16[272,256]{1,0:T(8,128)(2,1)} %get-tuple-element.54.rest_0_), channel_id=1, source_target_pairs={{0,112},{16,0},{32,16},{48,32},{64,48},{80,64},{96,80},{112,96},{1... | collective-permute-start | bytes 417800 | tf_op jit(solution)/shard_map/ppermute | solution.py:360
  14.5 5.2 %collective-permute-start.3 = (bf16[272,256]{1,0:T(8,128)(2,1)S(1)}, bf16[272,256]{1,0:T(8,128)(2,1)S(1)}, u32[]{:S(2)}, u32[]{:S(2)}) collective-permute-start(bf16[272,256]{1,0:T(8,128)(2,1)S(1)} %collective-permute-done.1.rest_1_), channel_id=1, source_target_pairs={{0,16},{16,32},{32,48},{48,64},{64,80},{80,96},{96,112},{112,0},{1... | collective-permute-start | bytes 417800 | tf_op jit(solution)/shard_map/ppermute | solution.py:360
  15.7 5.8 %collective-permute-start.4 = (bf16[272,256]{1,0:T(8,128)(2,1)S(1)}, bf16[272,256]{1,0:T(8,128)(2,1)S(1)}, u32[]{:S(2)}, u32[]{:S(2)}) collective-permute-start(bf16[272,256]{1,0:T(8,128)(2,1)S(1)} %collective-permute-done.2.rest_2_), channel_id=1, source_target_pairs={{0,112},{16,0},{32,16},{48,32},{64,48},{80,64},{96,80},{112,96},{1... | collective-permute-start | bytes 417800 | tf_op jit(solution)/shard_map/ppermute | solution.py:360
  19.7 5.1 %collective-permute-start.5 = (bf16[272,256]{1,0:T(8,128)(2,1)S(1)}, bf16[272,256]{1,0:T(8,128)(2,1)S(1)}, u32[]{:S(2)}, u32[]{:S(2)}) collective-permute-start(bf16[272,256]{1,0:T(8,128)(2,1)S(1)} %collective-permute-done.3.rest_3_), channel_id=1, source_target_pairs={{0,16},{16,32},{32,48},{48,64},{64,80},{80,96},{96,112},{112,0},{1... | collective-permute-start | bytes 417800 | tf_op jit(solution)/shard_map/ppermute | solution.py:360
  21.5 5.6 %collective-permute-start.6 = (bf16[272,256]{1,0:T(8,128)(2,1)S(1)}, bf16[272,256]{1,0:T(8,128)(2,1)S(1)}, u32[]{:S(2)}, u32[]{:S(2)}) collective-permute-start(bf16[272,256]{1,0:T(8,128)(2,1)S(1)} %collective-permute-done.4.rest_4_), channel_id=1, source_target_pairs={{0,112},{16,0},{32,16},{48,32},{64,48},{80,64},{96,80},{112,96},{1... | collective-permute-start | bytes 417800 | tf_op jit(solution)/shard_map/ppermute | solution.py:360
  24.8 5.1 %collective-permute-start.7 = (bf16[272,256]{1,0:T(8,128)(2,1)S(1)}, bf16[272,256]{1,0:T(8,128)(2,1)S(1)}, u32[]{:S(2)}, u32[]{:S(2)}) collective-permute-start(bf16[272,256]{1,0:T(8,128)(2,1)S(1)} %collective-permute-done.5.rest_0_.rest_5_), channel_id=1, source_target_pairs={{0,16},{16,32},{32,48},{48,64},{64,80},{80,96},{96,112},{112,0},{1... | collective-permute-start | bytes 417800 | tf_op jit(solution)/shard_map/ppermute | solution.py:360
  31.8 3.9 %collective-permute-start.10 = (f32[8,256]{1,0:T(8,128)S(1)}, f32[8,256]{1,0:T(8,128)S(1)}, u32[]{:S(2)}, u32[]{:S(2)}) collective-permute-start(f32[8,256]{1,0:T(8,128)S(1)} %get-tuple-element.62), channel_id=1, source_target_pairs={{0,112},{16,96},{32,80},{48,64},{64,48},{80,32},{96,16},{112,0},{1... | collective-permute-start | bytes 24584 | tf_op jit(solution)/shard_map/ppermute | solution.py:352
  31.8 4.6 %collective-permute-start.9 = (f32[8,256]{1,0:T(8,128)S(1)}, f32[8,256]{1,0:T(8,128)S(1)}, u32[]{:S(2)}, u32[]{:S(2)}) collective-permute-start(f32[8,256]{1,0:T(8,128)S(1)} %get-tuple-element.62), channel_id=1, source_target_pairs={{0,96},{16,112},{32,64},{48,80},{64,32},{80,48},{96,0},{112,16},{1... | collective-permute-start | bytes 24584 | tf_op jit(solution)/shard_map/ppermute | solution.py:352
  36.8 3.5 %collective-permute-start.11 = (f32[8,256]{1,0:T(8,128)S(1)}, f32[8,256]{1,0:T(8,128)S(1)}, u32[]{:S(2)}, u32[]{:S(2)}) collective-permute-start(f32[8,256]{1,0:T(8,128)S(1)} %add_add_fusion), channel_id=1, source_target_pairs={{0,32},{16,48},{32,0},{48,16},{64,96},{80,112},{96,64},{112,80},{1... | collective-permute-start | bytes 24584 | tf_op jit(solution)/shard_map/ppermute | solution.py:352
  46.1 12.3 %collective-permute-start.12 = (bf16[4,4,128,256]{3,2,1,0:T(8,128)(2,1)S(1)}, bf16[4,4,128,256]{3,2,1,0:T(8,128)(2,1)S(1)}, u32[]{:S(2)}, u32[]{:S(2)}) collective-permute-start(bf16[4,4,128,256]{3,2,1,0:T(8,128)(2,1)S(1)} %backward.3), channel_id=1, source_target_pairs={{0,1},{1,0},{2,3},{3,2},{4,5},{5,4},{6,7},{7,6},{8,9},{9,8},{10,11... | collective-permute-start | bytes 3145736 | tf_op jit(solution)/shard_map/ppermute | solution.py:352
  53.4 13.9 %collective-permute-start.16 = (bf16[4,256,256]{2,1,0:T(8,128)(2,1)S(1)}, bf16[4,256,256]{2,1,0:T(8,128)(2,1)S(1)}, u32[]{:S(2)}, u32[]{:S(2)}) collective-permute-start(bf16[4,256,256]{2,1,0:T(8,128)(2,1)S(1)} %get-tuple-element.71), channel_id=1, source_target_pairs={{0,16},{16,0},{32,48},{48,32},{64,80},{80,64},{96,112},{112,96},{1... | collective-permute-start | bytes 1572872 | tf_op jit(solution)/shard_map/ppermute | solution.py:352
  58.9 8.6 %collective-permute-start.13 = (bf16[4,128,256]{2,1,0:T(8,128)(2,1)S(1)}, bf16[4,128,256]{2,1,0:T(8,128)(2,1)S(1)}, u32[]{:S(2)}, u32[]{:S(2)}) collective-permute-start(bf16[4,128,256]{2,1,0:T(8,128)(2,1)S(1)} %get-tuple-element.85), channel_id=1, source_target_pairs={{0,128},{1,3},{2,130},{3,1},{4,132},{5,7},{6,134},{7,5},{128,0},{1... | collective-permute-start | bytes 786440 | tf_op jit(solution)/shard_map/ppermute | solution.py:377
  60.2 8.0 %collective-permute-start.15 = (bf16[4,128,256]{2,1,0:T(8,128)(2,1)S(1)}, bf16[4,128,256]{2,1,0:T(8,128)(2,1)S(1)}, u32[]{:S(2)}, u32[]{:S(2)}) collective-permute-start(bf16[4,128,256]{2,1,0:T(8,128)(2,1)S(1)} %get-tuple-element.86), channel_id=1, source_target_pairs={{0,136},{1,7},{2,138},{3,5},{4,140},{5,3},{6,142},{7,1},{128,8},{1... | collective-permute-start | bytes 786440 | tf_op jit(solution)/shard_map/ppermute | solution.py:377
  62.1 7.6 %collective-permute-start.14 = (bf16[4,128,256]{2,1,0:T(8,128)(2,1)S(1)}, bf16[4,128,256]{2,1,0:T(8,128)(2,1)S(1)}, u32[]{:S(2)}, u32[]{:S(2)}) collective-permute-start(bf16[4,128,256]{2,1,0:T(8,128)(2,1)S(1)} %get-tuple-element.87), channel_id=1, source_target_pairs={{0,8},{1,5},{2,10},{3,7},{4,12},{5,1},{6,14},{7,3},{128,136},{129,... | collective-permute-start | bytes 786440 | tf_op jit(solution)/shard_map/ppermute | solution.py:377
  69.9 3.3 %collective-permute-start.17 = (bf16[128,256]{1,0:T(8,128)(2,1)S(1)}, bf16[128,256]{1,0:T(8,128)(2,1)S(1)}, u32[]{:S(2)}, u32[]{:S(2)}) collective-permute-start(bf16[128,256]{1,0:T(8,128)(2,1)S(1)} %get-tuple-element.93), channel_id=1, source_target_pairs={{0,2},{1,129},{2,0},{3,131},{4,6},{5,133},{6,4},{7,135},{128,130},... | collective-permute-start | bytes 196616 | tf_op jit(solution)/shard_map/ppermute | solution.py:377
  70.0 4.4 %collective-permute-start.19 = (bf16[128,256]{1,0:T(8,128)(2,1)S(1)}, bf16[128,256]{1,0:T(8,128)(2,1)S(1)}, u32[]{:S(2)}, u32[]{:S(2)}) collective-permute-start(bf16[128,256]{1,0:T(8,128)(2,1)S(1)} %get-tuple-element.94), channel_id=1, source_target_pairs={{0,6},{1,137},{2,4},{3,139},{4,2},{5,141},{6,0},{7,143},{128,134},... | collective-permute-start | bytes 196616 | tf_op jit(solution)/shard_map/ppermute | solution.py:377
  72.5 4.6 %collective-permute-start.18 = (bf16[128,256]{1,0:T(8,128)(2,1)S(1)}, bf16[128,256]{1,0:T(8,128)(2,1)S(1)}, u32[]{:S(2)}, u32[]{:S(2)}) collective-permute-start(bf16[128,256]{1,0:T(8,128)(2,1)S(1)} %get-tuple-element.95), channel_id=1, source_target_pairs={{0,4},{1,9},{2,6},{3,11},{4,0},{5,13},{6,2},{7,15},{128,132},{129,... | collective-permute-start | bytes 196616 | tf_op jit(solution)/shard_map/ppermute | solution.py:377
  80.3 6.0 %collective-permute-start.23 = (bf16[128,256]{1,0:T(8,128)(2,1)S(1)}, bf16[128,256]{1,0:T(8,128)(2,1)S(1)}, u32[]{:S(2)}, u32[]{:S(2)}) collective-permute-start(bf16[128,256]{1,0:T(8,128)(2,1)S(1)} %add_convert_fusion.3), channel_id=1, source_target_pairs={{0,96},{16,112},{32,64},{48,80},{64,32},{80,48},{96,0},{112,16},{1... | collective-permute-start | bytes 196616 | tf_op jit(solution)/shard_map/ppermute | solution.py:352
  82.2 7.1 %collective-permute-start.22 = (bf16[128,256]{1,0:T(8,128)(2,1)S(1)}, bf16[128,256]{1,0:T(8,128)(2,1)S(1)}, u32[]{:S(2)}, u32[]{:S(2)}) collective-permute-start(bf16[128,256]{1,0:T(8,128)(2,1)S(1)} %add_convert_fusion.3), channel_id=1, source_target_pairs={{0,64},{16,80},{32,96},{48,112},{64,0},{80,16},{96,32},{112,48},{1... | collective-permute-start | bytes 196616 | tf_op jit(solution)/shard_map/ppermute | solution.py:352
  86.4 4.7 %collective-permute-start.21 = (bf16[128,256]{1,0:T(8,128)(2,1)S(1)}, bf16[128,256]{1,0:T(8,128)(2,1)S(1)}, u32[]{:S(2)}, u32[]{:S(2)}) collective-permute-start(bf16[128,256]{1,0:T(8,128)(2,1)S(1)} %add_convert_fusion.3), channel_id=1, source_target_pairs={{0,32},{16,48},{32,0},{48,16},{64,96},{80,112},{96,64},{112,80},{1... | collective-permute-start | bytes 196616 | tf_op jit(solution)/shard_map/ppermute | solution.py:352
  91.1 7.8 %collective-permute-start.26 = (bf16[128,256]{1,0:T(8,128)(2,1)S(1)}, bf16[128,256]{1,0:T(8,128)(2,1)S(1)}, u32[]{:S(2)}, u32[]{:S(2)}) collective-permute-start(bf16[128,256]{1,0:T(8,128)(2,1)S(1)} %add_convert_fusion.2), channel_id=1, source_target_pairs={{0,6},{1,137},{2,4},{3,139},{4,2},{5,141},{6,0},{7,143},{128,134},... | collective-permute-start | bytes 196616 | tf_op jit(solution)/shard_map/ppermute | solution.py:377
  91.7 8.5 %collective-permute-start.25 = (bf16[128,256]{1,0:T(8,128)(2,1)S(1)}, bf16[128,256]{1,0:T(8,128)(2,1)S(1)}, u32[]{:S(2)}, u32[]{:S(2)}) collective-permute-start(bf16[128,256]{1,0:T(8,128)(2,1)S(1)} %add_convert_fusion.2), channel_id=1, source_target_pairs={{0,4},{1,9},{2,6},{3,11},{4,0},{5,13},{6,2},{7,15},{128,132},{129,... | collective-permute-start | bytes 196616 | tf_op jit(solution)/shard_map/ppermute | solution.py:377
  93.3 7.0 %collective-permute-start.24 = (bf16[128,256]{1,0:T(8,128)(2,1)S(1)}, bf16[128,256]{1,0:T(8,128)(2,1)S(1)}, u32[]{:S(2)}, u32[]{:S(2)}) collective-permute-start(bf16[128,256]{1,0:T(8,128)(2,1)S(1)} %add_convert_fusion.2), channel_id=1, source_target_pairs={{0,2},{1,129},{2,0},{3,131},{4,6},{5,133},{6,4},{7,135},{128,130},... | collective-permute-start | bytes 196616 | tf_op jit(solution)/shard_map/ppermute | solution.py:377
  94.5 9.4 %collective-permute-start.30 = (bf16[256,256]{1,0:T(8,128)(2,1)S(1)}, bf16[256,256]{1,0:T(8,128)(2,1)S(1)}, u32[]{:S(2)}, u32[]{:S(2)}) collective-permute-start(bf16[256,256]{1,0:T(8,128)(2,1)S(1)} %get-tuple-element.88), channel_id=1, source_target_pairs={{0,64},{16,80},{32,96},{48,112},{64,0},{80,16},{96,32},{112,48},{1... | collective-permute-start | bytes 393224 | tf_op jit(solution)/shard_map/ppermute | solution.py:352
  97.1 7.3 %collective-permute-start.32 = (bf16[256,256]{1,0:T(8,128)(2,1)S(1)}, bf16[256,256]{1,0:T(8,128)(2,1)S(1)}, u32[]{:S(2)}, u32[]{:S(2)}) collective-permute-start(bf16[256,256]{1,0:T(8,128)(2,1)S(1)} %get-tuple-element.89), channel_id=1, source_target_pairs={{0,96},{16,112},{32,64},{48,80},{64,32},{80,48},{96,0},{112,16},{1... | collective-permute-start | bytes 393224 | tf_op jit(solution)/shard_map/ppermute | solution.py:352
  98.9 6.4 %collective-permute-start.31 = (bf16[256,256]{1,0:T(8,128)(2,1)S(1)}, bf16[256,256]{1,0:T(8,128)(2,1)S(1)}, u32[]{:S(2)}, u32[]{:S(2)}) collective-permute-start(bf16[256,256]{1,0:T(8,128)(2,1)S(1)} %get-tuple-element.90), channel_id=1, source_target_pairs={{0,32},{16,48},{32,0},{48,16},{64,96},{80,112},{96,64},{112,80},{1... | collective-permute-start | bytes 393224 | tf_op jit(solution)/shard_map/ppermute | solution.py:352
  100.3 9.3 %collective-permute-start.29 = (bf16[4,128,256]{2,1,0:T(8,128)(2,1)S(1)}, bf16[4,128,256]{2,1,0:T(8,128)(2,1)S(1)}, u32[]{:S(2)}, u32[]{:S(2)}) collective-permute-start(bf16[4,128,256]{2,1,0:T(8,128)(2,1)S(1)} %get-tuple-element.92), channel_id=1, source_target_pairs={{0,136},{1,7},{2,138},{3,5},{4,140},{5,3},{6,142},{7,1},{128,8},{1... | collective-permute-start | bytes 786440 | tf_op jit(solution)/shard_map/ppermute | solution.py:377
  102.8 6.9 %collective-permute-start.28 = (bf16[4,128,256]{2,1,0:T(8,128)(2,1)S(1)}, bf16[4,128,256]{2,1,0:T(8,128)(2,1)S(1)}, u32[]{:S(2)}, u32[]{:S(2)}) collective-permute-start(bf16[4,128,256]{2,1,0:T(8,128)(2,1)S(1)} %get-tuple-element.92), channel_id=1, source_target_pairs={{0,8},{1,5},{2,10},{3,7},{4,12},{5,1},{6,14},{7,3},{128,136},{129,... | collective-permute-start | bytes 786440 | tf_op jit(solution)/shard_map/ppermute | solution.py:377
  103.9 6.4 %collective-permute-start.27 = (bf16[4,128,256]{2,1,0:T(8,128)(2,1)S(1)}, bf16[4,128,256]{2,1,0:T(8,128)(2,1)S(1)}, u32[]{:S(2)}, u32[]{:S(2)}) collective-permute-start(bf16[4,128,256]{2,1,0:T(8,128)(2,1)S(1)} %get-tuple-element.92), channel_id=1, source_target_pairs={{0,128},{1,3},{2,130},{3,1},{4,132},{5,7},{6,134},{7,5},{128,0},{1... | collective-permute-start | bytes 786440 | tf_op jit(solution)/shard_map/ppermute | solution.py:377
  110.4 12.1 %collective-permute-start.33 = (bf16[4,4,128,256]{3,2,1,0:T(8,128)(2,1)S(1)}, bf16[4,4,128,256]{3,2,1,0:T(8,128)(2,1)S(1)}, u32[]{:S(2)}, u32[]{:S(2)}) collective-permute-start(bf16[4,4,128,256]{3,2,1,0:T(8,128)(2,1)S(1)} %pad_maximum_fusion.x_ref), channel_id=1, source_target_pairs={{0,1},{1,0},{2,3},{3,2},{4,5},{5,4},{6,7},{7,6},{8,9},{9,8},{10,11... | collective-permute-start | bytes 3145736 | tf_op jit(solution)/shard_map/ppermute | solution.py:352
  (8 other events, 37.5 us)

commit v6 on v5

--- a/solution.py
+++ b/solution.py
@@ -360,6 +360,16 @@
     return lax.ppermute(x, "z", [(i, (i + by) % NZ) for i in range(NZ)])
 
 
+def to_core(x, core):
+    return lax.ppermute(x, "core", [(1 - core, core)])
+
+
+def swap_on_core_1(x, k):
+    places = [(x_lo, z, x_hi, y) for x_lo in range(2) for z in range(NZ) for x_hi in range(2) for y in range(4)]
+    pairs = [(device(a, z, b, y, 1), device(a, z ^ k, b, y, 1)) for a, z, b, y in places]
+    return lax.ppermute(x, AXES, pairs)
+
+
 def device(x_lo, z, x_hi, y, core):
     return (((x_lo * 8 + z) * 2 + x_hi) * 4 + y) * 2 + core
 
@@ -392,18 +402,23 @@
 
 
 def all_reduce(mine, theirs, keep, send):
+    keep_0, send_0 = to_core(keep, 1), to_core(send, 1)
     half = add(mine, swap(theirs, "core", 1)).astype(BF)
+    half, keep_0, send_0 = lax.optimization_barrier((half, keep_0, send_0))
     quarter = add(half[0], *[plane_swap(half[k], k, 0) for k in (1, 2, 3)]).astype(BF)
-    keep = add(keep, swap(send, "z", 1)).astype(BF)
-    quarter, keep = lax.optimization_barrier((quarter, keep))
+    keep = add(keep, swap_on_core_1(send, 1)).astype(BF)
+    keep_0 = add(keep_0, swap_on_core_1(send_0, 1)).astype(BF)
+    quarter, keep, keep_0 = lax.optimization_barrier((quarter, keep, keep_0))
     part = add(quarter[0], *[plane_swap(quarter[k], k, 1) for k in (1, 2, 3)])
     part = sum_over_z(part, ((1,), (2, 4, 6)), BF).astype(BF)
-    part, keep = lax.optimization_barrier((part, keep))
+    part, keep, keep_0 = lax.optimization_barrier((part, keep, keep_0))
     quarter = jnp.stack([part] + [plane_swap(part, k, 1) for k in (1, 2, 3)])
-    user = add(keep[0], *[swap(keep[i], "z", k) for i, k in ((1, 4), (2, 2), (3, 6))])
+    both = [jnp.stack([keep[i], keep_0[i]]) for i in range(4)]
+    both = add(both[0], *[swap_on_core_1(both[i], k) for i, k in ((1, 4), (2, 2), (3, 6))])
     others = [plane_swap(quarter, k, 0) for k in (1, 2, 3)]
-    others, user = lax.optimization_barrier((others, user))
+    others, both = lax.optimization_barrier((others, both))
     half = jnp.stack([quarter] + others)
+    user = jnp.where(lax.axis_index("core") == 1, both[0], to_core(both[1].astype(BF), 0).astype(F32))
     return half, swap(half, "core", 1), user
 
 

time: 124 us -> 141 us (1.14)
  starting transfers between devices: 64.5 us -> 73.4 us
  waiting for transfers between devices: 32 us -> 38.7 us
    ppermute x0 -> x8, starting transfers between devices: none -> 23.6 us  [the longest x5 18.6 us: swap_on_core_1(): return lax.ppermute(x, AXES, pairs)]
    ppermute x15 -> x11, starting transfers between devices: 38.3 us -> 22.8 us  [swap(): lax.ppermute(x, axis, [(i, i ^ k) for i in range(SIZES[AXES.index(axis)])])]
    ppermute x12, waiting for transfers between devices: 11 us -> 23.5 us  [plane_swap(): return lax.ppermute(x, AXES, pairs)]
    ppermute x15 -> x11, waiting for transfers between devices: 16.3 us -> 10.4 us  [swap(): lax.ppermute(x, axis, [(i, i ^ k) for i in range(SIZES[AXES.index(axis)])])]
  transfers between devices with their start and end apart: 34 -> 38, of which waited for: 19 -> 19; matrix products, arithmetic and copies ran while one was open for 1% -> 1% of each run, Pallas kernels for 8% -> 8%
where the time goes in v6:
time: 141 us; the launch traced here: 140 us
  starting transfers between devices  73.4 us (52%)
  waiting for transfers between devices  38.7 us (27%)
  Pallas kernels  21.6 us (15%)
  local copies, waits for them, and re-layouts  3.25 us (2%)
  other arithmetic  2.03 us (1%)
    ppermute x12, waiting for transfers between devices, plane_swap(): return lax.ppermute(x, AXES, pairs)  23.5 us
    ppermute x11, starting transfers between devices, swap(): lax.ppermute(x, axis, [(i, i ^ k) for i in range(SIZES[AXES.index(axis)])])  22.8 us
    ppermute x5, starting transfers between devices, swap_on_core_1(): return lax.ppermute(x, AXES, pairs)  18.6 us
    ppermute x12, starting transfers between devices, plane_swap(): return lax.ppermute(x, AXES, pairs)  14.8 us
    ppermute x7, starting transfers between devices, shift(): return lax.ppermute(x, 'z', [(i, (i + by) % NZ) for i in range(NZ)])  12.1 us
    ppermute x11, waiting for transfers between devices, swap(): lax.ppermute(x, axis, [(i, i ^ k) for i in range(SIZES[AXES.index(axis)])])  10.4 us
    pallas_call x5, Pallas kernels, in_vmem(): pl.pallas_call(kernel, in_specs=[vm] * len(args), out_specs=[vm] * len(ou...  10.1 us
    ppermute x3, starting transfers between devices, to_core(): return lax.ppermute(x, 'core', [(1 - core, core)])  4.97 us
  transfers between devices with their start and end apart: 38, of which 19 were waited for; matrix products, arithmetic and copies ran while one was open for 1% of the time, Pallas kernels for 8%

profile of v6, /device:TPU:1, one launch (start us, length us, event | category | flops | bytes accessed | tf_op | source)
XLA Modules:
  0.0 140.2 jit_solution(3430378809893495960)
XLA Ops:
  2.6 2.5 %collective-permute-start.1 = (bf16[272,256]{1,0:T(8,128)(2,1)}, bf16[272,256]{1,0:T(8,128)(2,1)S(1)}, u32[]{:S(2)}, u32[]{:S(2)}) collective-permute-start(bf16[272,256]{1,0:T(8,128)(2,1)} %get-tuple-element.59.rest_0_), channel_id=1, source_target_pairs={{0,16},{16,32},{32,48},{48,64},{64,80},{80,96},{96,112},{112,0},{1... | collective-permute-start | bytes 417800 | tf_op jit(solution)/shard_map/ppermute | solution.py:360
  6.3 4.0 %collective-permute-start.2 = (bf16[272,256]{1,0:T(8,128)(2,1)}, bf16[272,256]{1,0:T(8,128)(2,1)S(1)}, u32[]{:S(2)}, u32[]{:S(2)}) collective-permute-start(bf16[272,256]{1,0:T(8,128)(2,1)} %get-tuple-element.59.rest_0_), channel_id=1, source_target_pairs={{0,112},{16,0},{32,16},{48,32},{64,48},{80,64},{96,80},{112,96},{1... | collective-permute-start | bytes 417800 | tf_op jit(solution)/shard_map/ppermute | solution.py:360
  15.7 2.7 %collective-permute-start.4 = (bf16[272,256]{1,0:T(8,128)(2,1)S(1)}, bf16[272,256]{1,0:T(8,128)(2,1)S(1)}, u32[]{:S(2)}, u32[]{:S(2)}) collective-permute-start(bf16[272,256]{1,0:T(8,128)(2,1)S(1)} %collective-permute-done.2.rest_2_), channel_id=1, source_target_pairs={{0,112},{16,0},{32,16},{48,32},{64,48},{80,64},{96,80},{112,96},{1... | collective-permute-start | bytes 417800 | tf_op jit(solution)/shard_map/ppermute | solution.py:360
  21.5 2.7 %collective-permute-start.6 = (bf16[272,256]{1,0:T(8,128)(2,1)S(1)}, bf16[272,256]{1,0:T(8,128)(2,1)S(1)}, u32[]{:S(2)}, u32[]{:S(2)}) collective-permute-start(bf16[272,256]{1,0:T(8,128)(2,1)S(1)} %collective-permute-done.4.rest_4_), channel_id=1, source_target_pairs={{0,112},{16,0},{32,16},{48,32},{64,48},{80,64},{96,80},{112,96},{1... | collective-permute-start | bytes 417800 | tf_op jit(solution)/shard_map/ppermute | solution.py:360
  24.8 2.2 %score.2 = (f32[8,256]{1,0:T(8,128)S(1)}, f32[8,256]{1,0:T(8,128)S(1)}, f32[1,256]{1,0:T(1,128)S(1)}, bf16[1024,1280]{1,0:T(8,128)(2,1)S(1)}) custom-call(bf16[512,256]{1,0:T(8,128)(2,1)S(1)} %get-tuple-element.51.near_emb, bf16[512,256]{1,0:T(8,128)(2,1)S(1)} %get-tuple-element.55.far_emb, f32[1024,128]{1,0:T(8,128)S(1)} %get-tuple-element.56.nid_ref, ...), custom_call_target="tpu_custom_call" | custom-call | flops 671088640 | bytes 5000000 | tf_op jit(solution)/shard_map/score/pallas_call | solution.py:198
  27.0 2.9 %collective-permute-done.7.rest_2_.rest_7_ = bf16[272,256]{1,0:T(8,128)(2,1)S(1)} collective-permute-done((bf16[272,256]{1,0:T(8,128)(2,1)S(1)}, bf16[272,256]{1,0:T(8,128)(2,1)S(1)}, u32[]{:S(2)}, u32[]{:S(2)}) %collective-permute-start.7) | collective-permute-done | bytes 139296 | tf_op jit(solution)/shard_map/ppermute | solution.py:360
  32.1 3.5 %collective-permute-start.9 = (f32[8,256]{1,0:T(8,128)S(1)}, f32[8,256]{1,0:T(8,128)S(1)}, u32[]{:S(2)}, u32[]{:S(2)}) collective-permute-start(f32[8,256]{1,0:T(8,128)S(1)} %get-tuple-element.67), channel_id=1, source_target_pairs={{0,96},{16,112},{32,64},{48,80},{64,32},{80,48},{96,0},{112,16},{1... | collective-permute-start | bytes 24584 | tf_op jit(solution)/shard_map/ppermute | solution.py:352
  36.8 4.1 %collective-permute-start.11 = (f32[8,256]{1,0:T(8,128)S(1)}, f32[8,256]{1,0:T(8,128)S(1)}, u32[]{:S(2)}, u32[]{:S(2)}) collective-permute-start(f32[8,256]{1,0:T(8,128)S(1)} %add_add_fusion), channel_id=1, source_target_pairs={{0,32},{16,48},{32,0},{48,16},{64,96},{80,112},{96,64},{112,80},{1... | collective-permute-start | bytes 24584 | tf_op jit(solution)/shard_map/ppermute | solution.py:352
  42.2 2.7 %grads.1 = (bf16[4,256,256]{2,1,0:T(8,128)(2,1)S(1)}, bf16[4,256,256]{2,1,0:T(8,128)(2,1)S(1)}, bf16[1280,256]{1,0:T(8,128)(2,1)S(1)}, f32[256,256]{1,0:T(8,128)S(1)}) custom-call(f32[8,256]{1,0:T(8,128)S(1)} %add.66.tot_ref, f32[8,256]{1,0:T(8,128)S(1)} %get-tuple-element.68.tloc_ref, f32[1,256]{1,0:T(1,128)S(1)} %get-tuple-element.69.pexp_ref, ...), custom_call_target="tpu_custom_call" | custom-call | flops 2147483648 | bytes 8000000 | tf_op jit(solution)/shard_map/grads/pallas_call | solution.py:252
  45.0 3.1 %backward.3 = bf16[4,4,128,256]{3,2,1,0:T(8,128)(2,1)S(1)} custom-call(bf16[1280,256]{1,0:T(8,128)(2,1)S(1)} %get-tuple-element.72.g_ref, bf16[768,256]{1,0:T(8,128)(2,1)S(1)} %get-tuple-element.73.feat_ref, bf16[528,256]{1,0:T(8,128)(2,1)S(1)} %collective-permute-done.far_ref, bf16[2048,256]{1,0:T(8,128)(2,1)S(1)} %get-tuple-element.54.w_out_ref, ...), custom_call_target="tpu_custom_call" | custom-call | flops 2013265920 | bytes 4000000 | tf_op jit(solution)/shard_map/backward/pallas_call | solution.py:141
  48.1 7.3 %collective-permute-start.12 = (bf16[4,4,128,256]{3,2,1,0:T(8,128)(2,1)S(1)}, bf16[4,4,128,256]{3,2,1,0:T(8,128)(2,1)S(1)}, u32[]{:S(2)}, u32[]{:S(2)}) collective-permute-start(bf16[4,4,128,256]{3,2,1,0:T(8,128)(2,1)S(1)} %backward.3), channel_id=1, source_target_pairs={{0,1},{1,0},{2,3},{3,2},{4,5},{5,4},{6,7},{7,6},{8,9},{9,8},{10,11... | collective-permute-start | bytes 3145736 | tf_op jit(solution)/shard_map/ppermute | solution.py:352
  58.0 2.1 %collective-permute-start.18 = (bf16[4,256,256]{2,1,0:T(8,128)(2,1)S(1)}, bf16[4,256,256]{2,1,0:T(8,128)(2,1)S(1)}, u32[]{:S(2)}, u32[]{:S(2)}) collective-permute-start(bf16[4,256,256]{2,1,0:T(8,128)(2,1)S(1)} %get-tuple-element.76), channel_id=1, source_target_pairs={{1,17},{3,19},{5,21},{7,23},{9,25},{11,27},{13,29},{15,31},{17,1},... | collective-permute-start | bytes 1572872 | tf_op jit(solution)/shard_map/ppermute | solution.py:370
  60.2 3.2 %backward.2 = bf16[4,4,128,256]{3,2,1,0:T(8,128)(2,1)S(1)} custom-call(bf16[1280,256]{1,0:T(8,128)(2,1)S(1)} %get-tuple-element.72.g_ref, bf16[768,256]{1,0:T(8,128)(2,1)S(1)} %get-tuple-element.73.feat_ref, bf16[528,256]{1,0:T(8,128)(2,1)S(1)} %collective-permute-done.far_ref, bf16[2048,256]{1,0:T(8,128)(2,1)S(1)} %get-tuple-element.54.w_out_ref, ...), custom_call_target="tpu_custom_call" | custom-call | flops 2013265920 | bytes 4000000 | tf_op jit(solution)/shard_map/backward/pallas_call | solution.py:141
  63.7 3.4 %collective-permute-start.19 = (bf16[4,256,256]{2,1,0:T(8,128)(2,1)S(1)}, bf16[4,256,256]{2,1,0:T(8,128)(2,1)S(1)}, u32[]{:S(2)}, u32[]{:S(2)}) collective-permute-start(bf16[4,256,256]{2,1,0:T(8,128)(2,1)S(1)} %collective-permute-done.14), channel_id=1, source_target_pairs={{1,17},{3,19},{5,21},{7,23},{9,25},{11,27},{13,29},{15,31},{17,1},... | collective-permute-start | bytes 1572872 | tf_op jit(solution)/shard_map/ppermute | solution.py:370
  68.6 2.6 %collective-permute-start.16 = (bf16[4,128,256]{2,1,0:T(8,128)(2,1)S(1)}, bf16[4,128,256]{2,1,0:T(8,128)(2,1)S(1)}, u32[]{:S(2)}, u32[]{:S(2)}) collective-permute-start(bf16[4,128,256]{2,1,0:T(8,128)(2,1)S(1)} %get-tuple-element.97), channel_id=1, source_target_pairs={{0,8},{1,5},{2,10},{3,7},{4,12},{5,1},{6,14},{7,3},{128,136},{129,... | collective-permute-start | bytes 786440 | tf_op jit(solution)/shard_map/ppermute | solution.py:387
  72.8 5.1 %collective-permute-done.16 = bf16[4,128,256]{2,1,0:T(8,128)(2,1)S(1)} collective-permute-done((bf16[4,128,256]{2,1,0:T(8,128)(2,1)S(1)}, bf16[4,128,256]{2,1,0:T(8,128)(2,1)S(1)}, u32[]{:S(2)}, u32[]{:S(2)}) %collective-permute-start.16) | collective-permute-done | bytes 262176 | tf_op jit(solution)/shard_map/ppermute | solution.py:387
  77.8 2.6 %collective-permute-done.17 = bf16[4,128,256]{2,1,0:T(8,128)(2,1)S(1)} collective-permute-done((bf16[4,128,256]{2,1,0:T(8,128)(2,1)S(1)}, bf16[4,128,256]{2,1,0:T(8,128)(2,1)S(1)}, u32[]{:S(2)}, u32[]{:S(2)}) %collective-permute-start.17) | collective-permute-done | bytes 262176 | tf_op jit(solution)/shard_map/ppermute | solution.py:387
  81.1 2.8 %collective-permute-start.21 = (bf16[128,256]{1,0:T(8,128)(2,1)S(1)}, bf16[128,256]{1,0:T(8,128)(2,1)S(1)}, u32[]{:S(2)}, u32[]{:S(2)}) collective-permute-start(bf16[128,256]{1,0:T(8,128)(2,1)S(1)} %get-tuple-element.110), channel_id=1, source_target_pairs={{0,4},{1,9},{2,6},{3,11},{4,0},{5,13},{6,2},{7,15},{128,132},{129,... | collective-permute-start | bytes 196616 | tf_op jit(solution)/shard_map/ppermute | solution.py:387
  86.2 2.0 %collective-permute-done.22 = bf16[128,256]{1,0:T(8,128)(2,1)S(1)} collective-permute-done((bf16[128,256]{1,0:T(8,128)(2,1)S(1)}, bf16[128,256]{1,0:T(8,128)(2,1)S(1)}, u32[]{:S(2)}, u32[]{:S(2)}) %collective-permute-start.22) | collective-permute-done | bytes 65568 | tf_op jit(solution)/shard_map/ppermute | solution.py:387
  88.3 3.1 %collective-permute-done.23 = bf16[128,256]{1,0:T(8,128)(2,1)S(1)} collective-permute-done((bf16[128,256]{1,0:T(8,128)(2,1)S(1)}, bf16[128,256]{1,0:T(8,128)(2,1)S(1)}, u32[]{:S(2)}, u32[]{:S(2)}) %collective-permute-start.23) | collective-permute-done | bytes 65568 | tf_op jit(solution)/shard_map/ppermute | solution.py:352
  91.4 2.7 %collective-permute-start.24 = (bf16[128,256]{1,0:T(8,128)(2,1)S(1)}, bf16[128,256]{1,0:T(8,128)(2,1)S(1)}, u32[]{:S(2)}, u32[]{:S(2)}) collective-permute-start(bf16[128,256]{1,0:T(8,128)(2,1)S(1)} %add_convert_fusion.4), channel_id=1, source_target_pairs={{0,32},{16,48},{32,0},{48,16},{64,96},{80,112},{96,64},{112,80},{1... | collective-permute-start | bytes 196616 | tf_op jit(solution)/shard_map/ppermute | solution.py:352
  95.3 2.2 %collective-permute-start.26 = (bf16[128,256]{1,0:T(8,128)(2,1)S(1)}, bf16[128,256]{1,0:T(8,128)(2,1)S(1)}, u32[]{:S(2)}, u32[]{:S(2)}) collective-permute-start(bf16[128,256]{1,0:T(8,128)(2,1)S(1)} %add_convert_fusion.4), channel_id=1, source_target_pairs={{0,96},{16,112},{32,64},{48,80},{64,32},{80,48},{96,0},{112,16},{1... | collective-permute-start | bytes 196616 | tf_op jit(solution)/shard_map/ppermute | solution.py:352
  97.5 4.2 %collective-permute-done.25 = bf16[128,256]{1,0:T(8,128)(2,1)S(1)} collective-permute-done((bf16[128,256]{1,0:T(8,128)(2,1)S(1)}, bf16[128,256]{1,0:T(8,128)(2,1)S(1)}, u32[]{:S(2)}, u32[]{:S(2)}) %collective-permute-start.25) | collective-permute-done | bytes 65568 | tf_op jit(solution)/shard_map/ppermute | solution.py:352
  102.5 4.8 %collective-permute-start.33 = (bf16[2,256,256]{2,1,0:T(8,128)(2,1)S(1)}, bf16[2,256,256]{2,1,0:T(8,128)(2,1)S(1)}, u32[]{:S(2)}, u32[]{:S(2)}) collective-permute-start(bf16[2,256,256]{2,1,0:T(8,128)(2,1)S(1)} %pad_maximum_fusion.2), channel_id=1, source_target_pairs={{1,65},{3,67},{5,69},{7,71},{9,73},{11,75},{13,77},{15,79},{17,81}... | collective-permute-start | bytes 786440 | tf_op jit(solution)/shard_map/ppermute | solution.py:370
  107.4 5.5 %collective-permute-start.34 = (bf16[2,256,256]{2,1,0:T(8,128)(2,1)S(1)}, bf16[2,256,256]{2,1,0:T(8,128)(2,1)S(1)}, u32[]{:S(2)}, u32[]{:S(2)}) collective-permute-start(bf16[2,256,256]{2,1,0:T(8,128)(2,1)S(1)} %pad_maximum_fusion.3), channel_id=1, source_target_pairs={{1,33},{3,35},{5,37},{7,39},{9,41},{11,43},{13,45},{15,47},{17,49}... | collective-permute-start | bytes 786440 | tf_op jit(solution)/shard_map/ppermute | solution.py:370
  112.9 2.7 %collective-permute-start.35 = (bf16[2,256,256]{2,1,0:T(8,128)(2,1)S(1)}, bf16[2,256,256]{2,1,0:T(8,128)(2,1)S(1)}, u32[]{:S(2)}, u32[]{:S(2)}) collective-permute-start(bf16[2,256,256]{2,1,0:T(8,128)(2,1)S(1)} %pad_maximum_fusion.4), channel_id=1, source_target_pairs={{1,97},{3,99},{5,101},{7,103},{9,105},{11,107},{13,109},{15,111},{... | collective-permute-start | bytes 786440 | tf_op jit(solution)/shard_map/ppermute | solution.py:370
  115.8 2.0 %collective-permute-start.28 = (bf16[128,256]{1,0:T(8,128)(2,1)S(1)}, bf16[128,256]{1,0:T(8,128)(2,1)S(1)}, u32[]{:S(2)}, u32[]{:S(2)}) collective-permute-start(bf16[128,256]{1,0:T(8,128)(2,1)S(1)} %add_convert_fusion.3), channel_id=1, source_target_pairs={{0,4},{1,9},{2,6},{3,11},{4,0},{5,13},{6,2},{7,15},{128,132},{129,... | collective-permute-start | bytes 196616 | tf_op jit(solution)/shard_map/ppermute | solution.py:387
  120.5 2.7 %collective-permute-done.29 = bf16[128,256]{1,0:T(8,128)(2,1)S(1)} collective-permute-done((bf16[128,256]{1,0:T(8,128)(2,1)S(1)}, bf16[128,256]{1,0:T(8,128)(2,1)S(1)}, u32[]{:S(2)}, u32[]{:S(2)}) %collective-permute-start.29) | collective-permute-done | bytes 65568 | tf_op jit(solution)/shard_map/ppermute | solution.py:387
  124.5 2.7 %collective-permute-start.32 = (bf16[4,128,256]{2,1,0:T(8,128)(2,1)S(1)}, bf16[4,128,256]{2,1,0:T(8,128)(2,1)S(1)}, u32[]{:S(2)}, u32[]{:S(2)}) collective-permute-start(bf16[4,128,256]{2,1,0:T(8,128)(2,1)S(1)} %get-tuple-element.107), channel_id=1, source_target_pairs={{0,136},{1,7},{2,138},{3,5},{4,140},{5,3},{6,142},{7,1},{128,8},{1... | collective-permute-start | bytes 786440 | tf_op jit(solution)/shard_map/ppermute | solution.py:387
  128.9 2.3 %collective-permute-done.31 = bf16[4,128,256]{2,1,0:T(8,128)(2,1)S(1)} collective-permute-done((bf16[4,128,256]{2,1,0:T(8,128)(2,1)S(1)}, bf16[4,128,256]{2,1,0:T(8,128)(2,1)S(1)}, u32[]{:S(2)}, u32[]{:S(2)}) %collective-permute-start.31) | collective-permute-done | bytes 262176 | tf_op jit(solution)/shard_map/ppermute | solution.py:387
  131.2 2.6 %collective-permute-done.32 = bf16[4,128,256]{2,1,0:T(8,128)(2,1)S(1)} collective-permute-done((bf16[4,128,256]{2,1,0:T(8,128)(2,1)S(1)}, bf16[4,128,256]{2,1,0:T(8,128)(2,1)S(1)}, u32[]{:S(2)}, u32[]{:S(2)}) %collective-permute-start.32) | collective-permute-done | bytes 262176 | tf_op jit(solution)/shard_map/ppermute | solution.py:387
  134.0 2.4 %collective-permute-start.36 = (bf16[256,256]{1,0:T(8,128)(2,1)S(1)}, bf16[256,256]{1,0:T(8,128)(2,1)S(1)}, u32[]{:S(2)}, u32[]{:S(2)}) collective-permute-start(bf16[256,256]{1,0:T(8,128)(2,1)S(1)} %fusion.4), channel_id=1, source_target_pairs={{1,0},{3,2},{5,4},{7,6},{9,8},{11,10},{13,12},{15,14},{17,16},{19,... | collective-permute-start | bytes 393224 | tf_op jit(solution)/shard_map/ppermute | solution.py:364
  (88 shorter events, 37.2 us)
Async XLA Ops:
  2.6 11.9 %collective-permute-start.1 = (bf16[272,256]{1,0:T(8,128)(2,1)}, bf16[272,256]{1,0:T(8,128)(2,1)S(1)}, u32[]{:S(2)}, u32[]{:S(2)}) collective-permute-start(bf16[272,256]{1,0:T(8,128)(2,1)} %get-tuple-element.59.rest_0_), channel_id=1, source_target_pairs={{0,16},{16,32},{32,48},{48,64},{64,80},{80,96},{96,112},{112,0},{1... | collective-permute-start | bytes 417800 | tf_op jit(solution)/shard_map/ppermute | solution.py:360
  5.1 14.6 %collective-permute-start = (bf16[528,256]{1,0:T(8,128)(2,1)}, bf16[528,256]{1,0:T(8,128)(2,1)S(1)}, u32[]{:S(2)}, u32[]{:S(2)}) collective-permute-start(bf16[528,256]{1,0:T(8,128)(2,1)} %get-tuple-element.49.near_ref), channel_id=1, source_target_pairs={{0,128},{128,0},{1,129},{129,1},{2,130},{130,2},{3,131},{131,3},{4... | collective-permute-start | bytes 811016 | tf_op jit(solution)/shard_map/ppermute | solution.py:352
  6.3 9.3 %collective-permute-start.2 = (bf16[272,256]{1,0:T(8,128)(2,1)}, bf16[272,256]{1,0:T(8,128)(2,1)S(1)}, u32[]{:S(2)}, u32[]{:S(2)}) collective-permute-start(bf16[272,256]{1,0:T(8,128)(2,1)} %get-tuple-element.59.rest_0_), channel_id=1, source_target_pairs={{0,112},{16,0},{32,16},{48,32},{64,48},{80,64},{96,80},{112,96},{1... | collective-permute-start | bytes 417800 | tf_op jit(solution)/shard_map/ppermute | solution.py:360
  14.5 5.2 %collective-permute-start.3 = (bf16[272,256]{1,0:T(8,128)(2,1)S(1)}, bf16[272,256]{1,0:T(8,128)(2,1)S(1)}, u32[]{:S(2)}, u32[]{:S(2)}) collective-permute-start(bf16[272,256]{1,0:T(8,128)(2,1)S(1)} %collective-permute-done.1.rest_1_), channel_id=1, source_target_pairs={{0,16},{16,32},{32,48},{48,64},{64,80},{80,96},{96,112},{112,0},{1... | collective-permute-start | bytes 417800 | tf_op jit(solution)/shard_map/ppermute | solution.py:360
  15.7 5.8 %collective-permute-start.4 = (bf16[272,256]{1,0:T(8,128)(2,1)S(1)}, bf16[272,256]{1,0:T(8,128)(2,1)S(1)}, u32[]{:S(2)}, u32[]{:S(2)}) collective-permute-start(bf16[272,256]{1,0:T(8,128)(2,1)S(1)} %collective-permute-done.2.rest_2_), channel_id=1, source_target_pairs={{0,112},{16,0},{32,16},{48,32},{64,48},{80,64},{96,80},{112,96},{1... | collective-permute-start | bytes 417800 | tf_op jit(solution)/shard_map/ppermute | solution.py:360
  19.7 5.1 %collective-permute-start.5 = (bf16[272,256]{1,0:T(8,128)(2,1)S(1)}, bf16[272,256]{1,0:T(8,128)(2,1)S(1)}, u32[]{:S(2)}, u32[]{:S(2)}) collective-permute-start(bf16[272,256]{1,0:T(8,128)(2,1)S(1)} %collective-permute-done.3.rest_3_), channel_id=1, source_target_pairs={{0,16},{16,32},{32,48},{48,64},{64,80},{80,96},{96,112},{112,0},{1... | collective-permute-start | bytes 417800 | tf_op jit(solution)/shard_map/ppermute | solution.py:360
  21.5 5.6 %collective-permute-start.6 = (bf16[272,256]{1,0:T(8,128)(2,1)S(1)}, bf16[272,256]{1,0:T(8,128)(2,1)S(1)}, u32[]{:S(2)}, u32[]{:S(2)}) collective-permute-start(bf16[272,256]{1,0:T(8,128)(2,1)S(1)} %collective-permute-done.4.rest_4_), channel_id=1, source_target_pairs={{0,112},{16,0},{32,16},{48,32},{64,48},{80,64},{96,80},{112,96},{1... | collective-permute-start | bytes 417800 | tf_op jit(solution)/shard_map/ppermute | solution.py:360
  24.8 5.1 %collective-permute-start.7 = (bf16[272,256]{1,0:T(8,128)(2,1)S(1)}, bf16[272,256]{1,0:T(8,128)(2,1)S(1)}, u32[]{:S(2)}, u32[]{:S(2)}) collective-permute-start(bf16[272,256]{1,0:T(8,128)(2,1)S(1)} %collective-permute-done.5.rest_0_.rest_5_), channel_id=1, source_target_pairs={{0,16},{16,32},{32,48},{48,64},{64,80},{80,96},{96,112},{112,0},{1... | collective-permute-start | bytes 417800 | tf_op jit(solution)/shard_map/ppermute | solution.py:360
  32.1 4.7 %collective-permute-start.9 = (f32[8,256]{1,0:T(8,128)S(1)}, f32[8,256]{1,0:T(8,128)S(1)}, u32[]{:S(2)}, u32[]{:S(2)}) collective-permute-start(f32[8,256]{1,0:T(8,128)S(1)} %get-tuple-element.67), channel_id=1, source_target_pairs={{0,96},{16,112},{32,64},{48,80},{64,32},{80,48},{96,0},{112,16},{1... | collective-permute-start | bytes 24584 | tf_op jit(solution)/shard_map/ppermute | solution.py:352
  36.8 5.4 %collective-permute-start.11 = (f32[8,256]{1,0:T(8,128)S(1)}, f32[8,256]{1,0:T(8,128)S(1)}, u32[]{:S(2)}, u32[]{:S(2)}) collective-permute-start(f32[8,256]{1,0:T(8,128)S(1)} %add_add_fusion), channel_id=1, source_target_pairs={{0,32},{16,48},{32,0},{48,16},{64,96},{80,112},{96,64},{112,80},{1... | collective-permute-start | bytes 24584 | tf_op jit(solution)/shard_map/ppermute | solution.py:352
  48.1 15.2 %collective-permute-start.12 = (bf16[4,4,128,256]{3,2,1,0:T(8,128)(2,1)S(1)}, bf16[4,4,128,256]{3,2,1,0:T(8,128)(2,1)S(1)}, u32[]{:S(2)}, u32[]{:S(2)}) collective-permute-start(bf16[4,4,128,256]{3,2,1,0:T(8,128)(2,1)S(1)} %backward.3), channel_id=1, source_target_pairs={{0,1},{1,0},{2,3},{3,2},{4,5},{5,4},{6,7},{7,6},{8,9},{9,8},{10,11... | collective-permute-start | bytes 3145736 | tf_op jit(solution)/shard_map/ppermute | solution.py:352
  55.5 8.3 %collective-permute-start.13 = (bf16[4,256,256]{2,1,0:T(8,128)(2,1)S(1)}, bf16[4,256,256]{2,1,0:T(8,128)(2,1)S(1)}, u32[]{:S(2)}, u32[]{:S(2)}) collective-permute-start(bf16[4,256,256]{2,1,0:T(8,128)(2,1)S(1)} %get-tuple-element.75), channel_id=1, source_target_pairs={{0,1},{2,3},{4,5},{6,7},{8,9},{10,11},{12,13},{14,15},{16,17},{18,... | collective-permute-start | bytes 1572872 | tf_op jit(solution)/shard_map/ppermute | solution.py:364
  56.7 7.0 %collective-permute-start.14 = (bf16[4,256,256]{2,1,0:T(8,128)(2,1)S(1)}, bf16[4,256,256]{2,1,0:T(8,128)(2,1)S(1)}, u32[]{:S(2)}, u32[]{:S(2)}) collective-permute-start(bf16[4,256,256]{2,1,0:T(8,128)(2,1)S(1)} %get-tuple-element.76), channel_id=1, source_target_pairs={{0,1},{2,3},{4,5},{6,7},{8,9},{10,11},{12,13},{14,15},{16,17},{18,... | collective-permute-start | bytes 1572872 | tf_op jit(solution)/shard_map/ppermute | solution.py:364
  58.0 13.1 %collective-permute-start.18 = (bf16[4,256,256]{2,1,0:T(8,128)(2,1)S(1)}, bf16[4,256,256]{2,1,0:T(8,128)(2,1)S(1)}, u32[]{:S(2)}, u32[]{:S(2)}) collective-permute-start(bf16[4,256,256]{2,1,0:T(8,128)(2,1)S(1)} %get-tuple-element.76), channel_id=1, source_target_pairs={{1,17},{3,19},{5,21},{7,23},{9,25},{11,27},{13,29},{15,31},{17,1},... | collective-permute-start | bytes 1572872 | tf_op jit(solution)/shard_map/ppermute | solution.py:370
  63.7 16.8 %collective-permute-start.19 = (bf16[4,256,256]{2,1,0:T(8,128)(2,1)S(1)}, bf16[4,256,256]{2,1,0:T(8,128)(2,1)S(1)}, u32[]{:S(2)}, u32[]{:S(2)}) collective-permute-start(bf16[4,256,256]{2,1,0:T(8,128)(2,1)S(1)} %collective-permute-done.14), channel_id=1, source_target_pairs={{1,17},{3,19},{5,21},{7,23},{9,25},{11,27},{13,29},{15,31},{17,1},... | collective-permute-start | bytes 1572872 | tf_op jit(solution)/shard_map/ppermute | solution.py:370
  67.2 5.6 %collective-permute-start.15 = (bf16[4,128,256]{2,1,0:T(8,128)(2,1)S(1)}, bf16[4,128,256]{2,1,0:T(8,128)(2,1)S(1)}, u32[]{:S(2)}, u32[]{:S(2)}) collective-permute-start(bf16[4,128,256]{2,1,0:T(8,128)(2,1)S(1)} %get-tuple-element.95), channel_id=1, source_target_pairs={{0,128},{1,3},{2,130},{3,1},{4,132},{5,7},{6,134},{7,5},{128,0},{1... | collective-permute-start | bytes 786440 | tf_op jit(solution)/shard_map/ppermute | solution.py:387
  68.6 9.3 %collective-permute-start.16 = (bf16[4,128,256]{2,1,0:T(8,128)(2,1)S(1)}, bf16[4,128,256]{2,1,0:T(8,128)(2,1)S(1)}, u32[]{:S(2)}, u32[]{:S(2)}) collective-permute-start(bf16[4,128,256]{2,1,0:T(8,128)(2,1)S(1)} %get-tuple-element.97), channel_id=1, source_target_pairs={{0,8},{1,5},{2,10},{3,7},{4,12},{5,1},{6,14},{7,3},{128,136},{129,... | collective-permute-start | bytes 786440 | tf_op jit(solution)/shard_map/ppermute | solution.py:387
  71.2 9.2 %collective-permute-start.17 = (bf16[4,128,256]{2,1,0:T(8,128)(2,1)S(1)}, bf16[4,128,256]{2,1,0:T(8,128)(2,1)S(1)}, u32[]{:S(2)}, u32[]{:S(2)}) collective-permute-start(bf16[4,128,256]{2,1,0:T(8,128)(2,1)S(1)} %get-tuple-element.96), channel_id=1, source_target_pairs={{0,136},{1,7},{2,138},{3,5},{4,140},{5,3},{6,142},{7,1},{128,8},{1... | collective-permute-start | bytes 786440 | tf_op jit(solution)/shard_map/ppermute | solution.py:387
  81.1 5.1 %collective-permute-start.21 = (bf16[128,256]{1,0:T(8,128)(2,1)S(1)}, bf16[128,256]{1,0:T(8,128)(2,1)S(1)}, u32[]{:S(2)}, u32[]{:S(2)}) collective-permute-start(bf16[128,256]{1,0:T(8,128)(2,1)S(1)} %get-tuple-element.110), channel_id=1, source_target_pairs={{0,4},{1,9},{2,6},{3,11},{4,0},{5,13},{6,2},{7,15},{128,132},{129,... | collective-permute-start | bytes 196616 | tf_op jit(solution)/shard_map/ppermute | solution.py:387
  83.8 4.3 %collective-permute-start.22 = (bf16[128,256]{1,0:T(8,128)(2,1)S(1)}, bf16[128,256]{1,0:T(8,128)(2,1)S(1)}, u32[]{:S(2)}, u32[]{:S(2)}) collective-permute-start(bf16[128,256]{1,0:T(8,128)(2,1)S(1)} %get-tuple-element.109), channel_id=1, source_target_pairs={{0,6},{1,137},{2,4},{3,139},{4,2},{5,141},{6,0},{7,143},{128,134},... | collective-permute-start | bytes 196616 | tf_op jit(solution)/shard_map/ppermute | solution.py:387
  91.4 6.1 %collective-permute-start.24 = (bf16[128,256]{1,0:T(8,128)(2,1)S(1)}, bf16[128,256]{1,0:T(8,128)(2,1)S(1)}, u32[]{:S(2)}, u32[]{:S(2)}) collective-permute-start(bf16[128,256]{1,0:T(8,128)(2,1)S(1)} %add_convert_fusion.4), channel_id=1, source_target_pairs={{0,32},{16,48},{32,0},{48,16},{64,96},{80,112},{96,64},{112,80},{1... | collective-permute-start | bytes 196616 | tf_op jit(solution)/shard_map/ppermute | solution.py:352
  94.2 7.6 %collective-permute-start.25 = (bf16[128,256]{1,0:T(8,128)(2,1)S(1)}, bf16[128,256]{1,0:T(8,128)(2,1)S(1)}, u32[]{:S(2)}, u32[]{:S(2)}) collective-permute-start(bf16[128,256]{1,0:T(8,128)(2,1)S(1)} %add_convert_fusion.4), channel_id=1, source_target_pairs={{0,64},{16,80},{32,96},{48,112},{64,0},{80,16},{96,32},{112,48},{1... | collective-permute-start | bytes 196616 | tf_op jit(solution)/shard_map/ppermute | solution.py:352
  95.3 7.0 %collective-permute-start.26 = (bf16[128,256]{1,0:T(8,128)(2,1)S(1)}, bf16[128,256]{1,0:T(8,128)(2,1)S(1)}, u32[]{:S(2)}, u32[]{:S(2)}) collective-permute-start(bf16[128,256]{1,0:T(8,128)(2,1)S(1)} %add_convert_fusion.4), channel_id=1, source_target_pairs={{0,96},{16,112},{32,64},{48,80},{64,32},{80,48},{96,0},{112,16},{1... | collective-permute-start | bytes 196616 | tf_op jit(solution)/shard_map/ppermute | solution.py:352
  102.5 22.0 %collective-permute-start.33 = (bf16[2,256,256]{2,1,0:T(8,128)(2,1)S(1)}, bf16[2,256,256]{2,1,0:T(8,128)(2,1)S(1)}, u32[]{:S(2)}, u32[]{:S(2)}) collective-permute-start(bf16[2,256,256]{2,1,0:T(8,128)(2,1)S(1)} %pad_maximum_fusion.2), channel_id=1, source_target_pairs={{1,65},{3,67},{5,69},{7,71},{9,73},{11,75},{13,77},{15,79},{17,81}... | collective-permute-start | bytes 786440 | tf_op jit(solution)/shard_map/ppermute | solution.py:370
  107.4 19.9 %collective-permute-start.34 = (bf16[2,256,256]{2,1,0:T(8,128)(2,1)S(1)}, bf16[2,256,256]{2,1,0:T(8,128)(2,1)S(1)}, u32[]{:S(2)}, u32[]{:S(2)}) collective-permute-start(bf16[2,256,256]{2,1,0:T(8,128)(2,1)S(1)} %pad_maximum_fusion.3), channel_id=1, source_target_pairs={{1,33},{3,35},{5,37},{7,39},{9,41},{11,43},{13,45},{15,47},{17,49}... | collective-permute-start | bytes 786440 | tf_op jit(solution)/shard_map/ppermute | solution.py:370
  112.9 14.3 %collective-permute-start.35 = (bf16[2,256,256]{2,1,0:T(8,128)(2,1)S(1)}, bf16[2,256,256]{2,1,0:T(8,128)(2,1)S(1)}, u32[]{:S(2)}, u32[]{:S(2)}) collective-permute-start(bf16[2,256,256]{2,1,0:T(8,128)(2,1)S(1)} %pad_maximum_fusion.4), channel_id=1, source_target_pairs={{1,97},{3,99},{5,101},{7,103},{9,105},{11,107},{13,109},{15,111},{... | collective-permute-start | bytes 786440 | tf_op jit(solution)/shard_map/ppermute | solution.py:370
  115.8 4.7 %collective-permute-start.28 = (bf16[128,256]{1,0:T(8,128)(2,1)S(1)}, bf16[128,256]{1,0:T(8,128)(2,1)S(1)}, u32[]{:S(2)}, u32[]{:S(2)}) collective-permute-start(bf16[128,256]{1,0:T(8,128)(2,1)S(1)} %add_convert_fusion.3), channel_id=1, source_target_pairs={{0,4},{1,9},{2,6},{3,11},{4,0},{5,13},{6,2},{7,15},{128,132},{129,... | collective-permute-start | bytes 196616 | tf_op jit(solution)/shard_map/ppermute | solution.py:387
  118.9 4.3 %collective-permute-start.29 = (bf16[128,256]{1,0:T(8,128)(2,1)S(1)}, bf16[128,256]{1,0:T(8,128)(2,1)S(1)}, u32[]{:S(2)}, u32[]{:S(2)}) collective-permute-start(bf16[128,256]{1,0:T(8,128)(2,1)S(1)} %add_convert_fusion.3), channel_id=1, source_target_pairs={{0,6},{1,137},{2,4},{3,139},{4,2},{5,141},{6,0},{7,143},{128,134},... | collective-permute-start | bytes 196616 | tf_op jit(solution)/shard_map/ppermute | solution.py:387
  123.3 5.6 %collective-permute-start.30 = (bf16[4,128,256]{2,1,0:T(8,128)(2,1)S(1)}, bf16[4,128,256]{2,1,0:T(8,128)(2,1)S(1)}, u32[]{:S(2)}, u32[]{:S(2)}) collective-permute-start(bf16[4,128,256]{2,1,0:T(8,128)(2,1)S(1)} %get-tuple-element.107), channel_id=1, source_target_pairs={{0,128},{1,3},{2,130},{3,1},{4,132},{5,7},{6,134},{7,5},{128,0},{1... | collective-permute-start | bytes 786440 | tf_op jit(solution)/shard_map/ppermute | solution.py:387
  123.4 7.8 %collective-permute-start.31 = (bf16[4,128,256]{2,1,0:T(8,128)(2,1)S(1)}, bf16[4,128,256]{2,1,0:T(8,128)(2,1)S(1)}, u32[]{:S(2)}, u32[]{:S(2)}) collective-permute-start(bf16[4,128,256]{2,1,0:T(8,128)(2,1)S(1)} %get-tuple-element.107), channel_id=1, source_target_pairs={{0,8},{1,5},{2,10},{3,7},{4,12},{5,1},{6,14},{7,3},{128,136},{129,... | collective-permute-start | bytes 786440 | tf_op jit(solution)/shard_map/ppermute | solution.py:387
  124.5 9.3 %collective-permute-start.32 = (bf16[4,128,256]{2,1,0:T(8,128)(2,1)S(1)}, bf16[4,128,256]{2,1,0:T(8,128)(2,1)S(1)}, u32[]{:S(2)}, u32[]{:S(2)}) collective-permute-start(bf16[4,128,256]{2,1,0:T(8,128)(2,1)S(1)} %get-tuple-element.107), channel_id=1, source_target_pairs={{0,136},{1,7},{2,138},{3,5},{4,140},{5,3},{6,142},{7,1},{128,8},{1... | collective-permute-start | bytes 786440 | tf_op jit(solution)/shard_map/ppermute | solution.py:387
  133.9 4.7 %collective-permute-start.37 = (bf16[4,4,128,256]{3,2,1,0:T(8,128)(2,1)S(1)}, bf16[4,4,128,256]{3,2,1,0:T(8,128)(2,1)S(1)}, u32[]{:S(2)}, u32[]{:S(2)}) collective-permute-start(bf16[4,4,128,256]{3,2,1,0:T(8,128)(2,1)S(1)} %pad_maximum_fusion.x_ref), channel_id=1, source_target_pairs={{0,1},{1,0},{2,3},{3,2},{4,5},{5,4},{6,7},{7,6},{8,9},{9,8},{10,11... | collective-permute-start | bytes 3145736 | tf_op jit(solution)/shard_map/ppermute | solution.py:352
  (12 other events, 53.3 us)

commit v7 on v5

--- a/solution.py
+++ b/solution.py
@@ -19,7 +19,7 @@
 CHUNKS = H // TILE
 NZ = 8
 OFFSETS = (0, -1, 1, -2, 2, -3, 3, 4)
-FIRST = 5
+FIRST = 7
 VMEM_LIMIT = 24 * 1024 * 1024
 
 WIDE = 512
@@ -91,7 +91,7 @@
             pltpu.SemaphoreType.DMA((5,)),
         ],
         compiler_params=params(60 * 1024 * 1024),
-        cost_estimate=cost(0, 1e6),
+        cost_estimate=cost(1e10, 1e6),
         name="pack",
     )(user_emb, pos_id.reshape(1, U), neg_feat, neg_id.reshape(1, N), neg_bucket.reshape(1, N))
 
@@ -100,12 +100,11 @@
     return jnp.maximum(mm(feat, w_in_ref[...]), 0.0).astype(BF)
 
 
-def hidden_kernel(near_ref, pos_ref, w_in_ref, hid_ref, feat_ref, tail_ref, w_in_out):
+def hidden_kernel(near_ref, pos_ref, w_in_ref, hid_ref, feat_ref, w_in_out):
     for m, feat in enumerate((near_ref[0:TILE], near_ref[TILE:N], pos_ref[...])):
         rows = slice(m * TILE, (m + 1) * TILE)
         feat_ref[rows] = feat
         hid_ref[rows] = hidden(feat, w_in_ref)
-    tail_ref[...] = near_ref[N : N + 16]
     w_in_out[...] = w_in_ref[...]
 
 
@@ -116,9 +115,9 @@
         ref[first : first + TILE] = mm(hid, w_out_ref[...]).astype(BF)
 
 
-def far_kernel(near_tail, far_ref, w_in_ref, w_out_ref, table_ref, hid_ref, emb_ref, nid_ref, bias_ref):
+def far_kernel(near_ref, far_ref, w_in_ref, w_out_ref, table_ref, hid_ref, emb_ref, nid_ref, bias_ref):
     lane = lax.broadcasted_iota(I32, (TILE, 128), 1).astype(F32)
-    for side, tail in enumerate((near_tail[...], far_ref[N : N + 16])):
+    for side, tail in enumerate((near_ref[N : N + 16], far_ref[N : N + 16])):
         tail = jnp.concatenate([tail.astype(F32), jnp.zeros((112, E), F32)], axis=0).T
         for block in range(2):
             rows = slice((2 * side + block) * TILE, (2 * side + block + 1) * TILE)
@@ -397,14 +396,18 @@
     keep = add(keep, swap(send, "z", 1)).astype(BF)
     quarter, keep = lax.optimization_barrier((quarter, keep))
     part = add(quarter[0], *[plane_swap(quarter[k], k, 1) for k in (1, 2, 3)])
+    user_2 = swap(keep[2], "z", 2)
+    part, user_2 = lax.optimization_barrier((part, user_2))
     part = sum_over_z(part, ((1,), (2, 4, 6)), BF).astype(BF)
     part, keep = lax.optimization_barrier((part, keep))
     quarter = jnp.stack([part] + [plane_swap(part, k, 1) for k in (1, 2, 3)])
-    user = add(keep[0], *[swap(keep[i], "z", k) for i, k in ((1, 4), (2, 2), (3, 6))])
+    user_6 = swap(keep[3], "z", 6)
+    quarter, user_6, keep = lax.optimization_barrier((quarter, user_6, keep))
     others = [plane_swap(quarter, k, 0) for k in (1, 2, 3)]
-    others, user = lax.optimization_barrier((others, user))
+    user_4 = swap(keep[1], "z", 4)
+    others, user_4 = lax.optimization_barrier((others, user_4))
     half = jnp.stack([quarter] + others)
-    return half, swap(half, "core", 1), user
+    return half, swap(half, "core", 1), add(keep[0], user_2, user_4, user_6)
 
 
 def on_device(user_emb, pos_feat, pos_id, neg_feat, neg_id, neg_bucket, logq_table, w_in, w_out):
@@ -412,12 +415,12 @@
     up, down = shift(mine, 1), shift(mine, -1)
     far = swap(near, "x_lo", 1)
     users = [mine, up, down]
-    hid, feat, tail, w_in = in_vmem(
+    hid, feat, w_in = in_vmem(
         hidden_kernel,
         "hidden",
         2 * (N + U) * E * H,
-        [((N + U, H), BF), ((N + U, E), BF), ((16, E), BF), ((E, H), BF)],
-        near,
+        [((N + U, H), BF), ((N + U, E), BF), ((E, H), BF)],
+        neg_feat,
         pos_feat,
         w_in,
     )
@@ -433,7 +436,7 @@
         "far",
         4 * N * E * H,
         [((N, H), BF), ((N, E), BF), ((NN, 128), F32), ((NN, 128), F32)],
-        tail,
+        near,
         far,
         w_in,
         w_out,

time: 124 us -> 125 us (level)
  starting transfers between devices: 64.5 us -> 67.6 us
  local copies, waits for them, and re-layouts: 3.19 us -> 0.13 us
    ppermute x15, waiting for transfers between devices: 16.3 us -> 23.9 us  [swap(): lax.ppermute(x, axis, [(i, i ^ k) for i in range(SIZES[AXES.index(axis)])])]
    ppermute x12, waiting for transfers between devices: 11 us -> 3.54 us  [plane_swap(): return lax.ppermute(x, AXES, pairs)]
    ppermute x15, starting transfers between devices: 38.3 us -> 41.5 us  [swap(): lax.ppermute(x, axis, [(i, i ^ k) for i in range(SIZES[AXES.index(axis)])])]
    unnamed x12 -> x14, local copies, waits for them, and re-layouts: 3.1 us -> 0.03 us
  transfers between devices with their start and end apart: 34 -> 34, of which waited for: 19 -> 17; matrix products, arithmetic and copies ran while one was open for 1% -> 1% of each run, Pallas kernels for 8% -> 9%
where the time goes in v7:
time: 125 us
  starting transfers between devices  67.6 us (54%)
  waiting for transfers between devices  32.9 us (26%)
  Pallas kernels  21.5 us (17%)
  other arithmetic  1.7 us (1%)
    ppermute x15, starting transfers between devices, swap(): lax.ppermute(x, axis, [(i, i ^ k) for i in range(SIZES[AXES.index(axis)])])  41.5 us
    ppermute x15, waiting for transfers between devices, swap(): lax.ppermute(x, axis, [(i, i ^ k) for i in range(SIZES[AXES.index(axis)])])  23.9 us
    ppermute x12, starting transfers between devices, plane_swap(): return lax.ppermute(x, AXES, pairs)  14.1 us
    ppermute x7, starting transfers between devices, shift(): return lax.ppermute(x, 'z', [(i, (i + by) % NZ) for i in range(NZ)])  11.9 us
    pallas_call x5, Pallas kernels, in_vmem(): pl.pallas_call(kernel, in_specs=[vm] * len(args), out_specs=[vm] * len(ou...  10 us
    ppermute x7, waiting for transfers between devices, shift(): return lax.ppermute(x, 'z', [(i, (i + by) % NZ) for i in range(NZ)])  5.46 us
    pallas_call x2, Pallas kernels, score(): pl.pallas_call(functools.partial(score_kernel, ks), in_specs=[vm] * (7 +...  4.06 us
    ppermute x12, waiting for transfers between devices, plane_swap(): return lax.ppermute(x, AXES, pairs)  3.54 us
  transfers between devices with their start and end apart: 34, of which 17 were waited for; matrix products, arithmetic and copies ran while one was open for 1% of the time, Pallas kernels for 9%

profile of v7, /device:TPU:1, one launch (start us, length us, event | category | flops | bytes accessed | tf_op | source)
XLA Modules:
  0.0 124.9 jit_solution(11580790024460089276)
XLA Ops:
  0.7 2.0 %pack.1 = (bf16[272,256]{1,0:T(8,128)(2,1)}, bf16[528,256]{1,0:T(8,128)(2,1)}) custom-call(bf16[256,256]{1,0:T(8,128)(2,1)} %user_hbm.1, s32[1,256]{1,0:T(1,128)} %bitcast.52, bf16[512,256]{1,0:T(8,128)(2,1)} %feat_hbm.1, s32[1,512]{1,0:T(1,128)} %bitcast.50, s32[1,512]{1,0:T(1,128)} %bitcast.51), custom_call_target="tpu_custom_call" | custom-call | flops 10000000000 | bytes 1000000 | tf_op jit(solution)/shard_map/pack/pallas_call | solution.py:82
  2.6 2.5 %collective-permute-start.1 = (bf16[272,256]{1,0:T(8,128)(2,1)}, bf16[272,256]{1,0:T(8,128)(2,1)S(1)}, u32[]{:S(2)}, u32[]{:S(2)}) collective-permute-start(bf16[272,256]{1,0:T(8,128)(2,1)} %get-tuple-element.57.rest_0_), channel_id=1, source_target_pairs={{0,16},{16,32},{32,48},{48,64},{64,80},{80,96},{96,112},{112,0},{1... | collective-permute-start | bytes 417800 | tf_op jit(solution)/shard_map/ppermute | solution.py:359
  5.2 4.0 %collective-permute-start.2 = (bf16[272,256]{1,0:T(8,128)(2,1)}, bf16[272,256]{1,0:T(8,128)(2,1)S(1)}, u32[]{:S(2)}, u32[]{:S(2)}) collective-permute-start(bf16[272,256]{1,0:T(8,128)(2,1)} %get-tuple-element.57.rest_0_), channel_id=1, source_target_pairs={{0,112},{16,0},{32,16},{48,32},{64,48},{80,64},{96,80},{112,96},{1... | collective-permute-start | bytes 417800 | tf_op jit(solution)/shard_map/ppermute | solution.py:359
  12.7 2.7 %collective-permute-start.4 = (bf16[272,256]{1,0:T(8,128)(2,1)S(1)}, bf16[272,256]{1,0:T(8,128)(2,1)S(1)}, u32[]{:S(2)}, u32[]{:S(2)}) collective-permute-start(bf16[272,256]{1,0:T(8,128)(2,1)S(1)} %collective-permute-done.2.rest_2_), channel_id=1, source_target_pairs={{0,112},{16,0},{32,16},{48,32},{64,48},{80,64},{96,80},{112,96},{1... | collective-permute-start | bytes 417800 | tf_op jit(solution)/shard_map/ppermute | solution.py:359
  17.9 2.7 %collective-permute-start.6 = (bf16[272,256]{1,0:T(8,128)(2,1)S(1)}, bf16[272,256]{1,0:T(8,128)(2,1)S(1)}, u32[]{:S(2)}, u32[]{:S(2)}) collective-permute-start(bf16[272,256]{1,0:T(8,128)(2,1)S(1)} %collective-permute-done.4.rest_4_), channel_id=1, source_target_pairs={{0,112},{16,0},{32,16},{48,32},{64,48},{80,64},{96,80},{112,96},{1... | collective-permute-start | bytes 417800 | tf_op jit(solution)/shard_map/ppermute | solution.py:359
  20.5 1.7 %far.1 = (bf16[512,2048]{1,0:T(8,128)(2,1)S(1)}, bf16[512,256]{1,0:T(8,128)(2,1)S(1)}, f32[1024,128]{1,0:T(8,128)S(1)}, f32[1024,128]{1,0:T(8,128)S(1)}) custom-call(bf16[528,256]{1,0:T(8,128)(2,1)S(1)} %copy-done.2, bf16[528,256]{1,0:T(8,128)(2,1)S(1)} %collective-permute-done.far_ref, bf16[256,2048]{1,0:T(8,128)(2,1)S(1)} %get-tuple-element.51.w_in_ref, ...), custom_call_target="tpu_custom_call" | custom-call | flops 1073741824 | bytes 4000000 | tf_op jit(solution)/shard_map/far/pallas_call | solution.py:140
  23.0 3.0 %score.2 = (f32[8,256]{1,0:T(8,128)S(1)}, f32[8,256]{1,0:T(8,128)S(1)}, f32[1,256]{1,0:T(1,128)S(1)}, bf16[1024,1792]{1,0:T(8,128)(2,1)S(1)}) custom-call(bf16[512,256]{1,0:T(8,128)(2,1)S(1)} %get-tuple-element.49.near_emb, bf16[512,256]{1,0:T(8,128)(2,1)S(1)} %get-tuple-element.53.far_emb, f32[1024,128]{1,0:T(8,128)S(1)} %get-tuple-element.54.nid_ref, ...), custom_call_target="tpu_custom_call" | custom-call | flops 939524096 | bytes 5000000 | tf_op jit(solution)/shard_map/score/pallas_call | solution.py:197
  26.0 2.1 %collective-permute-done.7.rest_0_.rest_7_ = bf16[272,256]{1,0:T(8,128)(2,1)S(1)} collective-permute-done((bf16[272,256]{1,0:T(8,128)(2,1)S(1)}, bf16[272,256]{1,0:T(8,128)(2,1)S(1)}, u32[]{:S(2)}, u32[]{:S(2)}) %collective-permute-start.7) | collective-permute-done | bytes 139296 | tf_op jit(solution)/shard_map/ppermute | solution.py:359
  31.2 1.8 %collective-permute-start.8 = (f32[8,256]{1,0:T(8,128)S(1)}, f32[8,256]{1,0:T(8,128)S(1)}, u32[]{:S(2)}, u32[]{:S(2)}) collective-permute-start(f32[8,256]{1,0:T(8,128)S(1)} %get-tuple-element.65), channel_id=1, source_target_pairs={{0,16},{16,0},{32,48},{48,32},{64,80},{80,64},{96,112},{112,96},{1... | collective-permute-start | bytes 24584 | tf_op jit(solution)/shard_map/ppermute | solution.py:351
  34.4 2.0 %collective-permute-start.11 = (f32[8,256]{1,0:T(8,128)S(1)}, f32[8,256]{1,0:T(8,128)S(1)}, u32[]{:S(2)}, u32[]{:S(2)}) collective-permute-start(f32[8,256]{1,0:T(8,128)S(1)} %add_add_fusion), channel_id=1, source_target_pairs={{0,32},{16,48},{32,0},{48,16},{64,96},{80,112},{96,64},{112,80},{1... | collective-permute-start | bytes 24584 | tf_op jit(solution)/shard_map/ppermute | solution.py:351
  36.4 1.7 %collective-permute-done.11 = f32[8,256]{1,0:T(8,128)S(1)} collective-permute-done((f32[8,256]{1,0:T(8,128)S(1)}, f32[8,256]{1,0:T(8,128)S(1)}, u32[]{:S(2)}, u32[]{:S(2)}) %collective-permute-start.11) | collective-permute-done | bytes 8224 | tf_op jit(solution)/shard_map/ppermute | solution.py:351
  38.1 2.7 %grads.1 = (bf16[4,256,256]{2,1,0:T(8,128)(2,1)S(1)}, bf16[4,256,256]{2,1,0:T(8,128)(2,1)S(1)}, bf16[1280,256]{1,0:T(8,128)(2,1)S(1)}, f32[256,256]{1,0:T(8,128)S(1)}) custom-call(f32[8,256]{1,0:T(8,128)S(1)} %add.63.tot_ref, f32[8,256]{1,0:T(8,128)S(1)} %get-tuple-element.66.tloc_ref, f32[1,256]{1,0:T(1,128)S(1)} %get-tuple-element.67.pexp_ref, ...), custom_call_target="tpu_custom_call" | custom-call | flops 2147483648 | bytes 8000000 | tf_op jit(solution)/shard_map/grads/pallas_call | solution.py:251
  40.9 3.2 %backward.3 = bf16[4,4,128,256]{3,2,1,0:T(8,128)(2,1)S(1)} custom-call(bf16[1280,256]{1,0:T(8,128)(2,1)S(1)} %get-tuple-element.70.g_ref, bf16[768,256]{1,0:T(8,128)(2,1)S(1)} %get-tuple-element.71.feat_ref, bf16[528,256]{1,0:T(8,128)(2,1)S(1)} %collective-permute-done.far_ref, bf16[2048,256]{1,0:T(8,128)(2,1)S(1)} %get-tuple-element.52.w_out_ref, ...), custom_call_target="tpu_custom_call" | custom-call | flops 2013265920 | bytes 4000000 | tf_op jit(solution)/shard_map/backward/pallas_call | solution.py:140
  44.0 6.7 %collective-permute-start.12 = (bf16[4,4,128,256]{3,2,1,0:T(8,128)(2,1)S(1)}, bf16[4,4,128,256]{3,2,1,0:T(8,128)(2,1)S(1)}, u32[]{:S(2)}, u32[]{:S(2)}) collective-permute-start(bf16[4,4,128,256]{3,2,1,0:T(8,128)(2,1)S(1)} %backward.3), channel_id=1, source_target_pairs={{0,1},{1,0},{2,3},{3,2},{4,5},{5,4},{6,7},{7,6},{8,9},{9,8},{10,11... | collective-permute-start | bytes 3145736 | tf_op jit(solution)/shard_map/ppermute | solution.py:351
  50.8 1.7 %collective-permute-start.16 = (bf16[4,256,256]{2,1,0:T(8,128)(2,1)S(1)}, bf16[4,256,256]{2,1,0:T(8,128)(2,1)S(1)}, u32[]{:S(2)}, u32[]{:S(2)}) collective-permute-start(bf16[4,256,256]{2,1,0:T(8,128)(2,1)S(1)} %get-tuple-element.74), channel_id=1, source_target_pairs={{0,16},{16,0},{32,48},{48,32},{64,80},{80,64},{96,112},{112,96},{1... | collective-permute-start | bytes 1572872 | tf_op jit(solution)/shard_map/ppermute | solution.py:351
  52.5 3.1 %backward.2 = bf16[4,4,128,256]{3,2,1,0:T(8,128)(2,1)S(1)} custom-call(bf16[1280,256]{1,0:T(8,128)(2,1)S(1)} %get-tuple-element.70.g_ref, bf16[768,256]{1,0:T(8,128)(2,1)S(1)} %get-tuple-element.71.feat_ref, bf16[528,256]{1,0:T(8,128)(2,1)S(1)} %collective-permute-done.far_ref, bf16[2048,256]{1,0:T(8,128)(2,1)S(1)} %get-tuple-element.52.w_out_ref, ...), custom_call_target="tpu_custom_call" | custom-call | flops 2013265920 | bytes 4000000 | tf_op jit(solution)/shard_map/backward/pallas_call | solution.py:140
  57.5 1.9 %collective-permute-start.15 = (bf16[4,128,256]{2,1,0:T(8,128)(2,1)S(1)}, bf16[4,128,256]{2,1,0:T(8,128)(2,1)S(1)}, u32[]{:S(2)}, u32[]{:S(2)}) collective-permute-start(bf16[4,128,256]{2,1,0:T(8,128)(2,1)S(1)} %get-tuple-element.94), channel_id=1, source_target_pairs={{0,136},{1,7},{2,138},{3,5},{4,140},{5,3},{6,142},{7,1},{128,8},{1... | collective-permute-start | bytes 786440 | tf_op jit(solution)/shard_map/ppermute | solution.py:376
  60.1 4.5 %collective-permute-done.16 = bf16[4,256,256]{2,1,0:T(8,128)(2,1)S(1)} collective-permute-done((bf16[4,256,256]{2,1,0:T(8,128)(2,1)S(1)}, bf16[4,256,256]{2,1,0:T(8,128)(2,1)S(1)}, u32[]{:S(2)}, u32[]{:S(2)}) %collective-permute-start.16) | collective-permute-done | bytes 524320 | tf_op jit(solution)/shard_map/ppermute | solution.py:351
  68.2 1.8 %collective-permute-start.19 = (bf16[128,256]{1,0:T(8,128)(2,1)S(1)}, bf16[128,256]{1,0:T(8,128)(2,1)S(1)}, u32[]{:S(2)}, u32[]{:S(2)}) collective-permute-start(bf16[128,256]{1,0:T(8,128)(2,1)S(1)} %get-tuple-element.97), channel_id=1, source_target_pairs={{0,6},{1,137},{2,4},{3,139},{4,2},{5,141},{6,0},{7,143},{128,134},... | collective-permute-start | bytes 196616 | tf_op jit(solution)/shard_map/ppermute | solution.py:376
  70.6 2.7 %collective-permute-start.20 = (bf16[256,256]{1,0:T(8,128)(2,1)S(1)}, bf16[256,256]{1,0:T(8,128)(2,1)S(1)}, u32[]{:S(2)}, u32[]{:S(2)}) collective-permute-start(bf16[256,256]{1,0:T(8,128)(2,1)S(1)} %slice_bitcast_fusion.6), channel_id=1, source_target_pairs={{0,32},{16,48},{32,0},{48,16},{64,96},{80,112},{96,64},{112,80},{1... | collective-permute-start | bytes 393224 | tf_op jit(solution)/shard_map/ppermute | solution.py:351
  74.7 3.6 %collective-permute-done.20 = bf16[256,256]{1,0:T(8,128)(2,1)S(1)} collective-permute-done((bf16[256,256]{1,0:T(8,128)(2,1)S(1)}, bf16[256,256]{1,0:T(8,128)(2,1)S(1)}, u32[]{:S(2)}, u32[]{:S(2)}) %collective-permute-start.20) | collective-permute-done | bytes 131104 | tf_op jit(solution)/shard_map/ppermute | solution.py:351
  78.3 3.1 %collective-permute-done.21 = bf16[128,256]{1,0:T(8,128)(2,1)S(1)} collective-permute-done((bf16[128,256]{1,0:T(8,128)(2,1)S(1)}, bf16[128,256]{1,0:T(8,128)(2,1)S(1)}, u32[]{:S(2)}, u32[]{:S(2)}) %collective-permute-start.21) | collective-permute-done | bytes 65568 | tf_op jit(solution)/shard_map/ppermute | solution.py:351
  81.5 3.5 %collective-permute-start.23 = (bf16[128,256]{1,0:T(8,128)(2,1)S(1)}, bf16[128,256]{1,0:T(8,128)(2,1)S(1)}, u32[]{:S(2)}, u32[]{:S(2)}) collective-permute-start(bf16[128,256]{1,0:T(8,128)(2,1)S(1)} %add_convert_fusion.3), channel_id=1, source_target_pairs={{0,64},{16,80},{32,96},{48,112},{64,0},{80,16},{96,32},{112,48},{1... | collective-permute-start | bytes 196616 | tf_op jit(solution)/shard_map/ppermute | solution.py:351
  85.0 2.1 %collective-permute-start.22 = (bf16[128,256]{1,0:T(8,128)(2,1)S(1)}, bf16[128,256]{1,0:T(8,128)(2,1)S(1)}, u32[]{:S(2)}, u32[]{:S(2)}) collective-permute-start(bf16[128,256]{1,0:T(8,128)(2,1)S(1)} %add_convert_fusion.3), channel_id=1, source_target_pairs={{0,32},{16,48},{32,0},{48,16},{64,96},{80,112},{96,64},{112,80},{1... | collective-permute-start | bytes 196616 | tf_op jit(solution)/shard_map/ppermute | solution.py:351
  88.6 2.3 %collective-permute-done.22 = bf16[128,256]{1,0:T(8,128)(2,1)S(1)} collective-permute-done((bf16[128,256]{1,0:T(8,128)(2,1)S(1)}, bf16[128,256]{1,0:T(8,128)(2,1)S(1)}, u32[]{:S(2)}, u32[]{:S(2)}) %collective-permute-start.22) | collective-permute-done | bytes 65568 | tf_op jit(solution)/shard_map/ppermute | solution.py:351
  91.0 2.7 %collective-permute-start.27 = (bf16[128,256]{1,0:T(8,128)(2,1)S(1)}, bf16[128,256]{1,0:T(8,128)(2,1)S(1)}, u32[]{:S(2)}, u32[]{:S(2)}) collective-permute-start(bf16[128,256]{1,0:T(8,128)(2,1)S(1)} %add_convert_fusion.2), channel_id=1, source_target_pairs={{0,6},{1,137},{2,4},{3,139},{4,2},{5,141},{6,0},{7,143},{128,134},... | collective-permute-start | bytes 196616 | tf_op jit(solution)/shard_map/ppermute | solution.py:376
  94.3 3.9 %collective-permute-start.28 = (bf16[256,256]{1,0:T(8,128)(2,1)S(1)}, bf16[256,256]{1,0:T(8,128)(2,1)S(1)}, u32[]{:S(2)}, u32[]{:S(2)}) collective-permute-start(bf16[256,256]{1,0:T(8,128)(2,1)S(1)} %slice_bitcast_fusion.5), channel_id=1, source_target_pairs={{0,96},{16,112},{32,64},{48,80},{64,32},{80,48},{96,0},{112,16},{1... | collective-permute-start | bytes 393224 | tf_op jit(solution)/shard_map/ppermute | solution.py:351
  98.3 2.4 %collective-permute-done.28 = bf16[256,256]{1,0:T(8,128)(2,1)S(1)} collective-permute-done((bf16[256,256]{1,0:T(8,128)(2,1)S(1)}, bf16[256,256]{1,0:T(8,128)(2,1)S(1)}, u32[]{:S(2)}, u32[]{:S(2)}) %collective-permute-start.28) | collective-permute-done | bytes 131104 | tf_op jit(solution)/shard_map/ppermute | solution.py:351
  100.7 1.9 %collective-permute-start.31 = (bf16[4,128,256]{2,1,0:T(8,128)(2,1)S(1)}, bf16[4,128,256]{2,1,0:T(8,128)(2,1)S(1)}, u32[]{:S(2)}, u32[]{:S(2)}) collective-permute-start(bf16[4,128,256]{2,1,0:T(8,128)(2,1)S(1)} %pad_maximum_fusion.1), channel_id=1, source_target_pairs={{0,136},{1,7},{2,138},{3,5},{4,140},{5,3},{6,142},{7,1},{128,8},{1... | collective-permute-start | bytes 786440 | tf_op jit(solution)/shard_map/ppermute | solution.py:376
  103.9 4.4 %collective-permute-start.32 = (bf16[256,256]{1,0:T(8,128)(2,1)S(1)}, bf16[256,256]{1,0:T(8,128)(2,1)S(1)}, u32[]{:S(2)}, u32[]{:S(2)}) collective-permute-start(bf16[256,256]{1,0:T(8,128)(2,1)S(1)} %slice_bitcast_fusion.4), channel_id=1, source_target_pairs={{0,64},{16,80},{32,96},{48,112},{64,0},{80,16},{96,32},{112,48},{1... | collective-permute-start | bytes 393224 | tf_op jit(solution)/shard_map/ppermute | solution.py:351
  108.4 3.4 %collective-permute-done.32 = bf16[256,256]{1,0:T(8,128)(2,1)S(1)} collective-permute-done((bf16[256,256]{1,0:T(8,128)(2,1)S(1)}, bf16[256,256]{1,0:T(8,128)(2,1)S(1)}, u32[]{:S(2)}, u32[]{:S(2)}) %collective-permute-start.32) | collective-permute-done | bytes 131104 | tf_op jit(solution)/shard_map/ppermute | solution.py:351
  111.9 9.2 %collective-permute-start.33 = (bf16[4,4,128,256]{3,2,1,0:T(8,128)(2,1)S(1)}, bf16[4,4,128,256]{3,2,1,0:T(8,128)(2,1)S(1)}, u32[]{:S(2)}, u32[]{:S(2)}) collective-permute-start(bf16[4,4,128,256]{3,2,1,0:T(8,128)(2,1)S(1)} %pad_maximum_fusion.x_ref), channel_id=1, source_target_pairs={{0,1},{1,0},{2,3},{3,2},{4,5},{5,4},{6,7},{7,6},{8,9},{9,8},{10,11... | collective-permute-start | bytes 3145736 | tf_op jit(solution)/shard_map/ppermute | solution.py:351
  (78 shorter events, 26.8 us)
Async XLA Ops:
  2.6 10.1 %collective-permute-start.1 = (bf16[272,256]{1,0:T(8,128)(2,1)}, bf16[272,256]{1,0:T(8,128)(2,1)S(1)}, u32[]{:S(2)}, u32[]{:S(2)}) collective-permute-start(bf16[272,256]{1,0:T(8,128)(2,1)} %get-tuple-element.57.rest_0_), channel_id=1, source_target_pairs={{0,16},{16,32},{32,48},{48,64},{64,80},{80,96},{96,112},{112,0},{1... | collective-permute-start | bytes 417800 | tf_op jit(solution)/shard_map/ppermute | solution.py:359
  5.2 7.6 %collective-permute-start.2 = (bf16[272,256]{1,0:T(8,128)(2,1)}, bf16[272,256]{1,0:T(8,128)(2,1)S(1)}, u32[]{:S(2)}, u32[]{:S(2)}) collective-permute-start(bf16[272,256]{1,0:T(8,128)(2,1)} %get-tuple-element.57.rest_0_), channel_id=1, source_target_pairs={{0,112},{16,0},{32,16},{48,32},{64,48},{80,64},{96,80},{112,96},{1... | collective-permute-start | bytes 417800 | tf_op jit(solution)/shard_map/ppermute | solution.py:359
  9.2 11.3 %collective-permute-start = (bf16[528,256]{1,0:T(8,128)(2,1)}, bf16[528,256]{1,0:T(8,128)(2,1)S(1)}, u32[]{:S(2)}, u32[]{:S(2)}) collective-permute-start(bf16[528,256]{1,0:T(8,128)(2,1)} %get-tuple-element.50.near_ref), channel_id=1, source_target_pairs={{0,128},{128,0},{1,129},{129,1},{2,130},{130,2},{3,131},{131,3},{4... | collective-permute-start | bytes 811016 | tf_op jit(solution)/shard_map/ppermute | solution.py:351
  12.7 5.1 %collective-permute-start.3 = (bf16[272,256]{1,0:T(8,128)(2,1)S(1)}, bf16[272,256]{1,0:T(8,128)(2,1)S(1)}, u32[]{:S(2)}, u32[]{:S(2)}) collective-permute-start(bf16[272,256]{1,0:T(8,128)(2,1)S(1)} %collective-permute-done.1.rest_1_), channel_id=1, source_target_pairs={{0,16},{16,32},{32,48},{48,64},{64,80},{80,96},{96,112},{112,0},{1... | collective-permute-start | bytes 417800 | tf_op jit(solution)/shard_map/ppermute | solution.py:359
  12.7 5.1 %collective-permute-start.4 = (bf16[272,256]{1,0:T(8,128)(2,1)S(1)}, bf16[272,256]{1,0:T(8,128)(2,1)S(1)}, u32[]{:S(2)}, u32[]{:S(2)}) collective-permute-start(bf16[272,256]{1,0:T(8,128)(2,1)S(1)} %collective-permute-done.2.rest_2_), channel_id=1, source_target_pairs={{0,112},{16,0},{32,16},{48,32},{64,48},{80,64},{96,80},{112,96},{1... | collective-permute-start | bytes 417800 | tf_op jit(solution)/shard_map/ppermute | solution.py:359
  17.9 5.1 %collective-permute-start.5 = (bf16[272,256]{1,0:T(8,128)(2,1)S(1)}, bf16[272,256]{1,0:T(8,128)(2,1)S(1)}, u32[]{:S(2)}, u32[]{:S(2)}) collective-permute-start(bf16[272,256]{1,0:T(8,128)(2,1)S(1)} %collective-permute-done.3.rest_3_), channel_id=1, source_target_pairs={{0,16},{16,32},{32,48},{48,64},{64,80},{80,96},{96,112},{112,0},{1... | collective-permute-start | bytes 417800 | tf_op jit(solution)/shard_map/ppermute | solution.py:359
  17.9 5.1 %collective-permute-start.6 = (bf16[272,256]{1,0:T(8,128)(2,1)S(1)}, bf16[272,256]{1,0:T(8,128)(2,1)S(1)}, u32[]{:S(2)}, u32[]{:S(2)}) collective-permute-start(bf16[272,256]{1,0:T(8,128)(2,1)S(1)} %collective-permute-done.4.rest_4_), channel_id=1, source_target_pairs={{0,112},{16,0},{32,16},{48,32},{64,48},{80,64},{96,80},{112,96},{1... | collective-permute-start | bytes 417800 | tf_op jit(solution)/shard_map/ppermute | solution.py:359
  23.0 5.1 %collective-permute-start.7 = (bf16[272,256]{1,0:T(8,128)(2,1)S(1)}, bf16[272,256]{1,0:T(8,128)(2,1)S(1)}, u32[]{:S(2)}, u32[]{:S(2)}) collective-permute-start(bf16[272,256]{1,0:T(8,128)(2,1)S(1)} %collective-permute-done.5.rest_5_), channel_id=1, source_target_pairs={{0,16},{16,32},{32,48},{48,64},{64,80},{80,96},{96,112},{112,0},{1... | collective-permute-start | bytes 417800 | tf_op jit(solution)/shard_map/ppermute | solution.py:359
  29.1 3.9 %collective-permute-start.10 = (f32[8,256]{1,0:T(8,128)S(1)}, f32[8,256]{1,0:T(8,128)S(1)}, u32[]{:S(2)}, u32[]{:S(2)}) collective-permute-start(f32[8,256]{1,0:T(8,128)S(1)} %get-tuple-element.65), channel_id=1, source_target_pairs={{0,112},{16,96},{32,80},{48,64},{64,48},{80,32},{96,16},{112,0},{1... | collective-permute-start | bytes 24584 | tf_op jit(solution)/shard_map/ppermute | solution.py:351
  29.7 4.6 %collective-permute-start.9 = (f32[8,256]{1,0:T(8,128)S(1)}, f32[8,256]{1,0:T(8,128)S(1)}, u32[]{:S(2)}, u32[]{:S(2)}) collective-permute-start(f32[8,256]{1,0:T(8,128)S(1)} %get-tuple-element.65), channel_id=1, source_target_pairs={{0,96},{16,112},{32,64},{48,80},{64,32},{80,48},{96,0},{112,16},{1... | collective-permute-start | bytes 24584 | tf_op jit(solution)/shard_map/ppermute | solution.py:351
  34.4 3.8 %collective-permute-start.11 = (f32[8,256]{1,0:T(8,128)S(1)}, f32[8,256]{1,0:T(8,128)S(1)}, u32[]{:S(2)}, u32[]{:S(2)}) collective-permute-start(f32[8,256]{1,0:T(8,128)S(1)} %add_add_fusion), channel_id=1, source_target_pairs={{0,32},{16,48},{32,0},{48,16},{64,96},{80,112},{96,64},{112,80},{1... | collective-permute-start | bytes 24584 | tf_op jit(solution)/shard_map/ppermute | solution.py:351
  44.0 11.6 %collective-permute-start.12 = (bf16[4,4,128,256]{3,2,1,0:T(8,128)(2,1)S(1)}, bf16[4,4,128,256]{3,2,1,0:T(8,128)(2,1)S(1)}, u32[]{:S(2)}, u32[]{:S(2)}) collective-permute-start(bf16[4,4,128,256]{3,2,1,0:T(8,128)(2,1)S(1)} %backward.3), channel_id=1, source_target_pairs={{0,1},{1,0},{2,3},{3,2},{4,5},{5,4},{6,7},{7,6},{8,9},{9,8},{10,11... | collective-permute-start | bytes 3145736 | tf_op jit(solution)/shard_map/ppermute | solution.py:351
  50.8 13.8 %collective-permute-start.16 = (bf16[4,256,256]{2,1,0:T(8,128)(2,1)S(1)}, bf16[4,256,256]{2,1,0:T(8,128)(2,1)S(1)}, u32[]{:S(2)}, u32[]{:S(2)}) collective-permute-start(bf16[4,256,256]{2,1,0:T(8,128)(2,1)S(1)} %get-tuple-element.74), channel_id=1, source_target_pairs={{0,16},{16,0},{32,48},{48,32},{64,80},{80,64},{96,112},{112,96},{1... | collective-permute-start | bytes 1572872 | tf_op jit(solution)/shard_map/ppermute | solution.py:351
  56.1 8.6 %collective-permute-start.13 = (bf16[4,128,256]{2,1,0:T(8,128)(2,1)S(1)}, bf16[4,128,256]{2,1,0:T(8,128)(2,1)S(1)}, u32[]{:S(2)}, u32[]{:S(2)}) collective-permute-start(bf16[4,128,256]{2,1,0:T(8,128)(2,1)S(1)} %get-tuple-element.93), channel_id=1, source_target_pairs={{0,128},{1,3},{2,130},{3,1},{4,132},{5,7},{6,134},{7,5},{128,0},{1... | collective-permute-start | bytes 786440 | tf_op jit(solution)/shard_map/ppermute | solution.py:376
  57.5 8.0 %collective-permute-start.15 = (bf16[4,128,256]{2,1,0:T(8,128)(2,1)S(1)}, bf16[4,128,256]{2,1,0:T(8,128)(2,1)S(1)}, u32[]{:S(2)}, u32[]{:S(2)}) collective-permute-start(bf16[4,128,256]{2,1,0:T(8,128)(2,1)S(1)} %get-tuple-element.94), channel_id=1, source_target_pairs={{0,136},{1,7},{2,138},{3,5},{4,140},{5,3},{6,142},{7,1},{128,8},{1... | collective-permute-start | bytes 786440 | tf_op jit(solution)/shard_map/ppermute | solution.py:376
  59.4 7.6 %collective-permute-start.14 = (bf16[4,128,256]{2,1,0:T(8,128)(2,1)S(1)}, bf16[4,128,256]{2,1,0:T(8,128)(2,1)S(1)}, u32[]{:S(2)}, u32[]{:S(2)}) collective-permute-start(bf16[4,128,256]{2,1,0:T(8,128)(2,1)S(1)} %get-tuple-element.95), channel_id=1, source_target_pairs={{0,8},{1,5},{2,10},{3,7},{4,12},{5,1},{6,14},{7,3},{128,136},{129,... | collective-permute-start | bytes 786440 | tf_op jit(solution)/shard_map/ppermute | solution.py:376
  67.1 6.3 %collective-permute-start.17 = (bf16[128,256]{1,0:T(8,128)(2,1)S(1)}, bf16[128,256]{1,0:T(8,128)(2,1)S(1)}, u32[]{:S(2)}, u32[]{:S(2)}) collective-permute-start(bf16[128,256]{1,0:T(8,128)(2,1)S(1)} %get-tuple-element.96), channel_id=1, source_target_pairs={{0,2},{1,129},{2,0},{3,131},{4,6},{5,133},{6,4},{7,135},{128,130},... | collective-permute-start | bytes 196616 | tf_op jit(solution)/shard_map/ppermute | solution.py:376
  68.2 5.2 %collective-permute-start.19 = (bf16[128,256]{1,0:T(8,128)(2,1)S(1)}, bf16[128,256]{1,0:T(8,128)(2,1)S(1)}, u32[]{:S(2)}, u32[]{:S(2)}) collective-permute-start(bf16[128,256]{1,0:T(8,128)(2,1)S(1)} %get-tuple-element.97), channel_id=1, source_target_pairs={{0,6},{1,137},{2,4},{3,139},{4,2},{5,141},{6,0},{7,143},{128,134},... | collective-permute-start | bytes 196616 | tf_op jit(solution)/shard_map/ppermute | solution.py:376
  70.0 4.6 %collective-permute-start.18 = (bf16[128,256]{1,0:T(8,128)(2,1)S(1)}, bf16[128,256]{1,0:T(8,128)(2,1)S(1)}, u32[]{:S(2)}, u32[]{:S(2)}) collective-permute-start(bf16[128,256]{1,0:T(8,128)(2,1)S(1)} %get-tuple-element.98), channel_id=1, source_target_pairs={{0,4},{1,9},{2,6},{3,11},{4,0},{5,13},{6,2},{7,15},{128,132},{129,... | collective-permute-start | bytes 196616 | tf_op jit(solution)/shard_map/ppermute | solution.py:376
  70.6 7.6 %collective-permute-start.20 = (bf16[256,256]{1,0:T(8,128)(2,1)S(1)}, bf16[256,256]{1,0:T(8,128)(2,1)S(1)}, u32[]{:S(2)}, u32[]{:S(2)}) collective-permute-start(bf16[256,256]{1,0:T(8,128)(2,1)S(1)} %slice_bitcast_fusion.6), channel_id=1, source_target_pairs={{0,32},{16,48},{32,0},{48,16},{64,96},{80,112},{96,64},{112,80},{1... | collective-permute-start | bytes 393224 | tf_op jit(solution)/shard_map/ppermute | solution.py:351
  81.4 5.7 %collective-permute-start.24 = (bf16[128,256]{1,0:T(8,128)(2,1)S(1)}, bf16[128,256]{1,0:T(8,128)(2,1)S(1)}, u32[]{:S(2)}, u32[]{:S(2)}) collective-permute-start(bf16[128,256]{1,0:T(8,128)(2,1)S(1)} %add_convert_fusion.3), channel_id=1, source_target_pairs={{0,96},{16,112},{32,64},{48,80},{64,32},{80,48},{96,0},{112,16},{1... | collective-permute-start | bytes 196616 | tf_op jit(solution)/shard_map/ppermute | solution.py:351
  81.5 7.1 %collective-permute-start.23 = (bf16[128,256]{1,0:T(8,128)(2,1)S(1)}, bf16[128,256]{1,0:T(8,128)(2,1)S(1)}, u32[]{:S(2)}, u32[]{:S(2)}) collective-permute-start(bf16[128,256]{1,0:T(8,128)(2,1)S(1)} %add_convert_fusion.3), channel_id=1, source_target_pairs={{0,64},{16,80},{32,96},{48,112},{64,0},{80,16},{96,32},{112,48},{1... | collective-permute-start | bytes 196616 | tf_op jit(solution)/shard_map/ppermute | solution.py:351
  85.0 5.9 %collective-permute-start.22 = (bf16[128,256]{1,0:T(8,128)(2,1)S(1)}, bf16[128,256]{1,0:T(8,128)(2,1)S(1)}, u32[]{:S(2)}, u32[]{:S(2)}) collective-permute-start(bf16[128,256]{1,0:T(8,128)(2,1)S(1)} %add_convert_fusion.3), channel_id=1, source_target_pairs={{0,32},{16,48},{32,0},{48,16},{64,96},{80,112},{96,64},{112,80},{1... | collective-permute-start | bytes 196616 | tf_op jit(solution)/shard_map/ppermute | solution.py:351
  91.0 7.2 %collective-permute-start.27 = (bf16[128,256]{1,0:T(8,128)(2,1)S(1)}, bf16[128,256]{1,0:T(8,128)(2,1)S(1)}, u32[]{:S(2)}, u32[]{:S(2)}) collective-permute-start(bf16[128,256]{1,0:T(8,128)(2,1)S(1)} %add_convert_fusion.2), channel_id=1, source_target_pairs={{0,6},{1,137},{2,4},{3,139},{4,2},{5,141},{6,0},{7,143},{128,134},... | collective-permute-start | bytes 196616 | tf_op jit(solution)/shard_map/ppermute | solution.py:376
  93.6 4.6 %collective-permute-start.26 = (bf16[128,256]{1,0:T(8,128)(2,1)S(1)}, bf16[128,256]{1,0:T(8,128)(2,1)S(1)}, u32[]{:S(2)}, u32[]{:S(2)}) collective-permute-start(bf16[128,256]{1,0:T(8,128)(2,1)S(1)} %add_convert_fusion.2), channel_id=1, source_target_pairs={{0,4},{1,9},{2,6},{3,11},{4,0},{5,13},{6,2},{7,15},{128,132},{129,... | collective-permute-start | bytes 196616 | tf_op jit(solution)/shard_map/ppermute | solution.py:376
  94.0 4.2 %collective-permute-start.25 = (bf16[128,256]{1,0:T(8,128)(2,1)S(1)}, bf16[128,256]{1,0:T(8,128)(2,1)S(1)}, u32[]{:S(2)}, u32[]{:S(2)}) collective-permute-start(bf16[128,256]{1,0:T(8,128)(2,1)S(1)} %add_convert_fusion.2), channel_id=1, source_target_pairs={{0,2},{1,129},{2,0},{3,131},{4,6},{5,133},{6,4},{7,135},{128,130},... | collective-permute-start | bytes 196616 | tf_op jit(solution)/shard_map/ppermute | solution.py:376
  94.3 6.3 %collective-permute-start.28 = (bf16[256,256]{1,0:T(8,128)(2,1)S(1)}, bf16[256,256]{1,0:T(8,128)(2,1)S(1)}, u32[]{:S(2)}, u32[]{:S(2)}) collective-permute-start(bf16[256,256]{1,0:T(8,128)(2,1)S(1)} %slice_bitcast_fusion.5), channel_id=1, source_target_pairs={{0,96},{16,112},{32,64},{48,80},{64,32},{80,48},{96,0},{112,16},{1... | collective-permute-start | bytes 393224 | tf_op jit(solution)/shard_map/ppermute | solution.py:351
  100.7 11.1 %collective-permute-start.31 = (bf16[4,128,256]{2,1,0:T(8,128)(2,1)S(1)}, bf16[4,128,256]{2,1,0:T(8,128)(2,1)S(1)}, u32[]{:S(2)}, u32[]{:S(2)}) collective-permute-start(bf16[4,128,256]{2,1,0:T(8,128)(2,1)S(1)} %pad_maximum_fusion.1), channel_id=1, source_target_pairs={{0,136},{1,7},{2,138},{3,5},{4,140},{5,3},{6,142},{7,1},{128,8},{1... | collective-permute-start | bytes 786440 | tf_op jit(solution)/shard_map/ppermute | solution.py:376
  102.6 9.2 %collective-permute-start.30 = (bf16[4,128,256]{2,1,0:T(8,128)(2,1)S(1)}, bf16[4,128,256]{2,1,0:T(8,128)(2,1)S(1)}, u32[]{:S(2)}, u32[]{:S(2)}) collective-permute-start(bf16[4,128,256]{2,1,0:T(8,128)(2,1)S(1)} %pad_maximum_fusion.1), channel_id=1, source_target_pairs={{0,8},{1,5},{2,10},{3,7},{4,12},{5,1},{6,14},{7,3},{128,136},{129,... | collective-permute-start | bytes 786440 | tf_op jit(solution)/shard_map/ppermute | solution.py:376
  102.6 9.2 %collective-permute-start.29 = (bf16[4,128,256]{2,1,0:T(8,128)(2,1)S(1)}, bf16[4,128,256]{2,1,0:T(8,128)(2,1)S(1)}, u32[]{:S(2)}, u32[]{:S(2)}) collective-permute-start(bf16[4,128,256]{2,1,0:T(8,128)(2,1)S(1)} %pad_maximum_fusion.1), channel_id=1, source_target_pairs={{0,128},{1,3},{2,130},{3,1},{4,132},{5,7},{6,134},{7,5},{128,0},{1... | collective-permute-start | bytes 786440 | tf_op jit(solution)/shard_map/ppermute | solution.py:376
  103.9 7.8 %collective-permute-start.32 = (bf16[256,256]{1,0:T(8,128)(2,1)S(1)}, bf16[256,256]{1,0:T(8,128)(2,1)S(1)}, u32[]{:S(2)}, u32[]{:S(2)}) collective-permute-start(bf16[256,256]{1,0:T(8,128)(2,1)S(1)} %slice_bitcast_fusion.4), channel_id=1, source_target_pairs={{0,64},{16,80},{32,96},{48,112},{64,0},{80,16},{96,32},{112,48},{1... | collective-permute-start | bytes 393224 | tf_op jit(solution)/shard_map/ppermute | solution.py:351
  111.9 11.4 %collective-permute-start.33 = (bf16[4,4,128,256]{3,2,1,0:T(8,128)(2,1)S(1)}, bf16[4,4,128,256]{3,2,1,0:T(8,128)(2,1)S(1)}, u32[]{:S(2)}, u32[]{:S(2)}) collective-permute-start(bf16[4,4,128,256]{3,2,1,0:T(8,128)(2,1)S(1)} %pad_maximum_fusion.x_ref), channel_id=1, source_target_pairs={{0,1},{1,0},{2,3},{3,2},{4,5},{5,4},{6,7},{7,6},{8,9},{9,8},{10,11... | collective-permute-start | bytes 3145736 | tf_op jit(solution)/shard_map/ppermute | solution.py:351
  (9 other events, 70.6 us)

commit v8 on v7

--- a/solution.py
+++ b/solution.py
@@ -18,6 +18,7 @@
 TILE = 256
 CHUNKS = H // TILE
 NZ = 8
+ORDER = (3, 2, 1)
 OFFSETS = (0, -1, 1, -2, 2, -3, 3, 4)
 FIRST = 7
 VMEM_LIMIT = 24 * 1024 * 1024
@@ -271,7 +272,7 @@
 
 def order():
     core = lax.axis_index("core")
-    xx, y = lax.axis_index("x_hi") * 2 + lax.axis_index("x_lo"), lax.axis_index("y")
+    xx, y = near(lax.axis_index("x_hi") * 2 + lax.axis_index("x_lo")), near(lax.axis_index("y"))
     return core, jnp.where(core == 0, xx, y), jnp.where(core == 0, y, xx)
 
 
@@ -363,13 +364,17 @@
     return (((x_lo * 8 + z) * 2 + x_hi) * 4 + y) * 2 + core
 
 
+def near(place):
+    return place ^ (place >> 1)
+
+
 def plane_swap(x, k, x_core):
     pairs = []
     for z in range(8):
         for xx in range(4):
             for y in range(4):
                 for core in range(2):
-                    to_x, to_y = (xx ^ k, y) if core == x_core else (xx, y ^ k)
+                    to_x, to_y = (near(near(xx) ^ k), y) if core == x_core else (xx, near(near(y) ^ k))
                     pairs.append(
                         (device(xx & 1, z, xx >> 1, y, core), device(to_x & 1, z, to_x >> 1, to_y, core))
                     )
@@ -390,24 +395,26 @@
     return x
 
 
+def gathered(x, x_core, *beside):
+    got = {k: plane_swap(x, k, x_core) for k in (1, 2, 3)}
+    if beside:
+        got, beside = lax.optimization_barrier((got, beside))
+    got = jnp.stack([x] + [got[k] for k in (1, 2, 3)])
+    return (got, *beside) if beside else got
+
+
 def all_reduce(mine, theirs, keep, send):
     half = add(mine, swap(theirs, "core", 1)).astype(BF)
-    quarter = add(half[0], *[plane_swap(half[k], k, 0) for k in (1, 2, 3)]).astype(BF)
+    quarter = add(half[0], *[plane_swap(half[k], k, 0) for k in ORDER]).astype(BF)
     keep = add(keep, swap(send, "z", 1)).astype(BF)
     quarter, keep = lax.optimization_barrier((quarter, keep))
-    part = add(quarter[0], *[plane_swap(quarter[k], k, 1) for k in (1, 2, 3)])
-    user_2 = swap(keep[2], "z", 2)
-    part, user_2 = lax.optimization_barrier((part, user_2))
-    part = sum_over_z(part, ((1,), (2, 4, 6)), BF).astype(BF)
+    part = add(quarter[0], *[plane_swap(quarter[k], k, 1) for k in ORDER])
+    part = sum_over_z(part, ((1, 6, 7), (2,)), BF).astype(BF)
     part, keep = lax.optimization_barrier((part, keep))
-    quarter = jnp.stack([part] + [plane_swap(part, k, 1) for k in (1, 2, 3)])
-    user_6 = swap(keep[3], "z", 6)
-    quarter, user_6, keep = lax.optimization_barrier((quarter, user_6, keep))
-    others = [plane_swap(quarter, k, 0) for k in (1, 2, 3)]
-    user_4 = swap(keep[1], "z", 4)
-    others, user_4 = lax.optimization_barrier((others, user_4))
-    half = jnp.stack([quarter] + others)
-    return half, swap(half, "core", 1), add(keep[0], user_2, user_4, user_6)
+    quarter = gathered(part, 1)
+    user = add(keep[0], *[swap(keep[i], "z", k) for i, k in ((1, 4), (2, 2), (3, 6))])
+    half, user = gathered(quarter, 0, user)
+    return half, swap(half, "core", 1), user
 
 
 def on_device(user_emb, pos_feat, pos_id, neg_feat, neg_id, neg_bucket, logq_table, w_in, w_out):

time: 125 us -> 119 us (0.952); the launches traced: 125 us -> 118 us
  starting transfers between devices: 67.6 us -> 63.2 us
  waiting for transfers between devices: 32.9 us -> 30 us
    ppermute x15, waiting for transfers between devices: 23.9 us -> 12.2 us  [swap(): lax.ppermute(x, axis, [(i, i ^ k) for i in range(SIZES[AXES.index(axis)])])]
    ppermute x12, waiting for transfers between devices: 3.54 us -> 12.3 us  [plane_swap(): return lax.ppermute(x, AXES, pairs)]
    ppermute x15, starting transfers between devices: 41.5 us -> 33.9 us  [swap(): lax.ppermute(x, axis, [(i, i ^ k) for i in range(SIZES[AXES.index(axis)])])]
    ppermute x12, starting transfers between devices: 14.1 us -> 17.4 us  [plane_swap(): return lax.ppermute(x, AXES, pairs)]
  transfers between devices with their start and end apart: 34 -> 34, of which waited for: 17 -> 19; matrix products, arithmetic and copies ran while one was open for 1% -> 1% of each run, Pallas kernels for 9% -> 10%
where the time goes in v8:
time: 119 us; the launch traced here: 118 us
  starting transfers between devices  63.2 us (53%)
  waiting for transfers between devices  30 us (25%)
  Pallas kernels  21.6 us (18%)
  other arithmetic  1.72 us (1%)
    ppermute x15, starting transfers between devices, swap(): lax.ppermute(x, axis, [(i, i ^ k) for i in range(SIZES[AXES.index(axis)])])  33.9 us
    ppermute x12, starting transfers between devices, plane_swap(): return lax.ppermute(x, AXES, pairs)  17.4 us
    ppermute x12, waiting for transfers between devices, plane_swap(): return lax.ppermute(x, AXES, pairs)  12.3 us
    ppermute x15, waiting for transfers between devices, swap(): lax.ppermute(x, axis, [(i, i ^ k) for i in range(SIZES[AXES.index(axis)])])  12.2 us
    ppermute x7, starting transfers between devices, shift(): return lax.ppermute(x, 'z', [(i, (i + by) % NZ) for i in range(NZ)])  11.9 us
    pallas_call x5, Pallas kernels, in_vmem(): pl.pallas_call(kernel, in_specs=[vm] * len(args), out_specs=[vm] * len(ou...  10 us
    ppermute x7, waiting for transfers between devices, shift(): return lax.ppermute(x, 'z', [(i, (i + by) % NZ) for i in range(NZ)])  5.45 us
    pallas_call x2, Pallas kernels, score(): pl.pallas_call(functools.partial(score_kernel, ks), in_specs=[vm] * (7 +...  4.06 us
  transfers between devices with their start and end apart: 34, of which 19 were waited for; matrix products, arithmetic and copies ran while one was open for 1% of the time, Pallas kernels for 10%

profile of v8, /device:TPU:1, one launch (start us, length us, event | category | flops | bytes accessed | tf_op | source)
XLA Modules:
  0.0 117.6 jit_solution(15446085751561182070)
XLA Ops:
  0.7 2.0 %pack.1 = (bf16[272,256]{1,0:T(8,128)(2,1)}, bf16[528,256]{1,0:T(8,128)(2,1)}) custom-call(bf16[256,256]{1,0:T(8,128)(2,1)} %user_hbm.1, s32[1,256]{1,0:T(1,128)} %bitcast.52, bf16[512,256]{1,0:T(8,128)(2,1)} %feat_hbm.1, s32[1,512]{1,0:T(1,128)} %bitcast.50, s32[1,512]{1,0:T(1,128)} %bitcast.51), custom_call_target="tpu_custom_call" | custom-call | flops 10000000000 | bytes 1000000 | tf_op jit(solution)/shard_map/pack/pallas_call | solution.py:83
  2.6 2.5 %collective-permute-start.1 = (bf16[272,256]{1,0:T(8,128)(2,1)}, bf16[272,256]{1,0:T(8,128)(2,1)S(1)}, u32[]{:S(2)}, u32[]{:S(2)}) collective-permute-start(bf16[272,256]{1,0:T(8,128)(2,1)} %get-tuple-element.52.rest_0_), channel_id=1, source_target_pairs={{0,16},{16,32},{32,48},{48,64},{64,80},{80,96},{96,112},{112,0},{1... | collective-permute-start | bytes 417800 | tf_op jit(solution)/shard_map/ppermute | solution.py:360
  5.2 4.0 %collective-permute-start.2 = (bf16[272,256]{1,0:T(8,128)(2,1)}, bf16[272,256]{1,0:T(8,128)(2,1)S(1)}, u32[]{:S(2)}, u32[]{:S(2)}) collective-permute-start(bf16[272,256]{1,0:T(8,128)(2,1)} %get-tuple-element.52.rest_0_), channel_id=1, source_target_pairs={{0,112},{16,0},{32,16},{48,32},{64,48},{80,64},{96,80},{112,96},{1... | collective-permute-start | bytes 417800 | tf_op jit(solution)/shard_map/ppermute | solution.py:360
  12.7 2.7 %collective-permute-start.4 = (bf16[272,256]{1,0:T(8,128)(2,1)S(1)}, bf16[272,256]{1,0:T(8,128)(2,1)S(1)}, u32[]{:S(2)}, u32[]{:S(2)}) collective-permute-start(bf16[272,256]{1,0:T(8,128)(2,1)S(1)} %collective-permute-done.2.rest_2_), channel_id=1, source_target_pairs={{0,112},{16,0},{32,16},{48,32},{64,48},{80,64},{96,80},{112,96},{1... | collective-permute-start | bytes 417800 | tf_op jit(solution)/shard_map/ppermute | solution.py:360
  17.9 2.7 %collective-permute-start.6 = (bf16[272,256]{1,0:T(8,128)(2,1)S(1)}, bf16[272,256]{1,0:T(8,128)(2,1)S(1)}, u32[]{:S(2)}, u32[]{:S(2)}) collective-permute-start(bf16[272,256]{1,0:T(8,128)(2,1)S(1)} %collective-permute-done.4.rest_4_), channel_id=1, source_target_pairs={{0,112},{16,0},{32,16},{48,32},{64,48},{80,64},{96,80},{112,96},{1... | collective-permute-start | bytes 417800 | tf_op jit(solution)/shard_map/ppermute | solution.py:360
  20.5 1.7 %far.1 = (bf16[512,2048]{1,0:T(8,128)(2,1)S(1)}, bf16[512,256]{1,0:T(8,128)(2,1)S(1)}, f32[1024,128]{1,0:T(8,128)S(1)}, f32[1024,128]{1,0:T(8,128)S(1)}) custom-call(bf16[528,256]{1,0:T(8,128)(2,1)S(1)} %copy-done.2, bf16[528,256]{1,0:T(8,128)(2,1)S(1)} %collective-permute-done.far_ref, bf16[256,2048]{1,0:T(8,128)(2,1)S(1)} %get-tuple-element.46.w_in_ref, ...), custom_call_target="tpu_custom_call" | custom-call | flops 1073741824 | bytes 4000000 | tf_op jit(solution)/shard_map/far/pallas_call | solution.py:141
  23.0 3.0 %score.2 = (f32[8,256]{1,0:T(8,128)S(1)}, f32[8,256]{1,0:T(8,128)S(1)}, f32[1,256]{1,0:T(1,128)S(1)}, bf16[1024,1792]{1,0:T(8,128)(2,1)S(1)}) custom-call(bf16[512,256]{1,0:T(8,128)(2,1)S(1)} %get-tuple-element.44.near_emb, bf16[512,256]{1,0:T(8,128)(2,1)S(1)} %get-tuple-element.48.far_emb, f32[1024,128]{1,0:T(8,128)S(1)} %get-tuple-element.49.nid_ref, ...), custom_call_target="tpu_custom_call" | custom-call | flops 939524096 | bytes 5000000 | tf_op jit(solution)/shard_map/score/pallas_call | solution.py:198
  26.0 2.1 %collective-permute-done.7.rest_0_.rest_7_ = bf16[272,256]{1,0:T(8,128)(2,1)S(1)} collective-permute-done((bf16[272,256]{1,0:T(8,128)(2,1)S(1)}, bf16[272,256]{1,0:T(8,128)(2,1)S(1)}, u32[]{:S(2)}, u32[]{:S(2)}) %collective-permute-start.7) | collective-permute-done | bytes 139296 | tf_op jit(solution)/shard_map/ppermute | solution.py:360
  31.2 1.8 %collective-permute-start.8 = (f32[8,256]{1,0:T(8,128)S(1)}, f32[8,256]{1,0:T(8,128)S(1)}, u32[]{:S(2)}, u32[]{:S(2)}) collective-permute-start(f32[8,256]{1,0:T(8,128)S(1)} %get-tuple-element.60), channel_id=1, source_target_pairs={{0,16},{16,0},{32,48},{48,32},{64,80},{80,64},{96,112},{112,96},{1... | collective-permute-start | bytes 24584 | tf_op jit(solution)/shard_map/ppermute | solution.py:352
  34.4 2.0 %collective-permute-start.11 = (f32[8,256]{1,0:T(8,128)S(1)}, f32[8,256]{1,0:T(8,128)S(1)}, u32[]{:S(2)}, u32[]{:S(2)}) collective-permute-start(f32[8,256]{1,0:T(8,128)S(1)} %add_add_fusion), channel_id=1, source_target_pairs={{0,32},{16,48},{32,0},{48,16},{64,96},{80,112},{96,64},{112,80},{1... | collective-permute-start | bytes 24584 | tf_op jit(solution)/shard_map/ppermute | solution.py:352
  36.4 1.7 %collective-permute-done.11 = f32[8,256]{1,0:T(8,128)S(1)} collective-permute-done((f32[8,256]{1,0:T(8,128)S(1)}, f32[8,256]{1,0:T(8,128)S(1)}, u32[]{:S(2)}, u32[]{:S(2)}) %collective-permute-start.11) | collective-permute-done | bytes 8224 | tf_op jit(solution)/shard_map/ppermute | solution.py:352
  38.2 2.7 %grads.1 = (bf16[4,256,256]{2,1,0:T(8,128)(2,1)S(1)}, bf16[4,256,256]{2,1,0:T(8,128)(2,1)S(1)}, bf16[1280,256]{1,0:T(8,128)(2,1)S(1)}, f32[256,256]{1,0:T(8,128)S(1)}) custom-call(f32[8,256]{1,0:T(8,128)S(1)} %add.63.tot_ref, f32[8,256]{1,0:T(8,128)S(1)} %get-tuple-element.61.tloc_ref, f32[1,256]{1,0:T(1,128)S(1)} %get-tuple-element.62.pexp_ref, ...), custom_call_target="tpu_custom_call" | custom-call | flops 2147483648 | bytes 8000000 | tf_op jit(solution)/shard_map/grads/pallas_call | solution.py:252
  40.9 3.1 %backward.3 = bf16[4,4,128,256]{3,2,1,0:T(8,128)(2,1)S(1)} custom-call(bf16[1280,256]{1,0:T(8,128)(2,1)S(1)} %get-tuple-element.65.g_ref, bf16[768,256]{1,0:T(8,128)(2,1)S(1)} %get-tuple-element.66.feat_ref, bf16[528,256]{1,0:T(8,128)(2,1)S(1)} %collective-permute-done.far_ref, bf16[2048,256]{1,0:T(8,128)(2,1)S(1)} %get-tuple-element.47.w_out_ref, ...), custom_call_target="tpu_custom_call" | custom-call | flops 2013265920 | bytes 4000000 | tf_op jit(solution)/shard_map/backward/pallas_call | solution.py:141
  44.1 6.7 %collective-permute-start.12 = (bf16[4,4,128,256]{3,2,1,0:T(8,128)(2,1)S(1)}, bf16[4,4,128,256]{3,2,1,0:T(8,128)(2,1)S(1)}, u32[]{:S(2)}, u32[]{:S(2)}) collective-permute-start(bf16[4,4,128,256]{3,2,1,0:T(8,128)(2,1)S(1)} %backward.3), channel_id=1, source_target_pairs={{0,1},{1,0},{2,3},{3,2},{4,5},{5,4},{6,7},{7,6},{8,9},{9,8},{10,11... | collective-permute-start | bytes 3145736 | tf_op jit(solution)/shard_map/ppermute | solution.py:352
  50.8 1.7 %collective-permute-start.16 = (bf16[4,256,256]{2,1,0:T(8,128)(2,1)S(1)}, bf16[4,256,256]{2,1,0:T(8,128)(2,1)S(1)}, u32[]{:S(2)}, u32[]{:S(2)}) collective-permute-start(bf16[4,256,256]{2,1,0:T(8,128)(2,1)S(1)} %get-tuple-element.69), channel_id=1, source_target_pairs={{0,16},{16,0},{32,48},{48,32},{64,80},{80,64},{96,112},{112,96},{1... | collective-permute-start | bytes 1572872 | tf_op jit(solution)/shard_map/ppermute | solution.py:352
  52.5 3.1 %backward.2 = bf16[4,4,128,256]{3,2,1,0:T(8,128)(2,1)S(1)} custom-call(bf16[1280,256]{1,0:T(8,128)(2,1)S(1)} %get-tuple-element.65.g_ref, bf16[768,256]{1,0:T(8,128)(2,1)S(1)} %get-tuple-element.66.feat_ref, bf16[528,256]{1,0:T(8,128)(2,1)S(1)} %collective-permute-done.far_ref, bf16[2048,256]{1,0:T(8,128)(2,1)S(1)} %get-tuple-element.47.w_out_ref, ...), custom_call_target="tpu_custom_call" | custom-call | flops 2013265920 | bytes 4000000 | tf_op jit(solution)/shard_map/backward/pallas_call | solution.py:141
  56.1 3.0 %collective-permute-start.13 = (bf16[4,128,256]{2,1,0:T(8,128)(2,1)S(1)}, bf16[4,128,256]{2,1,0:T(8,128)(2,1)S(1)}, u32[]{:S(2)}, u32[]{:S(2)}) collective-permute-start(bf16[4,128,256]{2,1,0:T(8,128)(2,1)S(1)} %get-tuple-element.83), channel_id=1, source_target_pairs={{0,8},{1,5},{2,10},{3,7},{4,12},{5,1},{6,14},{7,3},{128,136},{129,... | collective-permute-start | bytes 786440 | tf_op jit(solution)/shard_map/ppermute | solution.py:381
  59.9 4.7 %collective-permute-done.16 = bf16[4,256,256]{2,1,0:T(8,128)(2,1)S(1)} collective-permute-done((bf16[4,256,256]{2,1,0:T(8,128)(2,1)S(1)}, bf16[4,256,256]{2,1,0:T(8,128)(2,1)S(1)}, u32[]{:S(2)}, u32[]{:S(2)}) %collective-permute-start.16) | collective-permute-done | bytes 524320 | tf_op jit(solution)/shard_map/ppermute | solution.py:352
  64.7 1.7 %collective-permute-done.15 = bf16[4,128,256]{2,1,0:T(8,128)(2,1)S(1)} collective-permute-done((bf16[4,128,256]{2,1,0:T(8,128)(2,1)S(1)}, bf16[4,128,256]{2,1,0:T(8,128)(2,1)S(1)}, u32[]{:S(2)}, u32[]{:S(2)}) %collective-permute-start.15) | collective-permute-done | bytes 262176 | tf_op jit(solution)/shard_map/ppermute | solution.py:381
  66.6 2.8 %collective-permute-start.17 = (bf16[128,256]{1,0:T(8,128)(2,1)S(1)}, bf16[128,256]{1,0:T(8,128)(2,1)S(1)}, u32[]{:S(2)}, u32[]{:S(2)}) collective-permute-start(bf16[128,256]{1,0:T(8,128)(2,1)S(1)} %get-tuple-element.91), channel_id=1, source_target_pairs={{0,4},{1,9},{2,6},{3,11},{4,0},{5,13},{6,2},{7,15},{128,132},{129,... | collective-permute-start | bytes 196616 | tf_op jit(solution)/shard_map/ppermute | solution.py:381
  71.3 1.5 %collective-permute-done.19 = bf16[128,256]{1,0:T(8,128)(2,1)S(1)} collective-permute-done((bf16[128,256]{1,0:T(8,128)(2,1)S(1)}, bf16[128,256]{1,0:T(8,128)(2,1)S(1)}, u32[]{:S(2)}, u32[]{:S(2)}) %collective-permute-start.19) | collective-permute-done | bytes 65568 | tf_op jit(solution)/shard_map/ppermute | solution.py:381
  74.8 2.6 %collective-permute-start.21 = (bf16[128,256]{1,0:T(8,128)(2,1)S(1)}, bf16[128,256]{1,0:T(8,128)(2,1)S(1)}, u32[]{:S(2)}, u32[]{:S(2)}) collective-permute-start(bf16[128,256]{1,0:T(8,128)(2,1)S(1)} %fusion.7), channel_id=1, source_target_pairs={{0,96},{16,112},{32,64},{48,80},{64,32},{80,48},{96,0},{112,16},{1... | collective-permute-start | bytes 196616 | tf_op jit(solution)/shard_map/ppermute | solution.py:352
  78.5 1.5 %collective-permute-done.21 = bf16[128,256]{1,0:T(8,128)(2,1)S(1)} collective-permute-done((bf16[128,256]{1,0:T(8,128)(2,1)S(1)}, bf16[128,256]{1,0:T(8,128)(2,1)S(1)}, u32[]{:S(2)}, u32[]{:S(2)}) %collective-permute-start.21) | collective-permute-done | bytes 65568 | tf_op jit(solution)/shard_map/ppermute | solution.py:352
  80.6 4.3 %collective-permute-start.23 = (bf16[128,256]{1,0:T(8,128)(2,1)S(1)}, bf16[128,256]{1,0:T(8,128)(2,1)S(1)}, u32[]{:S(2)}, u32[]{:S(2)}) collective-permute-start(bf16[128,256]{1,0:T(8,128)(2,1)S(1)} %add_convert_fusion.3), channel_id=1, source_target_pairs={{0,32},{16,48},{32,0},{48,16},{64,96},{80,112},{96,64},{112,80},{1... | collective-permute-start | bytes 196616 | tf_op jit(solution)/shard_map/ppermute | solution.py:352
  84.9 1.7 %collective-permute-done.23 = bf16[128,256]{1,0:T(8,128)(2,1)S(1)} collective-permute-done((bf16[128,256]{1,0:T(8,128)(2,1)S(1)}, bf16[128,256]{1,0:T(8,128)(2,1)S(1)}, u32[]{:S(2)}, u32[]{:S(2)}) %collective-permute-start.23) | collective-permute-done | bytes 65568 | tf_op jit(solution)/shard_map/ppermute | solution.py:352
  87.9 1.7 %collective-permute-start.25 = (bf16[128,256]{1,0:T(8,128)(2,1)S(1)}, bf16[128,256]{1,0:T(8,128)(2,1)S(1)}, u32[]{:S(2)}, u32[]{:S(2)}) collective-permute-start(bf16[128,256]{1,0:T(8,128)(2,1)S(1)} %add_convert_fusion.2), channel_id=1, source_target_pairs={{0,6},{1,137},{2,4},{3,139},{4,2},{5,141},{6,0},{7,143},{128,134},... | collective-permute-start | bytes 196616 | tf_op jit(solution)/shard_map/ppermute | solution.py:381
  89.6 2.2 %collective-permute-start.30 = (bf16[256,256]{1,0:T(8,128)(2,1)S(1)}, bf16[256,256]{1,0:T(8,128)(2,1)S(1)}, u32[]{:S(2)}, u32[]{:S(2)}) collective-permute-start(bf16[256,256]{1,0:T(8,128)(2,1)S(1)} %get-tuple-element.86), channel_id=1, source_target_pairs={{0,64},{16,80},{32,96},{48,112},{64,0},{80,16},{96,32},{112,48},{1... | collective-permute-start | bytes 393224 | tf_op jit(solution)/shard_map/ppermute | solution.py:352
  91.8 3.4 %collective-permute-start.32 = (bf16[256,256]{1,0:T(8,128)(2,1)S(1)}, bf16[256,256]{1,0:T(8,128)(2,1)S(1)}, u32[]{:S(2)}, u32[]{:S(2)}) collective-permute-start(bf16[256,256]{1,0:T(8,128)(2,1)S(1)} %get-tuple-element.87), channel_id=1, source_target_pairs={{0,96},{16,112},{32,64},{48,80},{64,32},{80,48},{96,0},{112,16},{1... | collective-permute-start | bytes 393224 | tf_op jit(solution)/shard_map/ppermute | solution.py:352
  95.4 5.2 %collective-permute-start.29 = (bf16[4,128,256]{2,1,0:T(8,128)(2,1)S(1)}, bf16[4,128,256]{2,1,0:T(8,128)(2,1)S(1)}, u32[]{:S(2)}, u32[]{:S(2)}) collective-permute-start(bf16[4,128,256]{2,1,0:T(8,128)(2,1)S(1)} %get-tuple-element.90), channel_id=1, source_target_pairs={{0,8},{1,5},{2,10},{3,7},{4,12},{5,1},{6,14},{7,3},{128,136},{129,... | collective-permute-start | bytes 786440 | tf_op jit(solution)/shard_map/ppermute | solution.py:381
  102.5 2.1 %collective-permute-done.29 = bf16[4,128,256]{2,1,0:T(8,128)(2,1)S(1)} collective-permute-done((bf16[4,128,256]{2,1,0:T(8,128)(2,1)S(1)}, bf16[4,128,256]{2,1,0:T(8,128)(2,1)S(1)}, u32[]{:S(2)}, u32[]{:S(2)}) %collective-permute-start.29) | collective-permute-done | bytes 262176 | tf_op jit(solution)/shard_map/ppermute | solution.py:381
  104.6 3.4 %collective-permute-done.28 = bf16[4,128,256]{2,1,0:T(8,128)(2,1)S(1)} collective-permute-done((bf16[4,128,256]{2,1,0:T(8,128)(2,1)S(1)}, bf16[4,128,256]{2,1,0:T(8,128)(2,1)S(1)}, u32[]{:S(2)}, u32[]{:S(2)}) %collective-permute-start.28) | collective-permute-done | bytes 262176 | tf_op jit(solution)/shard_map/ppermute | solution.py:381
  109.4 4.3 %collective-permute-start.33 = (bf16[4,4,128,256]{3,2,1,0:T(8,128)(2,1)S(1)}, bf16[4,4,128,256]{3,2,1,0:T(8,128)(2,1)S(1)}, u32[]{:S(2)}, u32[]{:S(2)}) collective-permute-start(bf16[4,4,128,256]{3,2,1,0:T(8,128)(2,1)S(1)} %pad_maximum_fusion.x_ref), channel_id=1, source_target_pairs={{0,1},{1,0},{2,3},{3,2},{4,5},{5,4},{6,7},{7,6},{8,9},{9,8},{10,11... | collective-permute-start | bytes 3145736 | tf_op jit(solution)/shard_map/ppermute | solution.py:352
  (77 shorter events, 26.7 us)
Async XLA Ops:
  2.6 10.1 %collective-permute-start.1 = (bf16[272,256]{1,0:T(8,128)(2,1)}, bf16[272,256]{1,0:T(8,128)(2,1)S(1)}, u32[]{:S(2)}, u32[]{:S(2)}) collective-permute-start(bf16[272,256]{1,0:T(8,128)(2,1)} %get-tuple-element.52.rest_0_), channel_id=1, source_target_pairs={{0,16},{16,32},{32,48},{48,64},{64,80},{80,96},{96,112},{112,0},{1... | collective-permute-start | bytes 417800 | tf_op jit(solution)/shard_map/ppermute | solution.py:360
  5.2 7.6 %collective-permute-start.2 = (bf16[272,256]{1,0:T(8,128)(2,1)}, bf16[272,256]{1,0:T(8,128)(2,1)S(1)}, u32[]{:S(2)}, u32[]{:S(2)}) collective-permute-start(bf16[272,256]{1,0:T(8,128)(2,1)} %get-tuple-element.52.rest_0_), channel_id=1, source_target_pairs={{0,112},{16,0},{32,16},{48,32},{64,48},{80,64},{96,80},{112,96},{1... | collective-permute-start | bytes 417800 | tf_op jit(solution)/shard_map/ppermute | solution.py:360
  9.2 11.3 %collective-permute-start = (bf16[528,256]{1,0:T(8,128)(2,1)}, bf16[528,256]{1,0:T(8,128)(2,1)S(1)}, u32[]{:S(2)}, u32[]{:S(2)}) collective-permute-start(bf16[528,256]{1,0:T(8,128)(2,1)} %get-tuple-element.45.near_ref), channel_id=1, source_target_pairs={{0,128},{128,0},{1,129},{129,1},{2,130},{130,2},{3,131},{131,3},{4... | collective-permute-start | bytes 811016 | tf_op jit(solution)/shard_map/ppermute | solution.py:352
  12.7 5.1 %collective-permute-start.3 = (bf16[272,256]{1,0:T(8,128)(2,1)S(1)}, bf16[272,256]{1,0:T(8,128)(2,1)S(1)}, u32[]{:S(2)}, u32[]{:S(2)}) collective-permute-start(bf16[272,256]{1,0:T(8,128)(2,1)S(1)} %collective-permute-done.1.rest_1_), channel_id=1, source_target_pairs={{0,16},{16,32},{32,48},{48,64},{64,80},{80,96},{96,112},{112,0},{1... | collective-permute-start | bytes 417800 | tf_op jit(solution)/shard_map/ppermute | solution.py:360
  12.7 5.1 %collective-permute-start.4 = (bf16[272,256]{1,0:T(8,128)(2,1)S(1)}, bf16[272,256]{1,0:T(8,128)(2,1)S(1)}, u32[]{:S(2)}, u32[]{:S(2)}) collective-permute-start(bf16[272,256]{1,0:T(8,128)(2,1)S(1)} %collective-permute-done.2.rest_2_), channel_id=1, source_target_pairs={{0,112},{16,0},{32,16},{48,32},{64,48},{80,64},{96,80},{112,96},{1... | collective-permute-start | bytes 417800 | tf_op jit(solution)/shard_map/ppermute | solution.py:360
  17.9 5.1 %collective-permute-start.5 = (bf16[272,256]{1,0:T(8,128)(2,1)S(1)}, bf16[272,256]{1,0:T(8,128)(2,1)S(1)}, u32[]{:S(2)}, u32[]{:S(2)}) collective-permute-start(bf16[272,256]{1,0:T(8,128)(2,1)S(1)} %collective-permute-done.3.rest_3_), channel_id=1, source_target_pairs={{0,16},{16,32},{32,48},{48,64},{64,80},{80,96},{96,112},{112,0},{1... | collective-permute-start | bytes 417800 | tf_op jit(solution)/shard_map/ppermute | solution.py:360
  17.9 5.1 %collective-permute-start.6 = (bf16[272,256]{1,0:T(8,128)(2,1)S(1)}, bf16[272,256]{1,0:T(8,128)(2,1)S(1)}, u32[]{:S(2)}, u32[]{:S(2)}) collective-permute-start(bf16[272,256]{1,0:T(8,128)(2,1)S(1)} %collective-permute-done.4.rest_4_), channel_id=1, source_target_pairs={{0,112},{16,0},{32,16},{48,32},{64,48},{80,64},{96,80},{112,96},{1... | collective-permute-start | bytes 417800 | tf_op jit(solution)/shard_map/ppermute | solution.py:360
  23.0 5.1 %collective-permute-start.7 = (bf16[272,256]{1,0:T(8,128)(2,1)S(1)}, bf16[272,256]{1,0:T(8,128)(2,1)S(1)}, u32[]{:S(2)}, u32[]{:S(2)}) collective-permute-start(bf16[272,256]{1,0:T(8,128)(2,1)S(1)} %collective-permute-done.5.rest_5_), channel_id=1, source_target_pairs={{0,16},{16,32},{32,48},{48,64},{64,80},{80,96},{96,112},{112,0},{1... | collective-permute-start | bytes 417800 | tf_op jit(solution)/shard_map/ppermute | solution.py:360
  29.1 3.9 %collective-permute-start.10 = (f32[8,256]{1,0:T(8,128)S(1)}, f32[8,256]{1,0:T(8,128)S(1)}, u32[]{:S(2)}, u32[]{:S(2)}) collective-permute-start(f32[8,256]{1,0:T(8,128)S(1)} %get-tuple-element.60), channel_id=1, source_target_pairs={{0,112},{16,96},{32,80},{48,64},{64,48},{80,32},{96,16},{112,0},{1... | collective-permute-start | bytes 24584 | tf_op jit(solution)/shard_map/ppermute | solution.py:352
  29.7 4.6 %collective-permute-start.9 = (f32[8,256]{1,0:T(8,128)S(1)}, f32[8,256]{1,0:T(8,128)S(1)}, u32[]{:S(2)}, u32[]{:S(2)}) collective-permute-start(f32[8,256]{1,0:T(8,128)S(1)} %get-tuple-element.60), channel_id=1, source_target_pairs={{0,96},{16,112},{32,64},{48,80},{64,32},{80,48},{96,0},{112,16},{1... | collective-permute-start | bytes 24584 | tf_op jit(solution)/shard_map/ppermute | solution.py:352
  34.4 3.8 %collective-permute-start.11 = (f32[8,256]{1,0:T(8,128)S(1)}, f32[8,256]{1,0:T(8,128)S(1)}, u32[]{:S(2)}, u32[]{:S(2)}) collective-permute-start(f32[8,256]{1,0:T(8,128)S(1)} %add_add_fusion), channel_id=1, source_target_pairs={{0,32},{16,48},{32,0},{48,16},{64,96},{80,112},{96,64},{112,80},{1... | collective-permute-start | bytes 24584 | tf_op jit(solution)/shard_map/ppermute | solution.py:352
  44.1 11.6 %collective-permute-start.12 = (bf16[4,4,128,256]{3,2,1,0:T(8,128)(2,1)S(1)}, bf16[4,4,128,256]{3,2,1,0:T(8,128)(2,1)S(1)}, u32[]{:S(2)}, u32[]{:S(2)}) collective-permute-start(bf16[4,4,128,256]{3,2,1,0:T(8,128)(2,1)S(1)} %backward.3), channel_id=1, source_target_pairs={{0,1},{1,0},{2,3},{3,2},{4,5},{5,4},{6,7},{7,6},{8,9},{9,8},{10,11... | collective-permute-start | bytes 3145736 | tf_op jit(solution)/shard_map/ppermute | solution.py:352
  50.8 13.8 %collective-permute-start.16 = (bf16[4,256,256]{2,1,0:T(8,128)(2,1)S(1)}, bf16[4,256,256]{2,1,0:T(8,128)(2,1)S(1)}, u32[]{:S(2)}, u32[]{:S(2)}) collective-permute-start(bf16[4,256,256]{2,1,0:T(8,128)(2,1)S(1)} %get-tuple-element.69), channel_id=1, source_target_pairs={{0,16},{16,0},{32,48},{48,32},{64,80},{80,64},{96,112},{112,96},{1... | collective-permute-start | bytes 1572872 | tf_op jit(solution)/shard_map/ppermute | solution.py:352
  56.1 8.6 %collective-permute-start.13 = (bf16[4,128,256]{2,1,0:T(8,128)(2,1)S(1)}, bf16[4,128,256]{2,1,0:T(8,128)(2,1)S(1)}, u32[]{:S(2)}, u32[]{:S(2)}) collective-permute-start(bf16[4,128,256]{2,1,0:T(8,128)(2,1)S(1)} %get-tuple-element.83), channel_id=1, source_target_pairs={{0,8},{1,5},{2,10},{3,7},{4,12},{5,1},{6,14},{7,3},{128,136},{129,... | collective-permute-start | bytes 786440 | tf_op jit(solution)/shard_map/ppermute | solution.py:381
  59.1 7.3 %collective-permute-start.15 = (bf16[4,128,256]{2,1,0:T(8,128)(2,1)S(1)}, bf16[4,128,256]{2,1,0:T(8,128)(2,1)S(1)}, u32[]{:S(2)}, u32[]{:S(2)}) collective-permute-start(bf16[4,128,256]{2,1,0:T(8,128)(2,1)S(1)} %get-tuple-element.84), channel_id=1, source_target_pairs={{0,128},{1,3},{2,130},{3,1},{4,132},{5,7},{6,134},{7,5},{128,0},{1... | collective-permute-start | bytes 786440 | tf_op jit(solution)/shard_map/ppermute | solution.py:381
  59.5 6.9 %collective-permute-start.14 = (bf16[4,128,256]{2,1,0:T(8,128)(2,1)S(1)}, bf16[4,128,256]{2,1,0:T(8,128)(2,1)S(1)}, u32[]{:S(2)}, u32[]{:S(2)}) collective-permute-start(bf16[4,128,256]{2,1,0:T(8,128)(2,1)S(1)} %get-tuple-element.85), channel_id=1, source_target_pairs={{0,136},{1,7},{2,138},{3,5},{4,140},{5,3},{6,142},{7,1},{128,8},{1... | collective-permute-start | bytes 786440 | tf_op jit(solution)/shard_map/ppermute | solution.py:381
  66.6 4.7 %collective-permute-start.17 = (bf16[128,256]{1,0:T(8,128)(2,1)S(1)}, bf16[128,256]{1,0:T(8,128)(2,1)S(1)}, u32[]{:S(2)}, u32[]{:S(2)}) collective-permute-start(bf16[128,256]{1,0:T(8,128)(2,1)S(1)} %get-tuple-element.91), channel_id=1, source_target_pairs={{0,4},{1,9},{2,6},{3,11},{4,0},{5,13},{6,2},{7,15},{128,132},{129,... | collective-permute-start | bytes 196616 | tf_op jit(solution)/shard_map/ppermute | solution.py:381
  69.4 3.4 %collective-permute-start.19 = (bf16[128,256]{1,0:T(8,128)(2,1)S(1)}, bf16[128,256]{1,0:T(8,128)(2,1)S(1)}, u32[]{:S(2)}, u32[]{:S(2)}) collective-permute-start(bf16[128,256]{1,0:T(8,128)(2,1)S(1)} %get-tuple-element.92), channel_id=1, source_target_pairs={{0,2},{1,129},{2,0},{3,131},{4,6},{5,133},{6,4},{7,135},{128,130},... | collective-permute-start | bytes 196616 | tf_op jit(solution)/shard_map/ppermute | solution.py:381
  69.7 4.3 %collective-permute-start.18 = (bf16[128,256]{1,0:T(8,128)(2,1)S(1)}, bf16[128,256]{1,0:T(8,128)(2,1)S(1)}, u32[]{:S(2)}, u32[]{:S(2)}) collective-permute-start(bf16[128,256]{1,0:T(8,128)(2,1)S(1)} %get-tuple-element.93), channel_id=1, source_target_pairs={{0,6},{1,137},{2,4},{3,139},{4,2},{5,141},{6,0},{7,143},{128,134},... | collective-permute-start | bytes 196616 | tf_op jit(solution)/shard_map/ppermute | solution.py:381
  74.1 4.4 %collective-permute-start.22 = (bf16[128,256]{1,0:T(8,128)(2,1)S(1)}, bf16[128,256]{1,0:T(8,128)(2,1)S(1)}, u32[]{:S(2)}, u32[]{:S(2)}) collective-permute-start(bf16[128,256]{1,0:T(8,128)(2,1)S(1)} %fusion.7), channel_id=1, source_target_pairs={{0,112},{16,96},{32,80},{48,64},{64,48},{80,32},{96,16},{112,0},{1... | collective-permute-start | bytes 196616 | tf_op jit(solution)/shard_map/ppermute | solution.py:352
  74.8 5.2 %collective-permute-start.21 = (bf16[128,256]{1,0:T(8,128)(2,1)S(1)}, bf16[128,256]{1,0:T(8,128)(2,1)S(1)}, u32[]{:S(2)}, u32[]{:S(2)}) collective-permute-start(bf16[128,256]{1,0:T(8,128)(2,1)S(1)} %fusion.7), channel_id=1, source_target_pairs={{0,96},{16,112},{32,64},{48,80},{64,32},{80,48},{96,0},{112,16},{1... | collective-permute-start | bytes 196616 | tf_op jit(solution)/shard_map/ppermute | solution.py:352
  80.6 6.0 %collective-permute-start.23 = (bf16[128,256]{1,0:T(8,128)(2,1)S(1)}, bf16[128,256]{1,0:T(8,128)(2,1)S(1)}, u32[]{:S(2)}, u32[]{:S(2)}) collective-permute-start(bf16[128,256]{1,0:T(8,128)(2,1)S(1)} %add_convert_fusion.3), channel_id=1, source_target_pairs={{0,32},{16,48},{32,0},{48,16},{64,96},{80,112},{96,64},{112,80},{1... | collective-permute-start | bytes 196616 | tf_op jit(solution)/shard_map/ppermute | solution.py:352
  86.6 8.5 %collective-permute-start.26 = (bf16[128,256]{1,0:T(8,128)(2,1)S(1)}, bf16[128,256]{1,0:T(8,128)(2,1)S(1)}, u32[]{:S(2)}, u32[]{:S(2)}) collective-permute-start(bf16[128,256]{1,0:T(8,128)(2,1)S(1)} %add_convert_fusion.2), channel_id=1, source_target_pairs={{0,4},{1,9},{2,6},{3,11},{4,0},{5,13},{6,2},{7,15},{128,132},{129,... | collective-permute-start | bytes 196616 | tf_op jit(solution)/shard_map/ppermute | solution.py:381
  87.9 7.4 %collective-permute-start.25 = (bf16[128,256]{1,0:T(8,128)(2,1)S(1)}, bf16[128,256]{1,0:T(8,128)(2,1)S(1)}, u32[]{:S(2)}, u32[]{:S(2)}) collective-permute-start(bf16[128,256]{1,0:T(8,128)(2,1)S(1)} %add_convert_fusion.2), channel_id=1, source_target_pairs={{0,6},{1,137},{2,4},{3,139},{4,2},{5,141},{6,0},{7,143},{128,134},... | collective-permute-start | bytes 196616 | tf_op jit(solution)/shard_map/ppermute | solution.py:381
  89.6 5.8 %collective-permute-start.24 = (bf16[128,256]{1,0:T(8,128)(2,1)S(1)}, bf16[128,256]{1,0:T(8,128)(2,1)S(1)}, u32[]{:S(2)}, u32[]{:S(2)}) collective-permute-start(bf16[128,256]{1,0:T(8,128)(2,1)S(1)} %add_convert_fusion.2), channel_id=1, source_target_pairs={{0,2},{1,129},{2,0},{3,131},{4,6},{5,133},{6,4},{7,135},{128,130},... | collective-permute-start | bytes 196616 | tf_op jit(solution)/shard_map/ppermute | solution.py:381
  89.6 12.3 %collective-permute-start.30 = (bf16[256,256]{1,0:T(8,128)(2,1)S(1)}, bf16[256,256]{1,0:T(8,128)(2,1)S(1)}, u32[]{:S(2)}, u32[]{:S(2)}) collective-permute-start(bf16[256,256]{1,0:T(8,128)(2,1)S(1)} %get-tuple-element.86), channel_id=1, source_target_pairs={{0,64},{16,80},{32,96},{48,112},{64,0},{80,16},{96,32},{112,48},{1... | collective-permute-start | bytes 393224 | tf_op jit(solution)/shard_map/ppermute | solution.py:352
  91.8 10.6 %collective-permute-start.32 = (bf16[256,256]{1,0:T(8,128)(2,1)S(1)}, bf16[256,256]{1,0:T(8,128)(2,1)S(1)}, u32[]{:S(2)}, u32[]{:S(2)}) collective-permute-start(bf16[256,256]{1,0:T(8,128)(2,1)S(1)} %get-tuple-element.87), channel_id=1, source_target_pairs={{0,96},{16,112},{32,64},{48,80},{64,32},{80,48},{96,0},{112,16},{1... | collective-permute-start | bytes 393224 | tf_op jit(solution)/shard_map/ppermute | solution.py:352
  95.2 7.2 %collective-permute-start.31 = (bf16[256,256]{1,0:T(8,128)(2,1)S(1)}, bf16[256,256]{1,0:T(8,128)(2,1)S(1)}, u32[]{:S(2)}, u32[]{:S(2)}) collective-permute-start(bf16[256,256]{1,0:T(8,128)(2,1)S(1)} %get-tuple-element.88), channel_id=1, source_target_pairs={{0,32},{16,48},{32,0},{48,16},{64,96},{80,112},{96,64},{112,80},{1... | collective-permute-start | bytes 393224 | tf_op jit(solution)/shard_map/ppermute | solution.py:352
  95.4 9.2 %collective-permute-start.29 = (bf16[4,128,256]{2,1,0:T(8,128)(2,1)S(1)}, bf16[4,128,256]{2,1,0:T(8,128)(2,1)S(1)}, u32[]{:S(2)}, u32[]{:S(2)}) collective-permute-start(bf16[4,128,256]{2,1,0:T(8,128)(2,1)S(1)} %get-tuple-element.90), channel_id=1, source_target_pairs={{0,8},{1,5},{2,10},{3,7},{4,12},{5,1},{6,14},{7,3},{128,136},{129,... | collective-permute-start | bytes 786440 | tf_op jit(solution)/shard_map/ppermute | solution.py:381
  100.6 7.5 %collective-permute-start.28 = (bf16[4,128,256]{2,1,0:T(8,128)(2,1)S(1)}, bf16[4,128,256]{2,1,0:T(8,128)(2,1)S(1)}, u32[]{:S(2)}, u32[]{:S(2)}) collective-permute-start(bf16[4,128,256]{2,1,0:T(8,128)(2,1)S(1)} %get-tuple-element.90), channel_id=1, source_target_pairs={{0,136},{1,7},{2,138},{3,5},{4,140},{5,3},{6,142},{7,1},{128,8},{1... | collective-permute-start | bytes 786440 | tf_op jit(solution)/shard_map/ppermute | solution.py:381
  101.9 7.4 %collective-permute-start.27 = (bf16[4,128,256]{2,1,0:T(8,128)(2,1)S(1)}, bf16[4,128,256]{2,1,0:T(8,128)(2,1)S(1)}, u32[]{:S(2)}, u32[]{:S(2)}) collective-permute-start(bf16[4,128,256]{2,1,0:T(8,128)(2,1)S(1)} %get-tuple-element.90), channel_id=1, source_target_pairs={{0,128},{1,3},{2,130},{3,1},{4,132},{5,7},{6,134},{7,5},{128,0},{1... | collective-permute-start | bytes 786440 | tf_op jit(solution)/shard_map/ppermute | solution.py:381
  109.4 6.6 %collective-permute-start.33 = (bf16[4,4,128,256]{3,2,1,0:T(8,128)(2,1)S(1)}, bf16[4,4,128,256]{3,2,1,0:T(8,128)(2,1)S(1)}, u32[]{:S(2)}, u32[]{:S(2)}) collective-permute-start(bf16[4,4,128,256]{3,2,1,0:T(8,128)(2,1)S(1)} %pad_maximum_fusion.x_ref), channel_id=1, source_target_pairs={{0,1},{1,0},{2,3},{3,2},{4,5},{5,4},{6,7},{7,6},{8,9},{9,8},{10,11... | collective-permute-start | bytes 3145736 | tf_op jit(solution)/shard_map/ppermute | solution.py:352
  (9 other events, 70.6 us)
